TPU v7x, 32 devices: a whole 2x2x4 slice. The times are simulated.
32 devices in a mesh: space: 8 (over y, x, core), chan: 4 (over z).
Axes of the slice: x: 2, y: 2, z: 4, core: 2. Of those that a mesh axis runs over, the one named last changes fastest.
Arguments:
- volume: bfloat16 [128, 32, 16, 128], P('chan', 'space'), may hold values from -6 to 6
- kernel: bfloat16 [128, 3, 3, 3, 128], P('chan'), may hold values from -0.109375 to 0.109375
- upstream: bfloat16 [128, 8, 4, 32], P('chan', 'space'), may hold values from -24 to 24
Outputs:
- pooled: bfloat16 [128, 8, 4, 32], P('chan', 'space')
- volume_grad: bfloat16 [128, 32, 16, 128], P('chan', 'space')
- kernel_grad: float32 [128, 3, 3, 3, 128], P('chan')
All inputs are finite; a program needn't handle non-finite values.
Results may differ from a plain program's by a relative error of at most 0.013.
Values may be sent and summed in bfloat16 or wider, within the bound.
No kernel may reach another device: no remote copies, remote signals or barrier semaphores. Data moves between devices by JAX's collectives and lax.ppermute only.
A program may use at most 64 MiB of HBM per device.

v0:
```python
import jax
import jax.numpy as jnp
from jax import lax
from jax.sharding import PartitionSpec as P

slope_neg = 0.3
tap_table = ((1, 0, 0), (2, 1, 0), (0, 1, 1))


def from_behind(block, axis, distance):
    devices = range(lax.axis_size(axis))
    route = [(i - distance, i) for i in devices if i - distance in devices]
    return lax.ppermute(block, axis, route)


def strided_conv(operand, filters):
    return lax.conv_general_dilated(
        operand[None],
        filters,
        (2, 2, 2),
        ((0, 0), (1, 1), (1, 1)),
        dimension_numbers=("NCDHW", "IDHWO", "NCDHW"),
        preferred_element_type=jnp.float32,
    )[0]


def on_device(volume, kernel, upstream):
    in_block = volume.shape[0]
    out_block = upstream.shape[0]
    out_depth = volume.shape[1] // 2
    out_rows = volume.shape[2] // 2
    out_cols = volume.shape[3] // 2
    lower_rim = from_behind(volume[:, -1:], "space", 1)
    padded = jnp.concatenate([lower_rim, volume], axis=1)
    own_first = lax.axis_index("chan") * out_block
    empty = jnp.zeros((out_block, out_depth, out_rows, out_cols), jnp.float32)
    columns = lax.dynamic_slice_in_dim(
        lax.all_gather(kernel, "chan", axis=0, tiled=True), own_first, out_block, 4
    )
    pre = empty + strided_conv(lax.all_gather(padded, "chan", axis=0, tiled=True), columns)
    activated = jnp.where(pre > 0, pre, slope_neg * pre)
    block_shape = (out_block, out_depth // 2, 2, out_rows // 2, 2, out_cols // 2, 2)
    pooled = jnp.mean(activated.reshape(block_shape), axis=(2, 4, 6)).astype(jnp.bfloat16)
    spread = upstream.astype(jnp.float32) * 0.125
    spread = jnp.broadcast_to(spread[:, :, None, :, None, :, None], block_shape).reshape(pre.shape)
    pre_grad = (spread * jnp.where(pre > 0, 1.0, slope_neg)).astype(jnp.bfloat16)
    upper_rim = from_behind(pre_grad[:, :1], "space", -1)
    extended = jnp.concatenate([pre_grad, upper_rim], axis=1)
    panel = lax.all_gather(extended, "chan", axis=0, tiled=True)
    offset = jnp.int32(0)
    phase_grad = jnp.zeros((2, 2, 2, in_block, out_depth, out_rows, out_cols), jnp.float32)
    weight_grad = jnp.zeros((in_block, 3, 3, 3, kernel.shape[4]), jnp.float32)
    columns = lax.dynamic_slice_in_dim(kernel, offset, panel.shape[0], 4)
    grad_pad = jnp.pad(panel, ((0, 0), (0, 0), (0, 1), (0, 1)))
    phase_sums = {}
    for depth_tap, depth_par, depth_off in tap_table:
        for row_tap, row_par, row_off in tap_table:
            for col_tap, col_par, col_off in tap_table:
                shifted = grad_pad[
                    :,
                    depth_off : depth_off + out_depth,
                    row_off : row_off + out_rows,
                    col_off : col_off + out_cols,
                ]
                term = jnp.einsum(
                    "co,ozyx->czyx",
                    columns[:, depth_tap, row_tap, col_tap, :],
                    shifted,
                    preferred_element_type=jnp.float32,
                )
                phase_key = (depth_par, row_par, col_par)
                if phase_key in phase_sums:
                    phase_sums[phase_key] = phase_sums[phase_key] + term
                else:
                    phase_sums[phase_key] = term
    stacked = jnp.stack(
        [
            phase_sums[first, second, third]
            for first in (0, 1)
            for second in (0, 1)
            for third in (0, 1)
        ]
    )
    phase_grad = stacked.reshape(phase_grad.shape)
    weight_part = lax.conv_general_dilated(
        padded[None],
        panel[:, :out_depth][None],
        (1, 1, 1),
        ((0, 0), (1, 0), (1, 0)),
        rhs_dilation=(2, 2, 2),
        dimension_numbers=("CNDHW", "IODHW", "NDHWC"),
        preferred_element_type=jnp.float32,
    )
    weight_grad = lax.dynamic_update_slice_in_dim(weight_grad, weight_part, offset, 4)
    phase_grad, weight_grad = (phase_grad, weight_grad)
    input_grad = phase_grad.transpose(3, 4, 0, 5, 1, 6, 2).reshape(volume.shape)
    kernel_grad = lax.psum(weight_grad, "space")
    return (pooled, input_grad.astype(jnp.bfloat16), kernel_grad)


def solution(mesh):
    return jax.shard_map(
        on_device,
        mesh=mesh,
        in_specs=(
            P("chan", "space", None, None),
            P("chan", None, None, None, None),
            P("chan", "space", None, None),
        ),
        out_specs=(
            P("chan", "space", None, None),
            P("chan", "space", None, None),
            P("chan", None, None, None, None),
        ),
        check_vma=False,
    )
```

profile of v0, /device:TPU:0, one launch (start us, length us, event | category | flops | bytes accessed | tf_op | source)
XLA Modules:
  0.0 203.9 jit_solution(17295172723243483448)
XLA Ops:
  8.1 2.4 %collective-permute-start = (bf16[32,1,16,128]{3,2,1,0:T(8,128)(2,1)S(1)}, bf16[32,1,16,128]{3,2,1,0:T(8,128)(2,1)S(1)}, u32[]{:S(2)}, u32[]{:S(2)}) collective-permute-start(bf16[32,1,16,128]{3,2,1,0:T(8,128)(2,1)S(1)} %slice.133), channel_id=1, source_target_pairs={{0,4},{4,8},{8,12},{12,16},{16,20},{20,24},{24,28},{1,5},{5,9},{9,... | collective-permute-start | bytes 393224 | tf_op jit(solution)/shard_map/ppermute | solution.py:13
  10.5 1.0 collective-permute-done
  11.5 1.1 constant_dynamic-update-slice_fusion
  15.1 24.7 %all_gather.10 = bf16[128,3,3,3,128]{4,0,3,2,1:T(8,128)(2,1)S(1)} all-gather(bf16[32,3,3,3,128]{4,0,3,2,1:T(8,128)(2,1)} %param.4), channel_id=1, replica_groups=mesh['space'=8,'chan'=4] {'chan'}, dimensions={0}, use_global_device_ids=true | all-gather | bytes 1105920 | tf_op jit(solution)/shard_map/all_gather | solution.py:38
  39.8 8.5 %copy.53 = bf16[1,32,5,16,128]{1,0,4,3,2:T(2,128)(2,1)} copy(bf16[1,32,5,16,128]{4,3,2,1,0:T(8,128)(2,1)} %bitcast.287) | data formatting | bytes 1310720 | tf_op jit(solution)/shard_map/broadcast_in_dim | solution.py:86
  48.3 31.2 %all-gather.2.cloned.1.call-done = bf16[128,5,16,128]{3,2,1,0:T(8,128)(2,1)} async-done(((bf16[32,5,16,128]{3,2,1,0:T(8,128)(2,1)}), bf16[128,5,16,128]{3,2,1,0:T(8,128)(2,1)}) %all-gather.2.cloned.1.call-update) | async-done | bytes 2621456 | tf_op jit(solution)/shard_map/all_gather | solution.py:40
  79.5 4.6 %copy.41 = bf16[128,5,16,128]{0,2,3,1:T(8,128)(2,1)S(1)} copy(bf16[128,5,16,128]{3,2,1,0:T(8,128)(2,1)} %all-gather.2.cloned.1.call-done) | data formatting | bytes 5242880 | tf_op jit(solution)/shard_map/all_gather | solution.py:40
  84.6 1.1 copy.43
  85.9 2.3 %compare_select_fusion = (f32[2,8,8,9,32]{4,2,3,1,0:T(8,128)S(1)}, f32[2,8,8,9,32]{4,2,3,1,0:T(8,128)S(1)}) fusion(bf16[128,3,3,3,128]{4,0,3,2,1:T(8,128)(2,1)S(1)} %all_gather.10, s32[]{:T(128)S(6)} %select_n.16, bf16[128,5,16,1,7,2]{0,4,5,2,1,3:T(8,128)(2,1)S(1)} %slice.173, bf16[128,5,16,1,8,18]{0,4,5,2,1,3:T(8,128)(2,1)S(1)} %copy.43, ...), kind=kOutput, calls=%fused_computation.55 | convolution fusion | flops 254201856 | bytes 4415564 | tf_op jit(solution)/shard_map/conv_general_dilated | solution.py:17
  88.5 1.4 collective-permute-start.1
  92.3 18.5 %all_gather.11 = bf16[128,3,8,64]{3,2,1,0:T(8,128)(2,1)S(1)} all-gather(bf16[32,3,8,64]{3,2,1,0:T(8,128)(2,1)S(1)} %copy.48), channel_id=1, replica_groups=mesh['space'=8,'chan'=4] {'chan'}, dimensions={0}, use_global_device_ids=true | all-gather | bytes 491520 | tf_op jit(solution)/shard_map/all_gather | solution.py:49
  111.3 1.0 fusion.73
  112.9 1.1 fusion.75
  115.3 1.1 fusion.46
  118.8 1.0 convolution_add_fusion.5
  119.8 1.1 fusion.13
  120.9 1.0 convolution_add_fusion.12
  121.9 1.0 fusion.12
  122.9 1.0 convolution_add_fusion.11
  123.9 13.8 %fusion.43 = f32[32,3,3,3,128]{4,0,3,2,1:T(8,128)} fusion(bf16[1,32,5,16,128]{1,0,4,3,2:T(2,128)(2,1)} %copy.53, bf16[1,128,2,8,64]{1,4,3,2,0:T(8,128)(2,1)} %slice_bitcast_fusion.1), kind=kOutput, calls=%fused_computation.60 | convolution fusion | flops 215924736 | bytes 1359872 | tf_op jit(solution)/shard_map/conv_general_dilated | solution.py:85
  137.8 1.4 fusion.16
  139.2 1.1 fusion.35
  140.2 1.1 fusion.33
  141.3 1.0 fusion.39
  142.3 1.1 fusion.31
  143.4 1.3 fusion.29
  144.7 1.1 fusion.27
  145.8 1.0 fusion.37
  146.8 1.5 copy.52
  148.4 1.8 copy.56
  150.1 45.1 %all-reduce.3.cloned.1.call-done = f32[32,3,3,3,128]{4,0,3,2,1:T(8,128)} async-done(((f32[32,3,3,3,128]{4,0,3,2,1:T(8,128)}), f32[32,3,3,3,128]{4,0,3,2,1:T(8,128)}) %all-reduce.3.cloned.1.call-update) | async-done | bytes 442384 | tf_op jit(solution)/shard_map/psum | solution.py:97
  195.3 1.8 copy.96
  (43 shorter events, 11.4 us)
Async XLA Ops:
  7.2 72.3 %all-gather.2.cloned.1.call-start = ((), (), s32[]{:S(2)}) async-start(), calls=%async_computation | async-start | bytes 3276800 | tf_op jit(solution)/shard_map/all_gather | solution.py:40
  8.1 3.3 %collective-permute-start = (bf16[32,1,16,128]{3,2,1,0:T(8,128)(2,1)S(1)}, bf16[32,1,16,128]{3,2,1,0:T(8,128)(2,1)S(1)}, u32[]{:S(2)}, u32[]{:S(2)}) collective-permute-start(bf16[32,1,16,128]{3,2,1,0:T(8,128)(2,1)S(1)} %slice.133), channel_id=1, source_target_pairs={{0,4},{4,8},{8,12},{12,16},{16,20},{20,24},{24,28},{1,5},{5,9},{9,... | collective-permute-start | bytes 393224 | tf_op jit(solution)/shard_map/ppermute | solution.py:13
  12.6 0.9 copy-start
  13.5 181.8 %all-reduce.3.cloned.1.call-start = ((), (), s32[]{:S(2)}) async-start(), calls=%async_computation.1 | async-start | bytes 884736 | tf_op jit(solution)/shard_map/psum | solution.py:97
  84.6 1.3 copy-start.3
  85.9 2.5 %copy-start.2 = (f32[32,4,32]{0,1,2:T(4,128)S(1)}, f32[32,4,32]{0,1,2:T(4,128)}, u32[]{:S(2)}) copy-start(f32[32,4,32]{0,1,2:T(4,128)} %copy.46) | copy-start | bytes 49156
  88.5 22.8 %copy-start.1 = (bf16[32,3,3,3,128]{4,0,3,2,1:T(8,128)(2,1)S(1)}, bf16[32,3,3,3,128]{4,0,3,2,1:T(8,128)(2,1)}, u32[]{:S(2)}) copy-start(bf16[32,3,3,3,128]{4,0,3,2,1:T(8,128)(2,1)} %param.4) | copy-start | bytes 663556
  88.5 3.4 %collective-permute-start.1 = (bf16[32,1,8,64]{0,2,3,1:T(8,128)(2,1)S(1)}, bf16[32,1,8,64]{0,2,3,1:T(8,128)(2,1)S(1)}, u32[]{:S(2)}, u32[]{:S(2)}) collective-permute-start(bf16[32,1,8,64]{0,2,3,1:T(8,128)(2,1)S(1)} %slice.176), channel_id=1, source_target_pairs={{4,0},{8,4},{12,8},{16,12},{20,16},{24,20},{28,24},{5,1},{9,5},{13... | collective-permute-start | bytes 98312 | tf_op jit(solution)/shard_map/ppermute | solution.py:13
Sparse Core Ops, SparseCore 0:
  13.6 65.7 all-gather.1
  137.9 57.3 all-reduce.2
where the time goes:
time: 205 us; the launch traced here: 204 us
  waiting for transfers between devices  78.1 us (38%)
  blocking collectives  43.2 us (21%)
  matrix products  37 us (18%)
  local copies, waits for them, and re-layouts  26.2 us (13%)
  between operations  14.3 us (7%)
  starting transfers between devices  3.87 us (2%)
    psum x1, waiting for transfers between devices, on_device(): kernel_grad = lax.psum(weight_grad, 'space')  45.1 us
    all_gather x1, waiting for transfers between devices, on_device(): lax.all_gather(padded, 'chan', axis=0, tiled=True)  31.2 us
    all_gather x1, blocking collectives, on_device(): lax.all_gather(kernel, 'chan', axis=0, tiled=True)  24.7 us
    dot_general x27, matrix products, on_device(): jnp.einsum('co,ozyx->czyx', columns[:, depth_tap, row_tap, col_tap, :], s...  20.9 us
    all_gather x1, blocking collectives, on_device(): panel = lax.all_gather(extended, 'chan', axis=0, tiled=True)  18.5 us
    conv_general_dilated x1, matrix products, on_device(): lax.conv_general_dilated(padded[None], panel[:, :out_depth][None], (1, 1,...  13.8 us
    broadcast_in_dim x1, local copies, waits for them, and re-layouts, on_device(): padded[None]  8.48 us
    unnamed x12, local copies, waits for them, and re-layouts  5.21 us
  transfers between devices with their start and end apart: 4, of which 4 were waited for; matrix products, arithmetic and copies ran while one was open for 11% of the time, Pallas kernels for 0%

commit v1 on v0

v1 whole, which is shorter than its diff:
```python
import functools

import jax
import jax.numpy as jnp
from jax import lax
from jax.experimental import pallas as pl
from jax.experimental.pallas import tpu as pltpu
from jax.sharding import PartitionSpec as P

SLOPE = 0.3
VMEM = 56 * 1024 * 1024
FEW = 4


def params():
    return pltpu.CompilerParams(vmem_limit_bytes=VMEM)


def pair_matrix(transposed, wid, half):
    shape = (3 * wid, 2 * wid) if transposed else (2 * wid, 3 * wid)
    long, short = (0, 1) if transposed else (1, 0)
    src = lax.broadcasted_iota(jnp.int32, shape, short)
    dst = lax.broadcasted_iota(jnp.int32, shape, long)
    e = (dst >= wid).astype(jnp.int32) + (dst >= 2 * wid).astype(jnp.int32)
    rest = dst - e * wid
    h = (rest >= half).astype(jnp.int32)
    x = 2 * (rest - h * half) + e - 1
    hit = (x >= 0) & (x < wid) & (src == h * wid + x)
    return jnp.where(hit, 1.0, 0.0).astype(jnp.bfloat16)


def fwd_kernel(n, ob, vol_ref, rim_ref, w_ref, cols_ref, *rest):
    part_refs = rest[:-2] if n > 1 else rest[:-1]
    wide_ref = rest[-2] if n > 1 else rest[-1]
    cb, planes, hgt, wid = vol_ref.shape
    half = wid // 2
    groups = hgt // 4
    lanes = groups * wid
    sel = pair_matrix(False, wid, half)
    zero = jnp.zeros((cb, wid), jnp.float32)
    for p in range(-1, planes):
        plane = rim_ref[:, 0] if p < 0 else vol_ref[:, p]
        wide_ref[...] = plane.astype(jnp.float32).reshape(cb * hgt, wid)
        row = [wide_ref[pl.ds(y, cb, stride=hgt), :] for y in range(hgt)]
        cls = [[row[4 * j + r] for j in range(groups)] for r in range(4)]

        def stack(blocks):
            return jnp.concatenate(blocks, axis=0).astype(jnp.bfloat16)

        back = stack([zero] + cls[3][:-1])
        cls = [stack(c) for c in cls]
        for b, (left, right) in enumerate(((back, cls[1]), (cls[0], cls[2]), (cls[1], cls[3]))):
            taps = jnp.dot(
                jnp.concatenate([left, right], axis=1), sel, preferred_element_type=jnp.float32
            )
            for e in range(3):
                block = taps[:, e * wid : (e + 1) * wid].astype(jnp.bfloat16)
                block = jnp.concatenate(
                    [block[j * cb : (j + 1) * cb] for j in range(groups)], axis=1
                )
                for z in range(planes // 2):
                    a = p + 1 - 2 * z
                    if 0 <= a <= 2:
                        tap = (a * 3 + b) * 3 + e
                        cols_ref[tap * cb : (tap + 1) * cb, z * lanes : (z + 1) * lanes] = block
    part = lax.dot_general(
        w_ref[...],
        cols_ref[...],
        (((0,), (0,)), ((), ())),
        preferred_element_type=jnp.float32,
    )
    if n == 1:
        part_refs[0][...] = part
        return
    all_ref = rest[-1]
    all_ref[...] = part
    me = lax.axis_index("chan")
    for k, ref in enumerate(part_refs):
        start = pl.multiple_of(lax.rem(me + k, n) * ob, ob)
        ref[...] = all_ref[pl.ds(start, ob), :]


def act_kernel(up_ref, *rest):
    *part_refs, pooled_ref, grad_ref = rest
    pre = part_refs[0][...]
    for ref in part_refs[1:]:
        pre = pre + ref[...]
    groups, ob, small = up_ref.shape
    wid = 4 * small
    lanes = groups * wid
    grow_r = lax.broadcasted_iota(jnp.int32, (small, wid), 0)
    grow_c = lax.broadcasted_iota(jnp.int32, (small, wid), 1)
    grow_c = grow_c - jnp.where(grow_c >= 2 * small, 2 * small, 0)
    grow = jnp.where((grow_c >= 2 * grow_r) & (grow_c <= 2 * grow_r + 1), 1.0, 0.0)
    pool_r = lax.broadcasted_iota(jnp.int32, (wid, small), 0)
    pool_c = lax.broadcasted_iota(jnp.int32, (wid, small), 1)
    pool_r = pool_r - jnp.where(pool_r >= 2 * small, 2 * small, 0)
    pool = jnp.where((pool_r >= 2 * pool_c) & (pool_r <= 2 * pool_c + 1), 0.125, 0.0)
    grow = grow.astype(jnp.bfloat16)
    scale = jnp.where(pre > 0, 1.0, SLOPE)
    act = jnp.where(pre > 0, pre, SLOPE * pre)
    act = act[:, :lanes] + act[:, lanes:]
    for j in range(groups):
        spread = jnp.dot(up_ref[j], grow, preferred_element_type=jnp.float32) * 0.125
        for z in range(2):
            at = slice(z * lanes + j * wid, z * lanes + (j + 1) * wid)
            grad_ref[:, at] = (spread * scale[:, at]).astype(jnp.bfloat16)
        pooled_ref[j] = jnp.dot(
            act[:, j * wid : (j + 1) * wid],
            pool,
            precision=lax.Precision.HIGHEST,
            preferred_element_type=jnp.float32,
        ).astype(jnp.bfloat16)


def weight_kernel(n, cols_ref, *rest):
    *block_refs, wgrad_ref, grad_ref = rest
    if n == 1:
        grad_ref[...] = block_refs[0][...]
    else:
        me = lax.axis_index("chan")
        ob = block_refs[0].shape[0]
        for k, ref in enumerate(block_refs):
            start = pl.multiple_of(lax.rem(me + n - k, n) * ob, ob)
            grad_ref[pl.ds(start, ob), :] = ref[...]
    wgrad_ref[...] = lax.dot_general(
        cols_ref[...],
        grad_ref[...],
        (((1,), (1,)), ((), ())),
        preferred_element_type=jnp.float32,
    )


def input_kernel(w_ref, grad_ref, rim_ref, out_ref, wide_ref):
    cb, planes, hgt, wid = out_ref.shape
    half = wid // 2
    groups = hgt // 4
    lanes = groups * wid
    taps = 9 * cb
    spread = pair_matrix(True, wid, half)
    spread = jnp.concatenate([spread, spread], axis=0)
    keep = lax.broadcasted_iota(jnp.int32, (3 * cb, lanes), 1) < lanes - half
    w = [w_ref[a * taps : (a + 1) * taps, :] for a in range(3)]
    behind = jnp.concatenate([w[2], w[0]], axis=1)
    g = [grad_ref[:, z * lanes : (z + 1) * lanes] for z in range(planes // 2)]
    g.append(rim_ref[...])
    for i in range(planes):
        z = i // 2
        if i % 2 == 0:
            e_all = jnp.dot(w[1], g[z], preferred_element_type=jnp.float32)
        else:
            e_all = jnp.dot(
                behind,
                jnp.concatenate([g[z], g[z + 1]], axis=0),
                preferred_element_type=jnp.float32,
            )
        by_b = [e_all[b * 3 * cb : (b + 1) * 3 * cb] for b in range(3)]
        shifted = pltpu.roll(by_b[0], lanes - half, 1)
        rows = (by_b[1], by_b[2] + jnp.where(keep, shifted, 0.0))
        left = []
        for f in rows:
            for j in range(groups):
                t = f[:, j * wid : (j + 1) * wid]
                left.append(
                    jnp.concatenate([t[e * cb : (e + 1) * cb] for e in range(3)], axis=1)
                )
        left = jnp.concatenate(left, axis=0)
        high = left.astype(jnp.bfloat16)
        low = (left - high.astype(jnp.float32)).astype(jnp.bfloat16)
        full = jnp.dot(
            jnp.concatenate([high, low], axis=1), spread, preferred_element_type=jnp.float32
        )
        for par in range(2):
            for j in range(groups):
                for h in range(2):
                    y = 2 * (2 * j + h) + par
                    at = (par * groups + j) * cb
                    wide_ref[pl.ds(i * hgt + y, cb, stride=planes * hgt), :] = full[
                        at : at + cb, h * wid : (h + 1) * wid
                    ]
    out_ref[...] = wide_ref[...].reshape(cb, planes, hgt, wid).astype(jnp.bfloat16)


def shifted_by(block, axis, k):
    n = lax.axis_size(axis)
    return lax.ppermute(block, axis, [(i, (i + k) % n) for i in range(n)])


def swapped(block, axis, bit):
    n = lax.axis_size(axis)
    return lax.ppermute(block, axis, [(i, i ^ bit) for i in range(n)])


def sum_over(term, axis):
    n = lax.axis_size(axis)
    if n & (n - 1):
        return lax.psum(term, axis)
    if n > 1:
        term = term + swapped(term, axis, 1)
    bits = [1 << b for b in range(1, n.bit_length() - 1)]
    halves = jnp.split(term, 2, axis=0)
    for first, second in zip(bits, bits[::-1]):
        sent = [h.astype(jnp.bfloat16) for h in halves]
        got = [swapped(s, axis, bit) for s, bit in zip(sent, (first, second))]
        halves = [s.astype(jnp.float32) + r.astype(jnp.float32) for s, r in zip(sent, got)]
    return jnp.concatenate(halves, axis=0)


def on_device(volume, kernel, upstream):
    cb, planes, hgt, wid = volume.shape
    ob = upstream.shape[0]
    out_ch = kernel.shape[4]
    n_chan, n_space = lax.axis_size("chan"), lax.axis_size("space")
    direct = n_chan <= FEW
    n = n_chan if direct else 1
    taps = 27 * cb
    lanes = hgt // 4 * wid
    cells = planes // 2 * lanes
    rim = lax.ppermute(volume[:, -1:], "space", [(i, i + 1) for i in range(n_space - 1)])
    weights = kernel.transpose(1, 2, 3, 0, 4).reshape(taps, out_ch)
    up = upstream[:, 0].transpose(1, 0, 2)

    part_shape = jax.ShapeDtypeStruct((ob if direct else out_ch, cells), jnp.float32)
    scratch = [pltpu.VMEM((cb * hgt, wid), jnp.float32)]
    if n > 1:
        scratch.append(pltpu.VMEM((out_ch, cells), jnp.float32))
    cols, *parts = pl.pallas_call(
        functools.partial(fwd_kernel, n, ob),
        out_shape=[jax.ShapeDtypeStruct((taps, cells), jnp.bfloat16)] + [part_shape] * n,
        scratch_shapes=scratch,
        compiler_params=params(),
    )(volume, rim, weights)
    if direct:
        parts = parts[:1] + [shifted_by(parts[k], "chan", k) for k in range(1, n)]
    else:
        parts = [lax.psum_scatter(parts[0], "chan", scatter_dimension=0, tiled=True)]

    pooled, own = pl.pallas_call(
        act_kernel,
        out_shape=[
            jax.ShapeDtypeStruct(up.shape, jnp.bfloat16),
            jax.ShapeDtypeStruct((ob, cells), jnp.bfloat16),
        ],
        compiler_params=params(),
    )(up, *parts)
    pooled = pooled.transpose(1, 0, 2)[:, None]
    if direct:
        blocks = [own] + [shifted_by(own, "chan", k) for k in range(1, n)]
    else:
        blocks = [lax.all_gather(own, "chan", axis=0, tiled=True)]

    weight_grad, grad = pl.pallas_call(
        functools.partial(weight_kernel, n),
        out_shape=[
            jax.ShapeDtypeStruct((taps, out_ch), jnp.float32),
            jax.ShapeDtypeStruct((out_ch, cells), jnp.bfloat16),
        ],
        compiler_params=params(),
    )(cols, *blocks)
    weight_grad = sum_over(weight_grad, "space")
    weight_grad = weight_grad.reshape(3, 3, 3, cb, out_ch).transpose(3, 0, 1, 2, 4)

    after = lax.ppermute(grad[:, :lanes], "space", [(i + 1, i) for i in range(n_space - 1)])
    input_grad = pl.pallas_call(
        input_kernel,
        out_shape=jax.ShapeDtypeStruct(volume.shape, jnp.bfloat16),
        scratch_shapes=[pltpu.VMEM((cb * planes * hgt, wid), jnp.float32)],
        compiler_params=params(),
    )(weights, grad, after)
    return pooled, input_grad, weight_grad


def solution(mesh):
    return jax.shard_map(
        on_device,
        mesh=mesh,
        in_specs=(
            P("chan", "space", None, None),
            P("chan", None, None, None, None),
            P("chan", "space", None, None),
        ),
        out_specs=(
            P("chan", "space", None, None),
            P("chan", "space", None, None),
            P("chan", None, None, None, None),
        ),
        check_vma=False,
    )
```

time: 205 us -> 65.1 us (0.32)
  waiting for transfers between devices: 78.1 us -> 22.4 us
  blocking collectives: 43.2 us -> 0 us
  matrix products: 37 us -> 0 us
  local copies, waits for them, and re-layouts: 26.2 us -> 6.52 us
  starting transfers between devices: 3.87 us -> 20.7 us
  between operations: 14.3 us -> 0.71 us
  Pallas kernels: 0 us -> 12.2 us
    psum x1 -> x0, waiting for transfers between devices: 45.1 us -> none  [on_device(): kernel_grad = lax.psum(weight_grad, 'space')]
    all_gather x2 -> x0, blocking collectives: 43.2 us -> none  [the longest x1 24.7 us: on_device(): lax.all_gather(kernel, 'chan', axis=0, tiled=True)]
    all_gather x1 -> x0, waiting for transfers between devices: 31.2 us -> none  [on_device(): lax.all_gather(padded, 'chan', axis=0, tiled=True)]
    dot_general x27 -> x0, matrix products: 20.9 us -> none  [on_device(): jnp.einsum('co,ozyx->czyx', columns[:, depth_tap, row_tap, col_tap, :], s...]
    ppermute x2 -> x13, waiting for transfers between devices: 1.74 us -> 22.4 us  [the longest x6 13.1 us: shifted_by(): return lax.ppermute(block, axis, [(i, (i + k) % n) for i in range(n)])]
    ppermute x2 -> x13, starting transfers between devices: 3.79 us -> 20.7 us  [the longest x6 11.1 us: shifted_by(): return lax.ppermute(block, axis, [(i, (i + k) % n) for i in range(n)])]
    conv_general_dilated x2 -> x0, matrix products: 16.1 us -> none  [the longest x1 13.8 us: on_device(): lax.conv_general_dilated(padded[None], panel[:, :out_depth][None], (1, 1,...]
    pallas_call x0 -> x4, Pallas kernels: none -> 12.2 us  [the longest x1 3.78 us: on_device(): pl.pallas_call(input_kernel, out_shape=jax.ShapeDtypeStruct(volume.shape,...]
  transfers between devices with their start and end apart: 4 -> 13, of which waited for: 4 -> 8; matrix products, arithmetic and copies ran while one was open for 11% -> 5% of each run, Pallas kernels for 0% -> 6%
where the time goes in v1:
time: 65.1 us; the launch traced here: 64.5 us
  waiting for transfers between devices  22.4 us (34%)
  starting transfers between devices  20.7 us (32%)
  Pallas kernels  12.2 us (19%)
  local copies, waits for them, and re-layouts  6.52 us (10%)
  other arithmetic  1.96 us (3%)
  between operations  0.71 us (1%)
    ppermute x6, waiting for transfers between devices, shifted_by(): return lax.ppermute(block, axis, [(i, (i + k) % n) for i in range(n)])  13.1 us
    ppermute x6, starting transfers between devices, shifted_by(): return lax.ppermute(block, axis, [(i, (i + k) % n) for i in range(n)])  11.1 us
    ppermute x5, waiting for transfers between devices, swapped(): return lax.ppermute(block, axis, [(i, i ^ bit) for i in range(n)])  8.35 us
    ppermute x5, starting transfers between devices, swapped(): return lax.ppermute(block, axis, [(i, i ^ bit) for i in range(n)])  5.92 us
    unnamed x20, local copies, waits for them, and re-layouts  4.67 us
    pallas_call x1, Pallas kernels, on_device(): pl.pallas_call(input_kernel, out_shape=jax.ShapeDtypeStruct(volume.shape,...  3.78 us
    pallas_call x1, Pallas kernels, on_device(): pl.pallas_call(functools.partial(fwd_kernel, n, ob), out_shape=[jax.Shape...  3.42 us
    pallas_call x1, Pallas kernels, on_device(): pl.pallas_call(functools.partial(weight_kernel, n), out_shape=[jax.ShapeD...  2.99 us
  transfers between devices with their start and end apart: 13, of which 8 were waited for; matrix products, arithmetic and copies ran while one was open for 5% of the time, Pallas kernels for 6%

profile of v1, /device:TPU:0, one launch (start us, length us, event | category | flops | bytes accessed | tf_op | source)
XLA Modules:
  0.0 64.5 jit_solution(247444582150752324)
XLA Ops:
  0.6 0.9 %slice.6 = bf16[32,1,16,128]{3,2,1,0:T(8,128)(2,1)S(1)} slice(bf16[32,4,16,128]{3,2,1,0:T(8,128)(2,1)} %vol_ref.1), slice={[0:32], [3:4], [0:16], [0:128]} | slice | bytes 262144 | tf_op jit(solution)/shard_map/slice | solution.py:219
  1.6 2.4 %collective-permute-start = (bf16[32,1,16,128]{3,2,1,0:T(8,128)(2,1)S(1)}, bf16[32,1,16,128]{3,2,1,0:T(8,128)(2,1)S(1)}, u32[]{:S(2)}, u32[]{:S(2)}) collective-permute-start(bf16[32,1,16,128]{3,2,1,0:T(8,128)(2,1)S(1)} %slice.6), channel_id=1, source_target_pairs={{0,4},{4,8},{8,12},{12,16},{16,20},{20,24},{24,28},{1,5},{5,9},{9,... | collective-permute-start | bytes 393224 | tf_op jit(solution)/shard_map/ppermute | solution.py:219
  3.9 1.0 %collective-permute-done.rim_ref = bf16[32,1,16,128]{3,2,1,0:T(8,128)(2,1)S(1)} collective-permute-done((bf16[32,1,16,128]{3,2,1,0:T(8,128)(2,1)S(1)}, bf16[32,1,16,128]{3,2,1,0:T(8,128)(2,1)S(1)}, u32[]{:S(2)}, u32[]{:S(2)}) %collective-permute-start) | collective-permute-done | bytes 131104 | tf_op jit(solution)/shard_map/ppermute | solution.py:219
  4.9 0.7 %copy-done.4 = bf16[32,1,16,128]{3,2,1,0:T(8,128)(2,1)} copy-done((bf16[32,1,16,128]{3,2,1,0:T(8,128)(2,1)}, bf16[32,1,16,128]{3,2,1,0:T(8,128)(2,1)S(1)}, u32[]{:S(2)}) %copy-start.4) | copy-done | bytes 131096
  5.5 3.4 %shard_map.58 = (bf16[864,1024]{1,0:T(8,128)(2,1)}, f32[32,1024]{1,0:T(8,128)}, f32[32,1024]{1,0:T(8,128)}, f32[32,1024]{1,0:T(8,128)}, f32[32,1024]{1,0:T(8,128)}) custom-call(bf16[32,4,16,128]{3,2,1,0:T(8,128)(2,1)} %vol_ref.1, bf16[32,1,16,128]{3,2,1,0:T(8,128)(2,1)} %copy-done.4, bf16[864,128]{1,0:T(8,128)(2,1)} %bitcast.14), custom_call_target="tpu_custom_call" | custom-call | tf_op jit(solution)/shard_map/pallas_call | solution.py:227
  9.0 2.4 %collective-permute-start.1 = (f32[32,1024]{1,0:T(8,128)}, f32[32,1024]{1,0:T(8,128)S(1)}, u32[]{:S(2)}, u32[]{:S(2)}) collective-permute-start(f32[32,1024]{1,0:T(8,128)} %get-tuple-element.13), channel_id=1, source_target_pairs={{0,1},{1,2},{2,3},{3,0},{4,5},{5,6},{6,7},{7,4},{8,9},{9,10},{10,1... | collective-permute-start | bytes 393224 | tf_op jit(solution)/shard_map/ppermute | solution.py:186
  11.4 2.6 %collective-permute-start.2 = (f32[32,1024]{1,0:T(8,128)}, f32[32,1024]{1,0:T(8,128)S(1)}, u32[]{:S(2)}, u32[]{:S(2)}) collective-permute-start(f32[32,1024]{1,0:T(8,128)} %get-tuple-element.14), channel_id=1, source_target_pairs={{0,2},{1,3},{2,0},{3,1},{4,6},{5,7},{6,4},{7,5},{8,10},{9,11},{10,... | collective-permute-start | bytes 393224 | tf_op jit(solution)/shard_map/ppermute | solution.py:186
  14.0 1.3 %collective-permute-start.3 = (f32[32,1024]{1,0:T(8,128)}, f32[32,1024]{1,0:T(8,128)S(1)}, u32[]{:S(2)}, u32[]{:S(2)}) collective-permute-start(f32[32,1024]{1,0:T(8,128)} %get-tuple-element.15), channel_id=1, source_target_pairs={{0,3},{1,0},{2,1},{3,2},{4,7},{5,4},{6,5},{7,6},{8,11},{9,8},{10,9... | collective-permute-start | bytes 393224 | tf_op jit(solution)/shard_map/ppermute | solution.py:186
  15.3 1.4 %copy.9 = bf16[32,1,4,32]{3,0,2,1:T(8,128)(2,1)} copy(bf16[32,1,4,32]{3,2,1,0:T(4,128)(2,1)} %param.5) | data formatting | bytes 16384 | tf_op args[2]
  16.7 6.2 %collective-permute-done.2.rest_2_ = f32[32,1024]{1,0:T(8,128)S(1)} collective-permute-done((f32[32,1024]{1,0:T(8,128)}, f32[32,1024]{1,0:T(8,128)S(1)}, u32[]{:S(2)}, u32[]{:S(2)}) %collective-permute-start.2) | collective-permute-done | bytes 131104 | tf_op jit(solution)/shard_map/ppermute | solution.py:186
  22.9 0.6 copy-done.2
  23.6 2.1 %shard_map.59 = (bf16[4,32,32]{2,1,0:T(8,128)(2,1)}, bf16[32,1024]{1,0:T(8,128)(2,1)}) custom-call(bf16[4,32,32]{2,1,0:T(8,128)(2,1)} %bitcast.17, f32[32,1024]{1,0:T(8,128)} %get-tuple-element.12.rest_0_, f32[32,1024]{1,0:T(8,128)} %copy-done.1, f32[32,1024]{1,0:T(8,128)} %copy-done.2, f32[32,1024]{1,0:T(8,128)} %copy-done.3), custom_call_target="tpu_custom_call" | custom-call | tf_op jit(solution)/shard_map/pallas_call | solution.py:238
  25.7 3.5 %collective-permute-start.6 = (bf16[32,1024]{1,0:T(8,128)(2,1)}, bf16[32,1024]{1,0:T(8,128)(2,1)S(1)}, u32[]{:S(2)}, u32[]{:S(2)}) collective-permute-start(bf16[32,1024]{1,0:T(8,128)(2,1)} %get-tuple-element.18.rest_0_), channel_id=1, source_target_pairs={{0,3},{1,0},{2,1},{3,2},{4,7},{5,4},{6,5},{7,6},{8,11},{9,8},{10,9... | collective-permute-start | bytes 196616 | tf_op jit(solution)/shard_map/ppermute | solution.py:186
  29.2 1.2 %collective-permute-start.5 = (bf16[32,1024]{1,0:T(8,128)(2,1)}, bf16[32,1024]{1,0:T(8,128)(2,1)S(1)}, u32[]{:S(2)}, u32[]{:S(2)}) collective-permute-start(bf16[32,1024]{1,0:T(8,128)(2,1)} %get-tuple-element.18.rest_0_), channel_id=1, source_target_pairs={{0,2},{1,3},{2,0},{3,1},{4,6},{5,7},{6,4},{7,5},{8,10},{9,11},{10,... | collective-permute-start | bytes 196616 | tf_op jit(solution)/shard_map/ppermute | solution.py:186
  30.5 1.5 %collective-permute-done.6.rest_3_ = bf16[32,1024]{1,0:T(8,128)(2,1)S(1)} collective-permute-done((bf16[32,1024]{1,0:T(8,128)(2,1)}, bf16[32,1024]{1,0:T(8,128)(2,1)S(1)}, u32[]{:S(2)}, u32[]{:S(2)}) %collective-permute-start.6) | collective-permute-done | bytes 65568 | tf_op jit(solution)/shard_map/ppermute | solution.py:186
  31.9 5.4 %collective-permute-done.5.rest_2_ = bf16[32,1024]{1,0:T(8,128)(2,1)S(1)} collective-permute-done((bf16[32,1024]{1,0:T(8,128)(2,1)}, bf16[32,1024]{1,0:T(8,128)(2,1)S(1)}, u32[]{:S(2)}, u32[]{:S(2)}) %collective-permute-start.5) | collective-permute-done | bytes 65568 | tf_op jit(solution)/shard_map/ppermute | solution.py:186
  37.4 0.6 copy-done.6
  38.0 3.0 %shard_map.60 = (f32[864,128]{1,0:T(8,128)}, bf16[128,1024]{1,0:T(8,128)(2,1)}) custom-call(bf16[864,1024]{1,0:T(8,128)(2,1)} %get-tuple-element.17.cols_ref, bf16[32,1024]{1,0:T(8,128)(2,1)} %get-tuple-element.18.rest_0_, bf16[32,1024]{1,0:T(8,128)(2,1)} %copy-done.7, bf16[32,1024]{1,0:T(8,128)(2,1)} %copy-done.6, bf16[32,1024]{1,0:T(8,128)(2,1)} %copy-done.5), custom_call_target="tpu_custom_call" | custom-call | tf_op jit(solution)/shard_map/pallas_call | solution.py:252
  41.0 2.0 %collective-permute-done.8 = f32[864,128]{1,0:T(8,128)S(1)} collective-permute-done((f32[864,128]{1,0:T(8,128)}, f32[864,128]{1,0:T(8,128)S(1)}, u32[]{:S(2)}, u32[]{:S(2)}) %collective-permute-start.8) | collective-permute-done | bytes 442400 | tf_op jit(solution)/shard_map/ppermute | solution.py:191
  43.0 1.1 %add_convert_fusion = bf16[864,128]{1,0:T(8,128)(2,1)S(1)} fusion(f32[864,128]{1,0:T(8,128)} %get-tuple-element.20, f32[864,128]{1,0:T(8,128)S(1)} %collective-permute-done.8), kind=kLoop, calls=%fused_computation.1 | loop fusion | flops 221184 | bytes 1105920 | tf_op jit(solution)/shard_map/convert.1
  44.1 3.8 %collective-permute-start.9 = (bf16[432,128]{1,0:T(8,128)(2,1)S(1)}, bf16[432,128]{1,0:T(8,128)(2,1)S(1)}, u32[]{:S(2)}, u32[]{:S(2)}) collective-permute-start(bf16[432,128]{1,0:T(8,128)(2,1)S(1)} %get-tuple-element.26), channel_id=1, source_target_pairs={{0,8},{4,12},{8,0},{12,4},{16,24},{20,28},{24,16},{28,20},{1,9},{5... | collective-permute-start | bytes 331784 | tf_op jit(solution)/shard_map/ppermute | solution.py:191
  47.9 0.9 %slice.7 = bf16[128,512]{1,0:T(8,128)(2,1)S(1)} slice(bf16[128,1024]{1,0:T(8,128)(2,1)} %get-tuple-element.19.grad_ref), slice={[0:128], [0:512]} | slice | bytes 262144 | tf_op jit(solution)/shard_map/slice | solution.py:263
  48.8 1.3 %collective-permute-start.7 = (bf16[128,512]{1,0:T(8,128)(2,1)S(1)}, bf16[128,512]{1,0:T(8,128)(2,1)S(1)}, u32[]{:S(2)}, u32[]{:S(2)}) collective-permute-start(bf16[128,512]{1,0:T(8,128)(2,1)S(1)} %slice.7), channel_id=1, source_target_pairs={{4,0},{8,4},{12,8},{16,12},{20,16},{24,20},{28,24},{5,1},{9,5},{13... | collective-permute-start | bytes 393224 | tf_op jit(solution)/shard_map/ppermute | solution.py:263
  50.1 1.1 %collective-permute-done.9 = bf16[432,128]{1,0:T(8,128)(2,1)S(1)} collective-permute-done((bf16[432,128]{1,0:T(8,128)(2,1)S(1)}, bf16[432,128]{1,0:T(8,128)(2,1)S(1)}, u32[]{:S(2)}, u32[]{:S(2)}) %collective-permute-start.9) | collective-permute-done | bytes 110624 | tf_op jit(solution)/shard_map/ppermute | solution.py:191
  51.2 1.5 %collective-permute-done.11 = bf16[432,128]{1,0:T(8,128)(2,1)S(1)} collective-permute-done((bf16[432,128]{1,0:T(8,128)(2,1)S(1)}, bf16[432,128]{1,0:T(8,128)(2,1)S(1)}, u32[]{:S(2)}, u32[]{:S(2)}) %collective-permute-start.11) | collective-permute-done | bytes 110624 | tf_op jit(solution)/shard_map/ppermute | solution.py:191
  52.7 0.8 %collective-permute-start.10 = (bf16[432,128]{1,0:T(8,128)(2,1)S(1)}, bf16[432,128]{1,0:T(8,128)(2,1)S(1)}, u32[]{:S(2)}, u32[]{:S(2)}) collective-permute-start(bf16[432,128]{1,0:T(8,128)(2,1)S(1)} %get-tuple-element.24), channel_id=1, source_target_pairs={{0,16},{4,20},{8,24},{12,28},{16,0},{20,4},{24,8},{28,12},{1,17},{... | collective-permute-start | bytes 331784 | tf_op jit(solution)/shard_map/ppermute | solution.py:191
  53.5 0.6 copy.7
  54.1 0.7 %copy-done = bf16[128,512]{1,0:T(8,128)(2,1)} copy-done((bf16[128,512]{1,0:T(8,128)(2,1)}, bf16[128,512]{1,0:T(8,128)(2,1)S(1)}, u32[]{:S(2)}) %copy-start) | copy-done | bytes 131096
  54.8 3.8 %shard_map.61 = bf16[32,4,16,128]{3,2,1,0:T(8,128)(2,1)} custom-call(bf16[864,128]{1,0:T(8,128)(2,1)} %bitcast.15, bf16[128,1024]{1,0:T(8,128)(2,1)} %get-tuple-element.19.grad_ref, bf16[128,512]{1,0:T(8,128)(2,1)} %copy-done), custom_call_target="tpu_custom_call" | custom-call | tf_op jit(solution)/shard_map/pallas_call | solution.py:264
  58.6 1.3 %collective-permute-start.12 = (bf16[432,128]{1,0:T(8,128)(2,1)S(1)}, bf16[432,128]{1,0:T(8,128)(2,1)S(1)}, u32[]{:S(2)}, u32[]{:S(2)}) collective-permute-start(bf16[432,128]{1,0:T(8,128)(2,1)S(1)} %get-tuple-element.25), channel_id=1, source_target_pairs={{0,8},{4,12},{8,0},{12,4},{16,24},{20,28},{24,16},{28,20},{1,9},{5... | collective-permute-start | bytes 331784 | tf_op jit(solution)/shard_map/ppermute | solution.py:191
  59.9 3.8 %collective-permute-done.12 = bf16[432,128]{1,0:T(8,128)(2,1)S(1)} collective-permute-done((bf16[432,128]{1,0:T(8,128)(2,1)S(1)}, bf16[432,128]{1,0:T(8,128)(2,1)S(1)}, u32[]{:S(2)}, u32[]{:S(2)}) %collective-permute-start.12) | collective-permute-done | bytes 110624 | tf_op jit(solution)/shard_map/ppermute | solution.py:191
  63.8 0.8 %pad_maximum_fusion = f32[864,128]{1,0:T(8,128)} fusion(f32[432,128]{1,0:T(8,128)S(1)} %convert_add_fusion, f32[432,128]{1,0:T(8,128)S(1)} %convert_add_fusion.1), kind=kLoop, calls=%fused_computation | loop fusion | flops 110592 | bytes 884736 | tf_op jit(solution)/shard_map/concatenate | solution.py:206
  (26 shorter events, 0.3 us)
Async XLA Ops:
  1.6 3.3 %collective-permute-start = (bf16[32,1,16,128]{3,2,1,0:T(8,128)(2,1)S(1)}, bf16[32,1,16,128]{3,2,1,0:T(8,128)(2,1)S(1)}, u32[]{:S(2)}, u32[]{:S(2)}) collective-permute-start(bf16[32,1,16,128]{3,2,1,0:T(8,128)(2,1)S(1)} %slice.6), channel_id=1, source_target_pairs={{0,4},{4,8},{8,12},{12,16},{16,20},{20,24},{24,28},{1,5},{5,9},{9,... | collective-permute-start | bytes 393224 | tf_op jit(solution)/shard_map/ppermute | solution.py:219
  4.9 0.7 %copy-start.4 = (bf16[32,1,16,128]{3,2,1,0:T(8,128)(2,1)}, bf16[32,1,16,128]{3,2,1,0:T(8,128)(2,1)S(1)}, u32[]{:S(2)}) copy-start(bf16[32,1,16,128]{3,2,1,0:T(8,128)(2,1)S(1)} %collective-permute-done.rim_ref) | copy-start | bytes 393220
  9.0 7.7 %collective-permute-start.1 = (f32[32,1024]{1,0:T(8,128)}, f32[32,1024]{1,0:T(8,128)S(1)}, u32[]{:S(2)}, u32[]{:S(2)}) collective-permute-start(f32[32,1024]{1,0:T(8,128)} %get-tuple-element.13), channel_id=1, source_target_pairs={{0,1},{1,2},{2,3},{3,0},{4,5},{5,6},{6,7},{7,4},{8,9},{9,10},{10,1... | collective-permute-start | bytes 393224 | tf_op jit(solution)/shard_map/ppermute | solution.py:186
  11.4 11.5 %collective-permute-start.2 = (f32[32,1024]{1,0:T(8,128)}, f32[32,1024]{1,0:T(8,128)S(1)}, u32[]{:S(2)}, u32[]{:S(2)}) collective-permute-start(f32[32,1024]{1,0:T(8,128)} %get-tuple-element.14), channel_id=1, source_target_pairs={{0,2},{1,3},{2,0},{3,1},{4,6},{5,7},{6,4},{7,5},{8,10},{9,11},{10,... | collective-permute-start | bytes 393224 | tf_op jit(solution)/shard_map/ppermute | solution.py:186
  14.0 9.0 %collective-permute-start.3 = (f32[32,1024]{1,0:T(8,128)}, f32[32,1024]{1,0:T(8,128)S(1)}, u32[]{:S(2)}, u32[]{:S(2)}) collective-permute-start(f32[32,1024]{1,0:T(8,128)} %get-tuple-element.15), channel_id=1, source_target_pairs={{0,3},{1,0},{2,1},{3,2},{4,7},{5,4},{6,5},{7,6},{8,11},{9,8},{10,9... | collective-permute-start | bytes 393224 | tf_op jit(solution)/shard_map/ppermute | solution.py:186
  16.7 6.2 %copy-start.1 = (f32[32,1024]{1,0:T(8,128)}, f32[32,1024]{1,0:T(8,128)S(1)}, u32[]{:S(2)}) copy-start(f32[32,1024]{1,0:T(8,128)S(1)} %collective-permute-done.1.rest_1_) | copy-start | bytes 393220
  22.9 0.6 %copy-start.2 = (f32[32,1024]{1,0:T(8,128)}, f32[32,1024]{1,0:T(8,128)S(1)}, u32[]{:S(2)}) copy-start(f32[32,1024]{1,0:T(8,128)S(1)} %collective-permute-done.2.rest_2_) | copy-start | bytes 393220
  22.9 0.7 %copy-start.3 = (f32[32,1024]{1,0:T(8,128)}, f32[32,1024]{1,0:T(8,128)S(1)}, u32[]{:S(2)}) copy-start(f32[32,1024]{1,0:T(8,128)S(1)} %collective-permute-done.3.rest_3_) | copy-start | bytes 393220
  25.7 6.3 %collective-permute-start.6 = (bf16[32,1024]{1,0:T(8,128)(2,1)}, bf16[32,1024]{1,0:T(8,128)(2,1)S(1)}, u32[]{:S(2)}, u32[]{:S(2)}) collective-permute-start(bf16[32,1024]{1,0:T(8,128)(2,1)} %get-tuple-element.18.rest_0_), channel_id=1, source_target_pairs={{0,3},{1,0},{2,1},{3,2},{4,7},{5,4},{6,5},{7,6},{8,11},{9,8},{10,9... | collective-permute-start | bytes 196616 | tf_op jit(solution)/shard_map/ppermute | solution.py:186
  29.2 8.1 %collective-permute-start.5 = (bf16[32,1024]{1,0:T(8,128)(2,1)}, bf16[32,1024]{1,0:T(8,128)(2,1)S(1)}, u32[]{:S(2)}, u32[]{:S(2)}) collective-permute-start(bf16[32,1024]{1,0:T(8,128)(2,1)} %get-tuple-element.18.rest_0_), channel_id=1, source_target_pairs={{0,2},{1,3},{2,0},{3,1},{4,6},{5,7},{6,4},{7,5},{8,10},{9,11},{10,... | collective-permute-start | bytes 196616 | tf_op jit(solution)/shard_map/ppermute | solution.py:186
  30.5 6.9 %collective-permute-start.4 = (bf16[32,1024]{1,0:T(8,128)(2,1)}, bf16[32,1024]{1,0:T(8,128)(2,1)S(1)}, u32[]{:S(2)}, u32[]{:S(2)}) collective-permute-start(bf16[32,1024]{1,0:T(8,128)(2,1)} %get-tuple-element.18.rest_0_), channel_id=1, source_target_pairs={{0,1},{1,2},{2,3},{3,0},{4,5},{5,6},{6,7},{7,4},{8,9},{9,10},{10,1... | collective-permute-start | bytes 196616 | tf_op jit(solution)/shard_map/ppermute | solution.py:186
  31.9 5.4 %copy-start.5 = (bf16[32,1024]{1,0:T(8,128)(2,1)}, bf16[32,1024]{1,0:T(8,128)(2,1)S(1)}, u32[]{:S(2)}) copy-start(bf16[32,1024]{1,0:T(8,128)(2,1)S(1)} %collective-permute-done.6.rest_3_) | copy-start | bytes 196612
  37.3 0.6 copy-start.6
  37.3 0.6 copy-start.7
  38.0 15.5 %copy-start.8 = (bf16[4,32,32]{2,1,0:T(8,128)(2,1)S(1)}, bf16[4,32,32]{2,1,0:T(8,128)(2,1)}, u32[]{:S(2)}) copy-start(bf16[4,32,32]{2,1,0:T(8,128)(2,1)} %get-tuple-element.16) | copy-start | bytes 24580
  41.0 2.0 %collective-permute-start.8 = (f32[864,128]{1,0:T(8,128)}, f32[864,128]{1,0:T(8,128)S(1)}, u32[]{:S(2)}, u32[]{:S(2)}) collective-permute-start(f32[864,128]{1,0:T(8,128)} %get-tuple-element.20), channel_id=1, source_target_pairs={{0,4},{4,0},{8,12},{12,8},{16,20},{20,16},{24,28},{28,24},{1,5},{5... | collective-permute-start | bytes 1327112 | tf_op jit(solution)/shard_map/ppermute | solution.py:191
  44.1 7.2 %collective-permute-start.9 = (bf16[432,128]{1,0:T(8,128)(2,1)S(1)}, bf16[432,128]{1,0:T(8,128)(2,1)S(1)}, u32[]{:S(2)}, u32[]{:S(2)}) collective-permute-start(bf16[432,128]{1,0:T(8,128)(2,1)S(1)} %get-tuple-element.26), channel_id=1, source_target_pairs={{0,8},{4,12},{8,0},{12,4},{16,24},{20,28},{24,16},{28,20},{1,9},{5... | collective-permute-start | bytes 331784 | tf_op jit(solution)/shard_map/ppermute | solution.py:191
  47.9 4.8 %collective-permute-start.11 = (bf16[432,128]{1,0:T(8,128)(2,1)S(1)}, bf16[432,128]{1,0:T(8,128)(2,1)S(1)}, u32[]{:S(2)}, u32[]{:S(2)}) collective-permute-start(bf16[432,128]{1,0:T(8,128)(2,1)S(1)} %get-tuple-element.27), channel_id=1, source_target_pairs={{0,16},{4,20},{8,24},{12,28},{16,0},{20,4},{24,8},{28,12},{1,17},{... | collective-permute-start | bytes 331784 | tf_op jit(solution)/shard_map/ppermute | solution.py:191
  48.8 5.3 %collective-permute-start.7 = (bf16[128,512]{1,0:T(8,128)(2,1)S(1)}, bf16[128,512]{1,0:T(8,128)(2,1)S(1)}, u32[]{:S(2)}, u32[]{:S(2)}) collective-permute-start(bf16[128,512]{1,0:T(8,128)(2,1)S(1)} %slice.7), channel_id=1, source_target_pairs={{4,0},{8,4},{12,8},{16,12},{20,16},{24,20},{28,24},{5,1},{9,5},{13... | collective-permute-start | bytes 393224 | tf_op jit(solution)/shard_map/ppermute | solution.py:263
  52.7 7.1 %collective-permute-start.10 = (bf16[432,128]{1,0:T(8,128)(2,1)S(1)}, bf16[432,128]{1,0:T(8,128)(2,1)S(1)}, u32[]{:S(2)}, u32[]{:S(2)}) collective-permute-start(bf16[432,128]{1,0:T(8,128)(2,1)S(1)} %get-tuple-element.24), channel_id=1, source_target_pairs={{0,16},{4,20},{8,24},{12,28},{16,0},{20,4},{24,8},{28,12},{1,17},{... | collective-permute-start | bytes 331784 | tf_op jit(solution)/shard_map/ppermute | solution.py:191
  54.1 0.7 %copy-start = (bf16[128,512]{1,0:T(8,128)(2,1)}, bf16[128,512]{1,0:T(8,128)(2,1)S(1)}, u32[]{:S(2)}) copy-start(bf16[128,512]{1,0:T(8,128)(2,1)S(1)} %collective-permute-done.7.rim_ref) | copy-start | bytes 393220
  58.6 5.2 %collective-permute-start.12 = (bf16[432,128]{1,0:T(8,128)(2,1)S(1)}, bf16[432,128]{1,0:T(8,128)(2,1)S(1)}, u32[]{:S(2)}, u32[]{:S(2)}) collective-permute-start(bf16[432,128]{1,0:T(8,128)(2,1)S(1)} %get-tuple-element.25), channel_id=1, source_target_pairs={{0,8},{4,12},{8,0},{12,4},{16,24},{20,28},{24,16},{28,20},{1,9},{5... | collective-permute-start | bytes 331784 | tf_op jit(solution)/shard_map/ppermute | solution.py:191

commit v2 on v1

--- a/solution.py
+++ b/solution.py
@@ -29,18 +29,15 @@
     return jnp.where(hit, 1.0, 0.0).astype(jnp.bfloat16)
 
 
-def fwd_kernel(n, ob, vol_ref, rim_ref, w_ref, cols_ref, *rest):
+def fwd_kernel(n, ob, behind_ref, even_ref, odd_ref, w_ref, cols_ref, *rest):
     part_refs = rest[:-2] if n > 1 else rest[:-1]
     wide_ref = rest[-2] if n > 1 else rest[-1]
-    cb, planes, hgt, wid = vol_ref.shape
-    half = wid // 2
+    cb, _, hgt, wid = even_ref.shape
     groups = hgt // 4
-    lanes = groups * wid
-    sel = pair_matrix(False, wid, half)
+    sel = pair_matrix(False, wid, wid // 2)
     zero = jnp.zeros((cb, wid), jnp.float32)
-    for p in range(-1, planes):
-        plane = rim_ref[:, 0] if p < 0 else vol_ref[:, p]
-        wide_ref[...] = plane.astype(jnp.float32).reshape(cb * hgt, wid)
+    for a, plane_ref in enumerate((behind_ref, even_ref, odd_ref)):
+        wide_ref[...] = plane_ref[:, 0].astype(jnp.float32).reshape(cb * hgt, wid)
         row = [wide_ref[pl.ds(y, cb, stride=hgt), :] for y in range(hgt)]
         cls = [[row[4 * j + r] for j in range(groups)] for r in range(4)]
 
@@ -55,14 +52,10 @@
             )
             for e in range(3):
                 block = taps[:, e * wid : (e + 1) * wid].astype(jnp.bfloat16)
-                block = jnp.concatenate(
+                tap = (a * 3 + b) * 3 + e
+                cols_ref[tap * cb : (tap + 1) * cb, :] = jnp.concatenate(
                     [block[j * cb : (j + 1) * cb] for j in range(groups)], axis=1
                 )
-                for z in range(planes // 2):
-                    a = p + 1 - 2 * z
-                    if 0 <= a <= 2:
-                        tap = (a * 3 + b) * 3 + e
-                        cols_ref[tap * cb : (tap + 1) * cb, z * lanes : (z + 1) * lanes] = block
     part = lax.dot_general(
         w_ref[...],
         cols_ref[...],
@@ -80,32 +73,38 @@
         ref[...] = all_ref[pl.ds(start, ob), :]
 
 
-def act_kernel(up_ref, *rest):
-    *part_refs, pooled_ref, grad_ref = rest
+def spread_kernel(up_ref, out_ref):
+    groups, ob, small = up_ref.shape
+    wid = 4 * small
+    r = lax.broadcasted_iota(jnp.int32, (small, wid), 0)
+    c = lax.broadcasted_iota(jnp.int32, (small, wid), 1)
+    c = c - jnp.where(c >= 2 * small, 2 * small, 0)
+    grow = jnp.where((c >= 2 * r) & (c <= 2 * r + 1), 1.0, 0.0).astype(jnp.bfloat16)
+    for j in range(groups):
+        spread = jnp.dot(up_ref[j], grow, preferred_element_type=jnp.float32)
+        out_ref[:, j * wid : (j + 1) * wid] = spread * 0.125
+
+
+def act_kernel(spread_ref, *rest):
+    *part_refs, grad_ref, act_ref = rest
     pre = part_refs[0][...]
     for ref in part_refs[1:]:
         pre = pre + ref[...]
-    groups, ob, small = up_ref.shape
+    grad = spread_ref[...] * jnp.where(pre > 0, 1.0, SLOPE)
+    grad_ref[...] = grad.astype(jnp.bfloat16)
+    act_ref[...] = jnp.where(pre > 0, pre, SLOPE * pre)
+
+
+def pool_kernel(one_ref, two_ref, out_ref):
+    groups, ob, small = out_ref.shape
     wid = 4 * small
-    lanes = groups * wid
-    grow_r = lax.broadcasted_iota(jnp.int32, (small, wid), 0)
-    grow_c = lax.broadcasted_iota(jnp.int32, (small, wid), 1)
-    grow_c = grow_c - jnp.where(grow_c >= 2 * small, 2 * small, 0)
-    grow = jnp.where((grow_c >= 2 * grow_r) & (grow_c <= 2 * grow_r + 1), 1.0, 0.0)
-    pool_r = lax.broadcasted_iota(jnp.int32, (wid, small), 0)
-    pool_c = lax.broadcasted_iota(jnp.int32, (wid, small), 1)
-    pool_r = pool_r - jnp.where(pool_r >= 2 * small, 2 * small, 0)
-    pool = jnp.where((pool_r >= 2 * pool_c) & (pool_r <= 2 * pool_c + 1), 0.125, 0.0)
-    grow = grow.astype(jnp.bfloat16)
-    scale = jnp.where(pre > 0, 1.0, SLOPE)
-    act = jnp.where(pre > 0, pre, SLOPE * pre)
-    act = act[:, :lanes] + act[:, lanes:]
+    r = lax.broadcasted_iota(jnp.int32, (wid, small), 0)
+    c = lax.broadcasted_iota(jnp.int32, (wid, small), 1)
+    r = r - jnp.where(r >= 2 * small, 2 * small, 0)
+    pool = jnp.where((r >= 2 * c) & (r <= 2 * c + 1), 0.125, 0.0)
+    act = one_ref[...] + two_ref[...]
     for j in range(groups):
-        spread = jnp.dot(up_ref[j], grow, preferred_element_type=jnp.float32) * 0.125
-        for z in range(2):
-            at = slice(z * lanes + j * wid, z * lanes + (j + 1) * wid)
-            grad_ref[:, at] = (spread * scale[:, at]).astype(jnp.bfloat16)
-        pooled_ref[j] = jnp.dot(
+        out_ref[j] = jnp.dot(
             act[:, j * wid : (j + 1) * wid],
             pool,
             precision=lax.Precision.HIGHEST,
@@ -113,8 +112,11 @@
         ).astype(jnp.bfloat16)
 
 
-def weight_kernel(n, cols_ref, *rest):
-    *block_refs, wgrad_ref, grad_ref = rest
+def weight_kernel(n, first, *refs):
+    if first:
+        cols_ref, *block_refs, wgrad_ref, grad_ref = refs
+    else:
+        sum_ref, cols_ref, *block_refs, wgrad_ref, grad_ref = refs
     if n == 1:
         grad_ref[...] = block_refs[0][...]
     else:
@@ -123,15 +125,17 @@
         for k, ref in enumerate(block_refs):
             start = pl.multiple_of(lax.rem(me + n - k, n) * ob, ob)
             grad_ref[pl.ds(start, ob), :] = ref[...]
-    wgrad_ref[...] = lax.dot_general(
+    term = lax.dot_general(
         cols_ref[...],
         grad_ref[...],
         (((1,), (1,)), ((), ())),
         preferred_element_type=jnp.float32,
     )
-
-
-def input_kernel(w_ref, grad_ref, rim_ref, out_ref, wide_ref):
+    wgrad_ref[...] = term if first else sum_ref[...] + term
+
+
+def input_kernel(w_ref, *rest):
+    *grad_refs, out_ref, wide_ref = rest
     cb, planes, hgt, wid = out_ref.shape
     half = wid // 2
     groups = hgt // 4
@@ -142,8 +146,7 @@
     keep = lax.broadcasted_iota(jnp.int32, (3 * cb, lanes), 1) < lanes - half
     w = [w_ref[a * taps : (a + 1) * taps, :] for a in range(3)]
     behind = jnp.concatenate([w[2], w[0]], axis=1)
-    g = [grad_ref[:, z * lanes : (z + 1) * lanes] for z in range(planes // 2)]
-    g.append(rim_ref[...])
+    g = [ref[...] for ref in grad_refs]
     for i in range(planes):
         z = i // 2
         if i % 2 == 0:
@@ -214,59 +217,83 @@
     direct = n_chan <= FEW
     n = n_chan if direct else 1
     taps = 27 * cb
-    lanes = hgt // 4 * wid
-    cells = planes // 2 * lanes
+    cells = hgt // 4 * wid
+    f32, bf16 = jnp.float32, jnp.bfloat16
     rim = lax.ppermute(volume[:, -1:], "space", [(i, i + 1) for i in range(n_space - 1)])
     weights = kernel.transpose(1, 2, 3, 0, 4).reshape(taps, out_ch)
     up = upstream[:, 0].transpose(1, 0, 2)
-
-    part_shape = jax.ShapeDtypeStruct((ob if direct else out_ch, cells), jnp.float32)
-    scratch = [pltpu.VMEM((cb * hgt, wid), jnp.float32)]
+    spread = pl.pallas_call(
+        spread_kernel,
+        out_shape=jax.ShapeDtypeStruct((ob, cells), f32),
+        compiler_params=params(),
+    )(up)
+
+    scratch = [pltpu.VMEM((cb * hgt, wid), f32)]
     if n > 1:
-        scratch.append(pltpu.VMEM((out_ch, cells), jnp.float32))
-    cols, *parts = pl.pallas_call(
-        functools.partial(fwd_kernel, n, ob),
-        out_shape=[jax.ShapeDtypeStruct((taps, cells), jnp.bfloat16)] + [part_shape] * n,
-        scratch_shapes=scratch,
+        scratch.append(pltpu.VMEM((out_ch, cells), f32))
+    part_shape = jax.ShapeDtypeStruct((ob if direct else out_ch, cells), f32)
+    whole = pl.BlockSpec(memory_space=pltpu.VMEM)
+
+    def plane(p):
+        return pl.BlockSpec((cb, 1, hgt, wid), lambda i: (0, max(p, 0), 0, 0))
+
+    out_planes = range(planes // 2)
+    cols, grads, acts = {}, {}, {}
+    for z in reversed(out_planes):
+        cols[z], *parts = pl.pallas_call(
+            functools.partial(fwd_kernel, n, ob),
+            grid=(1,),
+            in_specs=[plane(2 * z - 1), plane(2 * z), plane(2 * z + 1), whole],
+            out_specs=[whole] * (n + 1),
+            out_shape=[jax.ShapeDtypeStruct((taps, cells), bf16)] + [part_shape] * n,
+            scratch_shapes=scratch,
+            compiler_params=params(),
+        )(volume if z else rim, volume, volume, weights)
+        if direct:
+            parts = parts[:1] + [shifted_by(parts[k], "chan", k) for k in range(1, n)]
+        else:
+            parts = [lax.psum_scatter(parts[0], "chan", scatter_dimension=0, tiled=True)]
+        own, acts[z] = pl.pallas_call(
+            act_kernel,
+            out_shape=[
+                jax.ShapeDtypeStruct((ob, cells), bf16),
+                jax.ShapeDtypeStruct((ob, cells), f32),
+            ],
+            compiler_params=params(),
+        )(spread, *parts)
+        if direct:
+            grads[z] = [own] + [shifted_by(own, "chan", k) for k in range(1, n)]
+        else:
+            grads[z] = [lax.all_gather(own, "chan", axis=0, tiled=True)]
+
+    pooled = pl.pallas_call(
+        pool_kernel,
+        out_shape=jax.ShapeDtypeStruct(up.shape, bf16),
         compiler_params=params(),
-    )(volume, rim, weights)
-    if direct:
-        parts = parts[:1] + [shifted_by(parts[k], "chan", k) for k in range(1, n)]
-    else:
-        parts = [lax.psum_scatter(parts[0], "chan", scatter_dimension=0, tiled=True)]
-
-    pooled, own = pl.pallas_call(
-        act_kernel,
-        out_shape=[
-            jax.ShapeDtypeStruct(up.shape, jnp.bfloat16),
-            jax.ShapeDtypeStruct((ob, cells), jnp.bfloat16),
-        ],
-        compiler_params=params(),
-    )(up, *parts)
+    )(acts[0], acts[1])
     pooled = pooled.transpose(1, 0, 2)[:, None]
-    if direct:
-        blocks = [own] + [shifted_by(own, "chan", k) for k in range(1, n)]
-    else:
-        blocks = [lax.all_gather(own, "chan", axis=0, tiled=True)]
-
-    weight_grad, grad = pl.pallas_call(
-        functools.partial(weight_kernel, n),
-        out_shape=[
-            jax.ShapeDtypeStruct((taps, out_ch), jnp.float32),
-            jax.ShapeDtypeStruct((out_ch, cells), jnp.bfloat16),
-        ],
-        compiler_params=params(),
-    )(cols, *blocks)
-    weight_grad = sum_over(weight_grad, "space")
+
+    weight_grad = []
+    for z in reversed(out_planes):
+        wgrad, grads[z] = pl.pallas_call(
+            functools.partial(weight_kernel, n, not weight_grad),
+            out_shape=[
+                jax.ShapeDtypeStruct((taps, out_ch), f32),
+                jax.ShapeDtypeStruct((out_ch, cells), bf16),
+            ],
+            compiler_params=params(),
+        )(*weight_grad, cols[z], *grads[z])
+        weight_grad = [wgrad]
+    after = lax.ppermute(grads[0], "space", [(i + 1, i) for i in range(n_space - 1)])
+    weight_grad = sum_over(weight_grad[0], "space")
     weight_grad = weight_grad.reshape(3, 3, 3, cb, out_ch).transpose(3, 0, 1, 2, 4)
 
-    after = lax.ppermute(grad[:, :lanes], "space", [(i + 1, i) for i in range(n_space - 1)])
     input_grad = pl.pallas_call(
         input_kernel,
-        out_shape=jax.ShapeDtypeStruct(volume.shape, jnp.bfloat16),
-        scratch_shapes=[pltpu.VMEM((cb * planes * hgt, wid), jnp.float32)],
+        out_shape=jax.ShapeDtypeStruct(volume.shape, bf16),
+        scratch_shapes=[pltpu.VMEM((cb * planes * hgt, wid), f32)],
         compiler_params=params(),
-    )(weights, grad, after)
+    )(weights, *[grads[z] for z in out_planes], after)
     return pooled, input_grad, weight_grad
 
 

time: 65.1 us -> 67.1 us (1.031)
  waiting for transfers between devices: 22.4 us -> 8.23 us
  Pallas kernels: 12.2 us -> 20.7 us
  starting transfers between devices: 20.7 us -> 28 us
    ppermute x6 -> x12, waiting for transfers between devices: 13.1 us -> 0.03 us  [shifted_by(): return lax.ppermute(block, axis, [(i, (i + k) % n) for i in range(n)])]
    pallas_call x3 -> x8, Pallas kernels: 8.47 us -> 16.8 us  [the longest x2 5.41 us: on_device(): pl.pallas_call(functools.partial(fwd_kernel, n, ob), grid=(1,), in_specs=...]
    ppermute x6 -> x12, starting transfers between devices: 11.1 us -> 19 us  [shifted_by(): return lax.ppermute(block, axis, [(i, (i + k) % n) for i in range(n)])]
    unnamed x20 -> x34, local copies, waits for them, and re-layouts: 4.67 us -> 5.82 us
    ppermute x1, waiting for transfers between devices: 0.96 us -> 0.01 us  [on_device(): lax.ppermute(volume[:, -1:], 'space', [(i, i + 1) for i in range(n_space...]
    slice x1 -> x0, local copies, waits for them, and re-layouts: 0.91 us -> none  [on_device(): grad[:, :lanes]]
  transfers between devices with their start and end apart: 13 -> 19, of which waited for: 8 -> 4; matrix products, arithmetic and copies ran while one was open for 5% -> 3% of each run, Pallas kernels for 6% -> 27%
where the time goes in v2:
time: 67.1 us; the launch traced here: 66.4 us
  starting transfers between devices  28 us (42%)
  Pallas kernels  20.7 us (31%)
  waiting for transfers between devices  8.23 us (12%)
  local copies, waits for them, and re-layouts  6.76 us (10%)
  other arithmetic  1.96 us (3%)
  between operations  0.8 us (1%)
    ppermute x12, starting transfers between devices, shifted_by(): return lax.ppermute(block, axis, [(i, (i + k) % n) for i in range(n)])  19 us
    ppermute x5, waiting for transfers between devices, swapped(): return lax.ppermute(block, axis, [(i, i ^ bit) for i in range(n)])  8.19 us
    unnamed x34, local copies, waits for them, and re-layouts  5.82 us
    pallas_call x2, Pallas kernels, on_device(): pl.pallas_call(functools.partial(fwd_kernel, n, ob), grid=(1,), in_specs=...  5.41 us
    ppermute x5, starting transfers between devices, swapped(): return lax.ppermute(block, axis, [(i, i ^ bit) for i in range(n)])  5.36 us
    pallas_call x2, Pallas kernels, on_device(): pl.pallas_call(functools.partial(weight_kernel, n, not weight_grad), out_...  4.85 us
    pallas_call x1, Pallas kernels, on_device(): pl.pallas_call(input_kernel, out_shape=jax.ShapeDtypeStruct(volume.shape,...  3.83 us
    pallas_call x2, Pallas kernels, on_device(): pl.pallas_call(act_kernel, out_shape=[jax.ShapeDtypeStruct((ob, cells), b...  3.25 us
  transfers between devices with their start and end apart: 19, of which 4 were waited for; matrix products, arithmetic and copies ran while one was open for 3% of the time, Pallas kernels for 27%

profile of v2, /device:TPU:0, one launch (start us, length us, event | category | flops | bytes accessed | tf_op | source)
XLA Modules:
  0.0 66.4 jit_solution(15567892850516420060)
XLA Ops:
  0.6 0.9 %slice.3 = bf16[32,1,16,128]{3,2,1,0:T(8,128)(2,1)S(1)} slice(bf16[32,4,16,128]{3,2,1,0:T(8,128)(2,1)} %odd_ref.3), slice={[0:32], [3:4], [0:16], [0:128]} | slice | bytes 262144 | tf_op jit(solution)/shard_map/slice | solution.py:222
  1.6 2.4 %collective-permute-start = (bf16[32,1,16,128]{3,2,1,0:T(8,128)(2,1)S(1)}, bf16[32,1,16,128]{3,2,1,0:T(8,128)(2,1)S(1)}, u32[]{:S(2)}, u32[]{:S(2)}) collective-permute-start(bf16[32,1,16,128]{3,2,1,0:T(8,128)(2,1)S(1)} %slice.3), channel_id=1, source_target_pairs={{0,4},{4,8},{8,12},{12,16},{16,20},{20,24},{24,28},{1,5},{5,9},{9,... | collective-permute-start | bytes 393224 | tf_op jit(solution)/shard_map/ppermute | solution.py:222
  3.9 2.7 %shard_map.61 = (bf16[864,512]{1,0:T(8,128)(2,1)}, f32[32,512]{1,0:T(8,128)}, f32[32,512]{1,0:T(8,128)}, f32[32,512]{1,0:T(8,128)}, f32[32,512]{1,0:T(8,128)}) custom-call(bf16[32,4,16,128]{3,2,1,0:T(8,128)(2,1)} %odd_ref.3, bf16[32,4,16,128]{3,2,1,0:T(8,128)(2,1)} %odd_ref.3, bf16[32,4,16,128]{3,2,1,0:T(8,128)(2,1)} %odd_ref.3, bf16[864,128]{1,0:T(8,128)(2,1)} %bitcast.14), custom_call_target="tpu_custom_call" | custom-call | tf_op jit(solution)/shard_map/pallas_call | solution.py:243
  6.7 2.4 %collective-permute-start.4 = (f32[32,512]{1,0:T(8,128)}, f32[32,512]{1,0:T(8,128)S(1)}, u32[]{:S(2)}, u32[]{:S(2)}) collective-permute-start(f32[32,512]{1,0:T(8,128)} %get-tuple-element.27), channel_id=1, source_target_pairs={{0,1},{1,2},{2,3},{3,0},{4,5},{5,6},{6,7},{7,4},{8,9},{9,10},{10,1... | collective-permute-start | bytes 196616 | tf_op jit(solution)/shard_map/ppermute | solution.py:189
  9.1 2.6 %collective-permute-start.5 = (f32[32,512]{1,0:T(8,128)}, f32[32,512]{1,0:T(8,128)S(1)}, u32[]{:S(2)}, u32[]{:S(2)}) collective-permute-start(f32[32,512]{1,0:T(8,128)} %get-tuple-element.28), channel_id=1, source_target_pairs={{0,2},{1,3},{2,0},{3,1},{4,6},{5,7},{6,4},{7,5},{8,10},{9,11},{10,... | collective-permute-start | bytes 196616 | tf_op jit(solution)/shard_map/ppermute | solution.py:189
  11.7 1.3 %collective-permute-start.6 = (f32[32,512]{1,0:T(8,128)}, f32[32,512]{1,0:T(8,128)S(1)}, u32[]{:S(2)}, u32[]{:S(2)}) collective-permute-start(f32[32,512]{1,0:T(8,128)} %get-tuple-element.29), channel_id=1, source_target_pairs={{0,3},{1,0},{2,1},{3,2},{4,7},{5,4},{6,5},{7,6},{8,11},{9,8},{10,9... | collective-permute-start | bytes 196616 | tf_op jit(solution)/shard_map/ppermute | solution.py:189
  13.0 0.7 copy-done.2
  13.7 2.7 %shard_map.59 = (bf16[864,512]{1,0:T(8,128)(2,1)}, f32[32,512]{1,0:T(8,128)}, f32[32,512]{1,0:T(8,128)}, f32[32,512]{1,0:T(8,128)}, f32[32,512]{1,0:T(8,128)}) custom-call(bf16[32,1,16,128]{3,2,1,0:T(8,128)(2,1)} %copy-done.2, bf16[32,4,16,128]{3,2,1,0:T(8,128)(2,1)} %odd_ref.3, bf16[32,4,16,128]{3,2,1,0:T(8,128)(2,1)} %odd_ref.3, bf16[864,128]{1,0:T(8,128)(2,1)} %bitcast.15), custom_call_target="tpu_custom_call" | custom-call | tf_op jit(solution)/shard_map/pallas_call | solution.py:243
  16.3 0.7 %collective-permute-start.1 = (f32[32,512]{1,0:T(8,128)}, f32[32,512]{1,0:T(8,128)S(1)}, u32[]{:S(2)}, u32[]{:S(2)}) collective-permute-start(f32[32,512]{1,0:T(8,128)} %get-tuple-element.22), channel_id=1, source_target_pairs={{0,1},{1,2},{2,3},{3,0},{4,5},{5,6},{6,7},{7,4},{8,9},{9,10},{10,1... | collective-permute-start | bytes 196616 | tf_op jit(solution)/shard_map/ppermute | solution.py:189
  17.4 2.9 %collective-permute-start.3 = (f32[32,512]{1,0:T(8,128)}, f32[32,512]{1,0:T(8,128)S(1)}, u32[]{:S(2)}, u32[]{:S(2)}) collective-permute-start(f32[32,512]{1,0:T(8,128)} %get-tuple-element.24), channel_id=1, source_target_pairs={{0,3},{1,0},{2,1},{3,2},{4,7},{5,4},{6,5},{7,6},{8,11},{9,8},{10,9... | collective-permute-start | bytes 196616 | tf_op jit(solution)/shard_map/ppermute | solution.py:189
  20.9 1.5 %shard_map.58.spread_ref = f32[32,512]{1,0:T(8,128)} custom-call(bf16[4,32,32]{2,1,0:T(8,128)(2,1)} %bitcast.19), custom_call_target="tpu_custom_call" | custom-call | tf_op jit(solution)/shard_map/pallas_call | solution.py:225
  23.0 1.6 %shard_map.62 = (bf16[32,512]{1,0:T(8,128)(2,1)}, f32[32,512]{1,0:T(8,128)}) custom-call(f32[32,512]{1,0:T(8,128)} %shard_map.58.spread_ref, f32[32,512]{1,0:T(8,128)} %get-tuple-element.26.rest_0_, f32[32,512]{1,0:T(8,128)} %copy-done.5, f32[32,512]{1,0:T(8,128)} %copy-done.7, f32[32,512]{1,0:T(8,128)} %copy-done.8), custom_call_target="tpu_custom_call" | custom-call | tf_op jit(solution)/shard_map/pallas_call | solution.py:256
  25.2 1.4 %collective-permute-start.8 = (bf16[32,512]{1,0:T(8,128)(2,1)}, bf16[32,512]{1,0:T(8,128)(2,1)S(1)}, u32[]{:S(2)}, u32[]{:S(2)}) collective-permute-start(bf16[32,512]{1,0:T(8,128)(2,1)} %get-tuple-element.32.refs_1_), channel_id=1, source_target_pairs={{0,2},{1,3},{2,0},{3,1},{4,6},{5,7},{6,4},{7,5},{8,10},{9,11},{10,... | collective-permute-start | bytes 98312 | tf_op jit(solution)/shard_map/ppermute | solution.py:189
  26.7 2.9 %collective-permute-start.9 = (bf16[32,512]{1,0:T(8,128)(2,1)}, bf16[32,512]{1,0:T(8,128)(2,1)S(1)}, u32[]{:S(2)}, u32[]{:S(2)}) collective-permute-start(bf16[32,512]{1,0:T(8,128)(2,1)} %get-tuple-element.32.refs_1_), channel_id=1, source_target_pairs={{0,3},{1,0},{2,1},{3,2},{4,7},{5,4},{6,5},{7,6},{8,11},{9,8},{10,9... | collective-permute-start | bytes 98312 | tf_op jit(solution)/shard_map/ppermute | solution.py:189
  30.2 1.6 %shard_map.60 = (bf16[32,512]{1,0:T(8,128)(2,1)}, f32[32,512]{1,0:T(8,128)}) custom-call(f32[32,512]{1,0:T(8,128)} %shard_map.58.spread_ref, f32[32,512]{1,0:T(8,128)} %get-tuple-element.21.rest_0_, f32[32,512]{1,0:T(8,128)} %copy-done.3, f32[32,512]{1,0:T(8,128)} %copy-done.4, f32[32,512]{1,0:T(8,128)} %copy-done.6), custom_call_target="tpu_custom_call" | custom-call | tf_op jit(solution)/shard_map/pallas_call | solution.py:256
  31.9 1.0 %collective-permute-start.11 = (bf16[32,512]{1,0:T(8,128)(2,1)}, bf16[32,512]{1,0:T(8,128)(2,1)S(1)}, u32[]{:S(2)}, u32[]{:S(2)}) collective-permute-start(bf16[32,512]{1,0:T(8,128)(2,1)} %get-tuple-element.35.refs_2_), channel_id=1, source_target_pairs={{0,2},{1,3},{2,0},{3,1},{4,6},{5,7},{6,4},{7,5},{8,10},{9,11},{10,... | collective-permute-start | bytes 98312 | tf_op jit(solution)/shard_map/ppermute | solution.py:189
  32.8 2.9 %collective-permute-start.12 = (bf16[32,512]{1,0:T(8,128)(2,1)}, bf16[32,512]{1,0:T(8,128)(2,1)S(1)}, u32[]{:S(2)}, u32[]{:S(2)}) collective-permute-start(bf16[32,512]{1,0:T(8,128)(2,1)} %get-tuple-element.35.refs_2_), channel_id=1, source_target_pairs={{0,3},{1,0},{2,1},{3,2},{4,7},{5,4},{6,5},{7,6},{8,11},{9,8},{10,9... | collective-permute-start | bytes 98312 | tf_op jit(solution)/shard_map/ppermute | solution.py:189
  36.4 2.4 %shard_map.64 = (f32[864,128]{1,0:T(8,128)}, bf16[128,512]{1,0:T(8,128)(2,1)}) custom-call(bf16[864,512]{1,0:T(8,128)(2,1)} %get-tuple-element.31.refs_0_, bf16[32,512]{1,0:T(8,128)(2,1)} %get-tuple-element.32.refs_1_, bf16[32,512]{1,0:T(8,128)(2,1)} %copy-done.9, bf16[32,512]{1,0:T(8,128)(2,1)} %copy-done.10, bf16[32,512]{1,0:T(8,128)(2,1)} %copy-done.11), custom_call_target="tpu_custom_call" | custom-call | tf_op jit(solution)/shard_map/pallas_call | solution.py:278
  39.4 2.5 %shard_map.65 = (f32[864,128]{1,0:T(8,128)}, bf16[128,512]{1,0:T(8,128)(2,1)}) custom-call(f32[864,128]{1,0:T(8,128)} %get-tuple-element.33.refs_0_, bf16[864,512]{1,0:T(8,128)(2,1)} %get-tuple-element.34.refs_1_, bf16[32,512]{1,0:T(8,128)(2,1)} %get-tuple-element.35.refs_2_, bf16[32,512]{1,0:T(8,128)(2,1)} %copy-done.12, bf16[32,512]{1,0:T(8,128)(2,1)} %copy-done.13, ...), custom_call_target="tpu_custom_call" | custom-call | tf_op jit(solution)/shard_map/pallas_call | solution.py:278
  41.9 2.0 %collective-permute-done.14 = f32[864,128]{1,0:T(8,128)S(1)} collective-permute-done((f32[864,128]{1,0:T(8,128)}, f32[864,128]{1,0:T(8,128)S(1)}, u32[]{:S(2)}, u32[]{:S(2)}) %collective-permute-start.14) | collective-permute-done | bytes 442400 | tf_op jit(solution)/shard_map/ppermute | solution.py:194
  43.9 1.1 %add_convert_fusion = bf16[864,128]{1,0:T(8,128)(2,1)S(1)} fusion(f32[864,128]{1,0:T(8,128)} %get-tuple-element.38, f32[864,128]{1,0:T(8,128)S(1)} %collective-permute-done.14), kind=kLoop, calls=%fused_computation.1 | loop fusion | flops 221184 | bytes 1105920 | tf_op jit(solution)/shard_map/convert.1
  45.0 1.7 %collective-permute-start.15 = (bf16[432,128]{1,0:T(8,128)(2,1)S(1)}, bf16[432,128]{1,0:T(8,128)(2,1)S(1)}, u32[]{:S(2)}, u32[]{:S(2)}) collective-permute-start(bf16[432,128]{1,0:T(8,128)(2,1)S(1)} %get-tuple-element.44), channel_id=1, source_target_pairs={{0,8},{4,12},{8,0},{12,4},{16,24},{20,28},{24,16},{28,20},{1,9},{5... | collective-permute-start | bytes 331784 | tf_op jit(solution)/shard_map/ppermute | solution.py:194
  46.7 1.5 %collective-permute-start.17 = (bf16[432,128]{1,0:T(8,128)(2,1)S(1)}, bf16[432,128]{1,0:T(8,128)(2,1)S(1)}, u32[]{:S(2)}, u32[]{:S(2)}) collective-permute-start(bf16[432,128]{1,0:T(8,128)(2,1)S(1)} %get-tuple-element.45), channel_id=1, source_target_pairs={{0,16},{4,20},{8,24},{12,28},{16,0},{20,4},{24,8},{28,12},{1,17},{... | collective-permute-start | bytes 331784 | tf_op jit(solution)/shard_map/ppermute | solution.py:194
  48.2 1.3 %collective-permute-start.13 = (bf16[128,512]{1,0:T(8,128)(2,1)S(1)}, bf16[128,512]{1,0:T(8,128)(2,1)S(1)}, u32[]{:S(2)}, u32[]{:S(2)}) collective-permute-start(bf16[128,512]{1,0:T(8,128)(2,1)S(1)} %copy-done), channel_id=1, source_target_pairs={{4,0},{8,4},{12,8},{16,12},{20,16},{24,20},{28,24},{5,1},{9,5},{13... | collective-permute-start | bytes 393224 | tf_op jit(solution)/shard_map/ppermute | solution.py:287
  50.2 1.4 %collective-permute-done.17 = bf16[432,128]{1,0:T(8,128)(2,1)S(1)} collective-permute-done((bf16[432,128]{1,0:T(8,128)(2,1)S(1)}, bf16[432,128]{1,0:T(8,128)(2,1)S(1)}, u32[]{:S(2)}, u32[]{:S(2)}) %collective-permute-start.17) | collective-permute-done | bytes 110624 | tf_op jit(solution)/shard_map/ppermute | solution.py:194
  51.6 1.6 %collective-permute-start.16 = (bf16[432,128]{1,0:T(8,128)(2,1)S(1)}, bf16[432,128]{1,0:T(8,128)(2,1)S(1)}, u32[]{:S(2)}, u32[]{:S(2)}) collective-permute-start(bf16[432,128]{1,0:T(8,128)(2,1)S(1)} %get-tuple-element.42), channel_id=1, source_target_pairs={{0,16},{4,20},{8,24},{12,28},{16,0},{20,4},{24,8},{28,12},{1,17},{... | collective-permute-start | bytes 331784 | tf_op jit(solution)/shard_map/ppermute | solution.py:194
  53.2 1.8 %shard_map.63 = bf16[4,32,32]{2,1,0:T(8,128)(2,1)} custom-call(f32[32,512]{1,0:T(8,128)} %get-tuple-element.25.one_ref, f32[32,512]{1,0:T(8,128)} %get-tuple-element.30.two_ref), custom_call_target="tpu_custom_call" | custom-call | tf_op jit(solution)/shard_map/pallas_call | solution.py:269
  55.0 1.4 %copy.7 = bf16[32,1,4,32]{3,2,1,0:T(4,128)(2,1)} copy(bf16[32,1,4,32]{3,0,2,1:T(8,128)(2,1)} %bitcast.18) | data formatting | bytes 16384
  56.4 0.7 copy-done.1
  57.0 3.8 %shard_map.66 = bf16[32,4,16,128]{3,2,1,0:T(8,128)(2,1)} custom-call(bf16[864,128]{1,0:T(8,128)(2,1)} %bitcast.16, bf16[128,512]{1,0:T(8,128)(2,1)} %get-tuple-element.36.rest_0_, bf16[128,512]{1,0:T(8,128)(2,1)} %get-tuple-element.37.rest_1_, bf16[128,512]{1,0:T(8,128)(2,1)} %copy-done.1), custom_call_target="tpu_custom_call" | custom-call | tf_op jit(solution)/shard_map/pallas_call | solution.py:291
  61.4 4.2 %collective-permute-done.18 = bf16[432,128]{1,0:T(8,128)(2,1)S(1)} collective-permute-done((bf16[432,128]{1,0:T(8,128)(2,1)S(1)}, bf16[432,128]{1,0:T(8,128)(2,1)S(1)}, u32[]{:S(2)}, u32[]{:S(2)}) %collective-permute-start.18) | collective-permute-done | bytes 110624 | tf_op jit(solution)/shard_map/ppermute | solution.py:194
  65.6 0.8 %pad_maximum_fusion = f32[864,128]{1,0:T(8,128)} fusion(f32[432,128]{1,0:T(8,128)S(1)} %convert_add_fusion, f32[432,128]{1,0:T(8,128)S(1)} %convert_add_fusion.1), kind=kLoop, calls=%fused_computation | loop fusion | flops 110592 | bytes 884736 | tf_op jit(solution)/shard_map/concatenate | solution.py:209
  (56 shorter events, 5.3 us)
Async XLA Ops:
  1.6 11.4 %collective-permute-start = (bf16[32,1,16,128]{3,2,1,0:T(8,128)(2,1)S(1)}, bf16[32,1,16,128]{3,2,1,0:T(8,128)(2,1)S(1)}, u32[]{:S(2)}, u32[]{:S(2)}) collective-permute-start(bf16[32,1,16,128]{3,2,1,0:T(8,128)(2,1)S(1)} %slice.3), channel_id=1, source_target_pairs={{0,4},{4,8},{8,12},{12,16},{16,20},{20,24},{24,28},{1,5},{5,9},{9,... | collective-permute-start | bytes 393224 | tf_op jit(solution)/shard_map/ppermute | solution.py:222
  6.7 10.7 %collective-permute-start.4 = (f32[32,512]{1,0:T(8,128)}, f32[32,512]{1,0:T(8,128)S(1)}, u32[]{:S(2)}, u32[]{:S(2)}) collective-permute-start(f32[32,512]{1,0:T(8,128)} %get-tuple-element.27), channel_id=1, source_target_pairs={{0,1},{1,2},{2,3},{3,0},{4,5},{5,6},{6,7},{7,4},{8,9},{9,10},{10,1... | collective-permute-start | bytes 196616 | tf_op jit(solution)/shard_map/ppermute | solution.py:189
  9.1 13.3 %collective-permute-start.5 = (f32[32,512]{1,0:T(8,128)}, f32[32,512]{1,0:T(8,128)S(1)}, u32[]{:S(2)}, u32[]{:S(2)}) collective-permute-start(f32[32,512]{1,0:T(8,128)} %get-tuple-element.28), channel_id=1, source_target_pairs={{0,2},{1,3},{2,0},{3,1},{4,6},{5,7},{6,4},{7,5},{8,10},{9,11},{10,... | collective-permute-start | bytes 196616 | tf_op jit(solution)/shard_map/ppermute | solution.py:189
  11.6 8.6 %copy-start.15 = (bf16[32,1,4,32]{3,2,1,0:T(4,128)(2,1)S(1)}, bf16[32,1,4,32]{3,2,1,0:T(4,128)(2,1)}, u32[]{:S(2)}) copy-start(bf16[32,1,4,32]{3,2,1,0:T(4,128)(2,1)} %param.5) | copy-start | bytes 24580
  11.7 10.7 %collective-permute-start.6 = (f32[32,512]{1,0:T(8,128)}, f32[32,512]{1,0:T(8,128)S(1)}, u32[]{:S(2)}, u32[]{:S(2)}) collective-permute-start(f32[32,512]{1,0:T(8,128)} %get-tuple-element.29), channel_id=1, source_target_pairs={{0,3},{1,0},{2,1},{3,2},{4,7},{5,4},{6,5},{7,6},{8,11},{9,8},{10,9... | collective-permute-start | bytes 196616 | tf_op jit(solution)/shard_map/ppermute | solution.py:189
  13.0 0.7 copy-start.2
  16.3 10.3 %collective-permute-start.1 = (f32[32,512]{1,0:T(8,128)}, f32[32,512]{1,0:T(8,128)S(1)}, u32[]{:S(2)}, u32[]{:S(2)}) collective-permute-start(f32[32,512]{1,0:T(8,128)} %get-tuple-element.22), channel_id=1, source_target_pairs={{0,1},{1,2},{2,3},{3,0},{4,5},{5,6},{6,7},{7,4},{8,9},{9,10},{10,1... | collective-permute-start | bytes 196616 | tf_op jit(solution)/shard_map/ppermute | solution.py:189
  17.0 12.6 %collective-permute-start.2 = (f32[32,512]{1,0:T(8,128)}, f32[32,512]{1,0:T(8,128)S(1)}, u32[]{:S(2)}, u32[]{:S(2)}) collective-permute-start(f32[32,512]{1,0:T(8,128)} %get-tuple-element.23), channel_id=1, source_target_pairs={{0,2},{1,3},{2,0},{3,1},{4,6},{5,7},{6,4},{7,5},{8,10},{9,11},{10,... | collective-permute-start | bytes 196616 | tf_op jit(solution)/shard_map/ppermute | solution.py:189
  17.4 5.0 %copy-start.5 = (f32[32,512]{1,0:T(8,128)}, f32[32,512]{1,0:T(8,128)S(1)}, u32[]{:S(2)}) copy-start(f32[32,512]{1,0:T(8,128)S(1)} %collective-permute-done.4.rest_1_) | copy-start | bytes 196612
  17.4 12.2 %collective-permute-start.3 = (f32[32,512]{1,0:T(8,128)}, f32[32,512]{1,0:T(8,128)S(1)}, u32[]{:S(2)}, u32[]{:S(2)}) collective-permute-start(f32[32,512]{1,0:T(8,128)} %get-tuple-element.24), channel_id=1, source_target_pairs={{0,3},{1,0},{2,1},{3,2},{4,7},{5,4},{6,5},{7,6},{8,11},{9,8},{10,9... | collective-permute-start | bytes 196616 | tf_op jit(solution)/shard_map/ppermute | solution.py:189
  22.4 0.6 copy-start.7
  22.4 0.6 copy-start.8
  24.7 8.2 %collective-permute-start.7 = (bf16[32,512]{1,0:T(8,128)(2,1)}, bf16[32,512]{1,0:T(8,128)(2,1)S(1)}, u32[]{:S(2)}, u32[]{:S(2)}) collective-permute-start(bf16[32,512]{1,0:T(8,128)(2,1)} %get-tuple-element.32.refs_1_), channel_id=1, source_target_pairs={{0,1},{1,2},{2,3},{3,0},{4,5},{5,6},{6,7},{7,4},{8,9},{9,10},{10,1... | collective-permute-start | bytes 98312 | tf_op jit(solution)/shard_map/ppermute | solution.py:189
  25.2 10.6 %collective-permute-start.8 = (bf16[32,512]{1,0:T(8,128)(2,1)}, bf16[32,512]{1,0:T(8,128)(2,1)S(1)}, u32[]{:S(2)}, u32[]{:S(2)}) collective-permute-start(bf16[32,512]{1,0:T(8,128)(2,1)} %get-tuple-element.32.refs_1_), channel_id=1, source_target_pairs={{0,2},{1,3},{2,0},{3,1},{4,6},{5,7},{6,4},{7,5},{8,10},{9,11},{10,... | collective-permute-start | bytes 98312 | tf_op jit(solution)/shard_map/ppermute | solution.py:189
  26.7 2.9 %copy-start.3 = (f32[32,512]{1,0:T(8,128)}, f32[32,512]{1,0:T(8,128)S(1)}, u32[]{:S(2)}) copy-start(f32[32,512]{1,0:T(8,128)S(1)} %collective-permute-done.1.rest_1_) | copy-start | bytes 196612
  26.7 9.1 %collective-permute-start.9 = (bf16[32,512]{1,0:T(8,128)(2,1)}, bf16[32,512]{1,0:T(8,128)(2,1)S(1)}, u32[]{:S(2)}, u32[]{:S(2)}) collective-permute-start(bf16[32,512]{1,0:T(8,128)(2,1)} %get-tuple-element.32.refs_1_), channel_id=1, source_target_pairs={{0,3},{1,0},{2,1},{3,2},{4,7},{5,4},{6,5},{7,6},{8,11},{9,8},{10,9... | collective-permute-start | bytes 98312 | tf_op jit(solution)/shard_map/ppermute | solution.py:189
  29.6 0.6 copy-start.4
  29.6 0.7 copy-start.6
  31.9 6.9 %collective-permute-start.10 = (bf16[32,512]{1,0:T(8,128)(2,1)}, bf16[32,512]{1,0:T(8,128)(2,1)S(1)}, u32[]{:S(2)}, u32[]{:S(2)}) collective-permute-start(bf16[32,512]{1,0:T(8,128)(2,1)} %get-tuple-element.35.refs_2_), channel_id=1, source_target_pairs={{0,1},{1,2},{2,3},{3,0},{4,5},{5,6},{6,7},{7,4},{8,9},{9,10},{10,1... | collective-permute-start | bytes 98312 | tf_op jit(solution)/shard_map/ppermute | solution.py:189
  31.9 6.9 %collective-permute-start.11 = (bf16[32,512]{1,0:T(8,128)(2,1)}, bf16[32,512]{1,0:T(8,128)(2,1)S(1)}, u32[]{:S(2)}, u32[]{:S(2)}) collective-permute-start(bf16[32,512]{1,0:T(8,128)(2,1)} %get-tuple-element.35.refs_2_), channel_id=1, source_target_pairs={{0,2},{1,3},{2,0},{3,1},{4,6},{5,7},{6,4},{7,5},{8,10},{9,11},{10,... | collective-permute-start | bytes 98312 | tf_op jit(solution)/shard_map/ppermute | solution.py:189
  32.8 2.9 %copy-start.9 = (bf16[32,512]{1,0:T(8,128)(2,1)}, bf16[32,512]{1,0:T(8,128)(2,1)S(1)}, u32[]{:S(2)}) copy-start(bf16[32,512]{1,0:T(8,128)(2,1)S(1)} %collective-permute-done.7.refs_2_) | copy-start | bytes 98308
  32.8 6.0 %collective-permute-start.12 = (bf16[32,512]{1,0:T(8,128)(2,1)}, bf16[32,512]{1,0:T(8,128)(2,1)S(1)}, u32[]{:S(2)}, u32[]{:S(2)}) collective-permute-start(bf16[32,512]{1,0:T(8,128)(2,1)} %get-tuple-element.35.refs_2_), channel_id=1, source_target_pairs={{0,3},{1,0},{2,1},{3,2},{4,7},{5,4},{6,5},{7,6},{8,11},{9,8},{10,9... | collective-permute-start | bytes 98312 | tf_op jit(solution)/shard_map/ppermute | solution.py:189
  35.8 0.6 copy-start.10
  38.8 0.6 copy-start.14
  41.9 2.0 %collective-permute-start.14 = (f32[864,128]{1,0:T(8,128)}, f32[864,128]{1,0:T(8,128)S(1)}, u32[]{:S(2)}, u32[]{:S(2)}) collective-permute-start(f32[864,128]{1,0:T(8,128)} %get-tuple-element.38), channel_id=1, source_target_pairs={{0,4},{4,0},{8,12},{12,8},{16,20},{20,16},{24,28},{28,24},{1,5},{5... | collective-permute-start | bytes 1327112 | tf_op jit(solution)/shard_map/ppermute | solution.py:194
  45.0 3.3 %copy-start = (bf16[128,512]{1,0:T(8,128)(2,1)S(1)}, bf16[128,512]{1,0:T(8,128)(2,1)}, u32[]{:S(2)}) copy-start(bf16[128,512]{1,0:T(8,128)(2,1)} %get-tuple-element.36.rest_0_) | copy-start | bytes 393220
  45.0 5.2 %collective-permute-start.15 = (bf16[432,128]{1,0:T(8,128)(2,1)S(1)}, bf16[432,128]{1,0:T(8,128)(2,1)S(1)}, u32[]{:S(2)}, u32[]{:S(2)}) collective-permute-start(bf16[432,128]{1,0:T(8,128)(2,1)S(1)} %get-tuple-element.44), channel_id=1, source_target_pairs={{0,8},{4,12},{8,0},{12,4},{16,24},{20,28},{24,16},{28,20},{1,9},{5... | collective-permute-start | bytes 331784 | tf_op jit(solution)/shard_map/ppermute | solution.py:194
  46.7 4.8 %collective-permute-start.17 = (bf16[432,128]{1,0:T(8,128)(2,1)S(1)}, bf16[432,128]{1,0:T(8,128)(2,1)S(1)}, u32[]{:S(2)}, u32[]{:S(2)}) collective-permute-start(bf16[432,128]{1,0:T(8,128)(2,1)S(1)} %get-tuple-element.45), channel_id=1, source_target_pairs={{0,16},{4,20},{8,24},{12,28},{16,0},{20,4},{24,8},{28,12},{1,17},{... | collective-permute-start | bytes 331784 | tf_op jit(solution)/shard_map/ppermute | solution.py:194
  48.2 8.2 %collective-permute-start.13 = (bf16[128,512]{1,0:T(8,128)(2,1)S(1)}, bf16[128,512]{1,0:T(8,128)(2,1)S(1)}, u32[]{:S(2)}, u32[]{:S(2)}) collective-permute-start(bf16[128,512]{1,0:T(8,128)(2,1)S(1)} %copy-done), channel_id=1, source_target_pairs={{4,0},{8,4},{12,8},{16,12},{20,16},{24,20},{28,24},{5,1},{9,5},{13... | collective-permute-start | bytes 393224 | tf_op jit(solution)/shard_map/ppermute | solution.py:287
  51.6 9.8 %collective-permute-start.16 = (bf16[432,128]{1,0:T(8,128)(2,1)S(1)}, bf16[432,128]{1,0:T(8,128)(2,1)S(1)}, u32[]{:S(2)}, u32[]{:S(2)}) collective-permute-start(bf16[432,128]{1,0:T(8,128)(2,1)S(1)} %get-tuple-element.42), channel_id=1, source_target_pairs={{0,16},{4,20},{8,24},{12,28},{16,0},{20,4},{24,8},{28,12},{1,17},{... | collective-permute-start | bytes 331784 | tf_op jit(solution)/shard_map/ppermute | solution.py:194
  56.4 0.7 copy-start.1
  60.9 4.7 %collective-permute-start.18 = (bf16[432,128]{1,0:T(8,128)(2,1)S(1)}, bf16[432,128]{1,0:T(8,128)(2,1)S(1)}, u32[]{:S(2)}, u32[]{:S(2)}) collective-permute-start(bf16[432,128]{1,0:T(8,128)(2,1)S(1)} %get-tuple-element.43), channel_id=1, source_target_pairs={{0,8},{4,12},{8,0},{12,4},{16,24},{20,28},{24,16},{28,20},{1,9},{5... | collective-permute-start | bytes 331784 | tf_op jit(solution)/shard_map/ppermute | solution.py:194
  (3 other events, 1.8 us)

commit v3 on v2

--- a/solution.py
+++ b/solution.py
@@ -8,7 +8,7 @@
 from jax.sharding import PartitionSpec as P
 
 SLOPE = 0.3
-VMEM = 56 * 1024 * 1024
+VMEM = 24 * 1024 * 1024
 FEW = 4
 
 

time: 67.1 us -> 50.6 us (0.75)
  Pallas kernels: 20.7 us -> 5.58 us
  local copies, waits for them, and re-layouts: 6.76 us -> 2.68 us
  waiting for transfers between devices: 8.23 us -> 11.8 us
  other arithmetic: 1.96 us -> 0.97 us
    unnamed x34 -> x10, local copies, waits for them, and re-layouts: 5.82 us -> 1.7 us
    pallas_call x2, Pallas kernels: 4.85 us -> 0.82 us  [on_device(): pl.pallas_call(functools.partial(weight_kernel, n, not weight_grad), out_...]
    pallas_call x2, Pallas kernels: 5.41 us -> 1.59 us  [on_device(): pl.pallas_call(functools.partial(fwd_kernel, n, ob), grid=(1,), in_specs=...]
    pallas_call x2, Pallas kernels: 3.25 us -> 0.05 us  [on_device(): pl.pallas_call(act_kernel, out_shape=[jax.ShapeDtypeStruct((ob, cells), b...]
    ppermute x12, waiting for transfers between devices: 0.03 us -> 2.71 us  [shifted_by(): return lax.ppermute(block, axis, [(i, (i + k) % n) for i in range(n)])]
    ppermute x12, starting transfers between devices: 19 us -> 20.8 us  [shifted_by(): return lax.ppermute(block, axis, [(i, (i + k) % n) for i in range(n)])]
    pallas_call x1, Pallas kernels: 1.81 us -> 0.31 us  [on_device(): pl.pallas_call(pool_kernel, out_shape=jax.ShapeDtypeStruct(up.shape, bf16...]
    pallas_call x1, Pallas kernels: 1.52 us -> 0.13 us  [on_device(): pl.pallas_call(spread_kernel, out_shape=jax.ShapeDtypeStruct((ob, cells),...]
  transfers between devices with their start and end apart: 19 -> 19, of which waited for: 4 -> 7; matrix products, arithmetic and copies ran while one was open for 3% -> 1% of each run, Pallas kernels for 27% -> 10%
where the time goes in v3:
time: 50.6 us; the launch traced here: 50.4 us
  starting transfers between devices  28.5 us (56%)
  waiting for transfers between devices  11.8 us (23%)
  Pallas kernels  5.58 us (11%)
  local copies, waits for them, and re-layouts  2.68 us (5%)
  other arithmetic  0.97 us (2%)
  between operations  0.79 us (2%)
    ppermute x12, starting transfers between devices, shifted_by(): return lax.ppermute(block, axis, [(i, (i + k) % n) for i in range(n)])  20.8 us
    ppermute x5, waiting for transfers between devices, swapped(): return lax.ppermute(block, axis, [(i, i ^ bit) for i in range(n)])  9.1 us
    ppermute x5, starting transfers between devices, swapped(): return lax.ppermute(block, axis, [(i, i ^ bit) for i in range(n)])  4.08 us
    ppermute x12, waiting for transfers between devices, shifted_by(): return lax.ppermute(block, axis, [(i, (i + k) % n) for i in range(n)])  2.71 us
    pallas_call x1, Pallas kernels, on_device(): pl.pallas_call(input_kernel, out_shape=jax.ShapeDtypeStruct(volume.shape,...  2.68 us
    ppermute x1, starting transfers between devices, on_device(): lax.ppermute(volume[:, -1:], 'space', [(i, i + 1) for i in range(n_space...  2.36 us
    unnamed x10, local copies, waits for them, and re-layouts  1.7 us
    pallas_call x2, Pallas kernels, on_device(): pl.pallas_call(functools.partial(fwd_kernel, n, ob), grid=(1,), in_specs=...  1.59 us
  transfers between devices with their start and end apart: 19, of which 7 were waited for; matrix products, arithmetic and copies ran while one was open for 1% of the time, Pallas kernels for 10%

profile of v3, /device:TPU:0, one launch (start us, length us, event | category | flops | bytes accessed | tf_op | source)
XLA Modules:
  0.0 50.4 jit_solution(8281043388891446740)
XLA Ops:
  0.6 1.0 %slice.3 = bf16[32,1,16,128]{3,2,1,0:T(8,128)(2,1)S(1)} slice(bf16[32,4,16,128]{3,2,1,0:T(8,128)(2,1)} %odd_ref.3), slice={[0:32], [3:4], [0:16], [0:128]} | slice | bytes 262144 | tf_op jit(solution)/shard_map/slice | solution.py:222
  1.6 2.4 %collective-permute-start = (bf16[32,1,16,128]{3,2,1,0:T(8,128)(2,1)S(1)}, bf16[32,1,16,128]{3,2,1,0:T(8,128)(2,1)S(1)}, u32[]{:S(2)}, u32[]{:S(2)}) collective-permute-start(bf16[32,1,16,128]{3,2,1,0:T(8,128)(2,1)S(1)} %slice.3), channel_id=1, source_target_pairs={{0,4},{4,8},{8,12},{12,16},{16,20},{20,24},{24,28},{1,5},{5,9},{9,... | collective-permute-start | bytes 393224 | tf_op jit(solution)/shard_map/ppermute | solution.py:222
  4.0 1.0 %copy-done = bf16[32,4,16,128]{3,2,1,0:T(8,128)(2,1)S(1)} copy-done((bf16[32,4,16,128]{3,2,1,0:T(8,128)(2,1)S(1)}, bf16[32,4,16,128]{3,2,1,0:T(8,128)(2,1)}, u32[]{:S(2)}) %copy-start) | copy-done | bytes 524312
  5.0 0.8 %shard_map.61 = (bf16[864,512]{1,0:T(8,128)(2,1)S(1)}, f32[32,512]{1,0:T(8,128)S(1)}, f32[32,512]{1,0:T(8,128)S(1)}, f32[32,512]{1,0:T(8,128)S(1)}, f32[32,512]{1,0:T(8,128)S(1)}) custom-call(bf16[32,4,16,128]{3,2,1,0:T(8,128)(2,1)S(1)} %copy-done, bf16[32,4,16,128]{3,2,1,0:T(8,128)(2,1)S(1)} %copy-done, bf16[32,4,16,128]{3,2,1,0:T(8,128)(2,1)S(1)} %copy-done, ...), custom_call_target="tpu_custom_call" | custom-call | tf_op jit(solution)/shard_map/pallas_call | solution.py:243
  5.8 2.5 %collective-permute-start.4 = (f32[32,512]{1,0:T(8,128)S(1)}, f32[32,512]{1,0:T(8,128)S(1)}, u32[]{:S(2)}, u32[]{:S(2)}) collective-permute-start(f32[32,512]{1,0:T(8,128)S(1)} %get-tuple-element.27), channel_id=1, source_target_pairs={{0,1},{1,2},{2,3},{3,0},{4,5},{5,6},{6,7},{7,4},{8,9},{9,10},{10,1... | collective-permute-start | bytes 196616 | tf_op jit(solution)/shard_map/ppermute | solution.py:189
  8.3 2.6 %collective-permute-start.5 = (f32[32,512]{1,0:T(8,128)S(1)}, f32[32,512]{1,0:T(8,128)S(1)}, u32[]{:S(2)}, u32[]{:S(2)}) collective-permute-start(f32[32,512]{1,0:T(8,128)S(1)} %get-tuple-element.28), channel_id=1, source_target_pairs={{0,2},{1,3},{2,0},{3,1},{4,6},{5,7},{6,4},{7,5},{8,10},{9,11},{10,... | collective-permute-start | bytes 196616 | tf_op jit(solution)/shard_map/ppermute | solution.py:189
  10.9 1.3 %collective-permute-start.6 = (f32[32,512]{1,0:T(8,128)S(1)}, f32[32,512]{1,0:T(8,128)S(1)}, u32[]{:S(2)}, u32[]{:S(2)}) collective-permute-start(f32[32,512]{1,0:T(8,128)S(1)} %get-tuple-element.29), channel_id=1, source_target_pairs={{0,3},{1,0},{2,1},{3,2},{4,7},{5,4},{6,5},{7,6},{8,11},{9,8},{10,9... | collective-permute-start | bytes 196616 | tf_op jit(solution)/shard_map/ppermute | solution.py:189
  12.2 0.8 %shard_map.59 = (bf16[864,512]{1,0:T(8,128)(2,1)S(1)}, f32[32,512]{1,0:T(8,128)S(1)}, f32[32,512]{1,0:T(8,128)S(1)}, f32[32,512]{1,0:T(8,128)S(1)}, f32[32,512]{1,0:T(8,128)S(1)}) custom-call(bf16[32,1,16,128]{3,2,1,0:T(8,128)(2,1)S(1)} %collective-permute-done.behind_ref, bf16[32,4,16,128]{3,2,1,0:T(8,128)(2,1)S(1)} %copy-done.1, ...), custom_call_target="tpu_custom_call" | custom-call | tf_op jit(solution)/shard_map/pallas_call | solution.py:243
  13.0 0.7 %collective-permute-start.1 = (f32[32,512]{1,0:T(8,128)S(1)}, f32[32,512]{1,0:T(8,128)S(1)}, u32[]{:S(2)}, u32[]{:S(2)}) collective-permute-start(f32[32,512]{1,0:T(8,128)S(1)} %get-tuple-element.22), channel_id=1, source_target_pairs={{0,1},{1,2},{2,3},{3,0},{4,5},{5,6},{6,7},{7,4},{8,9},{9,10},{10,1... | collective-permute-start | bytes 196616 | tf_op jit(solution)/shard_map/ppermute | solution.py:189
  14.1 2.8 %collective-permute-start.3 = (f32[32,512]{1,0:T(8,128)S(1)}, f32[32,512]{1,0:T(8,128)S(1)}, u32[]{:S(2)}, u32[]{:S(2)}) collective-permute-start(f32[32,512]{1,0:T(8,128)S(1)} %get-tuple-element.24), channel_id=1, source_target_pairs={{0,3},{1,0},{2,1},{3,2},{4,7},{5,4},{6,5},{7,6},{8,11},{9,8},{10,9... | collective-permute-start | bytes 196616 | tf_op jit(solution)/shard_map/ppermute | solution.py:189
  17.1 0.9 %collective-permute-start.7 = (bf16[32,512]{1,0:T(8,128)(2,1)S(1)}, bf16[32,512]{1,0:T(8,128)(2,1)S(1)}, u32[]{:S(2)}, u32[]{:S(2)}) collective-permute-start(bf16[32,512]{1,0:T(8,128)(2,1)S(1)} %get-tuple-element.32.refs_1_), channel_id=1, source_target_pairs={{0,1},{1,2},{2,3},{3,0},{4,5},{5,6},{6,7},{7,4},{8,9},{9,10},{10,1... | collective-permute-start | bytes 98312 | tf_op jit(solution)/shard_map/ppermute | solution.py:189
  18.0 1.7 %collective-permute-start.8 = (bf16[32,512]{1,0:T(8,128)(2,1)S(1)}, bf16[32,512]{1,0:T(8,128)(2,1)S(1)}, u32[]{:S(2)}, u32[]{:S(2)}) collective-permute-start(bf16[32,512]{1,0:T(8,128)(2,1)S(1)} %get-tuple-element.32.refs_1_), channel_id=1, source_target_pairs={{0,2},{1,3},{2,0},{3,1},{4,6},{5,7},{6,4},{7,5},{8,10},{9,11},{10,... | collective-permute-start | bytes 98312 | tf_op jit(solution)/shard_map/ppermute | solution.py:189
  19.7 0.3 collective-permute-done.1.rest_1_
  20.0 2.1 %collective-permute-start.9 = (bf16[32,512]{1,0:T(8,128)(2,1)S(1)}, bf16[32,512]{1,0:T(8,128)(2,1)S(1)}, u32[]{:S(2)}, u32[]{:S(2)}) collective-permute-start(bf16[32,512]{1,0:T(8,128)(2,1)S(1)} %get-tuple-element.32.refs_1_), channel_id=1, source_target_pairs={{0,3},{1,0},{2,1},{3,2},{4,7},{5,4},{6,5},{7,6},{8,11},{9,8},{10,9... | collective-permute-start | bytes 98312 | tf_op jit(solution)/shard_map/ppermute | solution.py:189
  22.5 3.4 %collective-permute-start.10 = (bf16[32,512]{1,0:T(8,128)(2,1)S(1)}, bf16[32,512]{1,0:T(8,128)(2,1)S(1)}, u32[]{:S(2)}, u32[]{:S(2)}) collective-permute-start(bf16[32,512]{1,0:T(8,128)(2,1)S(1)} %get-tuple-element.35.refs_2_), channel_id=1, source_target_pairs={{0,1},{1,2},{2,3},{3,0},{4,5},{5,6},{6,7},{7,4},{8,9},{9,10},{10,1... | collective-permute-start | bytes 98312 | tf_op jit(solution)/shard_map/ppermute | solution.py:189
  25.9 0.3 collective-permute-start.11
  26.2 2.1 %collective-permute-start.12 = (bf16[32,512]{1,0:T(8,128)(2,1)S(1)}, bf16[32,512]{1,0:T(8,128)(2,1)S(1)}, u32[]{:S(2)}, u32[]{:S(2)}) collective-permute-start(bf16[32,512]{1,0:T(8,128)(2,1)S(1)} %get-tuple-element.35.refs_2_), channel_id=1, source_target_pairs={{0,3},{1,0},{2,1},{3,2},{4,7},{5,4},{6,5},{7,6},{8,11},{9,8},{10,9... | collective-permute-start | bytes 98312 | tf_op jit(solution)/shard_map/ppermute | solution.py:189
  28.4 0.4 shard_map.64
  28.8 2.1 %collective-permute-done.11.refs_4_ = bf16[32,512]{1,0:T(8,128)(2,1)S(1)} collective-permute-done((bf16[32,512]{1,0:T(8,128)(2,1)S(1)}, bf16[32,512]{1,0:T(8,128)(2,1)S(1)}, u32[]{:S(2)}, u32[]{:S(2)}) %collective-permute-start.11) | collective-permute-done | bytes 32800 | tf_op jit(solution)/shard_map/ppermute | solution.py:189
  30.8 0.4 shard_map.65
  31.3 1.8 %collective-permute-done.14 = f32[864,128]{1,0:T(8,128)S(1)} collective-permute-done((f32[864,128]{1,0:T(8,128)S(1)}, f32[864,128]{1,0:T(8,128)S(1)}, u32[]{:S(2)}, u32[]{:S(2)}) %collective-permute-start.14) | collective-permute-done | bytes 442400 | tf_op jit(solution)/shard_map/ppermute | solution.py:194
  33.2 1.5 %collective-permute-start.15 = (bf16[432,128]{1,0:T(8,128)(2,1)S(1)}, bf16[432,128]{1,0:T(8,128)(2,1)S(1)}, u32[]{:S(2)}, u32[]{:S(2)}) collective-permute-start(bf16[432,128]{1,0:T(8,128)(2,1)S(1)} %get-tuple-element.44), channel_id=1, source_target_pairs={{0,8},{4,12},{8,0},{12,4},{16,24},{20,28},{24,16},{28,20},{1,9},{5... | collective-permute-start | bytes 331784 | tf_op jit(solution)/shard_map/ppermute | solution.py:194
  34.7 0.3 collective-permute-start.17
  35.1 1.3 %collective-permute-start.13 = (bf16[128,512]{1,0:T(8,128)(2,1)S(1)}, bf16[128,512]{1,0:T(8,128)(2,1)S(1)}, u32[]{:S(2)}, u32[]{:S(2)}) collective-permute-start(bf16[128,512]{1,0:T(8,128)(2,1)S(1)} %get-tuple-element.36.rest_0_), channel_id=1, source_target_pairs={{4,0},{8,4},{12,8},{16,12},{20,16},{24,20},{28,24},{5,1},{9,5},{13... | collective-permute-start | bytes 393224 | tf_op jit(solution)/shard_map/ppermute | solution.py:287
  36.4 2.0 %collective-permute-done.15 = bf16[432,128]{1,0:T(8,128)(2,1)S(1)} collective-permute-done((bf16[432,128]{1,0:T(8,128)(2,1)S(1)}, bf16[432,128]{1,0:T(8,128)(2,1)S(1)}, u32[]{:S(2)}, u32[]{:S(2)}) %collective-permute-start.15) | collective-permute-done | bytes 110624 | tf_op jit(solution)/shard_map/ppermute | solution.py:194
  38.4 1.2 %collective-permute-done.17 = bf16[432,128]{1,0:T(8,128)(2,1)S(1)} collective-permute-done((bf16[432,128]{1,0:T(8,128)(2,1)S(1)}, bf16[432,128]{1,0:T(8,128)(2,1)S(1)}, u32[]{:S(2)}, u32[]{:S(2)}) %collective-permute-start.17) | collective-permute-done | bytes 110624 | tf_op jit(solution)/shard_map/ppermute | solution.py:194
  39.6 0.5 collective-permute-start.16
  40.4 0.6 %copy.7 = bf16[32,1,4,32]{3,2,1,0:T(4,128)(2,1)} copy(bf16[32,1,4,32]{3,0,2,1:T(8,128)(2,1)S(1)} %bitcast.17) | data formatting | bytes 16384
  41.0 2.7 %shard_map.66 = bf16[32,4,16,128]{3,2,1,0:T(8,128)(2,1)} custom-call(bf16[864,128]{1,0:T(8,128)(2,1)S(1)} %bitcast.16, bf16[128,512]{1,0:T(8,128)(2,1)S(1)} %get-tuple-element.36.rest_0_, bf16[128,512]{1,0:T(8,128)(2,1)S(1)} %get-tuple-element.37.rest_1_, bf16[128,512]{1,0:T(8,128)(2,1)S(1)} %collective-permute-done.13.rest_2_), custom_call_target="tpu_custom_call" | custom-call | tf_op jit(solution)/shard_map/pallas_call | solution.py:291
  43.7 1.7 %collective-permute-start.18 = (bf16[432,128]{1,0:T(8,128)(2,1)S(1)}, bf16[432,128]{1,0:T(8,128)(2,1)S(1)}, u32[]{:S(2)}, u32[]{:S(2)}) collective-permute-start(bf16[432,128]{1,0:T(8,128)(2,1)S(1)} %get-tuple-element.43), channel_id=1, source_target_pairs={{0,8},{4,12},{8,0},{12,4},{16,24},{20,28},{24,16},{28,20},{1,9},{5... | collective-permute-start | bytes 331784 | tf_op jit(solution)/shard_map/ppermute | solution.py:194
  45.4 4.1 %collective-permute-done.18 = bf16[432,128]{1,0:T(8,128)(2,1)S(1)} collective-permute-done((bf16[432,128]{1,0:T(8,128)(2,1)S(1)}, bf16[432,128]{1,0:T(8,128)(2,1)S(1)}, u32[]{:S(2)}, u32[]{:S(2)}) %collective-permute-start.18) | collective-permute-done | bytes 110624 | tf_op jit(solution)/shard_map/ppermute | solution.py:194
  49.6 0.8 %pad_maximum_fusion = f32[864,128]{1,0:T(8,128)} fusion(f32[432,128]{1,0:T(8,128)S(1)} %convert_add_fusion, f32[432,128]{1,0:T(8,128)S(1)} %convert_add_fusion.1), kind=kLoop, calls=%fused_computation | loop fusion | flops 110592 | bytes 884736 | tf_op jit(solution)/shard_map/concatenate | solution.py:209
  (32 shorter events, 1.4 us)
Async XLA Ops:
  0.6 3.4 %copy-start.2 = (bf16[32,3,3,3,128]{4,0,3,2,1:T(8,128)(2,1)S(1)}, bf16[32,3,3,3,128]{4,0,3,2,1:T(8,128)(2,1)}, u32[]{:S(2)}) copy-start(bf16[32,3,3,3,128]{4,0,3,2,1:T(8,128)(2,1)} %param.4) | copy-start | bytes 663556
  1.6 10.6 %collective-permute-start = (bf16[32,1,16,128]{3,2,1,0:T(8,128)(2,1)S(1)}, bf16[32,1,16,128]{3,2,1,0:T(8,128)(2,1)S(1)}, u32[]{:S(2)}, u32[]{:S(2)}) collective-permute-start(bf16[32,1,16,128]{3,2,1,0:T(8,128)(2,1)S(1)} %slice.3), channel_id=1, source_target_pairs={{0,4},{4,8},{8,12},{12,16},{16,20},{20,24},{24,28},{1,5},{5,9},{9,... | collective-permute-start | bytes 393224 | tf_op jit(solution)/shard_map/ppermute | solution.py:222
  4.0 1.0 %copy-start = (bf16[32,4,16,128]{3,2,1,0:T(8,128)(2,1)S(1)}, bf16[32,4,16,128]{3,2,1,0:T(8,128)(2,1)}, u32[]{:S(2)}) copy-start(bf16[32,4,16,128]{3,2,1,0:T(8,128)(2,1)} %odd_ref.3) | copy-start | bytes 1572868
  5.0 7.2 %copy-start.1 = (bf16[32,4,16,128]{3,2,1,0:T(8,128)(2,1)S(1)}, bf16[32,4,16,128]{3,2,1,0:T(8,128)(2,1)}, u32[]{:S(2)}) copy-start(bf16[32,4,16,128]{3,2,1,0:T(8,128)(2,1)} %odd_ref.3) | copy-start | bytes 1572868
  5.8 8.3 %collective-permute-start.4 = (f32[32,512]{1,0:T(8,128)S(1)}, f32[32,512]{1,0:T(8,128)S(1)}, u32[]{:S(2)}, u32[]{:S(2)}) collective-permute-start(f32[32,512]{1,0:T(8,128)S(1)} %get-tuple-element.27), channel_id=1, source_target_pairs={{0,1},{1,2},{2,3},{3,0},{4,5},{5,6},{6,7},{7,4},{8,9},{9,10},{10,1... | collective-permute-start | bytes 196616 | tf_op jit(solution)/shard_map/ppermute | solution.py:189
  8.3 8.8 %collective-permute-start.5 = (f32[32,512]{1,0:T(8,128)S(1)}, f32[32,512]{1,0:T(8,128)S(1)}, u32[]{:S(2)}, u32[]{:S(2)}) collective-permute-start(f32[32,512]{1,0:T(8,128)S(1)} %get-tuple-element.28), channel_id=1, source_target_pairs={{0,2},{1,3},{2,0},{3,1},{4,6},{5,7},{6,4},{7,5},{8,10},{9,11},{10,... | collective-permute-start | bytes 196616 | tf_op jit(solution)/shard_map/ppermute | solution.py:189
  10.9 6.0 %copy-start.3 = (bf16[32,1,4,32]{3,2,1,0:T(4,128)(2,1)S(1)}, bf16[32,1,4,32]{3,2,1,0:T(4,128)(2,1)}, u32[]{:S(2)}) copy-start(bf16[32,1,4,32]{3,2,1,0:T(4,128)(2,1)} %param.5) | copy-start | bytes 24580
  10.9 6.2 %collective-permute-start.6 = (f32[32,512]{1,0:T(8,128)S(1)}, f32[32,512]{1,0:T(8,128)S(1)}, u32[]{:S(2)}, u32[]{:S(2)}) collective-permute-start(f32[32,512]{1,0:T(8,128)S(1)} %get-tuple-element.29), channel_id=1, source_target_pairs={{0,3},{1,0},{2,1},{3,2},{4,7},{5,4},{6,5},{7,6},{8,11},{9,8},{10,9... | collective-permute-start | bytes 196616 | tf_op jit(solution)/shard_map/ppermute | solution.py:189
  13.0 7.0 %collective-permute-start.1 = (f32[32,512]{1,0:T(8,128)S(1)}, f32[32,512]{1,0:T(8,128)S(1)}, u32[]{:S(2)}, u32[]{:S(2)}) collective-permute-start(f32[32,512]{1,0:T(8,128)S(1)} %get-tuple-element.22), channel_id=1, source_target_pairs={{0,1},{1,2},{2,3},{3,0},{4,5},{5,6},{6,7},{7,4},{8,9},{9,10},{10,1... | collective-permute-start | bytes 196616 | tf_op jit(solution)/shard_map/ppermute | solution.py:189
  13.8 8.7 %collective-permute-start.2 = (f32[32,512]{1,0:T(8,128)S(1)}, f32[32,512]{1,0:T(8,128)S(1)}, u32[]{:S(2)}, u32[]{:S(2)}) collective-permute-start(f32[32,512]{1,0:T(8,128)S(1)} %get-tuple-element.23), channel_id=1, source_target_pairs={{0,2},{1,3},{2,0},{3,1},{4,6},{5,7},{6,4},{7,5},{8,10},{9,11},{10,... | collective-permute-start | bytes 196616 | tf_op jit(solution)/shard_map/ppermute | solution.py:189
  14.1 8.3 %collective-permute-start.3 = (f32[32,512]{1,0:T(8,128)S(1)}, f32[32,512]{1,0:T(8,128)S(1)}, u32[]{:S(2)}, u32[]{:S(2)}) collective-permute-start(f32[32,512]{1,0:T(8,128)S(1)} %get-tuple-element.24), channel_id=1, source_target_pairs={{0,3},{1,0},{2,1},{3,2},{4,7},{5,4},{6,5},{7,6},{8,11},{9,8},{10,9... | collective-permute-start | bytes 196616 | tf_op jit(solution)/shard_map/ppermute | solution.py:189
  17.1 9.1 %collective-permute-start.7 = (bf16[32,512]{1,0:T(8,128)(2,1)S(1)}, bf16[32,512]{1,0:T(8,128)(2,1)S(1)}, u32[]{:S(2)}, u32[]{:S(2)}) collective-permute-start(bf16[32,512]{1,0:T(8,128)(2,1)S(1)} %get-tuple-element.32.refs_1_), channel_id=1, source_target_pairs={{0,1},{1,2},{2,3},{3,0},{4,5},{5,6},{6,7},{7,4},{8,9},{9,10},{10,1... | collective-permute-start | bytes 98312 | tf_op jit(solution)/shard_map/ppermute | solution.py:189
  18.0 10.3 %collective-permute-start.8 = (bf16[32,512]{1,0:T(8,128)(2,1)S(1)}, bf16[32,512]{1,0:T(8,128)(2,1)S(1)}, u32[]{:S(2)}, u32[]{:S(2)}) collective-permute-start(bf16[32,512]{1,0:T(8,128)(2,1)S(1)} %get-tuple-element.32.refs_1_), channel_id=1, source_target_pairs={{0,2},{1,3},{2,0},{3,1},{4,6},{5,7},{6,4},{7,5},{8,10},{9,11},{10,... | collective-permute-start | bytes 98312 | tf_op jit(solution)/shard_map/ppermute | solution.py:189
  20.0 8.3 %collective-permute-start.9 = (bf16[32,512]{1,0:T(8,128)(2,1)S(1)}, bf16[32,512]{1,0:T(8,128)(2,1)S(1)}, u32[]{:S(2)}, u32[]{:S(2)}) collective-permute-start(bf16[32,512]{1,0:T(8,128)(2,1)S(1)} %get-tuple-element.32.refs_1_), channel_id=1, source_target_pairs={{0,3},{1,0},{2,1},{3,2},{4,7},{5,4},{6,5},{7,6},{8,11},{9,8},{10,9... | collective-permute-start | bytes 98312 | tf_op jit(solution)/shard_map/ppermute | solution.py:189
  22.5 6.3 %collective-permute-start.10 = (bf16[32,512]{1,0:T(8,128)(2,1)S(1)}, bf16[32,512]{1,0:T(8,128)(2,1)S(1)}, u32[]{:S(2)}, u32[]{:S(2)}) collective-permute-start(bf16[32,512]{1,0:T(8,128)(2,1)S(1)} %get-tuple-element.35.refs_2_), channel_id=1, source_target_pairs={{0,1},{1,2},{2,3},{3,0},{4,5},{5,6},{6,7},{7,4},{8,9},{9,10},{10,1... | collective-permute-start | bytes 98312 | tf_op jit(solution)/shard_map/ppermute | solution.py:189
  25.9 4.9 %collective-permute-start.11 = (bf16[32,512]{1,0:T(8,128)(2,1)S(1)}, bf16[32,512]{1,0:T(8,128)(2,1)S(1)}, u32[]{:S(2)}, u32[]{:S(2)}) collective-permute-start(bf16[32,512]{1,0:T(8,128)(2,1)S(1)} %get-tuple-element.35.refs_2_), channel_id=1, source_target_pairs={{0,2},{1,3},{2,0},{3,1},{4,6},{5,7},{6,4},{7,5},{8,10},{9,11},{10,... | collective-permute-start | bytes 98312 | tf_op jit(solution)/shard_map/ppermute | solution.py:189
  26.2 4.6 %collective-permute-start.12 = (bf16[32,512]{1,0:T(8,128)(2,1)S(1)}, bf16[32,512]{1,0:T(8,128)(2,1)S(1)}, u32[]{:S(2)}, u32[]{:S(2)}) collective-permute-start(bf16[32,512]{1,0:T(8,128)(2,1)S(1)} %get-tuple-element.35.refs_2_), channel_id=1, source_target_pairs={{0,3},{1,0},{2,1},{3,2},{4,7},{5,4},{6,5},{7,6},{8,11},{9,8},{10,9... | collective-permute-start | bytes 98312 | tf_op jit(solution)/shard_map/ppermute | solution.py:189
  31.2 1.9 %collective-permute-start.14 = (f32[864,128]{1,0:T(8,128)S(1)}, f32[864,128]{1,0:T(8,128)S(1)}, u32[]{:S(2)}, u32[]{:S(2)}) collective-permute-start(f32[864,128]{1,0:T(8,128)S(1)} %get-tuple-element.38), channel_id=1, source_target_pairs={{0,4},{4,0},{8,12},{12,8},{16,20},{20,16},{24,28},{28,24},{1,5},{5... | collective-permute-start | bytes 1327112 | tf_op jit(solution)/shard_map/ppermute | solution.py:194
  33.2 5.2 %collective-permute-start.15 = (bf16[432,128]{1,0:T(8,128)(2,1)S(1)}, bf16[432,128]{1,0:T(8,128)(2,1)S(1)}, u32[]{:S(2)}, u32[]{:S(2)}) collective-permute-start(bf16[432,128]{1,0:T(8,128)(2,1)S(1)} %get-tuple-element.44), channel_id=1, source_target_pairs={{0,8},{4,12},{8,0},{12,4},{16,24},{20,28},{24,16},{28,20},{1,9},{5... | collective-permute-start | bytes 331784 | tf_op jit(solution)/shard_map/ppermute | solution.py:194
  34.7 4.8 %collective-permute-start.17 = (bf16[432,128]{1,0:T(8,128)(2,1)S(1)}, bf16[432,128]{1,0:T(8,128)(2,1)S(1)}, u32[]{:S(2)}, u32[]{:S(2)}) collective-permute-start(bf16[432,128]{1,0:T(8,128)(2,1)S(1)} %get-tuple-element.45), channel_id=1, source_target_pairs={{0,16},{4,20},{8,24},{12,28},{16,0},{20,4},{24,8},{28,12},{1,17},{... | collective-permute-start | bytes 331784 | tf_op jit(solution)/shard_map/ppermute | solution.py:194
  35.1 6.0 %collective-permute-start.13 = (bf16[128,512]{1,0:T(8,128)(2,1)S(1)}, bf16[128,512]{1,0:T(8,128)(2,1)S(1)}, u32[]{:S(2)}, u32[]{:S(2)}) collective-permute-start(bf16[128,512]{1,0:T(8,128)(2,1)S(1)} %get-tuple-element.36.rest_0_), channel_id=1, source_target_pairs={{4,0},{8,4},{12,8},{16,12},{20,16},{24,20},{28,24},{5,1},{9,5},{13... | collective-permute-start | bytes 393224 | tf_op jit(solution)/shard_map/ppermute | solution.py:287
  39.6 5.8 %collective-permute-start.16 = (bf16[432,128]{1,0:T(8,128)(2,1)S(1)}, bf16[432,128]{1,0:T(8,128)(2,1)S(1)}, u32[]{:S(2)}, u32[]{:S(2)}) collective-permute-start(bf16[432,128]{1,0:T(8,128)(2,1)S(1)} %get-tuple-element.42), channel_id=1, source_target_pairs={{0,16},{4,20},{8,24},{12,28},{16,0},{20,4},{24,8},{28,12},{1,17},{... | collective-permute-start | bytes 331784 | tf_op jit(solution)/shard_map/ppermute | solution.py:194
  43.7 5.8 %collective-permute-start.18 = (bf16[432,128]{1,0:T(8,128)(2,1)S(1)}, bf16[432,128]{1,0:T(8,128)(2,1)S(1)}, u32[]{:S(2)}, u32[]{:S(2)}) collective-permute-start(bf16[432,128]{1,0:T(8,128)(2,1)S(1)} %get-tuple-element.43), channel_id=1, source_target_pairs={{0,8},{4,12},{8,0},{12,4},{16,24},{20,28},{24,16},{28,20},{1,9},{5... | collective-permute-start | bytes 331784 | tf_op jit(solution)/shard_map/ppermute | solution.py:194

commit v4 on v3

--- a/solution.py
+++ b/solution.py
@@ -9,6 +9,9 @@
 
 SLOPE = 0.3
 VMEM = 24 * 1024 * 1024
+XOR = True
+RS = (1, 2, 3)
+AG = (1, 2, 3)
 FEW = 4
 
 
@@ -29,15 +32,35 @@
     return jnp.where(hit, 1.0, 0.0).astype(jnp.bfloat16)
 
 
-def fwd_kernel(n, ob, behind_ref, even_ref, odd_ref, w_ref, cols_ref, *rest):
+def fwd_kernel(n, ob, z, *refs):
+    if z:
+        vol_hbm, w_hbm, vol_ref, w_ref, edge_ref, cols_ref, *rest, sems = refs
+        planes = vol_ref.shape[1]
+        copies = [
+            pltpu.make_async_copy(vol_hbm.at[:, p], vol_ref.at[:, p], sems.at[p])
+            for p in range(planes)
+        ]
+        w_copy = pltpu.make_async_copy(w_hbm, w_ref, sems.at[planes])
+        order = list(range(2 * z - 1, planes)) + list(range(2 * z - 1))
+        for i, p in enumerate(order):
+            copies[p].start()
+            if i == 2:
+                w_copy.start()
+    else:
+        rim_ref, vol_ref, w_ref, cols_ref, *rest = refs
     part_refs = rest[:-2] if n > 1 else rest[:-1]
     wide_ref = rest[-2] if n > 1 else rest[-1]
-    cb, _, hgt, wid = even_ref.shape
+    cb, _, hgt, wid = vol_ref.shape
     groups = hgt // 4
     sel = pair_matrix(False, wid, wid // 2)
     zero = jnp.zeros((cb, wid), jnp.float32)
-    for a, plane_ref in enumerate((behind_ref, even_ref, odd_ref)):
-        wide_ref[...] = plane_ref[:, 0].astype(jnp.float32).reshape(cb * hgt, wid)
+    for a in range(3):
+        if z:
+            copies[2 * z + a - 1].wait()
+            if a == 2:
+                edge_ref[...] = vol_ref[:, -1:]
+        plane = vol_ref[:, 2 * z + a - 1] if z or a else rim_ref[:, 0]
+        wide_ref[...] = plane.astype(jnp.float32).reshape(cb * hgt, wid)
         row = [wide_ref[pl.ds(y, cb, stride=hgt), :] for y in range(hgt)]
         cls = [[row[4 * j + r] for j in range(groups)] for r in range(4)]
 
@@ -56,6 +79,10 @@
                 cols_ref[tap * cb : (tap + 1) * cb, :] = jnp.concatenate(
                     [block[j * cb : (j + 1) * cb] for j in range(groups)], axis=1
                 )
+    if z:
+        w_copy.wait()
+        for p in range(2 * z - 1):
+            copies[p].wait()
     part = lax.dot_general(
         w_ref[...],
         cols_ref[...],
@@ -68,8 +95,8 @@
     all_ref = rest[-1]
     all_ref[...] = part
     me = lax.axis_index("chan")
-    for k, ref in enumerate(part_refs):
-        start = pl.multiple_of(lax.rem(me + k, n) * ob, ob)
+    for k, ref in zip((0,) + RS, part_refs):
+        start = pl.multiple_of((me ^ k if XOR else lax.rem(me + k, n)) * ob, ob)
         ref[...] = all_ref[pl.ds(start, ob), :]
 
 
@@ -112,26 +139,62 @@
         ).astype(jnp.bfloat16)
 
 
-def weight_kernel(n, first, *refs):
-    if first:
-        cols_ref, *block_refs, wgrad_ref, grad_ref = refs
-    else:
-        sum_ref, cols_ref, *block_refs, wgrad_ref, grad_ref = refs
+def in_order(n, block_refs, grad_ref):
     if n == 1:
         grad_ref[...] = block_refs[0][...]
-    else:
-        me = lax.axis_index("chan")
-        ob = block_refs[0].shape[0]
-        for k, ref in enumerate(block_refs):
-            start = pl.multiple_of(lax.rem(me + n - k, n) * ob, ob)
-            grad_ref[pl.ds(start, ob), :] = ref[...]
-    term = lax.dot_general(
+        return
+    me = lax.axis_index("chan")
+    ob = block_refs[0].shape[0]
+    for k, ref in zip((0,) + AG, block_refs):
+        start = pl.multiple_of((me ^ k if XOR else lax.rem(me + n - k, n)) * ob, ob)
+        grad_ref[pl.ds(start, ob), :] = ref[...]
+
+
+def weight_term(cols_ref, grad_ref):
+    return lax.dot_general(
         cols_ref[...],
         grad_ref[...],
         (((1,), (1,)), ((), ())),
         preferred_element_type=jnp.float32,
     )
-    wgrad_ref[...] = term if first else sum_ref[...] + term
+
+
+def weight_kernel(n, cols_ref, *refs):
+    *block_refs, wgrad_ref, grad_ref = refs
+    in_order(n, block_refs, grad_ref)
+    wgrad_ref[...] = weight_term(cols_ref, grad_ref)
+
+
+def last_weight_kernel(n, sum_ref, cols_ref, *refs):
+    *block_refs, keep_ref, send_ref, grad_ref, rows_ref = refs
+    in_order(n, block_refs, grad_ref)
+    taps, half = cols_ref.shape[0], keep_ref.shape[0]
+    rows_ref[0:taps, :] = sum_ref[...] + weight_term(cols_ref, grad_ref)
+    if 2 * half > taps:
+        rows_ref[taps:, :] = jnp.zeros((2 * half - taps, rows_ref.shape[1]), jnp.float32)
+    core = lax.rem(lax.axis_index("space"), 2)
+    keep_ref[...] = rows_ref[pl.ds(pl.multiple_of(core * half, 8), half), :]
+    send_ref[...] = rows_ref[pl.ds(pl.multiple_of((1 - core) * half, 8), half), :]
+
+
+def join_kernel(own_ref, other_ref, out_ref, sems):
+    half = own_ref.shape[0]
+    for core in range(2):
+
+        @pl.when(lax.rem(lax.axis_index("space"), 2) == core)
+        def _():
+            copies = []
+            for ref, start in ((own_ref, core * half), (other_ref, (1 - core) * half)):
+                size = min(half, out_ref.shape[0] - start)
+                copies.append(
+                    pltpu.make_async_copy(
+                        ref.at[pl.ds(0, size)], out_ref.at[pl.ds(start, size)], sems.at[start // half]
+                    )
+                )
+            for copy in copies:
+                copy.start()
+            for copy in copies:
+                copy.wait()
 
 
 def input_kernel(w_ref, *rest):
@@ -184,29 +247,9 @@
     out_ref[...] = wide_ref[...].reshape(cb, planes, hgt, wid).astype(jnp.bfloat16)
 
 
-def shifted_by(block, axis, k):
+def moved(block, axis, k):
     n = lax.axis_size(axis)
-    return lax.ppermute(block, axis, [(i, (i + k) % n) for i in range(n)])
-
-
-def swapped(block, axis, bit):
-    n = lax.axis_size(axis)
-    return lax.ppermute(block, axis, [(i, i ^ bit) for i in range(n)])
-
-
-def sum_over(term, axis):
-    n = lax.axis_size(axis)
-    if n & (n - 1):
-        return lax.psum(term, axis)
-    if n > 1:
-        term = term + swapped(term, axis, 1)
-    bits = [1 << b for b in range(1, n.bit_length() - 1)]
-    halves = jnp.split(term, 2, axis=0)
-    for first, second in zip(bits, bits[::-1]):
-        sent = [h.astype(jnp.bfloat16) for h in halves]
-        got = [swapped(s, axis, bit) for s, bit in zip(sent, (first, second))]
-        halves = [s.astype(jnp.float32) + r.astype(jnp.float32) for s, r in zip(sent, got)]
-    return jnp.concatenate(halves, axis=0)
+    return lax.ppermute(block, axis, [(i, i ^ k if XOR else (i + k) % n) for i in range(n)])
 
 
 def on_device(volume, kernel, upstream):
@@ -214,86 +257,111 @@
     ob = upstream.shape[0]
     out_ch = kernel.shape[4]
     n_chan, n_space = lax.axis_size("chan"), lax.axis_size("space")
-    direct = n_chan <= FEW
+    direct = n_chan <= FEW and n_chan & (n_chan - 1) == 0
     n = n_chan if direct else 1
     taps = 27 * cb
     cells = hgt // 4 * wid
     f32, bf16 = jnp.float32, jnp.bfloat16
-    rim = lax.ppermute(volume[:, -1:], "space", [(i, i + 1) for i in range(n_space - 1)])
+    shape = jax.ShapeDtypeStruct
     weights = kernel.transpose(1, 2, 3, 0, 4).reshape(taps, out_ch)
     up = upstream[:, 0].transpose(1, 0, 2)
     spread = pl.pallas_call(
-        spread_kernel,
-        out_shape=jax.ShapeDtypeStruct((ob, cells), f32),
-        compiler_params=params(),
+        spread_kernel, out_shape=shape((ob, cells), f32), compiler_params=params()
     )(up)
 
     scratch = [pltpu.VMEM((cb * hgt, wid), f32)]
     if n > 1:
         scratch.append(pltpu.VMEM((out_ch, cells), f32))
-    part_shape = jax.ShapeDtypeStruct((ob if direct else out_ch, cells), f32)
-    whole = pl.BlockSpec(memory_space=pltpu.VMEM)
-
-    def plane(p):
-        return pl.BlockSpec((cb, 1, hgt, wid), lambda i: (0, max(p, 0), 0, 0))
-
+    part_shapes = [shape((ob if direct else out_ch, cells), f32)] * n
+    cols_shape = [shape((taps, cells), bf16)]
     out_planes = range(planes // 2)
     cols, grads, acts = {}, {}, {}
+    rim = ()
     for z in reversed(out_planes):
-        cols[z], *parts = pl.pallas_call(
-            functools.partial(fwd_kernel, n, ob),
-            grid=(1,),
-            in_specs=[plane(2 * z - 1), plane(2 * z), plane(2 * z + 1), whole],
-            out_specs=[whole] * (n + 1),
-            out_shape=[jax.ShapeDtypeStruct((taps, cells), bf16)] + [part_shape] * n,
-            scratch_shapes=scratch,
-            compiler_params=params(),
-        )(volume if z else rim, volume, volume, weights)
+        call = functools.partial(fwd_kernel, n, ob, z)
+        if z:
+            vol, w, edge, cols[z], *parts = pl.pallas_call(
+                call,
+                in_specs=[pl.BlockSpec(memory_space=pltpu.HBM)] * 2,
+                out_shape=[
+                    shape(volume.shape, bf16),
+                    shape(weights.shape, bf16),
+                    shape((cb, 1, hgt, wid), bf16),
+                ]
+                + cols_shape
+                + part_shapes,
+                scratch_shapes=scratch + [pltpu.SemaphoreType.DMA((planes + 1,))],
+                compiler_params=params(),
+            )(*[pltpu.with_memory_space_constraint(x, pltpu.HBM) for x in (volume, weights)])
+            rim = lax.ppermute(edge, "space", [(i, i + 1) for i in range(n_space - 1)])
+        else:
+            cols[z], *parts = pl.pallas_call(
+                call,
+                out_shape=cols_shape + part_shapes,
+                scratch_shapes=scratch,
+                compiler_params=params(),
+            )(rim, vol, w)
         if direct:
-            parts = parts[:1] + [shifted_by(parts[k], "chan", k) for k in range(1, n)]
+            parts = parts[:1] + [moved(p, "chan", k) for k, p in zip(RS, parts[1:])]
         else:
             parts = [lax.psum_scatter(parts[0], "chan", scatter_dimension=0, tiled=True)]
         own, acts[z] = pl.pallas_call(
             act_kernel,
-            out_shape=[
-                jax.ShapeDtypeStruct((ob, cells), bf16),
-                jax.ShapeDtypeStruct((ob, cells), f32),
-            ],
+            out_shape=[shape((ob, cells), bf16), shape((ob, cells), f32)],
             compiler_params=params(),
         )(spread, *parts)
         if direct:
-            grads[z] = [own] + [shifted_by(own, "chan", k) for k in range(1, n)]
+            grads[z] = [own] + [moved(own, "chan", k) for k in AG]
         else:
             grads[z] = [lax.all_gather(own, "chan", axis=0, tiled=True)]
 
     pooled = pl.pallas_call(
-        pool_kernel,
-        out_shape=jax.ShapeDtypeStruct(up.shape, bf16),
-        compiler_params=params(),
+        pool_kernel, out_shape=shape(up.shape, bf16), compiler_params=params()
     )(acts[0], acts[1])
     pooled = pooled.transpose(1, 0, 2)[:, None]
-
-    weight_grad = []
-    for z in reversed(out_planes):
-        wgrad, grads[z] = pl.pallas_call(
-            functools.partial(weight_kernel, n, not weight_grad),
-            out_shape=[
-                jax.ShapeDtypeStruct((taps, out_ch), f32),
-                jax.ShapeDtypeStruct((out_ch, cells), bf16),
-            ],
-            compiler_params=params(),
-        )(*weight_grad, cols[z], *grads[z])
-        weight_grad = [wgrad]
-    after = lax.ppermute(grads[0], "space", [(i + 1, i) for i in range(n_space - 1)])
-    weight_grad = sum_over(weight_grad[0], "space")
+    half = -(-taps // 32) * 16
+    grad_shape = shape((out_ch, cells), bf16)
+    term, grads[1] = pl.pallas_call(
+        functools.partial(weight_kernel, n),
+        out_shape=[shape((taps, out_ch), f32), grad_shape],
+        compiler_params=params(),
+    )(cols[1], *grads[1])
+    keep, send, grads[0] = pl.pallas_call(
+        functools.partial(last_weight_kernel, n),
+        out_shape=[shape((half, out_ch), f32)] * 2 + [grad_shape],
+        scratch_shapes=[pltpu.VMEM((2 * half, out_ch), f32)],
+        compiler_params=params(),
+    )(term, cols[0], *grads[0])
+
+    rows = keep + lax.ppermute(send, "space", [(i, i ^ 1) for i in range(n_space)])
+    bits = [1 << b for b in range(1, n_space.bit_length() - 1)]
+    after = input_grad = None
+    for r, bit in enumerate(bits):
+        sent = rows.astype(bf16)
+        if r == 0:
+            sent, grads[0] = lax.optimization_barrier((sent, grads[0]))
+            after = lax.ppermute(grads[0], "space", [(i + 1, i) for i in range(n_space - 1)])
+        if r == len(bits) - 1:
+            sent, grads[1] = lax.optimization_barrier((sent, grads[1]))
+            input_grad = pl.pallas_call(
+                input_kernel,
+                out_shape=shape(volume.shape, bf16),
+                scratch_shapes=[pltpu.VMEM((cb * planes * hgt, wid), f32)],
+                compiler_params=params(),
+            )(w, grads[0], grads[1], after)
+        pairs = [(i, i ^ (bits[-1 - r] if i & 1 else bit)) for i in range(n_space)]
+        got = lax.ppermute(sent, "space", pairs)
+        rows = sent.astype(f32) + got.astype(f32)
+    rows, input_grad = lax.optimization_barrier((rows, input_grad))
+    other = lax.ppermute(rows, "space", [(i, i ^ 1) for i in range(n_space)])
+    weight_grad = pl.pallas_call(
+        join_kernel,
+        out_specs=pl.BlockSpec(memory_space=pltpu.HBM),
+        out_shape=shape((taps, out_ch), f32),
+        scratch_shapes=[pltpu.SemaphoreType.DMA((2,))],
+        compiler_params=params(),
+    )(rows, other)
     weight_grad = weight_grad.reshape(3, 3, 3, cb, out_ch).transpose(3, 0, 1, 2, 4)
-
-    input_grad = pl.pallas_call(
-        input_kernel,
-        out_shape=jax.ShapeDtypeStruct(volume.shape, bf16),
-        scratch_shapes=[pltpu.VMEM((cb * planes * hgt, wid), f32)],
-        compiler_params=params(),
-    )(weights, *[grads[z] for z in out_planes], after)
     return pooled, input_grad, weight_grad
 
 

time: 50.6 us -> 47.3 us (0.935)
  waiting for transfers between devices: 11.8 us -> 8.32 us
  Pallas kernels: 5.58 us -> 7.81 us
  local copies, waits for them, and re-layouts: 2.68 us -> 0.66 us
  starting transfers between devices: 28.5 us -> 29.5 us
  other arithmetic: 0.97 us -> 0.08 us
    ppermute x18 -> x17, waiting for transfers between devices: 11.8 us -> 8.32 us  [the longest x12 5.08 us: moved(): lax.ppermute(block, axis, [(i, i ^ k if XOR else (i + k) % n) for i in ra...]
    pallas_call x9 -> x10, Pallas kernels: 5.58 us -> 7.81 us  [the longest x1 2.69 us: on_device(): pl.pallas_call(input_kernel, out_shape=shape(volume.shape, bf16), scratch...]
    unnamed x10 -> x4, local copies, waits for them, and re-layouts: 1.7 us -> 0.66 us
    ppermute x18 -> x17, starting transfers between devices: 27.3 us -> 28.3 us  [the longest x12 18.4 us: moved(): lax.ppermute(block, axis, [(i, i ^ k if XOR else (i + k) % n) for i in ra...]
    slice x1 -> x0, local copies, waits for them, and re-layouts: 0.96 us -> none  [on_device(): volume[:, -1:]]
    concatenate x1 -> x0, other arithmetic: 0.79 us -> none  [sum_over(): return jnp.concatenate(halves, axis=0)]
  transfers between devices with their start and end apart: 19 -> 18, of which waited for: 7 -> 8; matrix products, arithmetic and copies ran while one was open for 1% -> 1% of each run, Pallas kernels for 10% -> 9%
where the time goes in v4:
time: 47.3 us; the launch traced here: 47.1 us
  starting transfers between devices  29.5 us (62%)
  waiting for transfers between devices  8.32 us (18%)
  Pallas kernels  7.81 us (17%)
  between operations  0.73 us (2%)
  local copies, waits for them, and re-layouts  0.66 us (1%)
    ppermute x12, starting transfers between devices, moved(): lax.ppermute(block, axis, [(i, i ^ k if XOR else (i + k) % n) for i in ra...  18.4 us
    ppermute x12, waiting for transfers between devices, moved(): lax.ppermute(block, axis, [(i, i ^ k if XOR else (i + k) % n) for i in ra...  5.08 us
    ppermute x2, starting transfers between devices, on_device(): got = lax.ppermute(sent, 'space', pairs)  4.6 us
    ppermute x1, starting transfers between devices, on_device(): other = lax.ppermute(rows, 'space', [(i, i ^ 1) for i in range(n_space)])  2.78 us
    pallas_call x1, Pallas kernels, on_device(): pl.pallas_call(input_kernel, out_shape=shape(volume.shape, bf16), scratch...  2.69 us
    ppermute x1, starting transfers between devices, on_device(): rim = lax.ppermute(edge, 'space', [(i, i + 1) for i in range(n_space - 1)])  2.36 us
    pallas_call x1, Pallas kernels, on_device(): pl.pallas_call(call, in_specs=[pl.BlockSpec(memory_space=pltpu.HBM)] * 2,...  2.17 us
    ppermute x2, waiting for transfers between devices, on_device(): got = lax.ppermute(sent, 'space', pairs)  1.63 us
  transfers between devices with their start and end apart: 18, of which 8 were waited for; matrix products, arithmetic and copies ran while one was open for 1% of the time, Pallas kernels for 9%

profile of v4, /device:TPU:0, one launch (start us, length us, event | category | flops | bytes accessed | tf_op | source)
XLA Modules:
  0.0 47.1 jit_solution(17645057389930435147)
XLA Ops:
  0.6 2.2 %shard_map.59 = (bf16[32,4,16,128]{3,2,1,0:T(8,128)(2,1)S(1)}, bf16[864,128]{1,0:T(8,128)(2,1)S(1)}, bf16[32,1,16,128]{3,2,1,0:T(8,128)(2,1)S(1)}, bf16[864,512]...) custom-call(bf16[32,4,16,128]{3,2,1,0:T(8,128)(2,1)} %refs_0_.1, ...), custom_call_target="tpu_custom_call" | custom-call | tf_op jit(solution)/shard_map/pallas_call | solution.py:283
  2.8 2.4 %collective-permute-start = (bf16[32,1,16,128]{3,2,1,0:T(8,128)(2,1)S(1)}, bf16[32,1,16,128]{3,2,1,0:T(8,128)(2,1)S(1)}, u32[]{:S(2)}, u32[]{:S(2)}) collective-permute-start(bf16[32,1,16,128]{3,2,1,0:T(8,128)(2,1)S(1)} %get-tuple-element.31), channel_id=1, source_target_pairs={{0,4},{4,8},{8,12},{12,16},{16,20},{20,24},{24,28},{1,5},{5,9},{9,... | collective-permute-start | bytes 393224 | tf_op jit(solution)/shard_map/ppermute | solution.py:296
  5.2 2.5 %collective-permute-start.4 = (f32[32,512]{1,0:T(8,128)S(1)}, f32[32,512]{1,0:T(8,128)S(1)}, u32[]{:S(2)}, u32[]{:S(2)}) collective-permute-start(f32[32,512]{1,0:T(8,128)S(1)} %get-tuple-element.40), channel_id=1, source_target_pairs={{0,1},{1,0},{2,3},{3,2},{4,5},{5,4},{6,7},{7,6},{8,9},{9,8},{10,11... | collective-permute-start | bytes 196616 | tf_op jit(solution)/shard_map/ppermute | solution.py:252
  7.6 2.6 %collective-permute-start.5 = (f32[32,512]{1,0:T(8,128)S(1)}, f32[32,512]{1,0:T(8,128)S(1)}, u32[]{:S(2)}, u32[]{:S(2)}) collective-permute-start(f32[32,512]{1,0:T(8,128)S(1)} %get-tuple-element.41), channel_id=1, source_target_pairs={{0,2},{1,3},{2,0},{3,1},{4,6},{5,7},{6,4},{7,5},{8,10},{9,11},{10,... | collective-permute-start | bytes 196616 | tf_op jit(solution)/shard_map/ppermute | solution.py:252
  10.3 0.8 %shard_map.60 = (bf16[864,512]{1,0:T(8,128)(2,1)S(1)}, f32[32,512]{1,0:T(8,128)S(1)}, f32[32,512]{1,0:T(8,128)S(1)}, f32[32,512]{1,0:T(8,128)S(1)}, f32[32,512]{1,0:T(8,128)S(1)}) custom-call(bf16[32,1,16,128]{3,2,1,0:T(8,128)(2,1)S(1)} %collective-permute-done.refs_0_, bf16[32,4,16,128]{3,2,1,0:T(8,128)(2,1)S(1)} %get-tuple-element.32.refs_1_, ...), custom_call_target="tpu_custom_call" | custom-call | tf_op jit(solution)/shard_map/pallas_call | solution.py:298
  11.1 0.9 %collective-permute-start.1 = (f32[32,512]{1,0:T(8,128)S(1)}, f32[32,512]{1,0:T(8,128)S(1)}, u32[]{:S(2)}, u32[]{:S(2)}) collective-permute-start(f32[32,512]{1,0:T(8,128)S(1)} %get-tuple-element.35), channel_id=1, source_target_pairs={{0,1},{1,0},{2,3},{3,2},{4,5},{5,4},{6,7},{7,6},{8,9},{9,8},{10,11... | collective-permute-start | bytes 196616 | tf_op jit(solution)/shard_map/ppermute | solution.py:252
  12.0 3.5 %collective-permute-start.2 = (f32[32,512]{1,0:T(8,128)S(1)}, f32[32,512]{1,0:T(8,128)S(1)}, u32[]{:S(2)}, u32[]{:S(2)}) collective-permute-start(f32[32,512]{1,0:T(8,128)S(1)} %get-tuple-element.36), channel_id=1, source_target_pairs={{0,2},{1,3},{2,0},{3,1},{4,6},{5,7},{6,4},{7,5},{8,10},{9,11},{10,... | collective-permute-start | bytes 196616 | tf_op jit(solution)/shard_map/ppermute | solution.py:252
  15.6 0.1 shard_map.58.spread_ref
  15.7 1.2 %collective-permute-done.6.rest_3_ = f32[32,512]{1,0:T(8,128)S(1)} collective-permute-done((f32[32,512]{1,0:T(8,128)S(1)}, f32[32,512]{1,0:T(8,128)S(1)}, u32[]{:S(2)}, u32[]{:S(2)}) %collective-permute-start.6) | collective-permute-done | bytes 65568 | tf_op jit(solution)/shard_map/ppermute | solution.py:252
  17.0 2.7 %collective-permute-start.9 = (bf16[32,512]{1,0:T(8,128)(2,1)S(1)}, bf16[32,512]{1,0:T(8,128)(2,1)S(1)}, u32[]{:S(2)}, u32[]{:S(2)}) collective-permute-start(bf16[32,512]{1,0:T(8,128)(2,1)S(1)} %get-tuple-element.45.refs_0_), channel_id=1, source_target_pairs={{0,3},{1,2},{2,1},{3,0},{4,7},{5,6},{6,5},{7,4},{8,11},{9,10},{10,... | collective-permute-start | bytes 98312 | tf_op jit(solution)/shard_map/ppermute | solution.py:252
  19.6 1.8 %collective-permute-start.7 = (bf16[32,512]{1,0:T(8,128)(2,1)S(1)}, bf16[32,512]{1,0:T(8,128)(2,1)S(1)}, u32[]{:S(2)}, u32[]{:S(2)}) collective-permute-start(bf16[32,512]{1,0:T(8,128)(2,1)S(1)} %get-tuple-element.45.refs_0_), channel_id=1, source_target_pairs={{0,1},{1,0},{2,3},{3,2},{4,5},{5,4},{6,7},{7,6},{8,9},{9,8},{10,11... | collective-permute-start | bytes 98312 | tf_op jit(solution)/shard_map/ppermute | solution.py:252
  21.4 0.4 collective-permute-done.3.rest_3_
  21.9 2.3 %collective-permute-start.12 = (bf16[32,512]{1,0:T(8,128)(2,1)S(1)}, bf16[32,512]{1,0:T(8,128)(2,1)S(1)}, u32[]{:S(2)}, u32[]{:S(2)}) collective-permute-start(bf16[32,512]{1,0:T(8,128)(2,1)S(1)} %get-tuple-element.48.refs_0_), channel_id=1, source_target_pairs={{0,3},{1,2},{2,1},{3,0},{4,7},{5,6},{6,5},{7,4},{8,11},{9,10},{10,... | collective-permute-start | bytes 98312 | tf_op jit(solution)/shard_map/ppermute | solution.py:252
  24.1 2.1 %collective-permute-start.11 = (bf16[32,512]{1,0:T(8,128)(2,1)S(1)}, bf16[32,512]{1,0:T(8,128)(2,1)S(1)}, u32[]{:S(2)}, u32[]{:S(2)}) collective-permute-start(bf16[32,512]{1,0:T(8,128)(2,1)S(1)} %get-tuple-element.48.refs_0_), channel_id=1, source_target_pairs={{0,2},{1,3},{2,0},{3,1},{4,6},{5,7},{6,4},{7,5},{8,10},{9,11},{10,... | collective-permute-start | bytes 98312 | tf_op jit(solution)/shard_map/ppermute | solution.py:252
  26.2 0.1 collective-permute-start.10
  26.3 0.4 shard_map.64
  26.7 1.2 %collective-permute-done.12.refs_3_ = bf16[32,512]{1,0:T(8,128)(2,1)S(1)} collective-permute-done((bf16[32,512]{1,0:T(8,128)(2,1)S(1)}, bf16[32,512]{1,0:T(8,128)(2,1)S(1)}, u32[]{:S(2)}, u32[]{:S(2)}) %collective-permute-start.12) | collective-permute-done | bytes 32800 | tf_op jit(solution)/shard_map/ppermute | solution.py:252
  27.9 1.1 %collective-permute-done.11.refs_2_ = bf16[32,512]{1,0:T(8,128)(2,1)S(1)} collective-permute-done((bf16[32,512]{1,0:T(8,128)(2,1)S(1)}, bf16[32,512]{1,0:T(8,128)(2,1)S(1)}, u32[]{:S(2)}, u32[]{:S(2)}) %collective-permute-start.11) | collective-permute-done | bytes 32800 | tf_op jit(solution)/shard_map/ppermute | solution.py:252
  29.0 1.1 %collective-permute-done.10.refs_1_ = bf16[32,512]{1,0:T(8,128)(2,1)S(1)} collective-permute-done((bf16[32,512]{1,0:T(8,128)(2,1)S(1)}, bf16[32,512]{1,0:T(8,128)(2,1)S(1)}, u32[]{:S(2)}, u32[]{:S(2)}) %collective-permute-start.10) | collective-permute-done | bytes 32800 | tf_op jit(solution)/shard_map/ppermute | solution.py:252
  30.2 0.5 shard_map.65
  30.6 0.1 collective-permute-start.13
  30.7 1.5 %collective-permute-done.13 = f32[432,128]{1,0:T(8,128)S(1)} collective-permute-done((f32[432,128]{1,0:T(8,128)S(1)}, f32[432,128]{1,0:T(8,128)S(1)}, u32[]{:S(2)}, u32[]{:S(2)}) %collective-permute-start.13) | collective-permute-done | bytes 221216 | tf_op jit(solution)/shard_map/ppermute | solution.py:336
  32.2 1.9 %collective-permute-start.14 = (bf16[432,128]{1,0:T(8,128)(2,1)S(1)}, bf16[432,128]{1,0:T(8,128)(2,1)S(1)}, u32[]{:S(2)}, u32[]{:S(2)}) collective-permute-start(bf16[432,128]{1,0:T(8,128)(2,1)S(1)} %add_convert_fusion.1), channel_id=1, source_target_pairs={{0,8},{4,20},{8,0},{12,28},{16,24},{20,4},{24,16},{28,12},{1,9},{5... | collective-permute-start | bytes 331784 | tf_op jit(solution)/shard_map/ppermute | solution.py:353
  34.1 1.3 %collective-permute-start.16 = (bf16[128,512]{1,0:T(8,128)(2,1)S(1)}, bf16[128,512]{1,0:T(8,128)(2,1)S(1)}, u32[]{:S(2)}, u32[]{:S(2)}) collective-permute-start(bf16[128,512]{1,0:T(8,128)(2,1)S(1)} %get-tuple-element.55.rest_0_), channel_id=1, source_target_pairs={{4,0},{8,4},{12,8},{16,12},{20,16},{24,20},{28,24},{5,1},{9,5},{13... | collective-permute-start | bytes 393224 | tf_op jit(solution)/shard_map/ppermute | solution.py:343
  35.4 1.6 %collective-permute-done.14 = bf16[432,128]{1,0:T(8,128)(2,1)S(1)} collective-permute-done((bf16[432,128]{1,0:T(8,128)(2,1)S(1)}, bf16[432,128]{1,0:T(8,128)(2,1)S(1)}, u32[]{:S(2)}, u32[]{:S(2)}) %collective-permute-start.14) | collective-permute-done | bytes 110624 | tf_op jit(solution)/shard_map/ppermute | solution.py:353
  37.0 2.7 %collective-permute-start.15 = (bf16[432,128]{1,0:T(8,128)(2,1)S(1)}, bf16[432,128]{1,0:T(8,128)(2,1)S(1)}, u32[]{:S(2)}, u32[]{:S(2)}) collective-permute-start(bf16[432,128]{1,0:T(8,128)(2,1)S(1)} %add_convert_fusion), channel_id=1, source_target_pairs={{0,16},{4,12},{8,24},{12,4},{16,0},{20,28},{24,8},{28,20},{1,17},{... | collective-permute-start | bytes 331784 | tf_op jit(solution)/shard_map/ppermute | solution.py:353
  39.7 2.7 %shard_map.66 = bf16[32,4,16,128]{3,2,1,0:T(8,128)(2,1)} custom-call(bf16[864,128]{1,0:T(8,128)(2,1)S(1)} %get-tuple-element.33.refs_2_.w_ref, bf16[128,512]{1,0:T(8,128)(2,1)S(1)} %get-tuple-element.55.rest_0_, bf16[128,512]{1,0:T(8,128)(2,1)S(1)} %get-tuple-element.56.rest_1_, bf16[128,512]{1,0:T(8,128)(2,1)S(1)} %collective-permute-done.16.rest_2_), custom_call_target="tpu_custom_call" | custom-call | tf_op jit(solution)/shard_map/pallas_call | solution.py:346
  42.5 2.8 %collective-permute-start.17 = (f32[432,128]{1,0:T(8,128)S(1)}, f32[432,128]{1,0:T(8,128)S(1)}, u32[]{:S(2)}, u32[]{:S(2)}) collective-permute-start(f32[432,128]{1,0:T(8,128)S(1)} %convert_add_fusion.own_ref), channel_id=1, source_target_pairs={{0,4},{4,0},{8,12},{12,8},{16,20},{20,16},{24,28},{28,24},{1,5},{5... | collective-permute-start | bytes 663560 | tf_op jit(solution)/shard_map/ppermute | solution.py:356
  45.3 0.3 shard_map.63
  45.6 0.6 %copy.7 = bf16[32,1,4,32]{3,2,1,0:T(4,128)(2,1)} copy(bf16[32,1,4,32]{3,0,2,1:T(8,128)(2,1)S(1)} %bitcast.14) | data formatting | bytes 16384
  46.2 0.1 collective-permute-done.17.other_ref
  46.4 0.8 %shard_map.67 = f32[864,128]{1,0:T(8,128)} custom-call(f32[432,128]{1,0:T(8,128)S(1)} %convert_add_fusion.own_ref, f32[432,128]{1,0:T(8,128)S(1)} %collective-permute-done.17.other_ref), custom_call_target="tpu_custom_call" | custom-call | tf_op jit(solution)/shard_map/pallas_call | solution.py:357
  (21 shorter events, 0.2 us)
Async XLA Ops:
  2.8 7.4 %collective-permute-start = (bf16[32,1,16,128]{3,2,1,0:T(8,128)(2,1)S(1)}, bf16[32,1,16,128]{3,2,1,0:T(8,128)(2,1)S(1)}, u32[]{:S(2)}, u32[]{:S(2)}) collective-permute-start(bf16[32,1,16,128]{3,2,1,0:T(8,128)(2,1)S(1)} %get-tuple-element.31), channel_id=1, source_target_pairs={{0,4},{4,8},{8,12},{12,16},{16,20},{20,24},{24,28},{1,5},{5,9},{9,... | collective-permute-start | bytes 393224 | tf_op jit(solution)/shard_map/ppermute | solution.py:296
  5.2 10.4 %collective-permute-start.4 = (f32[32,512]{1,0:T(8,128)S(1)}, f32[32,512]{1,0:T(8,128)S(1)}, u32[]{:S(2)}, u32[]{:S(2)}) collective-permute-start(f32[32,512]{1,0:T(8,128)S(1)} %get-tuple-element.40), channel_id=1, source_target_pairs={{0,1},{1,0},{2,3},{3,2},{4,5},{5,4},{6,7},{7,6},{8,9},{9,8},{10,11... | collective-permute-start | bytes 196616 | tf_op jit(solution)/shard_map/ppermute | solution.py:252
  7.6 8.0 %collective-permute-start.5 = (f32[32,512]{1,0:T(8,128)S(1)}, f32[32,512]{1,0:T(8,128)S(1)}, u32[]{:S(2)}, u32[]{:S(2)}) collective-permute-start(f32[32,512]{1,0:T(8,128)S(1)} %get-tuple-element.41), channel_id=1, source_target_pairs={{0,2},{1,3},{2,0},{3,1},{4,6},{5,7},{6,4},{7,5},{8,10},{9,11},{10,... | collective-permute-start | bytes 196616 | tf_op jit(solution)/shard_map/ppermute | solution.py:252
  10.2 6.7 %collective-permute-start.6 = (f32[32,512]{1,0:T(8,128)S(1)}, f32[32,512]{1,0:T(8,128)S(1)}, u32[]{:S(2)}, u32[]{:S(2)}) collective-permute-start(f32[32,512]{1,0:T(8,128)S(1)} %get-tuple-element.42), channel_id=1, source_target_pairs={{0,3},{1,2},{2,1},{3,0},{4,7},{5,6},{6,5},{7,4},{8,11},{9,10},{10,... | collective-permute-start | bytes 196616 | tf_op jit(solution)/shard_map/ppermute | solution.py:252
  10.3 5.3 %copy-start = (bf16[32,1,4,32]{3,2,1,0:T(4,128)(2,1)S(1)}, bf16[32,1,4,32]{3,2,1,0:T(4,128)(2,1)}, u32[]{:S(2)}) copy-start(bf16[32,1,4,32]{3,2,1,0:T(4,128)(2,1)} %param.5) | copy-start | bytes 24580
  11.1 8.6 %collective-permute-start.1 = (f32[32,512]{1,0:T(8,128)S(1)}, f32[32,512]{1,0:T(8,128)S(1)}, u32[]{:S(2)}, u32[]{:S(2)}) collective-permute-start(f32[32,512]{1,0:T(8,128)S(1)} %get-tuple-element.35), channel_id=1, source_target_pairs={{0,1},{1,0},{2,3},{3,2},{4,5},{5,4},{6,7},{7,6},{8,9},{9,8},{10,11... | collective-permute-start | bytes 196616 | tf_op jit(solution)/shard_map/ppermute | solution.py:252
  12.0 9.4 %collective-permute-start.2 = (f32[32,512]{1,0:T(8,128)S(1)}, f32[32,512]{1,0:T(8,128)S(1)}, u32[]{:S(2)}, u32[]{:S(2)}) collective-permute-start(f32[32,512]{1,0:T(8,128)S(1)} %get-tuple-element.36), channel_id=1, source_target_pairs={{0,2},{1,3},{2,0},{3,1},{4,6},{5,7},{6,4},{7,5},{8,10},{9,11},{10,... | collective-permute-start | bytes 196616 | tf_op jit(solution)/shard_map/ppermute | solution.py:252
  15.5 6.3 %collective-permute-start.3 = (f32[32,512]{1,0:T(8,128)S(1)}, f32[32,512]{1,0:T(8,128)S(1)}, u32[]{:S(2)}, u32[]{:S(2)}) collective-permute-start(f32[32,512]{1,0:T(8,128)S(1)} %get-tuple-element.37), channel_id=1, source_target_pairs={{0,3},{1,2},{2,1},{3,0},{4,7},{5,6},{6,5},{7,4},{8,11},{9,10},{10,... | collective-permute-start | bytes 196616 | tf_op jit(solution)/shard_map/ppermute | solution.py:252
  17.0 9.3 %collective-permute-start.9 = (bf16[32,512]{1,0:T(8,128)(2,1)S(1)}, bf16[32,512]{1,0:T(8,128)(2,1)S(1)}, u32[]{:S(2)}, u32[]{:S(2)}) collective-permute-start(bf16[32,512]{1,0:T(8,128)(2,1)S(1)} %get-tuple-element.45.refs_0_), channel_id=1, source_target_pairs={{0,3},{1,2},{2,1},{3,0},{4,7},{5,6},{6,5},{7,4},{8,11},{9,10},{10,... | collective-permute-start | bytes 98312 | tf_op jit(solution)/shard_map/ppermute | solution.py:252
  19.6 6.7 %collective-permute-start.8 = (bf16[32,512]{1,0:T(8,128)(2,1)S(1)}, bf16[32,512]{1,0:T(8,128)(2,1)S(1)}, u32[]{:S(2)}, u32[]{:S(2)}) collective-permute-start(bf16[32,512]{1,0:T(8,128)(2,1)S(1)} %get-tuple-element.45.refs_0_), channel_id=1, source_target_pairs={{0,2},{1,3},{2,0},{3,1},{4,6},{5,7},{6,4},{7,5},{8,10},{9,11},{10,... | collective-permute-start | bytes 98312 | tf_op jit(solution)/shard_map/ppermute | solution.py:252
  19.6 6.7 %collective-permute-start.7 = (bf16[32,512]{1,0:T(8,128)(2,1)S(1)}, bf16[32,512]{1,0:T(8,128)(2,1)S(1)}, u32[]{:S(2)}, u32[]{:S(2)}) collective-permute-start(bf16[32,512]{1,0:T(8,128)(2,1)S(1)} %get-tuple-element.45.refs_0_), channel_id=1, source_target_pairs={{0,1},{1,0},{2,3},{3,2},{4,5},{5,4},{6,7},{7,6},{8,9},{9,8},{10,11... | collective-permute-start | bytes 98312 | tf_op jit(solution)/shard_map/ppermute | solution.py:252
  21.9 6.1 %collective-permute-start.12 = (bf16[32,512]{1,0:T(8,128)(2,1)S(1)}, bf16[32,512]{1,0:T(8,128)(2,1)S(1)}, u32[]{:S(2)}, u32[]{:S(2)}) collective-permute-start(bf16[32,512]{1,0:T(8,128)(2,1)S(1)} %get-tuple-element.48.refs_0_), channel_id=1, source_target_pairs={{0,3},{1,2},{2,1},{3,0},{4,7},{5,6},{6,5},{7,4},{8,11},{9,10},{10,... | collective-permute-start | bytes 98312 | tf_op jit(solution)/shard_map/ppermute | solution.py:252
  24.1 4.9 %collective-permute-start.11 = (bf16[32,512]{1,0:T(8,128)(2,1)S(1)}, bf16[32,512]{1,0:T(8,128)(2,1)S(1)}, u32[]{:S(2)}, u32[]{:S(2)}) collective-permute-start(bf16[32,512]{1,0:T(8,128)(2,1)S(1)} %get-tuple-element.48.refs_0_), channel_id=1, source_target_pairs={{0,2},{1,3},{2,0},{3,1},{4,6},{5,7},{6,4},{7,5},{8,10},{9,11},{10,... | collective-permute-start | bytes 98312 | tf_op jit(solution)/shard_map/ppermute | solution.py:252
  26.2 3.9 %collective-permute-start.10 = (bf16[32,512]{1,0:T(8,128)(2,1)S(1)}, bf16[32,512]{1,0:T(8,128)(2,1)S(1)}, u32[]{:S(2)}, u32[]{:S(2)}) collective-permute-start(bf16[32,512]{1,0:T(8,128)(2,1)S(1)} %get-tuple-element.48.refs_0_), channel_id=1, source_target_pairs={{0,1},{1,0},{2,3},{3,2},{4,5},{5,4},{6,7},{7,6},{8,9},{9,8},{10,11... | collective-permute-start | bytes 98312 | tf_op jit(solution)/shard_map/ppermute | solution.py:252
  30.6 1.5 %collective-permute-start.13 = (f32[432,128]{1,0:T(8,128)S(1)}, f32[432,128]{1,0:T(8,128)S(1)}, u32[]{:S(2)}, u32[]{:S(2)}) collective-permute-start(f32[432,128]{1,0:T(8,128)S(1)} %get-tuple-element.50), channel_id=1, source_target_pairs={{0,4},{4,0},{8,12},{12,8},{16,20},{20,16},{24,28},{28,24},{1,5},{5... | collective-permute-start | bytes 663560 | tf_op jit(solution)/shard_map/ppermute | solution.py:336
  32.2 4.8 %collective-permute-start.14 = (bf16[432,128]{1,0:T(8,128)(2,1)S(1)}, bf16[432,128]{1,0:T(8,128)(2,1)S(1)}, u32[]{:S(2)}, u32[]{:S(2)}) collective-permute-start(bf16[432,128]{1,0:T(8,128)(2,1)S(1)} %add_convert_fusion.1), channel_id=1, source_target_pairs={{0,8},{4,20},{8,0},{12,28},{16,24},{20,4},{24,16},{28,12},{1,9},{5... | collective-permute-start | bytes 331784 | tf_op jit(solution)/shard_map/ppermute | solution.py:353
  34.1 5.6 %collective-permute-start.16 = (bf16[128,512]{1,0:T(8,128)(2,1)S(1)}, bf16[128,512]{1,0:T(8,128)(2,1)S(1)}, u32[]{:S(2)}, u32[]{:S(2)}) collective-permute-start(bf16[128,512]{1,0:T(8,128)(2,1)S(1)} %get-tuple-element.55.rest_0_), channel_id=1, source_target_pairs={{4,0},{8,4},{12,8},{16,12},{20,16},{24,20},{28,24},{5,1},{9,5},{13... | collective-permute-start | bytes 393224 | tf_op jit(solution)/shard_map/ppermute | solution.py:343
  37.0 5.4 %collective-permute-start.15 = (bf16[432,128]{1,0:T(8,128)(2,1)S(1)}, bf16[432,128]{1,0:T(8,128)(2,1)S(1)}, u32[]{:S(2)}, u32[]{:S(2)}) collective-permute-start(bf16[432,128]{1,0:T(8,128)(2,1)S(1)} %add_convert_fusion), channel_id=1, source_target_pairs={{0,16},{4,12},{8,24},{12,4},{16,0},{20,28},{24,8},{28,20},{1,17},{... | collective-permute-start | bytes 331784 | tf_op jit(solution)/shard_map/ppermute | solution.py:353
  42.5 3.9 %collective-permute-start.17 = (f32[432,128]{1,0:T(8,128)S(1)}, f32[432,128]{1,0:T(8,128)S(1)}, u32[]{:S(2)}, u32[]{:S(2)}) collective-permute-start(f32[432,128]{1,0:T(8,128)S(1)} %convert_add_fusion.own_ref), channel_id=1, source_target_pairs={{0,4},{4,0},{8,12},{12,8},{16,20},{20,16},{24,28},{28,24},{1,5},{5... | collective-permute-start | bytes 663560 | tf_op jit(solution)/shard_map/ppermute | solution.py:356

commit v5 on v4

--- a/solution.py
+++ b/solution.py
@@ -32,20 +32,21 @@
     return jnp.where(hit, 1.0, 0.0).astype(jnp.bfloat16)
 
 
+def load_kernel(vol_hbm, w_hbm, vol_ref, w_ref, edge_ref, sems):
+    planes = vol_ref.shape[1]
+    copies = [pltpu.make_async_copy(vol_hbm.at[:, planes - 1 :], edge_ref, sems.at[planes + 1])]
+    for p in reversed(range(planes)):
+        copies.append(pltpu.make_async_copy(vol_hbm.at[:, p], vol_ref.at[:, p], sems.at[p]))
+    copies.append(pltpu.make_async_copy(w_hbm, w_ref, sems.at[planes]))
+    for copy in copies:
+        copy.start()
+    for copy in copies:
+        copy.wait()
+
+
 def fwd_kernel(n, ob, z, *refs):
     if z:
-        vol_hbm, w_hbm, vol_ref, w_ref, edge_ref, cols_ref, *rest, sems = refs
-        planes = vol_ref.shape[1]
-        copies = [
-            pltpu.make_async_copy(vol_hbm.at[:, p], vol_ref.at[:, p], sems.at[p])
-            for p in range(planes)
-        ]
-        w_copy = pltpu.make_async_copy(w_hbm, w_ref, sems.at[planes])
-        order = list(range(2 * z - 1, planes)) + list(range(2 * z - 1))
-        for i, p in enumerate(order):
-            copies[p].start()
-            if i == 2:
-                w_copy.start()
+        vol_ref, w_ref, cols_ref, *rest = refs
     else:
         rim_ref, vol_ref, w_ref, cols_ref, *rest = refs
     part_refs = rest[:-2] if n > 1 else rest[:-1]
@@ -55,10 +56,6 @@
     sel = pair_matrix(False, wid, wid // 2)
     zero = jnp.zeros((cb, wid), jnp.float32)
     for a in range(3):
-        if z:
-            copies[2 * z + a - 1].wait()
-            if a == 2:
-                edge_ref[...] = vol_ref[:, -1:]
         plane = vol_ref[:, 2 * z + a - 1] if z or a else rim_ref[:, 0]
         wide_ref[...] = plane.astype(jnp.float32).reshape(cb * hgt, wid)
         row = [wide_ref[pl.ds(y, cb, stride=hgt), :] for y in range(hgt)]
@@ -79,10 +76,6 @@
                 cols_ref[tap * cb : (tap + 1) * cb, :] = jnp.concatenate(
                     [block[j * cb : (j + 1) * cb] for j in range(groups)], axis=1
                 )
-    if z:
-        w_copy.wait()
-        for p in range(2 * z - 1):
-            copies[p].wait()
     part = lax.dot_general(
         w_ref[...],
         cols_ref[...],
@@ -123,20 +116,23 @@
 
 
 def pool_kernel(one_ref, two_ref, out_ref):
-    groups, ob, small = out_ref.shape
+    ob, _, groups, small = out_ref.shape
     wid = 4 * small
     r = lax.broadcasted_iota(jnp.int32, (wid, small), 0)
     c = lax.broadcasted_iota(jnp.int32, (wid, small), 1)
     r = r - jnp.where(r >= 2 * small, 2 * small, 0)
     pool = jnp.where((r >= 2 * c) & (r <= 2 * c + 1), 0.125, 0.0)
     act = one_ref[...] + two_ref[...]
-    for j in range(groups):
-        out_ref[j] = jnp.dot(
+    means = [
+        jnp.dot(
             act[:, j * wid : (j + 1) * wid],
             pool,
             precision=lax.Precision.HIGHEST,
             preferred_element_type=jnp.float32,
-        ).astype(jnp.bfloat16)
+        )
+        for j in range(groups)
+    ]
+    out_ref[:, 0] = jnp.stack(means, axis=1).astype(jnp.bfloat16)
 
 
 def in_order(n, block_refs, grad_ref):
@@ -197,8 +193,10 @@
                 copy.wait()
 
 
-def input_kernel(w_ref, *rest):
-    *grad_refs, out_ref, wide_ref = rest
+def input_kernel(own, w_ref, *refs):
+    *grad_refs, out_ref, wide_ref, done_ref, sems = refs
+    if not own:
+        *grad_refs, _ = grad_refs
     cb, planes, hgt, wid = out_ref.shape
     half = wid // 2
     groups = hgt // 4
@@ -210,8 +208,9 @@
     w = [w_ref[a * taps : (a + 1) * taps, :] for a in range(3)]
     behind = jnp.concatenate([w[2], w[0]], axis=1)
     g = [ref[...] for ref in grad_refs]
-    for i in range(planes):
-        z = i // 2
+    copies = []
+    for i in range(planes - 1) if own else (planes - 1,):
+        z = i // 2 if own else 0
         if i % 2 == 0:
             e_all = jnp.dot(w[1], g[z], preferred_element_type=jnp.float32)
         else:
@@ -241,10 +240,15 @@
                 for h in range(2):
                     y = 2 * (2 * j + h) + par
                     at = (par * groups + j) * cb
-                    wide_ref[pl.ds(i * hgt + y, cb, stride=planes * hgt), :] = full[
+                    wide_ref[pl.ds(y, cb, stride=hgt), :] = full[
                         at : at + cb, h * wid : (h + 1) * wid
                     ]
-    out_ref[...] = wide_ref[...].reshape(cb, planes, hgt, wid).astype(jnp.bfloat16)
+        slot = i if own else 0
+        done_ref[slot] = wide_ref[...].reshape(cb, hgt, wid).astype(jnp.bfloat16)
+        copies.append(pltpu.make_async_copy(done_ref.at[slot], out_ref.at[:, i], sems.at[slot]))
+        copies[-1].start()
+    for copy in copies:
+        copy.wait()
 
 
 def moved(block, axis, k):
@@ -273,34 +277,27 @@
     if n > 1:
         scratch.append(pltpu.VMEM((out_ch, cells), f32))
     part_shapes = [shape((ob if direct else out_ch, cells), f32)] * n
-    cols_shape = [shape((taps, cells), bf16)]
     out_planes = range(planes // 2)
     cols, grads, acts = {}, {}, {}
-    rim = ()
+    vol, w, edge = pl.pallas_call(
+        load_kernel,
+        in_specs=[pl.BlockSpec(memory_space=pltpu.HBM)] * 2,
+        out_shape=[
+            shape(volume.shape, bf16),
+            shape(weights.shape, bf16),
+            shape((cb, 1, hgt, wid), bf16),
+        ],
+        scratch_shapes=[pltpu.SemaphoreType.DMA((planes + 2,))],
+        compiler_params=params(),
+    )(*[pltpu.with_memory_space_constraint(x, pltpu.HBM) for x in (volume, weights)])
+    rim = lax.ppermute(edge, "space", [(i, i + 1) for i in range(n_space - 1)])
     for z in reversed(out_planes):
-        call = functools.partial(fwd_kernel, n, ob, z)
-        if z:
-            vol, w, edge, cols[z], *parts = pl.pallas_call(
-                call,
-                in_specs=[pl.BlockSpec(memory_space=pltpu.HBM)] * 2,
-                out_shape=[
-                    shape(volume.shape, bf16),
-                    shape(weights.shape, bf16),
-                    shape((cb, 1, hgt, wid), bf16),
-                ]
-                + cols_shape
-                + part_shapes,
-                scratch_shapes=scratch + [pltpu.SemaphoreType.DMA((planes + 1,))],
-                compiler_params=params(),
-            )(*[pltpu.with_memory_space_constraint(x, pltpu.HBM) for x in (volume, weights)])
-            rim = lax.ppermute(edge, "space", [(i, i + 1) for i in range(n_space - 1)])
-        else:
-            cols[z], *parts = pl.pallas_call(
-                call,
-                out_shape=cols_shape + part_shapes,
-                scratch_shapes=scratch,
-                compiler_params=params(),
-            )(rim, vol, w)
+        cols[z], *parts = pl.pallas_call(
+            functools.partial(fwd_kernel, n, ob, z),
+            out_shape=[shape((taps, cells), bf16)] + part_shapes,
+            scratch_shapes=scratch,
+            compiler_params=params(),
+        )(*(() if z else (rim,)), vol, w)
         if direct:
             parts = parts[:1] + [moved(p, "chan", k) for k, p in zip(RS, parts[1:])]
         else:
@@ -315,10 +312,6 @@
         else:
             grads[z] = [lax.all_gather(own, "chan", axis=0, tiled=True)]
 
-    pooled = pl.pallas_call(
-        pool_kernel, out_shape=shape(up.shape, bf16), compiler_params=params()
-    )(acts[0], acts[1])
-    pooled = pooled.transpose(1, 0, 2)[:, None]
     half = -(-taps // 32) * 16
     grad_shape = shape((out_ch, cells), bf16)
     term, grads[1] = pl.pallas_call(
@@ -333,26 +326,48 @@
         compiler_params=params(),
     )(term, cols[0], *grads[0])
 
+    def input_call(own, *operands):
+        n_done = planes - 1 if own else 1
+        hbm = pl.BlockSpec(memory_space=pltpu.HBM)
+        vmem = pl.BlockSpec(memory_space=pltpu.VMEM)
+        return pl.pallas_call(
+            functools.partial(input_kernel, own),
+            in_specs=[vmem] * 3 + [hbm] * (not own),
+            out_specs=hbm,
+            out_shape=shape(volume.shape, bf16),
+            scratch_shapes=[
+                pltpu.VMEM((cb * hgt, wid), f32),
+                pltpu.VMEM((n_done, cb, hgt, wid), bf16),
+                pltpu.SemaphoreType.DMA((n_done,)),
+            ],
+            input_output_aliases={} if own else {3: 0},
+            compiler_params=params(),
+        )(*operands)
+
     rows = keep + lax.ppermute(send, "space", [(i, i ^ 1) for i in range(n_space)])
     bits = [1 << b for b in range(1, n_space.bit_length() - 1)]
-    after = input_grad = None
-    for r, bit in enumerate(bits):
+    groups = [bits[i : i + 2] for i in range(0, len(bits), 2)]
+    after = input_grad = pooled = None
+    for r, group in enumerate(groups):
         sent = rows.astype(bf16)
-        if r == 0:
-            sent, grads[0] = lax.optimization_barrier((sent, grads[0]))
+        if r == len(groups) - 1:
+            sent, grads, acts = lax.optimization_barrier((sent, grads, acts))
+        partners = [sum(group[b] * (k >> b & 1) for b in range(len(group))) for k in range(1, 1 << len(group))]
+        terms = [sent] + [
+            lax.ppermute(sent, "space", [(i, i ^ p) for i in range(n_space)]) for p in partners
+        ]
+        if r == len(groups) - 1:
             after = lax.ppermute(grads[0], "space", [(i + 1, i) for i in range(n_space - 1)])
-        if r == len(bits) - 1:
-            sent, grads[1] = lax.optimization_barrier((sent, grads[1]))
-            input_grad = pl.pallas_call(
-                input_kernel,
-                out_shape=shape(volume.shape, bf16),
-                scratch_shapes=[pltpu.VMEM((cb * planes * hgt, wid), f32)],
-                compiler_params=params(),
-            )(w, grads[0], grads[1], after)
-        pairs = [(i, i ^ (bits[-1 - r] if i & 1 else bit)) for i in range(n_space)]
-        got = lax.ppermute(sent, "space", pairs)
-        rows = sent.astype(f32) + got.astype(f32)
-    rows, input_grad = lax.optimization_barrier((rows, input_grad))
+            pooled = pl.pallas_call(
+                pool_kernel, out_shape=shape(upstream.shape, bf16), compiler_params=params()
+            )(acts[0], acts[1])
+            input_grad = input_call(True, w, grads[0], grads[1])
+        terms = [t.astype(f32) for t in terms]
+        while len(terms) > 1:
+            terms = [a + b for a, b in zip(terms[::2], terms[1::2])]
+        rows = terms[0]
+    rows, input_grad, pooled, after = lax.optimization_barrier((rows, input_grad, pooled, after))
+    input_grad = input_call(False, w, grads[1], after, input_grad)
     other = lax.ppermute(rows, "space", [(i, i ^ 1) for i in range(n_space)])
     weight_grad = pl.pallas_call(
         join_kernel,

time: 47.3 us -> 45.8 us (0.968)
  starting transfers between devices: 29.5 us -> 27.5 us
  Pallas kernels: 7.81 us -> 8.89 us
  local copies, waits for them, and re-layouts: 0.66 us -> 0.01 us
    ppermute x1, starting transfers between devices: 2.78 us -> 0.88 us  [on_device(): other = lax.ppermute(rows, 'space', [(i, i ^ 1) for i in range(n_space)])]
    pallas_call x4 -> x6, Pallas kernels: 5.98 us -> 7.05 us  [the longest x2 3.17 us: input_call(): pl.pallas_call(functools.partial(input_kernel, own), in_specs=[vmem] * 3...]
    unnamed x4 -> x3, local copies, waits for them, and re-layouts: 0.66 us -> 0.01 us
    ppermute x2 -> x3, starting transfers between devices: 4.6 us -> 4.15 us  [on_device(): lax.ppermute(sent, 'space', [(i, i ^ p) for i in range(n_space)])]
    ppermute x2 -> x3, waiting for transfers between devices: 1.63 us -> 1.46 us  [on_device(): lax.ppermute(sent, 'space', [(i, i ^ p) for i in range(n_space)])]
  transfers between devices with their start and end apart: 18 -> 19, of which waited for: 8 -> 6; matrix products, arithmetic and copies ran while one was open for 1% -> 0% of each run, Pallas kernels for 9% -> 14%
where the time goes in v5:
time: 45.8 us; the launch traced here: 45.6 us
  starting transfers between devices  27.5 us (60%)
  Pallas kernels  8.89 us (19%)
  waiting for transfers between devices  8.34 us (18%)
  between operations  0.76 us (2%)
    ppermute x12, starting transfers between devices, moved(): lax.ppermute(block, axis, [(i, i ^ k if XOR else (i + k) % n) for i in ra...  18.7 us
    ppermute x12, waiting for transfers between devices, moved(): lax.ppermute(block, axis, [(i, i ^ k if XOR else (i + k) % n) for i in ra...  5.47 us
    ppermute x3, starting transfers between devices, on_device(): lax.ppermute(sent, 'space', [(i, i ^ p) for i in range(n_space)])  4.15 us
    pallas_call x2, Pallas kernels, input_call(): pl.pallas_call(functools.partial(input_kernel, own), in_specs=[vmem] * 3...  3.17 us
    ppermute x1, starting transfers between devices, on_device(): rim = lax.ppermute(edge, 'space', [(i, i + 1) for i in range(n_space - 1)])  2.36 us
    pallas_call x2, Pallas kernels, on_device(): pl.pallas_call(functools.partial(fwd_kernel, n, ob, z), out_shape=[shape(...  1.61 us
    ppermute x3, waiting for transfers between devices, on_device(): lax.ppermute(sent, 'space', [(i, i ^ p) for i in range(n_space)])  1.46 us
    ppermute x1, waiting for transfers between devices, on_device(): lax.ppermute(send, 'space', [(i, i ^ 1) for i in range(n_space)])  1.4 us
  transfers between devices with their start and end apart: 19, of which 6 were waited for; matrix products, arithmetic and copies ran while one was open for 0% of the time, Pallas kernels for 14%

profile of v5, /device:TPU:0, one launch (start us, length us, event | category | flops | bytes accessed | tf_op | source)
XLA Modules:
  0.0 45.6 jit_solution(3078336299679849542)
XLA Ops:
  0.6 1.3 %shard_map.58 = (bf16[32,4,16,128]{3,2,1,0:T(8,128)(2,1)S(1)}, bf16[864,128]{1,0:T(8,128)(2,1)S(1)}, bf16[32,1,16,128]{3,2,1,0:T(8,128)(2,1)S(1)}) custom-call(bf16[32,4,16,128]{3,2,1,0:T(8,128)(2,1)} %vol_hbm.1, bf16[864,128]{1,0:T(8,128)(2,1)} %bitcast.13), custom_call_target="tpu_custom_call" | custom-call | tf_op jit(solution)/shard_map/pallas_call | solution.py:282
  1.9 2.4 %collective-permute-start.6 = (bf16[32,1,16,128]{3,2,1,0:T(8,128)(2,1)S(1)}, bf16[32,1,16,128]{3,2,1,0:T(8,128)(2,1)S(1)}, u32[]{:S(2)}, u32[]{:S(2)}) collective-permute-start(bf16[32,1,16,128]{3,2,1,0:T(8,128)(2,1)S(1)} %get-tuple-element.43), channel_id=1, source_target_pairs={{0,4},{4,8},{8,12},{12,16},{16,20},{20,24},{24,28},{1,5},{5,9},{9,... | collective-permute-start | bytes 393224 | tf_op jit(solution)/shard_map/ppermute | solution.py:293
  4.3 0.8 %shard_map.59 = (bf16[864,512]{1,0:T(8,128)(2,1)S(1)}, f32[32,512]{1,0:T(8,128)S(1)}, f32[32,512]{1,0:T(8,128)S(1)}, f32[32,512]{1,0:T(8,128)S(1)}, f32[32,512]{1,0:T(8,128)S(1)}) custom-call(bf16[32,4,16,128]{3,2,1,0:T(8,128)(2,1)S(1)} %get-tuple-element.34.refs_0_.refs_1_, bf16[864,128]{1,0:T(8,128)(2,1)S(1)} %get-tuple-element.35.refs_1_.refs_2_.w_ref), custom_call_target="tpu_custom_call" | custom-call | tf_op jit(solution)/shard_map/pallas_call | solution.py:295
  5.1 2.5 %collective-permute-start = (f32[32,512]{1,0:T(8,128)S(1)}, f32[32,512]{1,0:T(8,128)S(1)}, u32[]{:S(2)}, u32[]{:S(2)}) collective-permute-start(f32[32,512]{1,0:T(8,128)S(1)} %get-tuple-element.38), channel_id=1, source_target_pairs={{0,1},{1,0},{2,3},{3,2},{4,5},{5,4},{6,7},{7,6},{8,9},{9,8},{10,11... | collective-permute-start | bytes 196616 | tf_op jit(solution)/shard_map/ppermute | solution.py:256
  7.6 2.6 %collective-permute-start.1 = (f32[32,512]{1,0:T(8,128)S(1)}, f32[32,512]{1,0:T(8,128)S(1)}, u32[]{:S(2)}, u32[]{:S(2)}) collective-permute-start(f32[32,512]{1,0:T(8,128)S(1)} %get-tuple-element.39), channel_id=1, source_target_pairs={{0,2},{1,3},{2,0},{3,1},{4,6},{5,7},{6,4},{7,5},{8,10},{9,11},{10,... | collective-permute-start | bytes 196616 | tf_op jit(solution)/shard_map/ppermute | solution.py:256
  10.2 0.8 %shard_map.63 = (bf16[864,512]{1,0:T(8,128)(2,1)S(1)}, f32[32,512]{1,0:T(8,128)S(1)}, f32[32,512]{1,0:T(8,128)S(1)}, f32[32,512]{1,0:T(8,128)S(1)}, f32[32,512]{1,0:T(8,128)S(1)}) custom-call(bf16[32,1,16,128]{3,2,1,0:T(8,128)(2,1)S(1)} %collective-permute-done.6.refs_0_, bf16[32,4,16,128]{3,2,1,0:T(8,128)(2,1)S(1)} %get-tuple-element.34.refs_0_.refs_1_, ...), custom_call_target="tpu_custom_call" | custom-call | tf_op jit(solution)/shard_map/pallas_call | solution.py:295
  11.0 1.0 %collective-permute-start.7 = (f32[32,512]{1,0:T(8,128)S(1)}, f32[32,512]{1,0:T(8,128)S(1)}, u32[]{:S(2)}, u32[]{:S(2)}) collective-permute-start(f32[32,512]{1,0:T(8,128)S(1)} %get-tuple-element.46), channel_id=1, source_target_pairs={{0,1},{1,0},{2,3},{3,2},{4,5},{5,4},{6,7},{7,6},{8,9},{9,8},{10,11... | collective-permute-start | bytes 196616 | tf_op jit(solution)/shard_map/ppermute | solution.py:256
  12.0 3.5 %collective-permute-start.8 = (f32[32,512]{1,0:T(8,128)S(1)}, f32[32,512]{1,0:T(8,128)S(1)}, u32[]{:S(2)}, u32[]{:S(2)}) collective-permute-start(f32[32,512]{1,0:T(8,128)S(1)} %get-tuple-element.47), channel_id=1, source_target_pairs={{0,2},{1,3},{2,0},{3,1},{4,6},{5,7},{6,4},{7,5},{8,10},{9,11},{10,... | collective-permute-start | bytes 196616 | tf_op jit(solution)/shard_map/ppermute | solution.py:256
  15.6 1.2 %collective-permute-done.2.rest_3_ = f32[32,512]{1,0:T(8,128)S(1)} collective-permute-done((f32[32,512]{1,0:T(8,128)S(1)}, f32[32,512]{1,0:T(8,128)S(1)}, u32[]{:S(2)}, u32[]{:S(2)}) %collective-permute-start.2) | collective-permute-done | bytes 65568 | tf_op jit(solution)/shard_map/ppermute | solution.py:256
  16.9 1.2 %collective-permute-start.3 = (bf16[32,512]{1,0:T(8,128)(2,1)S(1)}, bf16[32,512]{1,0:T(8,128)(2,1)S(1)}, u32[]{:S(2)}, u32[]{:S(2)}) collective-permute-start(bf16[32,512]{1,0:T(8,128)(2,1)S(1)} %get-tuple-element.41.refs_0_), channel_id=1, source_target_pairs={{0,1},{1,0},{2,3},{3,2},{4,5},{5,4},{6,7},{7,6},{8,9},{9,8},{10,11... | collective-permute-start | bytes 98312 | tf_op jit(solution)/shard_map/ppermute | solution.py:256
  18.1 2.1 %collective-permute-start.4 = (bf16[32,512]{1,0:T(8,128)(2,1)S(1)}, bf16[32,512]{1,0:T(8,128)(2,1)S(1)}, u32[]{:S(2)}, u32[]{:S(2)}) collective-permute-start(bf16[32,512]{1,0:T(8,128)(2,1)S(1)} %get-tuple-element.41.refs_0_), channel_id=1, source_target_pairs={{0,2},{1,3},{2,0},{3,1},{4,6},{5,7},{6,4},{7,5},{8,10},{9,11},{10,... | collective-permute-start | bytes 98312 | tf_op jit(solution)/shard_map/ppermute | solution.py:256
  20.1 1.2 %collective-permute-start.5 = (bf16[32,512]{1,0:T(8,128)(2,1)S(1)}, bf16[32,512]{1,0:T(8,128)(2,1)S(1)}, u32[]{:S(2)}, u32[]{:S(2)}) collective-permute-start(bf16[32,512]{1,0:T(8,128)(2,1)S(1)} %get-tuple-element.41.refs_0_), channel_id=1, source_target_pairs={{0,3},{1,2},{2,1},{3,0},{4,7},{5,6},{6,5},{7,4},{8,11},{9,10},{10,... | collective-permute-start | bytes 98312 | tf_op jit(solution)/shard_map/ppermute | solution.py:256
  21.4 0.4 collective-permute-done.9.rest_3_
  21.7 2.3 %collective-permute-start.10 = (bf16[32,512]{1,0:T(8,128)(2,1)S(1)}, bf16[32,512]{1,0:T(8,128)(2,1)S(1)}, u32[]{:S(2)}, u32[]{:S(2)}) collective-permute-start(bf16[32,512]{1,0:T(8,128)(2,1)S(1)} %get-tuple-element.49.refs_0_), channel_id=1, source_target_pairs={{0,1},{1,0},{2,3},{3,2},{4,5},{5,4},{6,7},{7,6},{8,9},{9,8},{10,11... | collective-permute-start | bytes 98312 | tf_op jit(solution)/shard_map/ppermute | solution.py:256
  24.1 0.6 %collective-permute-start.11 = (bf16[32,512]{1,0:T(8,128)(2,1)S(1)}, bf16[32,512]{1,0:T(8,128)(2,1)S(1)}, u32[]{:S(2)}, u32[]{:S(2)}) collective-permute-start(bf16[32,512]{1,0:T(8,128)(2,1)S(1)} %get-tuple-element.49.refs_0_), channel_id=1, source_target_pairs={{0,2},{1,3},{2,0},{3,1},{4,6},{5,7},{6,4},{7,5},{8,10},{9,11},{10,... | collective-permute-start | bytes 98312 | tf_op jit(solution)/shard_map/ppermute | solution.py:256
  24.7 1.8 %collective-permute-start.12 = (bf16[32,512]{1,0:T(8,128)(2,1)S(1)}, bf16[32,512]{1,0:T(8,128)(2,1)S(1)}, u32[]{:S(2)}, u32[]{:S(2)}) collective-permute-start(bf16[32,512]{1,0:T(8,128)(2,1)S(1)} %get-tuple-element.49.refs_0_), channel_id=1, source_target_pairs={{0,3},{1,2},{2,1},{3,0},{4,7},{5,6},{6,5},{7,4},{8,11},{9,10},{10,... | collective-permute-start | bytes 98312 | tf_op jit(solution)/shard_map/ppermute | solution.py:256
  26.5 0.4 shard_map.62
  26.9 2.4 %collective-permute-done.11.refs_2_ = bf16[32,512]{1,0:T(8,128)(2,1)S(1)} collective-permute-done((bf16[32,512]{1,0:T(8,128)(2,1)S(1)}, bf16[32,512]{1,0:T(8,128)(2,1)S(1)}, u32[]{:S(2)}, u32[]{:S(2)}) %collective-permute-start.11) | collective-permute-done | bytes 32800 | tf_op jit(solution)/shard_map/ppermute | solution.py:256
  29.3 1.4 %collective-permute-done.12.refs_3_ = bf16[32,512]{1,0:T(8,128)(2,1)S(1)} collective-permute-done((bf16[32,512]{1,0:T(8,128)(2,1)S(1)}, bf16[32,512]{1,0:T(8,128)(2,1)S(1)}, u32[]{:S(2)}, u32[]{:S(2)}) %collective-permute-start.12) | collective-permute-done | bytes 32800 | tf_op jit(solution)/shard_map/ppermute | solution.py:256
  30.8 0.5 %shard_map.65 = (f32[432,128]{1,0:T(8,128)S(1)}, f32[432,128]{1,0:T(8,128)S(1)}, bf16[128,512]{1,0:T(8,128)(2,1)S(1)}) custom-call(f32[864,128]{1,0:T(8,128)S(1)} %get-tuple-element.42.sum_ref, bf16[864,512]{1,0:T(8,128)(2,1)S(1)} %get-tuple-element.44.cols_ref, bf16[32,512]{1,0:T(8,128)(2,1)S(1)} %get-tuple-element.49.refs_0_, ...), custom_call_target="tpu_custom_call" | custom-call | tf_op jit(solution)/shard_map/pallas_call | solution.py:322
  31.2 0.1 collective-permute-start.13
  31.4 1.4 %collective-permute-done.13 = f32[432,128]{1,0:T(8,128)S(1)} collective-permute-done((f32[432,128]{1,0:T(8,128)S(1)}, f32[432,128]{1,0:T(8,128)S(1)}, u32[]{:S(2)}, u32[]{:S(2)}) %collective-permute-start.13) | collective-permute-done | bytes 221216 | tf_op jit(solution)/shard_map/ppermute | solution.py:347
  32.8 2.6 %collective-permute-start.14 = (bf16[432,128]{1,0:T(8,128)(2,1)S(1)}, bf16[432,128]{1,0:T(8,128)(2,1)S(1)}, u32[]{:S(2)}, u32[]{:S(2)}) collective-permute-start(bf16[432,128]{1,0:T(8,128)(2,1)S(1)} %add_convert_fusion), channel_id=1, source_target_pairs={{0,8},{4,12},{8,0},{12,4},{16,24},{20,28},{24,16},{28,20},{1,9},{5... | collective-permute-start | bytes 331784 | tf_op jit(solution)/shard_map/ppermute | solution.py:357
  35.4 0.2 collective-permute-start.15
  35.6 1.3 %collective-permute-start.16 = (bf16[432,128]{1,0:T(8,128)(2,1)S(1)}, bf16[432,128]{1,0:T(8,128)(2,1)S(1)}, u32[]{:S(2)}, u32[]{:S(2)}) collective-permute-start(bf16[432,128]{1,0:T(8,128)(2,1)S(1)} %add_convert_fusion), channel_id=1, source_target_pairs={{0,24},{4,28},{8,16},{12,20},{16,8},{20,12},{24,0},{28,4},{1,25},{... | collective-permute-start | bytes 331784 | tf_op jit(solution)/shard_map/ppermute | solution.py:357
  36.9 1.3 %collective-permute-start.17 = (bf16[128,512]{1,0:T(8,128)(2,1)S(1)}, bf16[128,512]{1,0:T(8,128)(2,1)S(1)}, u32[]{:S(2)}, u32[]{:S(2)}) collective-permute-start(bf16[128,512]{1,0:T(8,128)(2,1)S(1)} %get-tuple-element.57.refs_0_), channel_id=1, source_target_pairs={{4,0},{8,4},{12,8},{16,12},{20,16},{24,20},{28,24},{5,1},{9,5},{13... | collective-permute-start | bytes 393224 | tf_op jit(solution)/shard_map/ppermute | solution.py:360
  38.2 1.9 %shard_map.66.refs_2_ = bf16[32,4,16,128]{3,2,1,0:T(8,128)(2,1)} custom-call(bf16[864,128]{1,0:T(8,128)(2,1)S(1)} %get-tuple-element.35.refs_1_.refs_2_.w_ref, bf16[128,512]{1,0:T(8,128)(2,1)S(1)} %get-tuple-element.57.refs_0_, bf16[128,512]{1,0:T(8,128)(2,1)S(1)} %get-tuple-element.58.refs_1_.refs_0_), custom_call_target="tpu_custom_call" | custom-call | tf_op jit(solution)/shard_map/pallas_call | solution.py:333
  40.2 1.0 %shard_map.67 = bf16[32,1,4,32]{3,2,1,0:T(4,128)(2,1)} custom-call(f32[32,512]{1,0:T(8,128)S(1)} %get-tuple-element.59.one_ref, f32[32,512]{1,0:T(8,128)S(1)} %get-tuple-element.60.two_ref), custom_call_target="tpu_custom_call" | custom-call | tf_op jit(solution)/shard_map/pallas_call | solution.py:361
  41.1 1.4 %collective-permute-done.15 = bf16[432,128]{1,0:T(8,128)(2,1)S(1)} collective-permute-done((bf16[432,128]{1,0:T(8,128)(2,1)S(1)}, bf16[432,128]{1,0:T(8,128)(2,1)S(1)}, u32[]{:S(2)}, u32[]{:S(2)}) %collective-permute-start.15) | collective-permute-done | bytes 110624 | tf_op jit(solution)/shard_map/ppermute | solution.py:357
  42.7 0.9 %collective-permute-start.18 = (f32[432,128]{1,0:T(8,128)S(1)}, f32[432,128]{1,0:T(8,128)S(1)}, u32[]{:S(2)}, u32[]{:S(2)}) collective-permute-start(f32[432,128]{1,0:T(8,128)S(1)} %add_add_fusion.own_ref), channel_id=1, source_target_pairs={{0,4},{4,0},{8,12},{12,8},{16,20},{20,16},{24,28},{28,24},{1,5},{5... | collective-permute-start | bytes 663560 | tf_op jit(solution)/shard_map/ppermute | solution.py:371
  43.5 1.2 %shard_map.68 = bf16[32,4,16,128]{3,2,1,0:T(8,128)(2,1)} custom-call(bf16[864,128]{1,0:T(8,128)(2,1)S(1)} %get-tuple-element.35.refs_1_.refs_2_.w_ref, bf16[128,512]{1,0:T(8,128)(2,1)S(1)} %get-tuple-element.58.refs_1_.refs_0_, bf16[128,512]{1,0:T(8,128)(2,1)S(1)} %collective-permute-done.17.refs_1_, ...), custom_call_target="tpu_custom_call", output_to_operand_aliasing={{}: (3, {})} | custom-call | tf_op jit(solution)/shard_map/pallas_call | solution.py:333
  44.8 0.8 %shard_map.69 = f32[864,128]{1,0:T(8,128)} custom-call(f32[432,128]{1,0:T(8,128)S(1)} %add_add_fusion.own_ref, f32[432,128]{1,0:T(8,128)S(1)} %collective-permute-done.18.other_ref), custom_call_target="tpu_custom_call" | custom-call | tf_op jit(solution)/shard_map/pallas_call | solution.py:372
  (23 shorter events, 0.3 us)
Async XLA Ops:
  1.9 8.2 %collective-permute-start.6 = (bf16[32,1,16,128]{3,2,1,0:T(8,128)(2,1)S(1)}, bf16[32,1,16,128]{3,2,1,0:T(8,128)(2,1)S(1)}, u32[]{:S(2)}, u32[]{:S(2)}) collective-permute-start(bf16[32,1,16,128]{3,2,1,0:T(8,128)(2,1)S(1)} %get-tuple-element.43), channel_id=1, source_target_pairs={{0,4},{4,8},{8,12},{12,16},{16,20},{20,24},{24,28},{1,5},{5,9},{9,... | collective-permute-start | bytes 393224 | tf_op jit(solution)/shard_map/ppermute | solution.py:293
  5.1 10.3 %collective-permute-start = (f32[32,512]{1,0:T(8,128)S(1)}, f32[32,512]{1,0:T(8,128)S(1)}, u32[]{:S(2)}, u32[]{:S(2)}) collective-permute-start(f32[32,512]{1,0:T(8,128)S(1)} %get-tuple-element.38), channel_id=1, source_target_pairs={{0,1},{1,0},{2,3},{3,2},{4,5},{5,4},{6,7},{7,6},{8,9},{9,8},{10,11... | collective-permute-start | bytes 196616 | tf_op jit(solution)/shard_map/ppermute | solution.py:256
  7.6 8.0 %collective-permute-start.1 = (f32[32,512]{1,0:T(8,128)S(1)}, f32[32,512]{1,0:T(8,128)S(1)}, u32[]{:S(2)}, u32[]{:S(2)}) collective-permute-start(f32[32,512]{1,0:T(8,128)S(1)} %get-tuple-element.39), channel_id=1, source_target_pairs={{0,2},{1,3},{2,0},{3,1},{4,6},{5,7},{6,4},{7,5},{8,10},{9,11},{10,... | collective-permute-start | bytes 196616 | tf_op jit(solution)/shard_map/ppermute | solution.py:256
  10.2 5.3 %copy-start = (bf16[32,1,4,32]{3,2,1,0:T(4,128)(2,1)S(1)}, bf16[32,1,4,32]{3,2,1,0:T(4,128)(2,1)}, u32[]{:S(2)}) copy-start(bf16[32,1,4,32]{3,2,1,0:T(4,128)(2,1)} %param.5) | copy-start | bytes 24580
  10.2 6.7 %collective-permute-start.2 = (f32[32,512]{1,0:T(8,128)S(1)}, f32[32,512]{1,0:T(8,128)S(1)}, u32[]{:S(2)}, u32[]{:S(2)}) collective-permute-start(f32[32,512]{1,0:T(8,128)S(1)} %get-tuple-element.40), channel_id=1, source_target_pairs={{0,3},{1,2},{2,1},{3,0},{4,7},{5,6},{6,5},{7,4},{8,11},{9,10},{10,... | collective-permute-start | bytes 196616 | tf_op jit(solution)/shard_map/ppermute | solution.py:256
  11.0 9.1 %collective-permute-start.7 = (f32[32,512]{1,0:T(8,128)S(1)}, f32[32,512]{1,0:T(8,128)S(1)}, u32[]{:S(2)}, u32[]{:S(2)}) collective-permute-start(f32[32,512]{1,0:T(8,128)S(1)} %get-tuple-element.46), channel_id=1, source_target_pairs={{0,1},{1,0},{2,3},{3,2},{4,5},{5,4},{6,7},{7,6},{8,9},{9,8},{10,11... | collective-permute-start | bytes 196616 | tf_op jit(solution)/shard_map/ppermute | solution.py:256
  12.0 9.4 %collective-permute-start.8 = (f32[32,512]{1,0:T(8,128)S(1)}, f32[32,512]{1,0:T(8,128)S(1)}, u32[]{:S(2)}, u32[]{:S(2)}) collective-permute-start(f32[32,512]{1,0:T(8,128)S(1)} %get-tuple-element.47), channel_id=1, source_target_pairs={{0,2},{1,3},{2,0},{3,1},{4,6},{5,7},{6,4},{7,5},{8,10},{9,11},{10,... | collective-permute-start | bytes 196616 | tf_op jit(solution)/shard_map/ppermute | solution.py:256
  15.5 6.2 %collective-permute-start.9 = (f32[32,512]{1,0:T(8,128)S(1)}, f32[32,512]{1,0:T(8,128)S(1)}, u32[]{:S(2)}, u32[]{:S(2)}) collective-permute-start(f32[32,512]{1,0:T(8,128)S(1)} %get-tuple-element.48), channel_id=1, source_target_pairs={{0,3},{1,2},{2,1},{3,0},{4,7},{5,6},{6,5},{7,4},{8,11},{9,10},{10,... | collective-permute-start | bytes 196616 | tf_op jit(solution)/shard_map/ppermute | solution.py:256
  16.9 7.8 %collective-permute-start.3 = (bf16[32,512]{1,0:T(8,128)(2,1)S(1)}, bf16[32,512]{1,0:T(8,128)(2,1)S(1)}, u32[]{:S(2)}, u32[]{:S(2)}) collective-permute-start(bf16[32,512]{1,0:T(8,128)(2,1)S(1)} %get-tuple-element.41.refs_0_), channel_id=1, source_target_pairs={{0,1},{1,0},{2,3},{3,2},{4,5},{5,4},{6,7},{7,6},{8,9},{9,8},{10,11... | collective-permute-start | bytes 98312 | tf_op jit(solution)/shard_map/ppermute | solution.py:256
  18.1 8.4 %collective-permute-start.4 = (bf16[32,512]{1,0:T(8,128)(2,1)S(1)}, bf16[32,512]{1,0:T(8,128)(2,1)S(1)}, u32[]{:S(2)}, u32[]{:S(2)}) collective-permute-start(bf16[32,512]{1,0:T(8,128)(2,1)S(1)} %get-tuple-element.41.refs_0_), channel_id=1, source_target_pairs={{0,2},{1,3},{2,0},{3,1},{4,6},{5,7},{6,4},{7,5},{8,10},{9,11},{10,... | collective-permute-start | bytes 98312 | tf_op jit(solution)/shard_map/ppermute | solution.py:256
  20.1 6.3 %collective-permute-start.5 = (bf16[32,512]{1,0:T(8,128)(2,1)S(1)}, bf16[32,512]{1,0:T(8,128)(2,1)S(1)}, u32[]{:S(2)}, u32[]{:S(2)}) collective-permute-start(bf16[32,512]{1,0:T(8,128)(2,1)S(1)} %get-tuple-element.41.refs_0_), channel_id=1, source_target_pairs={{0,3},{1,2},{2,1},{3,0},{4,7},{5,6},{6,5},{7,4},{8,11},{9,10},{10,... | collective-permute-start | bytes 98312 | tf_op jit(solution)/shard_map/ppermute | solution.py:256
  21.7 5.1 %collective-permute-start.10 = (bf16[32,512]{1,0:T(8,128)(2,1)S(1)}, bf16[32,512]{1,0:T(8,128)(2,1)S(1)}, u32[]{:S(2)}, u32[]{:S(2)}) collective-permute-start(bf16[32,512]{1,0:T(8,128)(2,1)S(1)} %get-tuple-element.49.refs_0_), channel_id=1, source_target_pairs={{0,1},{1,0},{2,3},{3,2},{4,5},{5,4},{6,7},{7,6},{8,9},{9,8},{10,11... | collective-permute-start | bytes 98312 | tf_op jit(solution)/shard_map/ppermute | solution.py:256
  24.1 5.3 %collective-permute-start.11 = (bf16[32,512]{1,0:T(8,128)(2,1)S(1)}, bf16[32,512]{1,0:T(8,128)(2,1)S(1)}, u32[]{:S(2)}, u32[]{:S(2)}) collective-permute-start(bf16[32,512]{1,0:T(8,128)(2,1)S(1)} %get-tuple-element.49.refs_0_), channel_id=1, source_target_pairs={{0,2},{1,3},{2,0},{3,1},{4,6},{5,7},{6,4},{7,5},{8,10},{9,11},{10,... | collective-permute-start | bytes 98312 | tf_op jit(solution)/shard_map/ppermute | solution.py:256
  24.7 6.1 %collective-permute-start.12 = (bf16[32,512]{1,0:T(8,128)(2,1)S(1)}, bf16[32,512]{1,0:T(8,128)(2,1)S(1)}, u32[]{:S(2)}, u32[]{:S(2)}) collective-permute-start(bf16[32,512]{1,0:T(8,128)(2,1)S(1)} %get-tuple-element.49.refs_0_), channel_id=1, source_target_pairs={{0,3},{1,2},{2,1},{3,0},{4,7},{5,6},{6,5},{7,4},{8,11},{9,10},{10,... | collective-permute-start | bytes 98312 | tf_op jit(solution)/shard_map/ppermute | solution.py:256
  31.2 1.5 %collective-permute-start.13 = (f32[432,128]{1,0:T(8,128)S(1)}, f32[432,128]{1,0:T(8,128)S(1)}, u32[]{:S(2)}, u32[]{:S(2)}) collective-permute-start(f32[432,128]{1,0:T(8,128)S(1)} %get-tuple-element.51), channel_id=1, source_target_pairs={{0,4},{4,0},{8,12},{12,8},{16,20},{20,16},{24,28},{28,24},{1,5},{5... | collective-permute-start | bytes 663560 | tf_op jit(solution)/shard_map/ppermute | solution.py:347
  32.8 8.4 %collective-permute-start.14 = (bf16[432,128]{1,0:T(8,128)(2,1)S(1)}, bf16[432,128]{1,0:T(8,128)(2,1)S(1)}, u32[]{:S(2)}, u32[]{:S(2)}) collective-permute-start(bf16[432,128]{1,0:T(8,128)(2,1)S(1)} %add_convert_fusion), channel_id=1, source_target_pairs={{0,8},{4,12},{8,0},{12,4},{16,24},{20,28},{24,16},{28,20},{1,9},{5... | collective-permute-start | bytes 331784 | tf_op jit(solution)/shard_map/ppermute | solution.py:357
  35.4 7.2 %collective-permute-start.15 = (bf16[432,128]{1,0:T(8,128)(2,1)S(1)}, bf16[432,128]{1,0:T(8,128)(2,1)S(1)}, u32[]{:S(2)}, u32[]{:S(2)}) collective-permute-start(bf16[432,128]{1,0:T(8,128)(2,1)S(1)} %add_convert_fusion), channel_id=1, source_target_pairs={{0,16},{4,20},{8,24},{12,28},{16,0},{20,4},{24,8},{28,12},{1,17},{... | collective-permute-start | bytes 331784 | tf_op jit(solution)/shard_map/ppermute | solution.py:357
  35.6 7.0 %collective-permute-start.16 = (bf16[432,128]{1,0:T(8,128)(2,1)S(1)}, bf16[432,128]{1,0:T(8,128)(2,1)S(1)}, u32[]{:S(2)}, u32[]{:S(2)}) collective-permute-start(bf16[432,128]{1,0:T(8,128)(2,1)S(1)} %add_convert_fusion), channel_id=1, source_target_pairs={{0,24},{4,28},{8,16},{12,20},{16,8},{20,12},{24,0},{28,4},{1,25},{... | collective-permute-start | bytes 331784 | tf_op jit(solution)/shard_map/ppermute | solution.py:357
  36.9 5.7 %collective-permute-start.17 = (bf16[128,512]{1,0:T(8,128)(2,1)S(1)}, bf16[128,512]{1,0:T(8,128)(2,1)S(1)}, u32[]{:S(2)}, u32[]{:S(2)}) collective-permute-start(bf16[128,512]{1,0:T(8,128)(2,1)S(1)} %get-tuple-element.57.refs_0_), channel_id=1, source_target_pairs={{4,0},{8,4},{12,8},{16,12},{20,16},{24,20},{28,24},{5,1},{9,5},{13... | collective-permute-start | bytes 393224 | tf_op jit(solution)/shard_map/ppermute | solution.py:360
  42.7 2.1 %collective-permute-start.18 = (f32[432,128]{1,0:T(8,128)S(1)}, f32[432,128]{1,0:T(8,128)S(1)}, u32[]{:S(2)}, u32[]{:S(2)}) collective-permute-start(f32[432,128]{1,0:T(8,128)S(1)} %add_add_fusion.own_ref), channel_id=1, source_target_pairs={{0,4},{4,0},{8,12},{12,8},{16,20},{20,16},{24,28},{28,24},{1,5},{5... | collective-permute-start | bytes 663560 | tf_op jit(solution)/shard_map/ppermute | solution.py:371

commit v6 on v5

--- a/solution.py
+++ b/solution.py
@@ -32,21 +32,25 @@
     return jnp.where(hit, 1.0, 0.0).astype(jnp.bfloat16)
 
 
-def load_kernel(vol_hbm, w_hbm, vol_ref, w_ref, edge_ref, sems):
+def load_kernel(vol_hbm, vol_ref, edge_ref, sems):
     planes = vol_ref.shape[1]
-    copies = [pltpu.make_async_copy(vol_hbm.at[:, planes - 1 :], edge_ref, sems.at[planes + 1])]
-    for p in reversed(range(planes)):
-        copies.append(pltpu.make_async_copy(vol_hbm.at[:, p], vol_ref.at[:, p], sems.at[p]))
-    copies.append(pltpu.make_async_copy(w_hbm, w_ref, sems.at[planes]))
+    copies = [
+        pltpu.make_async_copy(vol_hbm.at[:, p], vol_ref.at[:, p], sems.at[p])
+        for p in reversed(range(planes))
+    ]
     for copy in copies:
         copy.start()
-    for copy in copies:
+    copies[0].wait()
+    edge_ref[...] = vol_ref[:, planes - 1 :]
+    for copy in copies[1:]:
         copy.wait()
 
 
 def fwd_kernel(n, ob, z, *refs):
     if z:
-        vol_ref, w_ref, cols_ref, *rest = refs
+        vol_ref, w_hbm, w_ref, cols_ref, *rest, sem = refs
+        w_copy = pltpu.make_async_copy(w_hbm, w_ref, sem)
+        w_copy.start()
     else:
         rim_ref, vol_ref, w_ref, cols_ref, *rest = refs
     part_refs = rest[:-2] if n > 1 else rest[:-1]
@@ -76,9 +80,14 @@
                 cols_ref[tap * cb : (tap + 1) * cb, :] = jnp.concatenate(
                     [block[j * cb : (j + 1) * cb] for j in range(groups)], axis=1
                 )
+    if z:
+        w_copy.wait()
+    if cols_ref.shape[0] > 27 * cb:
+        pad = (cols_ref.shape[0] - 27 * cb, cols_ref.shape[1])
+        cols_ref[27 * cb :, :] = jnp.zeros(pad, jnp.bfloat16)
     part = lax.dot_general(
         w_ref[...],
-        cols_ref[...],
+        cols_ref[0 : 27 * cb, :],
         (((0,), (0,)), ((), ())),
         preferred_element_type=jnp.float32,
     )
@@ -115,7 +124,7 @@
     act_ref[...] = jnp.where(pre > 0, pre, SLOPE * pre)
 
 
-def pool_kernel(one_ref, two_ref, out_ref):
+def pool_planes(one_ref, two_ref, out_ref):
     ob, _, groups, small = out_ref.shape
     wid = 4 * small
     r = lax.broadcasted_iota(jnp.int32, (wid, small), 0)
@@ -146,31 +155,41 @@
         grad_ref[pl.ds(start, ob), :] = ref[...]
 
 
-def weight_term(cols_ref, grad_ref):
+def weight_term(cols, grad_ref):
     return lax.dot_general(
-        cols_ref[...],
+        cols,
         grad_ref[...],
         (((1,), (1,)), ((), ())),
         preferred_element_type=jnp.float32,
     )
 
 
-def weight_kernel(n, cols_ref, *refs):
-    *block_refs, wgrad_ref, grad_ref = refs
+def middle_kernel(n, w_ref, act_one_ref, act_two_ref, cols_ref, *refs):
+    *block_refs, wgrad_ref, grad_ref, pooled_ref, out_ref, wide_ref, done_ref, sems = refs
     in_order(n, block_refs, grad_ref)
-    wgrad_ref[...] = weight_term(cols_ref, grad_ref)
-
-
-def last_weight_kernel(n, sum_ref, cols_ref, *refs):
-    *block_refs, keep_ref, send_ref, grad_ref, rows_ref = refs
+    copies = input_planes([(2, (grad_ref[...],))], w_ref, out_ref, wide_ref, done_ref, sems)
+    wgrad_ref[...] = weight_term(cols_ref[...], grad_ref)
+    pool_planes(act_one_ref, act_two_ref, pooled_ref)
+    for copy in copies:
+        copy.wait()
+
+
+def send_kernel(n, sum_ref, cols_ref, *refs):
+    *block_refs, send_ref, grad_ref = refs
     in_order(n, block_refs, grad_ref)
-    taps, half = cols_ref.shape[0], keep_ref.shape[0]
-    rows_ref[0:taps, :] = sum_ref[...] + weight_term(cols_ref, grad_ref)
-    if 2 * half > taps:
-        rows_ref[taps:, :] = jnp.zeros((2 * half - taps, rows_ref.shape[1]), jnp.float32)
-    core = lax.rem(lax.axis_index("space"), 2)
-    keep_ref[...] = rows_ref[pl.ds(pl.multiple_of(core * half, 8), half), :]
-    send_ref[...] = rows_ref[pl.ds(pl.multiple_of((1 - core) * half, 8), half), :]
+    half = send_ref.shape[0]
+    start = pl.multiple_of((1 - lax.rem(lax.axis_index("space"), 2)) * half, 16)
+    send_ref[...] = sum_ref[pl.ds(start, half), :] + weight_term(
+        cols_ref[pl.ds(start, half), :], grad_ref
+    )
+
+
+def keep_kernel(sum_ref, cols_ref, grad_ref, keep_ref):
+    half = keep_ref.shape[0]
+    start = pl.multiple_of(lax.rem(lax.axis_index("space"), 2) * half, 16)
+    keep_ref[...] = sum_ref[pl.ds(start, half), :] + weight_term(
+        cols_ref[pl.ds(start, half), :], grad_ref
+    )
 
 
 def join_kernel(own_ref, other_ref, out_ref, sems):
@@ -193,11 +212,8 @@
                 copy.wait()
 
 
-def input_kernel(own, w_ref, *refs):
-    *grad_refs, out_ref, wide_ref, done_ref, sems = refs
-    if not own:
-        *grad_refs, _ = grad_refs
-    cb, planes, hgt, wid = out_ref.shape
+def input_planes(todo, w_ref, out_ref, wide_ref, done_ref, sems):
+    cb, _, hgt, wid = out_ref.shape
     half = wid // 2
     groups = hgt // 4
     lanes = groups * wid
@@ -207,17 +223,13 @@
     keep = lax.broadcasted_iota(jnp.int32, (3 * cb, lanes), 1) < lanes - half
     w = [w_ref[a * taps : (a + 1) * taps, :] for a in range(3)]
     behind = jnp.concatenate([w[2], w[0]], axis=1)
-    g = [ref[...] for ref in grad_refs]
     copies = []
-    for i in range(planes - 1) if own else (planes - 1,):
-        z = i // 2 if own else 0
+    for slot, (i, grads) in enumerate(todo):
         if i % 2 == 0:
-            e_all = jnp.dot(w[1], g[z], preferred_element_type=jnp.float32)
+            e_all = jnp.dot(w[1], grads[0], preferred_element_type=jnp.float32)
         else:
             e_all = jnp.dot(
-                behind,
-                jnp.concatenate([g[z], g[z + 1]], axis=0),
-                preferred_element_type=jnp.float32,
+                behind, jnp.concatenate(grads, axis=0), preferred_element_type=jnp.float32
             )
         by_b = [e_all[b * 3 * cb : (b + 1) * 3 * cb] for b in range(3)]
         shifted = pltpu.roll(by_b[0], lanes - half, 1)
@@ -243,11 +255,19 @@
                     wide_ref[pl.ds(y, cb, stride=hgt), :] = full[
                         at : at + cb, h * wid : (h + 1) * wid
                     ]
-        slot = i if own else 0
         done_ref[slot] = wide_ref[...].reshape(cb, hgt, wid).astype(jnp.bfloat16)
         copies.append(pltpu.make_async_copy(done_ref.at[slot], out_ref.at[:, i], sems.at[slot]))
         copies[-1].start()
-    for copy in copies:
+    return copies
+
+
+def input_kernel(last, w_ref, one_ref, two_ref, _, out_ref, *scratch):
+    one, two = one_ref[...], two_ref[...]
+    if last:
+        todo = [(out_ref.shape[1] - 1, (one, two))]
+    else:
+        todo = [(0, (one,)), (1, (one, two))]
+    for copy in input_planes(todo, w_ref, out_ref, *scratch):
         copy.wait()
 
 
@@ -279,25 +299,39 @@
     part_shapes = [shape((ob if direct else out_ch, cells), f32)] * n
     out_planes = range(planes // 2)
     cols, grads, acts = {}, {}, {}
-    vol, w, edge = pl.pallas_call(
+    vmem = pl.BlockSpec(memory_space=pltpu.VMEM)
+    hbm = pl.BlockSpec(memory_space=pltpu.HBM)
+
+    def from_hbm(x):
+        return pltpu.with_memory_space_constraint(x, pltpu.HBM)
+
+    half = -(-taps // 32) * 16
+    cols_shape = shape((2 * half, cells), bf16)
+    vol, edge = pl.pallas_call(
         load_kernel,
-        in_specs=[pl.BlockSpec(memory_space=pltpu.HBM)] * 2,
-        out_shape=[
-            shape(volume.shape, bf16),
-            shape(weights.shape, bf16),
-            shape((cb, 1, hgt, wid), bf16),
-        ],
-        scratch_shapes=[pltpu.SemaphoreType.DMA((planes + 2,))],
+        in_specs=[hbm],
+        out_shape=[shape(volume.shape, bf16), shape((cb, 1, hgt, wid), bf16)],
+        scratch_shapes=[pltpu.SemaphoreType.DMA((planes,))],
         compiler_params=params(),
-    )(*[pltpu.with_memory_space_constraint(x, pltpu.HBM) for x in (volume, weights)])
+    )(from_hbm(volume))
     rim = lax.ppermute(edge, "space", [(i, i + 1) for i in range(n_space - 1)])
     for z in reversed(out_planes):
-        cols[z], *parts = pl.pallas_call(
-            functools.partial(fwd_kernel, n, ob, z),
-            out_shape=[shape((taps, cells), bf16)] + part_shapes,
-            scratch_shapes=scratch,
-            compiler_params=params(),
-        )(*(() if z else (rim,)), vol, w)
+        call = functools.partial(fwd_kernel, n, ob, z)
+        if z:
+            w, cols[z], *parts = pl.pallas_call(
+                call,
+                in_specs=[vmem, hbm],
+                out_shape=[shape(weights.shape, bf16), cols_shape] + part_shapes,
+                scratch_shapes=scratch + [pltpu.SemaphoreType.DMA],
+                compiler_params=params(),
+            )(vol, from_hbm(weights))
+        else:
+            cols[z], *parts = pl.pallas_call(
+                call,
+                out_shape=[cols_shape] + part_shapes,
+                scratch_shapes=scratch,
+                compiler_params=params(),
+            )(rim, vol, w)
         if direct:
             parts = parts[:1] + [moved(p, "chan", k) for k, p in zip(RS, parts[1:])]
         else:
@@ -312,62 +346,69 @@
         else:
             grads[z] = [lax.all_gather(own, "chan", axis=0, tiled=True)]
 
-    half = -(-taps // 32) * 16
+    def input_scratch(count):
+        return [
+            pltpu.VMEM((cb * hgt, wid), f32),
+            pltpu.VMEM((count, cb, hgt, wid), bf16),
+            pltpu.SemaphoreType.DMA((count,)),
+        ]
+
+    def input_call(last, *operands):
+        return pl.pallas_call(
+            functools.partial(input_kernel, last),
+            in_specs=[vmem] * 3 + [hbm],
+            out_specs=hbm,
+            out_shape=shape(volume.shape, bf16),
+            scratch_shapes=input_scratch(1 if last else 2),
+            input_output_aliases={3: 0},
+            compiler_params=params(),
+        )(*operands)
+
     grad_shape = shape((out_ch, cells), bf16)
-    term, grads[1] = pl.pallas_call(
-        functools.partial(weight_kernel, n),
-        out_shape=[shape((taps, out_ch), f32), grad_shape],
+    term, grads[1], pooled, input_grad = pl.pallas_call(
+        functools.partial(middle_kernel, n),
+        out_specs=[vmem, vmem, vmem, hbm],
+        out_shape=[
+            shape((2 * half, out_ch), f32),
+            grad_shape,
+            shape(upstream.shape, bf16),
+            shape(volume.shape, bf16),
+        ],
+        scratch_shapes=input_scratch(1),
         compiler_params=params(),
-    )(cols[1], *grads[1])
-    keep, send, grads[0] = pl.pallas_call(
-        functools.partial(last_weight_kernel, n),
-        out_shape=[shape((half, out_ch), f32)] * 2 + [grad_shape],
-        scratch_shapes=[pltpu.VMEM((2 * half, out_ch), f32)],
+    )(w, acts[0], acts[1], cols[1], *grads[1])
+    send, grads[0] = pl.pallas_call(
+        functools.partial(send_kernel, n),
+        out_shape=[shape((half, out_ch), f32), grad_shape],
         compiler_params=params(),
     )(term, cols[0], *grads[0])
-
-    def input_call(own, *operands):
-        n_done = planes - 1 if own else 1
-        hbm = pl.BlockSpec(memory_space=pltpu.HBM)
-        vmem = pl.BlockSpec(memory_space=pltpu.VMEM)
-        return pl.pallas_call(
-            functools.partial(input_kernel, own),
-            in_specs=[vmem] * 3 + [hbm] * (not own),
-            out_specs=hbm,
-            out_shape=shape(volume.shape, bf16),
-            scratch_shapes=[
-                pltpu.VMEM((cb * hgt, wid), f32),
-                pltpu.VMEM((n_done, cb, hgt, wid), bf16),
-                pltpu.SemaphoreType.DMA((n_done,)),
-            ],
-            input_output_aliases={} if own else {3: 0},
-            compiler_params=params(),
-        )(*operands)
+    keep = pl.pallas_call(
+        keep_kernel,
+        out_shape=shape((half, out_ch), f32),
+        compiler_params=params(),
+    )(term, cols[0], grads[0])
 
     rows = keep + lax.ppermute(send, "space", [(i, i ^ 1) for i in range(n_space)])
     bits = [1 << b for b in range(1, n_space.bit_length() - 1)]
     groups = [bits[i : i + 2] for i in range(0, len(bits), 2)]
-    after = input_grad = pooled = None
+    after = None
     for r, group in enumerate(groups):
         sent = rows.astype(bf16)
         if r == len(groups) - 1:
-            sent, grads, acts = lax.optimization_barrier((sent, grads, acts))
+            sent, grads, input_grad = lax.optimization_barrier((sent, grads, input_grad))
         partners = [sum(group[b] * (k >> b & 1) for b in range(len(group))) for k in range(1, 1 << len(group))]
         terms = [sent] + [
             lax.ppermute(sent, "space", [(i, i ^ p) for i in range(n_space)]) for p in partners
         ]
         if r == len(groups) - 1:
             after = lax.ppermute(grads[0], "space", [(i + 1, i) for i in range(n_space - 1)])
-            pooled = pl.pallas_call(
-                pool_kernel, out_shape=shape(upstream.shape, bf16), compiler_params=params()
-            )(acts[0], acts[1])
-            input_grad = input_call(True, w, grads[0], grads[1])
+            input_grad = input_call(False, w, grads[0], grads[1], input_grad)
         terms = [t.astype(f32) for t in terms]
         while len(terms) > 1:
             terms = [a + b for a, b in zip(terms[::2], terms[1::2])]
         rows = terms[0]
-    rows, input_grad, pooled, after = lax.optimization_barrier((rows, input_grad, pooled, after))
-    input_grad = input_call(False, w, grads[1], after, input_grad)
+    rows, input_grad, after = lax.optimization_barrier((rows, input_grad, after))
+    input_grad = input_call(True, w, grads[1], after, input_grad)
     other = lax.ppermute(rows, "space", [(i, i ^ 1) for i in range(n_space)])
     weight_grad = pl.pallas_call(
         join_kernel,

time: 45.8 us -> 44.7 us (0.976)
  waiting for transfers between devices: 8.34 us -> 7.15 us
  Pallas kernels: 8.89 us -> 9.56 us
  starting transfers between devices: 27.5 us -> 26.9 us
    ppermute x12, waiting for transfers between devices: 5.47 us -> 3.57 us  [moved(): lax.ppermute(block, axis, [(i, i ^ k if XOR else (i + k) % n) for i in ra...]
    ppermute x3, waiting for transfers between devices: 1.46 us -> 2.39 us  [on_device(): lax.ppermute(sent, 'space', [(i, i ^ p) for i in range(n_space)])]
    pallas_call x8, Pallas kernels: 7.92 us -> 8.59 us  [the longest x2 2.89 us: input_call(): pl.pallas_call(functools.partial(input_kernel, last), in_specs=[vmem] * 3...]
    ppermute x3, starting transfers between devices: 4.15 us -> 3.55 us  [on_device(): lax.ppermute(sent, 'space', [(i, i ^ p) for i in range(n_space)])]
  transfers between devices with their start and end apart: 19 -> 19, of which waited for: 6 -> 7; matrix products, arithmetic and copies ran while one was open for 0% -> 0% of each run, Pallas kernels for 14% -> 17%
where the time goes in v6:
time: 44.7 us; the launch traced here: 44.5 us
  starting transfers between devices  26.9 us (60%)
  Pallas kernels  9.56 us (21%)
  waiting for transfers between devices  7.15 us (16%)
  between operations  0.79 us (2%)
    ppermute x12, starting transfers between devices, moved(): lax.ppermute(block, axis, [(i, i ^ k if XOR else (i + k) % n) for i in ra...  18.4 us
    ppermute x12, waiting for transfers between devices, moved(): lax.ppermute(block, axis, [(i, i ^ k if XOR else (i + k) % n) for i in ra...  3.57 us
    ppermute x3, starting transfers between devices, on_device(): lax.ppermute(sent, 'space', [(i, i ^ p) for i in range(n_space)])  3.55 us
    pallas_call x2, Pallas kernels, input_call(): pl.pallas_call(functools.partial(input_kernel, last), in_specs=[vmem] * 3...  2.89 us
    ppermute x3, waiting for transfers between devices, on_device(): lax.ppermute(sent, 'space', [(i, i ^ p) for i in range(n_space)])  2.39 us
    ppermute x1, starting transfers between devices, on_device(): rim = lax.ppermute(edge, 'space', [(i, i + 1) for i in range(n_space - 1)])  2.36 us
    pallas_call x1, Pallas kernels, on_device(): pl.pallas_call(functools.partial(middle_kernel, n), out_specs=[vmem, vmem...  1.89 us
    pallas_call x1, Pallas kernels, on_device(): pl.pallas_call(call, in_specs=[vmem, hbm], out_shape=[shape(weights.shape...  1.3 us
  transfers between devices with their start and end apart: 19, of which 7 were waited for; matrix products, arithmetic and copies ran while one was open for 0% of the time, Pallas kernels for 17%

profile of v6, /device:TPU:0, one launch (start us, length us, event | category | flops | bytes accessed | tf_op | source)
XLA Modules:
  0.0 44.5 jit_solution(9410743570591512656)
XLA Ops:
  0.6 1.1 %shard_map.58 = (bf16[32,4,16,128]{3,2,1,0:T(8,128)(2,1)S(1)}, bf16[32,1,16,128]{3,2,1,0:T(8,128)(2,1)S(1)}) custom-call(bf16[32,4,16,128]{3,2,1,0:T(8,128)(2,1)} %vol_hbm.1), custom_call_target="tpu_custom_call" | custom-call | tf_op jit(solution)/shard_map/pallas_call | solution.py:310
  1.8 2.4 %collective-permute-start = (bf16[32,1,16,128]{3,2,1,0:T(8,128)(2,1)S(1)}, bf16[32,1,16,128]{3,2,1,0:T(8,128)(2,1)S(1)}, u32[]{:S(2)}, u32[]{:S(2)}) collective-permute-start(bf16[32,1,16,128]{3,2,1,0:T(8,128)(2,1)S(1)} %get-tuple-element.35), channel_id=1, source_target_pairs={{0,4},{4,8},{8,12},{12,16},{16,20},{20,24},{24,28},{1,5},{5,9},{9,... | collective-permute-start | bytes 393224 | tf_op jit(solution)/shard_map/ppermute | solution.py:317
  4.1 1.3 %shard_map.59 = (bf16[864,128]{1,0:T(8,128)(2,1)S(1)}, bf16[864,512]{1,0:T(8,128)(2,1)S(1)}, f32[32,512]{1,0:T(8,128)S(1)}, f32[32,512]{1,0:T(8,128)S(1)}, f32[32,512]{1,0:T(8,128)S(1)}, /*index=5*/f32[32,512]{1,0:T(8,128)S(1)}) custom-call(bf16[32,4,16,128]{3,2,1,0:T(8,128)(2,1)S(1)} %get-tuple-element.33.refs_0_.refs_1_, bf16[864,128]{1,0:T(8,128)(2,1)} %bitcast.13), custom_call_target="tpu_custom_call" | custom-call | tf_op jit(solution)/shard_map/pallas_call | solution.py:321
  5.5 2.5 %collective-permute-start.4 = (f32[32,512]{1,0:T(8,128)S(1)}, f32[32,512]{1,0:T(8,128)S(1)}, u32[]{:S(2)}, u32[]{:S(2)}) collective-permute-start(f32[32,512]{1,0:T(8,128)S(1)} %get-tuple-element.42), channel_id=1, source_target_pairs={{0,1},{1,0},{2,3},{3,2},{4,5},{5,4},{6,7},{7,6},{8,9},{9,8},{10,11... | collective-permute-start | bytes 196616 | tf_op jit(solution)/shard_map/ppermute | solution.py:276
  7.9 2.6 %collective-permute-start.5 = (f32[32,512]{1,0:T(8,128)S(1)}, f32[32,512]{1,0:T(8,128)S(1)}, u32[]{:S(2)}, u32[]{:S(2)}) collective-permute-start(f32[32,512]{1,0:T(8,128)S(1)} %get-tuple-element.43), channel_id=1, source_target_pairs={{0,2},{1,3},{2,0},{3,1},{4,6},{5,7},{6,4},{7,5},{8,10},{9,11},{10,... | collective-permute-start | bytes 196616 | tf_op jit(solution)/shard_map/ppermute | solution.py:276
  10.5 0.8 %shard_map.61 = (bf16[864,512]{1,0:T(8,128)(2,1)S(1)}, f32[32,512]{1,0:T(8,128)S(1)}, f32[32,512]{1,0:T(8,128)S(1)}, f32[32,512]{1,0:T(8,128)S(1)}, f32[32,512]{1,0:T(8,128)S(1)}) custom-call(bf16[32,1,16,128]{3,2,1,0:T(8,128)(2,1)S(1)} %collective-permute-done.refs_0_, bf16[32,4,16,128]{3,2,1,0:T(8,128)(2,1)S(1)} %get-tuple-element.33.refs_0_.refs_1_, ...), custom_call_target="tpu_custom_call" | custom-call | tf_op jit(solution)/shard_map/pallas_call | solution.py:329
  11.4 0.9 %collective-permute-start.1 = (f32[32,512]{1,0:T(8,128)S(1)}, f32[32,512]{1,0:T(8,128)S(1)}, u32[]{:S(2)}, u32[]{:S(2)}) collective-permute-start(f32[32,512]{1,0:T(8,128)S(1)} %get-tuple-element.37), channel_id=1, source_target_pairs={{0,1},{1,0},{2,3},{3,2},{4,5},{5,4},{6,7},{7,6},{8,9},{9,8},{10,11... | collective-permute-start | bytes 196616 | tf_op jit(solution)/shard_map/ppermute | solution.py:276
  12.3 3.5 %collective-permute-start.2 = (f32[32,512]{1,0:T(8,128)S(1)}, f32[32,512]{1,0:T(8,128)S(1)}, u32[]{:S(2)}, u32[]{:S(2)}) collective-permute-start(f32[32,512]{1,0:T(8,128)S(1)} %get-tuple-element.38), channel_id=1, source_target_pairs={{0,2},{1,3},{2,0},{3,1},{4,6},{5,7},{6,4},{7,5},{8,10},{9,11},{10,... | collective-permute-start | bytes 196616 | tf_op jit(solution)/shard_map/ppermute | solution.py:276
  15.8 0.1 shard_map.60.spread_ref
  16.0 1.2 %collective-permute-done.6.rest_3_ = f32[32,512]{1,0:T(8,128)S(1)} collective-permute-done((f32[32,512]{1,0:T(8,128)S(1)}, f32[32,512]{1,0:T(8,128)S(1)}, u32[]{:S(2)}, u32[]{:S(2)}) %collective-permute-start.6) | collective-permute-done | bytes 65568 | tf_op jit(solution)/shard_map/ppermute | solution.py:276
  17.2 2.7 %collective-permute-start.9 = (bf16[32,512]{1,0:T(8,128)(2,1)S(1)}, bf16[32,512]{1,0:T(8,128)(2,1)S(1)}, u32[]{:S(2)}, u32[]{:S(2)}) collective-permute-start(bf16[32,512]{1,0:T(8,128)(2,1)S(1)} %get-tuple-element.47.refs_0_), channel_id=1, source_target_pairs={{0,3},{1,2},{2,1},{3,0},{4,7},{5,6},{6,5},{7,4},{8,11},{9,10},{10,... | collective-permute-start | bytes 98312 | tf_op jit(solution)/shard_map/ppermute | solution.py:276
  19.9 1.8 %collective-permute-start.7 = (bf16[32,512]{1,0:T(8,128)(2,1)S(1)}, bf16[32,512]{1,0:T(8,128)(2,1)S(1)}, u32[]{:S(2)}, u32[]{:S(2)}) collective-permute-start(bf16[32,512]{1,0:T(8,128)(2,1)S(1)} %get-tuple-element.47.refs_0_), channel_id=1, source_target_pairs={{0,1},{1,0},{2,3},{3,2},{4,5},{5,4},{6,7},{7,6},{8,9},{9,8},{10,11... | collective-permute-start | bytes 98312 | tf_op jit(solution)/shard_map/ppermute | solution.py:276
  21.7 0.4 collective-permute-done.3.rest_3_
  22.1 2.3 %collective-permute-start.12 = (bf16[32,512]{1,0:T(8,128)(2,1)S(1)}, bf16[32,512]{1,0:T(8,128)(2,1)S(1)}, u32[]{:S(2)}, u32[]{:S(2)}) collective-permute-start(bf16[32,512]{1,0:T(8,128)(2,1)S(1)} %get-tuple-element.51.refs_0_), channel_id=1, source_target_pairs={{0,3},{1,2},{2,1},{3,0},{4,7},{5,6},{6,5},{7,4},{8,11},{9,10},{10,... | collective-permute-start | bytes 98312 | tf_op jit(solution)/shard_map/ppermute | solution.py:276
  24.4 2.1 %collective-permute-start.11 = (bf16[32,512]{1,0:T(8,128)(2,1)S(1)}, bf16[32,512]{1,0:T(8,128)(2,1)S(1)}, u32[]{:S(2)}, u32[]{:S(2)}) collective-permute-start(bf16[32,512]{1,0:T(8,128)(2,1)S(1)} %get-tuple-element.51.refs_0_), channel_id=1, source_target_pairs={{0,2},{1,3},{2,0},{3,1},{4,6},{5,7},{6,4},{7,5},{8,10},{9,11},{10,... | collective-permute-start | bytes 98312 | tf_op jit(solution)/shard_map/ppermute | solution.py:276
  26.5 0.1 collective-permute-start.10
  26.6 1.9 %shard_map.64 = (f32[864,128]{1,0:T(8,128)S(1)}, bf16[128,512]{1,0:T(8,128)(2,1)S(1)}, bf16[32,1,4,32]{3,2,1,0:T(4,128)(2,1)}, bf16[32,4,16,128]{3,2,1,0:T(8,128)(2,1)}) custom-call(bf16[864,128]{1,0:T(8,128)(2,1)S(1)} %get-tuple-element.34.refs_2_.w_ref, f32[32,512]{1,0:T(8,128)S(1)} %get-tuple-element.40.act_one_ref, ...), custom_call_target="tpu_custom_call" | custom-call | tf_op jit(solution)/shard_map/pallas_call | solution.py:368
  28.5 0.8 %collective-permute-done.11.refs_2_ = bf16[32,512]{1,0:T(8,128)(2,1)S(1)} collective-permute-done((bf16[32,512]{1,0:T(8,128)(2,1)S(1)}, bf16[32,512]{1,0:T(8,128)(2,1)S(1)}, u32[]{:S(2)}, u32[]{:S(2)}) %collective-permute-start.11) | collective-permute-done | bytes 32800 | tf_op jit(solution)/shard_map/ppermute | solution.py:276
  29.3 1.1 %collective-permute-done.10.refs_1_ = bf16[32,512]{1,0:T(8,128)(2,1)S(1)} collective-permute-done((bf16[32,512]{1,0:T(8,128)(2,1)S(1)}, bf16[32,512]{1,0:T(8,128)(2,1)S(1)}, u32[]{:S(2)}, u32[]{:S(2)}) %collective-permute-start.10) | collective-permute-done | bytes 32800 | tf_op jit(solution)/shard_map/ppermute | solution.py:276
  30.4 0.3 shard_map.65
  30.8 0.3 shard_map.66
  31.1 1.2 %collective-permute-done.13 = f32[432,128]{1,0:T(8,128)S(1)} collective-permute-done((f32[432,128]{1,0:T(8,128)S(1)}, f32[432,128]{1,0:T(8,128)S(1)}, u32[]{:S(2)}, u32[]{:S(2)}) %collective-permute-start.13) | collective-permute-done | bytes 221216 | tf_op jit(solution)/shard_map/ppermute | solution.py:391
  32.3 2.0 %collective-permute-start.16 = (bf16[432,128]{1,0:T(8,128)(2,1)S(1)}, bf16[432,128]{1,0:T(8,128)(2,1)S(1)}, u32[]{:S(2)}, u32[]{:S(2)}) collective-permute-start(bf16[432,128]{1,0:T(8,128)(2,1)S(1)} %add_convert_fusion), channel_id=1, source_target_pairs={{0,24},{4,28},{8,16},{12,20},{16,8},{20,12},{24,0},{28,4},{1,25},{... | collective-permute-start | bytes 331784 | tf_op jit(solution)/shard_map/ppermute | solution.py:401
  34.3 1.5 %collective-permute-start.15 = (bf16[432,128]{1,0:T(8,128)(2,1)S(1)}, bf16[432,128]{1,0:T(8,128)(2,1)S(1)}, u32[]{:S(2)}, u32[]{:S(2)}) collective-permute-start(bf16[432,128]{1,0:T(8,128)(2,1)S(1)} %add_convert_fusion), channel_id=1, source_target_pairs={{0,16},{4,20},{8,24},{12,28},{16,0},{20,4},{24,8},{28,12},{1,17},{... | collective-permute-start | bytes 331784 | tf_op jit(solution)/shard_map/ppermute | solution.py:401
  35.7 0.1 collective-permute-start.14
  35.8 1.3 %collective-permute-start.17 = (bf16[128,512]{1,0:T(8,128)(2,1)S(1)}, bf16[128,512]{1,0:T(8,128)(2,1)S(1)}, u32[]{:S(2)}, u32[]{:S(2)}) collective-permute-start(bf16[128,512]{1,0:T(8,128)(2,1)S(1)} %get-tuple-element.58.grad_ref.one_ref), channel_id=1, source_target_pairs={{4,0},{8,4},{12,8},{16,12},{20,16},{24,20},{28,24},{5,1},{9,5},{13... | collective-permute-start | bytes 393224 | tf_op jit(solution)/shard_map/ppermute | solution.py:404
  37.1 1.6 %shard_map.67._ = bf16[32,4,16,128]{3,2,1,0:T(8,128)(2,1)} custom-call(bf16[864,128]{1,0:T(8,128)(2,1)S(1)} %get-tuple-element.34.refs_2_.w_ref, bf16[128,512]{1,0:T(8,128)(2,1)S(1)} %get-tuple-element.58.grad_ref.one_ref, bf16[128,512]{1,0:T(8,128)(2,1)S(1)} %get-tuple-element.56.two_ref.one_ref, ...), custom_call_target="tpu_custom_call", output_to_operand_aliasing={{}: (3, {})} | custom-call | tf_op jit(solution)/shard_map/pallas_call | solution.py:357
  38.8 1.9 %collective-permute-done.15 = bf16[432,128]{1,0:T(8,128)(2,1)S(1)} collective-permute-done((bf16[432,128]{1,0:T(8,128)(2,1)S(1)}, bf16[432,128]{1,0:T(8,128)(2,1)S(1)}, u32[]{:S(2)}, u32[]{:S(2)}) %collective-permute-start.15) | collective-permute-done | bytes 110624 | tf_op jit(solution)/shard_map/ppermute | solution.py:401
  40.7 0.5 %collective-permute-done.14 = bf16[432,128]{1,0:T(8,128)(2,1)S(1)} collective-permute-done((bf16[432,128]{1,0:T(8,128)(2,1)S(1)}, bf16[432,128]{1,0:T(8,128)(2,1)S(1)}, u32[]{:S(2)}, u32[]{:S(2)}) %collective-permute-start.14) | collective-permute-done | bytes 110624 | tf_op jit(solution)/shard_map/ppermute | solution.py:401
  41.2 1.2 %collective-permute-start.18 = (f32[432,128]{1,0:T(8,128)S(1)}, f32[432,128]{1,0:T(8,128)S(1)}, u32[]{:S(2)}, u32[]{:S(2)}) collective-permute-start(f32[432,128]{1,0:T(8,128)S(1)} %add_add_fusion.own_ref), channel_id=1, source_target_pairs={{0,4},{4,0},{8,12},{12,8},{16,20},{20,16},{24,28},{28,24},{1,5},{5... | collective-permute-start | bytes 663560 | tf_op jit(solution)/shard_map/ppermute | solution.py:412
  42.4 1.2 %shard_map.68 = bf16[32,4,16,128]{3,2,1,0:T(8,128)(2,1)} custom-call(bf16[864,128]{1,0:T(8,128)(2,1)S(1)} %get-tuple-element.34.refs_2_.w_ref, bf16[128,512]{1,0:T(8,128)(2,1)S(1)} %get-tuple-element.56.two_ref.one_ref, bf16[128,512]{1,0:T(8,128)(2,1)S(1)} %collective-permute-done.17.two_ref, ...), custom_call_target="tpu_custom_call", output_to_operand_aliasing={{}: (3, {})} | custom-call | tf_op jit(solution)/shard_map/pallas_call | solution.py:357
  43.7 0.8 %shard_map.69 = f32[864,128]{1,0:T(8,128)} custom-call(f32[432,128]{1,0:T(8,128)S(1)} %add_add_fusion.own_ref, f32[432,128]{1,0:T(8,128)S(1)} %collective-permute-done.18.other_ref), custom_call_target="tpu_custom_call" | custom-call | tf_op jit(solution)/shard_map/pallas_call | solution.py:413
  (23 shorter events, 0.3 us)
Async XLA Ops:
  1.8 8.8 %collective-permute-start = (bf16[32,1,16,128]{3,2,1,0:T(8,128)(2,1)S(1)}, bf16[32,1,16,128]{3,2,1,0:T(8,128)(2,1)S(1)}, u32[]{:S(2)}, u32[]{:S(2)}) collective-permute-start(bf16[32,1,16,128]{3,2,1,0:T(8,128)(2,1)S(1)} %get-tuple-element.35), channel_id=1, source_target_pairs={{0,4},{4,8},{8,12},{12,16},{16,20},{20,24},{24,28},{1,5},{5,9},{9,... | collective-permute-start | bytes 393224 | tf_op jit(solution)/shard_map/ppermute | solution.py:317
  5.5 10.4 %collective-permute-start.4 = (f32[32,512]{1,0:T(8,128)S(1)}, f32[32,512]{1,0:T(8,128)S(1)}, u32[]{:S(2)}, u32[]{:S(2)}) collective-permute-start(f32[32,512]{1,0:T(8,128)S(1)} %get-tuple-element.42), channel_id=1, source_target_pairs={{0,1},{1,0},{2,3},{3,2},{4,5},{5,4},{6,7},{7,6},{8,9},{9,8},{10,11... | collective-permute-start | bytes 196616 | tf_op jit(solution)/shard_map/ppermute | solution.py:276
  7.9 8.0 %collective-permute-start.5 = (f32[32,512]{1,0:T(8,128)S(1)}, f32[32,512]{1,0:T(8,128)S(1)}, u32[]{:S(2)}, u32[]{:S(2)}) collective-permute-start(f32[32,512]{1,0:T(8,128)S(1)} %get-tuple-element.43), channel_id=1, source_target_pairs={{0,2},{1,3},{2,0},{3,1},{4,6},{5,7},{6,4},{7,5},{8,10},{9,11},{10,... | collective-permute-start | bytes 196616 | tf_op jit(solution)/shard_map/ppermute | solution.py:276
  10.5 6.7 %collective-permute-start.6 = (f32[32,512]{1,0:T(8,128)S(1)}, f32[32,512]{1,0:T(8,128)S(1)}, u32[]{:S(2)}, u32[]{:S(2)}) collective-permute-start(f32[32,512]{1,0:T(8,128)S(1)} %get-tuple-element.44), channel_id=1, source_target_pairs={{0,3},{1,2},{2,1},{3,0},{4,7},{5,6},{6,5},{7,4},{8,11},{9,10},{10,... | collective-permute-start | bytes 196616 | tf_op jit(solution)/shard_map/ppermute | solution.py:276
  10.5 5.3 %copy-start = (bf16[32,1,4,32]{3,2,1,0:T(4,128)(2,1)S(1)}, bf16[32,1,4,32]{3,2,1,0:T(4,128)(2,1)}, u32[]{:S(2)}) copy-start(bf16[32,1,4,32]{3,2,1,0:T(4,128)(2,1)} %param.5) | copy-start | bytes 24580
  11.4 8.6 %collective-permute-start.1 = (f32[32,512]{1,0:T(8,128)S(1)}, f32[32,512]{1,0:T(8,128)S(1)}, u32[]{:S(2)}, u32[]{:S(2)}) collective-permute-start(f32[32,512]{1,0:T(8,128)S(1)} %get-tuple-element.37), channel_id=1, source_target_pairs={{0,1},{1,0},{2,3},{3,2},{4,5},{5,4},{6,7},{7,6},{8,9},{9,8},{10,11... | collective-permute-start | bytes 196616 | tf_op jit(solution)/shard_map/ppermute | solution.py:276
  12.3 9.4 %collective-permute-start.2 = (f32[32,512]{1,0:T(8,128)S(1)}, f32[32,512]{1,0:T(8,128)S(1)}, u32[]{:S(2)}, u32[]{:S(2)}) collective-permute-start(f32[32,512]{1,0:T(8,128)S(1)} %get-tuple-element.38), channel_id=1, source_target_pairs={{0,2},{1,3},{2,0},{3,1},{4,6},{5,7},{6,4},{7,5},{8,10},{9,11},{10,... | collective-permute-start | bytes 196616 | tf_op jit(solution)/shard_map/ppermute | solution.py:276
  15.8 6.3 %collective-permute-start.3 = (f32[32,512]{1,0:T(8,128)S(1)}, f32[32,512]{1,0:T(8,128)S(1)}, u32[]{:S(2)}, u32[]{:S(2)}) collective-permute-start(f32[32,512]{1,0:T(8,128)S(1)} %get-tuple-element.39), channel_id=1, source_target_pairs={{0,3},{1,2},{2,1},{3,0},{4,7},{5,6},{6,5},{7,4},{8,11},{9,10},{10,... | collective-permute-start | bytes 196616 | tf_op jit(solution)/shard_map/ppermute | solution.py:276
  17.2 9.3 %collective-permute-start.9 = (bf16[32,512]{1,0:T(8,128)(2,1)S(1)}, bf16[32,512]{1,0:T(8,128)(2,1)S(1)}, u32[]{:S(2)}, u32[]{:S(2)}) collective-permute-start(bf16[32,512]{1,0:T(8,128)(2,1)S(1)} %get-tuple-element.47.refs_0_), channel_id=1, source_target_pairs={{0,3},{1,2},{2,1},{3,0},{4,7},{5,6},{6,5},{7,4},{8,11},{9,10},{10,... | collective-permute-start | bytes 98312 | tf_op jit(solution)/shard_map/ppermute | solution.py:276
  19.9 6.7 %collective-permute-start.8 = (bf16[32,512]{1,0:T(8,128)(2,1)S(1)}, bf16[32,512]{1,0:T(8,128)(2,1)S(1)}, u32[]{:S(2)}, u32[]{:S(2)}) collective-permute-start(bf16[32,512]{1,0:T(8,128)(2,1)S(1)} %get-tuple-element.47.refs_0_), channel_id=1, source_target_pairs={{0,2},{1,3},{2,0},{3,1},{4,6},{5,7},{6,4},{7,5},{8,10},{9,11},{10,... | collective-permute-start | bytes 98312 | tf_op jit(solution)/shard_map/ppermute | solution.py:276
  19.9 6.7 %collective-permute-start.7 = (bf16[32,512]{1,0:T(8,128)(2,1)S(1)}, bf16[32,512]{1,0:T(8,128)(2,1)S(1)}, u32[]{:S(2)}, u32[]{:S(2)}) collective-permute-start(bf16[32,512]{1,0:T(8,128)(2,1)S(1)} %get-tuple-element.47.refs_0_), channel_id=1, source_target_pairs={{0,1},{1,0},{2,3},{3,2},{4,5},{5,4},{6,7},{7,6},{8,9},{9,8},{10,11... | collective-permute-start | bytes 98312 | tf_op jit(solution)/shard_map/ppermute | solution.py:276
  22.1 6.4 %collective-permute-start.12 = (bf16[32,512]{1,0:T(8,128)(2,1)S(1)}, bf16[32,512]{1,0:T(8,128)(2,1)S(1)}, u32[]{:S(2)}, u32[]{:S(2)}) collective-permute-start(bf16[32,512]{1,0:T(8,128)(2,1)S(1)} %get-tuple-element.51.refs_0_), channel_id=1, source_target_pairs={{0,3},{1,2},{2,1},{3,0},{4,7},{5,6},{6,5},{7,4},{8,11},{9,10},{10,... | collective-permute-start | bytes 98312 | tf_op jit(solution)/shard_map/ppermute | solution.py:276
  24.4 4.9 %collective-permute-start.11 = (bf16[32,512]{1,0:T(8,128)(2,1)S(1)}, bf16[32,512]{1,0:T(8,128)(2,1)S(1)}, u32[]{:S(2)}, u32[]{:S(2)}) collective-permute-start(bf16[32,512]{1,0:T(8,128)(2,1)S(1)} %get-tuple-element.51.refs_0_), channel_id=1, source_target_pairs={{0,2},{1,3},{2,0},{3,1},{4,6},{5,7},{6,4},{7,5},{8,10},{9,11},{10,... | collective-permute-start | bytes 98312 | tf_op jit(solution)/shard_map/ppermute | solution.py:276
  26.5 3.9 %collective-permute-start.10 = (bf16[32,512]{1,0:T(8,128)(2,1)S(1)}, bf16[32,512]{1,0:T(8,128)(2,1)S(1)}, u32[]{:S(2)}, u32[]{:S(2)}) collective-permute-start(bf16[32,512]{1,0:T(8,128)(2,1)S(1)} %get-tuple-element.51.refs_0_), channel_id=1, source_target_pairs={{0,1},{1,0},{2,3},{3,2},{4,5},{5,4},{6,7},{7,6},{8,9},{9,8},{10,11... | collective-permute-start | bytes 98312 | tf_op jit(solution)/shard_map/ppermute | solution.py:276
  30.7 1.5 %collective-permute-start.13 = (f32[432,128]{1,0:T(8,128)S(1)}, f32[432,128]{1,0:T(8,128)S(1)}, u32[]{:S(2)}, u32[]{:S(2)}) collective-permute-start(f32[432,128]{1,0:T(8,128)S(1)} %get-tuple-element.53), channel_id=1, source_target_pairs={{0,4},{4,0},{8,12},{12,8},{16,20},{20,16},{24,28},{28,24},{1,5},{5... | collective-permute-start | bytes 663560 | tf_op jit(solution)/shard_map/ppermute | solution.py:391
  32.3 6.5 %collective-permute-start.16 = (bf16[432,128]{1,0:T(8,128)(2,1)S(1)}, bf16[432,128]{1,0:T(8,128)(2,1)S(1)}, u32[]{:S(2)}, u32[]{:S(2)}) collective-permute-start(bf16[432,128]{1,0:T(8,128)(2,1)S(1)} %add_convert_fusion), channel_id=1, source_target_pairs={{0,24},{4,28},{8,16},{12,20},{16,8},{20,12},{24,0},{28,4},{1,25},{... | collective-permute-start | bytes 331784 | tf_op jit(solution)/shard_map/ppermute | solution.py:401
  34.3 6.5 %collective-permute-start.15 = (bf16[432,128]{1,0:T(8,128)(2,1)S(1)}, bf16[432,128]{1,0:T(8,128)(2,1)S(1)}, u32[]{:S(2)}, u32[]{:S(2)}) collective-permute-start(bf16[432,128]{1,0:T(8,128)(2,1)S(1)} %add_convert_fusion), channel_id=1, source_target_pairs={{0,16},{4,20},{8,24},{12,28},{16,0},{20,4},{24,8},{28,12},{1,17},{... | collective-permute-start | bytes 331784 | tf_op jit(solution)/shard_map/ppermute | solution.py:401
  35.7 5.5 %collective-permute-start.14 = (bf16[432,128]{1,0:T(8,128)(2,1)S(1)}, bf16[432,128]{1,0:T(8,128)(2,1)S(1)}, u32[]{:S(2)}, u32[]{:S(2)}) collective-permute-start(bf16[432,128]{1,0:T(8,128)(2,1)S(1)} %add_convert_fusion), channel_id=1, source_target_pairs={{0,8},{4,12},{8,0},{12,4},{16,24},{20,28},{24,16},{28,20},{1,9},{5... | collective-permute-start | bytes 331784 | tf_op jit(solution)/shard_map/ppermute | solution.py:401
  35.8 5.4 %collective-permute-start.17 = (bf16[128,512]{1,0:T(8,128)(2,1)S(1)}, bf16[128,512]{1,0:T(8,128)(2,1)S(1)}, u32[]{:S(2)}, u32[]{:S(2)}) collective-permute-start(bf16[128,512]{1,0:T(8,128)(2,1)S(1)} %get-tuple-element.58.grad_ref.one_ref), channel_id=1, source_target_pairs={{4,0},{8,4},{12,8},{16,12},{20,16},{24,20},{28,24},{5,1},{9,5},{13... | collective-permute-start | bytes 393224 | tf_op jit(solution)/shard_map/ppermute | solution.py:404
  41.2 2.4 %collective-permute-start.18 = (f32[432,128]{1,0:T(8,128)S(1)}, f32[432,128]{1,0:T(8,128)S(1)}, u32[]{:S(2)}, u32[]{:S(2)}) collective-permute-start(f32[432,128]{1,0:T(8,128)S(1)} %add_add_fusion.own_ref), channel_id=1, source_target_pairs={{0,4},{4,0},{8,12},{12,8},{16,20},{20,16},{24,28},{28,24},{1,5},{5... | collective-permute-start | bytes 663560 | tf_op jit(solution)/shard_map/ppermute | solution.py:412

commit v7 on v6

--- a/solution.py
+++ b/solution.py
@@ -10,8 +10,9 @@
 SLOPE = 0.3
 VMEM = 24 * 1024 * 1024
 XOR = True
-RS = (1, 2, 3)
-AG = (1, 2, 3)
+RS = {1: (3, 2, 1), 0: (3, 2, 1)}
+AG = {1: (1, 3, 2), 0: (2, 3, 1)}
+CHIPS = (0, 1, 2)
 FEW = 4
 
 
@@ -48,9 +49,7 @@
 
 def fwd_kernel(n, ob, z, *refs):
     if z:
-        vol_ref, w_hbm, w_ref, cols_ref, *rest, sem = refs
-        w_copy = pltpu.make_async_copy(w_hbm, w_ref, sem)
-        w_copy.start()
+        vol_ref, w_ref, cols_ref, *rest = refs
     else:
         rim_ref, vol_ref, w_ref, cols_ref, *rest = refs
     part_refs = rest[:-2] if n > 1 else rest[:-1]
@@ -80,8 +79,6 @@
                 cols_ref[tap * cb : (tap + 1) * cb, :] = jnp.concatenate(
                     [block[j * cb : (j + 1) * cb] for j in range(groups)], axis=1
                 )
-    if z:
-        w_copy.wait()
     if cols_ref.shape[0] > 27 * cb:
         pad = (cols_ref.shape[0] - 27 * cb, cols_ref.shape[1])
         cols_ref[27 * cb :, :] = jnp.zeros(pad, jnp.bfloat16)
@@ -97,7 +94,7 @@
     all_ref = rest[-1]
     all_ref[...] = part
     me = lax.axis_index("chan")
-    for k, ref in zip((0,) + RS, part_refs):
+    for k, ref in zip((0,) + RS[z], part_refs):
         start = pl.multiple_of((me ^ k if XOR else lax.rem(me + k, n)) * ob, ob)
         ref[...] = all_ref[pl.ds(start, ob), :]
 
@@ -144,13 +141,13 @@
     out_ref[:, 0] = jnp.stack(means, axis=1).astype(jnp.bfloat16)
 
 
-def in_order(n, block_refs, grad_ref):
+def in_order(n, z, block_refs, grad_ref):
     if n == 1:
         grad_ref[...] = block_refs[0][...]
         return
     me = lax.axis_index("chan")
     ob = block_refs[0].shape[0]
-    for k, ref in zip((0,) + AG, block_refs):
+    for k, ref in zip((0,) + AG[z], block_refs):
         start = pl.multiple_of((me ^ k if XOR else lax.rem(me + n - k, n)) * ob, ob)
         grad_ref[pl.ds(start, ob), :] = ref[...]
 
@@ -166,17 +163,19 @@
 
 def middle_kernel(n, w_ref, act_one_ref, act_two_ref, cols_ref, *refs):
     *block_refs, wgrad_ref, grad_ref, pooled_ref, out_ref, wide_ref, done_ref, sems = refs
-    in_order(n, block_refs, grad_ref)
-    copies = input_planes([(2, (grad_ref[...],))], w_ref, out_ref, wide_ref, done_ref, sems)
+    in_order(n, 1, block_refs, grad_ref)
+    input_planes([(grad_ref[...],)], w_ref, wide_ref, done_ref)
+    for copy in plane_copies(done_ref, out_ref, 2, sems):
+        copy.start()
     wgrad_ref[...] = weight_term(cols_ref[...], grad_ref)
     pool_planes(act_one_ref, act_two_ref, pooled_ref)
-    for copy in copies:
+    for copy in plane_copies(done_ref, out_ref, 2, sems):
         copy.wait()
 
 
 def send_kernel(n, sum_ref, cols_ref, *refs):
     *block_refs, send_ref, grad_ref = refs
-    in_order(n, block_refs, grad_ref)
+    in_order(n, 0, block_refs, grad_ref)
     half = send_ref.shape[0]
     start = pl.multiple_of((1 - lax.rem(lax.axis_index("space"), 2)) * half, 16)
     send_ref[...] = sum_ref[pl.ds(start, half), :] + weight_term(
@@ -192,18 +191,20 @@
     )
 
 
-def join_kernel(own_ref, other_ref, out_ref, sems):
+def join_kernel(own_ref, other_ref, plane_ref, _, out_ref, input_ref, sems):
     half = own_ref.shape[0]
     for core in range(2):
 
         @pl.when(lax.rem(lax.axis_index("space"), 2) == core)
         def _():
-            copies = []
+            copies = plane_copies(plane_ref, input_ref, input_ref.shape[1] - 1, sems)
             for ref, start in ((own_ref, core * half), (other_ref, (1 - core) * half)):
                 size = min(half, out_ref.shape[0] - start)
                 copies.append(
                     pltpu.make_async_copy(
-                        ref.at[pl.ds(0, size)], out_ref.at[pl.ds(start, size)], sems.at[start // half]
+                        ref.at[pl.ds(0, size)],
+                        out_ref.at[pl.ds(start, size)],
+                        sems.at[1 + start // half],
                     )
                 )
             for copy in copies:
@@ -212,8 +213,8 @@
                 copy.wait()
 
 
-def input_planes(todo, w_ref, out_ref, wide_ref, done_ref, sems):
-    cb, _, hgt, wid = out_ref.shape
+def input_planes(todo, w_ref, wide_ref, done_ref):
+    _, cb, hgt, wid = done_ref.shape
     half = wid // 2
     groups = hgt // 4
     lanes = groups * wid
@@ -223,9 +224,8 @@
     keep = lax.broadcasted_iota(jnp.int32, (3 * cb, lanes), 1) < lanes - half
     w = [w_ref[a * taps : (a + 1) * taps, :] for a in range(3)]
     behind = jnp.concatenate([w[2], w[0]], axis=1)
-    copies = []
-    for slot, (i, grads) in enumerate(todo):
-        if i % 2 == 0:
+    for slot, grads in enumerate(todo):
+        if len(grads) == 1:
             e_all = jnp.dot(w[1], grads[0], preferred_element_type=jnp.float32)
         else:
             e_all = jnp.dot(
@@ -256,19 +256,26 @@
                         at : at + cb, h * wid : (h + 1) * wid
                     ]
         done_ref[slot] = wide_ref[...].reshape(cb, hgt, wid).astype(jnp.bfloat16)
-        copies.append(pltpu.make_async_copy(done_ref.at[slot], out_ref.at[:, i], sems.at[slot]))
-        copies[-1].start()
-    return copies
-
-
-def input_kernel(last, w_ref, one_ref, two_ref, _, out_ref, *scratch):
+
+
+def plane_copies(done_ref, out_ref, first, sems):
+    return [
+        pltpu.make_async_copy(done_ref.at[i], out_ref.at[:, first + i], sems.at[i])
+        for i in range(done_ref.shape[0])
+    ]
+
+
+def input_kernel(w_ref, one_ref, two_ref, _, out_ref, wide_ref, done_ref, sems):
     one, two = one_ref[...], two_ref[...]
-    if last:
-        todo = [(out_ref.shape[1] - 1, (one, two))]
-    else:
-        todo = [(0, (one,)), (1, (one, two))]
-    for copy in input_planes(todo, w_ref, out_ref, *scratch):
+    input_planes([(one,), (one, two)], w_ref, wide_ref, done_ref)
+    for copy in plane_copies(done_ref, out_ref, 0, sems):
+        copy.start()
+    for copy in plane_copies(done_ref, out_ref, 0, sems):
         copy.wait()
+
+
+def edge_kernel(w_ref, one_ref, two_ref, done_ref, wide_ref):
+    input_planes([(one_ref[...], two_ref[...])], w_ref, wide_ref, done_ref)
 
 
 def moved(block, axis, k):
@@ -316,24 +323,14 @@
     )(from_hbm(volume))
     rim = lax.ppermute(edge, "space", [(i, i + 1) for i in range(n_space - 1)])
     for z in reversed(out_planes):
-        call = functools.partial(fwd_kernel, n, ob, z)
-        if z:
-            w, cols[z], *parts = pl.pallas_call(
-                call,
-                in_specs=[vmem, hbm],
-                out_shape=[shape(weights.shape, bf16), cols_shape] + part_shapes,
-                scratch_shapes=scratch + [pltpu.SemaphoreType.DMA],
-                compiler_params=params(),
-            )(vol, from_hbm(weights))
-        else:
-            cols[z], *parts = pl.pallas_call(
-                call,
-                out_shape=[cols_shape] + part_shapes,
-                scratch_shapes=scratch,
-                compiler_params=params(),
-            )(rim, vol, w)
+        cols[z], *parts = pl.pallas_call(
+            functools.partial(fwd_kernel, n, ob, z),
+            out_shape=[cols_shape] + part_shapes,
+            scratch_shapes=scratch,
+            compiler_params=params(),
+        )(*(() if z else (rim,)), vol, weights)
         if direct:
-            parts = parts[:1] + [moved(p, "chan", k) for k, p in zip(RS, parts[1:])]
+            parts = parts[:1] + [moved(p, "chan", k) for k, p in zip(RS[z], parts[1:])]
         else:
             parts = [lax.psum_scatter(parts[0], "chan", scatter_dimension=0, tiled=True)]
         own, acts[z] = pl.pallas_call(
@@ -342,28 +339,11 @@
             compiler_params=params(),
         )(spread, *parts)
         if direct:
-            grads[z] = [own] + [moved(own, "chan", k) for k in AG]
+            grads[z] = [own] + [moved(own, "chan", k) for k in AG[z]]
         else:
             grads[z] = [lax.all_gather(own, "chan", axis=0, tiled=True)]
 
-    def input_scratch(count):
-        return [
-            pltpu.VMEM((cb * hgt, wid), f32),
-            pltpu.VMEM((count, cb, hgt, wid), bf16),
-            pltpu.SemaphoreType.DMA((count,)),
-        ]
-
-    def input_call(last, *operands):
-        return pl.pallas_call(
-            functools.partial(input_kernel, last),
-            in_specs=[vmem] * 3 + [hbm],
-            out_specs=hbm,
-            out_shape=shape(volume.shape, bf16),
-            scratch_shapes=input_scratch(1 if last else 2),
-            input_output_aliases={3: 0},
-            compiler_params=params(),
-        )(*operands)
-
+    wide, plane = pltpu.VMEM((cb * hgt, wid), f32), (cb, hgt, wid)
     grad_shape = shape((out_ch, cells), bf16)
     term, grads[1], pooled, input_grad = pl.pallas_call(
         functools.partial(middle_kernel, n),
@@ -374,9 +354,9 @@
             shape(upstream.shape, bf16),
             shape(volume.shape, bf16),
         ],
-        scratch_shapes=input_scratch(1),
-        compiler_params=params(),
-    )(w, acts[0], acts[1], cols[1], *grads[1])
+        scratch_shapes=[wide, pltpu.VMEM((1,) + plane, bf16), pltpu.SemaphoreType.DMA((1,))],
+        compiler_params=params(),
+    )(weights, acts[0], acts[1], cols[1], *grads[1])
     send, grads[0] = pl.pallas_call(
         functools.partial(send_kernel, n),
         out_shape=[shape((half, out_ch), f32), grad_shape],
@@ -397,26 +377,44 @@
         if r == len(groups) - 1:
             sent, grads, input_grad = lax.optimization_barrier((sent, grads, input_grad))
         partners = [sum(group[b] * (k >> b & 1) for b in range(len(group))) for k in range(1, 1 << len(group))]
-        terms = [sent] + [
-            lax.ppermute(sent, "space", [(i, i ^ p) for i in range(n_space)]) for p in partners
-        ]
+        terms = [sent] + [None] * len(partners)
+        for k in CHIPS:
+            if k < len(partners):
+                terms[k + 1] = lax.ppermute(
+                    sent, "space", [(i, i ^ partners[k]) for i in range(n_space)]
+                )
         if r == len(groups) - 1:
             after = lax.ppermute(grads[0], "space", [(i + 1, i) for i in range(n_space - 1)])
-            input_grad = input_call(False, w, grads[0], grads[1], input_grad)
+            input_grad = pl.pallas_call(
+                input_kernel,
+                in_specs=[vmem] * 3 + [hbm],
+                out_specs=hbm,
+                out_shape=shape(volume.shape, bf16),
+                scratch_shapes=[wide, pltpu.VMEM((2,) + plane, bf16), pltpu.SemaphoreType.DMA((2,))],
+                input_output_aliases={3: 0},
+                compiler_params=params(),
+            )(weights, grads[0], grads[1], input_grad)
         terms = [t.astype(f32) for t in terms]
         while len(terms) > 1:
             terms = [a + b for a, b in zip(terms[::2], terms[1::2])]
         rows = terms[0]
     rows, input_grad, after = lax.optimization_barrier((rows, input_grad, after))
-    input_grad = input_call(True, w, grads[1], after, input_grad)
+    edge = pl.pallas_call(
+        edge_kernel,
+        out_shape=shape((1,) + plane, bf16),
+        scratch_shapes=[wide],
+        compiler_params=params(),
+    )(weights, grads[1], after)
     other = lax.ppermute(rows, "space", [(i, i ^ 1) for i in range(n_space)])
-    weight_grad = pl.pallas_call(
+    weight_grad, input_grad = pl.pallas_call(
         join_kernel,
-        out_specs=pl.BlockSpec(memory_space=pltpu.HBM),
-        out_shape=shape((taps, out_ch), f32),
-        scratch_shapes=[pltpu.SemaphoreType.DMA((2,))],
-        compiler_params=params(),
-    )(rows, other)
+        in_specs=[vmem] * 3 + [hbm],
+        out_specs=[hbm] * 2,
+        out_shape=[shape((taps, out_ch), f32), shape(volume.shape, bf16)],
+        scratch_shapes=[pltpu.SemaphoreType.DMA((3,))],
+        input_output_aliases={3: 1},
+        compiler_params=params(),
+    )(rows, other, edge, input_grad)
     weight_grad = weight_grad.reshape(3, 3, 3, cb, out_ch).transpose(3, 0, 1, 2, 4)
     return pooled, input_grad, weight_grad
 

time: 44.7 us -> 42.8 us (0.957)
  starting transfers between devices: 26.9 us -> 25.4 us
  Pallas kernels: 9.56 us -> 8.49 us
  waiting for transfers between devices: 7.15 us -> 7.86 us
    ppermute x12, starting transfers between devices: 18.4 us -> 17.3 us  [moved(): lax.ppermute(block, axis, [(i, i ^ k if XOR else (i + k) % n) for i in ra...]
    pallas_call x5, Pallas kernels: 5.8 us -> 4.7 us  [the longest x1 1.69 us: on_device(): pl.pallas_call(input_kernel, in_specs=[vmem] * 3 + [hbm], out_specs=hbm,...]
    ppermute x1, waiting for transfers between devices: 0.01 us -> 0.51 us  [on_device(): other = lax.ppermute(rows, 'space', [(i, i ^ 1) for i in range(n_space)])]
  transfers between devices with their start and end apart: 19 -> 19, of which waited for: 7 -> 8; matrix products, arithmetic and copies ran while one was open for 0% -> 0% of each run, Pallas kernels for 17% -> 15%
where the time goes in v7:
time: 42.8 us; the launch traced here: 42.7 us
  starting transfers between devices  25.4 us (59%)
  Pallas kernels  8.49 us (20%)
  waiting for transfers between devices  7.86 us (18%)
  between operations  0.79 us (2%)
    ppermute x12, starting transfers between devices, moved(): lax.ppermute(block, axis, [(i, i ^ k if XOR else (i + k) % n) for i in ra...  17.3 us
    ppermute x12, waiting for transfers between devices, moved(): lax.ppermute(block, axis, [(i, i ^ k if XOR else (i + k) % n) for i in ra...  3.76 us
    ppermute x3, starting transfers between devices, on_device(): lax.ppermute(sent, 'space', [(i, i ^ partners[k]) for i in range(n_space)])  3.55 us
    ppermute x3, waiting for transfers between devices, on_device(): lax.ppermute(sent, 'space', [(i, i ^ partners[k]) for i in range(n_space)])  2.39 us
    ppermute x1, starting transfers between devices, on_device(): rim = lax.ppermute(edge, 'space', [(i, i + 1) for i in range(n_space - 1)])  2.36 us
    pallas_call x1, Pallas kernels, on_device(): pl.pallas_call(functools.partial(middle_kernel, n), out_specs=[vmem, vmem...  1.89 us
    pallas_call x1, Pallas kernels, on_device(): pl.pallas_call(input_kernel, in_specs=[vmem] * 3 + [hbm], out_specs=hbm,...  1.69 us
    pallas_call x2, Pallas kernels, on_device(): pl.pallas_call(functools.partial(fwd_kernel, n, ob, z), out_shape=[cols_s...  1.6 us
  transfers between devices with their start and end apart: 19, of which 8 were waited for; matrix products, arithmetic and copies ran while one was open for 0% of the time, Pallas kernels for 15%

profile of v7, /device:TPU:0, one launch (start us, length us, event | category | flops | bytes accessed | tf_op | source)
XLA Modules:
  0.0 42.7 jit_solution(16073203865950847870)
XLA Ops:
  0.6 1.2 %shard_map.59 = (bf16[32,4,16,128]{3,2,1,0:T(8,128)(2,1)S(1)}, bf16[32,1,16,128]{3,2,1,0:T(8,128)(2,1)S(1)}) custom-call(bf16[32,4,16,128]{3,2,1,0:T(8,128)(2,1)} %vol_hbm.1), custom_call_target="tpu_custom_call" | custom-call | tf_op jit(solution)/shard_map/pallas_call | solution.py:317
  1.8 2.4 %collective-permute-start = (bf16[32,1,16,128]{3,2,1,0:T(8,128)(2,1)S(1)}, bf16[32,1,16,128]{3,2,1,0:T(8,128)(2,1)S(1)}, u32[]{:S(2)}, u32[]{:S(2)}) collective-permute-start(bf16[32,1,16,128]{3,2,1,0:T(8,128)(2,1)S(1)} %get-tuple-element.34), channel_id=1, source_target_pairs={{0,4},{4,8},{8,12},{12,16},{16,20},{20,24},{24,28},{1,5},{5,9},{9,... | collective-permute-start | bytes 393224 | tf_op jit(solution)/shard_map/ppermute | solution.py:324
  4.2 0.8 %shard_map.62 = (bf16[864,512]{1,0:T(8,128)(2,1)S(1)}, f32[32,512]{1,0:T(8,128)S(1)}, f32[32,512]{1,0:T(8,128)S(1)}, f32[32,512]{1,0:T(8,128)S(1)}, f32[32,512]{1,0:T(8,128)S(1)}) custom-call(bf16[32,4,16,128]{3,2,1,0:T(8,128)(2,1)S(1)} %get-tuple-element.35.refs_1_.refs_0_, bf16[864,128]{1,0:T(8,128)(2,1)S(1)} %bitcast.11), custom_call_target="tpu_custom_call" | custom-call | tf_op jit(solution)/shard_map/pallas_call | solution.py:326
  5.0 4.5 %collective-permute-start.4 = (f32[32,512]{1,0:T(8,128)S(1)}, f32[32,512]{1,0:T(8,128)S(1)}, u32[]{:S(2)}, u32[]{:S(2)}) collective-permute-start(f32[32,512]{1,0:T(8,128)S(1)} %get-tuple-element.42), channel_id=1, source_target_pairs={{0,3},{1,2},{2,1},{3,0},{4,7},{5,6},{6,5},{7,4},{8,11},{9,10},{10,... | collective-permute-start | bytes 196616 | tf_op jit(solution)/shard_map/ppermute | solution.py:283
  9.5 0.6 %collective-permute-start.6 = (f32[32,512]{1,0:T(8,128)S(1)}, f32[32,512]{1,0:T(8,128)S(1)}, u32[]{:S(2)}, u32[]{:S(2)}) collective-permute-start(f32[32,512]{1,0:T(8,128)S(1)} %get-tuple-element.44), channel_id=1, source_target_pairs={{0,1},{1,0},{2,3},{3,2},{4,5},{5,4},{6,7},{7,6},{8,9},{9,8},{10,11... | collective-permute-start | bytes 196616 | tf_op jit(solution)/shard_map/ppermute | solution.py:283
  10.2 0.8 %shard_map.60 = (bf16[864,512]{1,0:T(8,128)(2,1)S(1)}, f32[32,512]{1,0:T(8,128)S(1)}, f32[32,512]{1,0:T(8,128)S(1)}, f32[32,512]{1,0:T(8,128)S(1)}, f32[32,512]{1,0:T(8,128)S(1)}) custom-call(bf16[32,1,16,128]{3,2,1,0:T(8,128)(2,1)S(1)} %collective-permute-done.refs_0_, bf16[32,4,16,128]{3,2,1,0:T(8,128)(2,1)S(1)} %get-tuple-element.35.refs_1_.refs_0_, ...), custom_call_target="tpu_custom_call" | custom-call | tf_op jit(solution)/shard_map/pallas_call | solution.py:326
  11.0 3.8 %collective-permute-start.1 = (f32[32,512]{1,0:T(8,128)S(1)}, f32[32,512]{1,0:T(8,128)S(1)}, u32[]{:S(2)}, u32[]{:S(2)}) collective-permute-start(f32[32,512]{1,0:T(8,128)S(1)} %get-tuple-element.37), channel_id=1, source_target_pairs={{0,3},{1,2},{2,1},{3,0},{4,7},{5,6},{6,5},{7,4},{8,11},{9,10},{10,... | collective-permute-start | bytes 196616 | tf_op jit(solution)/shard_map/ppermute | solution.py:283
  14.8 0.6 %collective-permute-start.3 = (f32[32,512]{1,0:T(8,128)S(1)}, f32[32,512]{1,0:T(8,128)S(1)}, u32[]{:S(2)}, u32[]{:S(2)}) collective-permute-start(f32[32,512]{1,0:T(8,128)S(1)} %get-tuple-element.39), channel_id=1, source_target_pairs={{0,1},{1,0},{2,3},{3,2},{4,5},{5,4},{6,7},{7,6},{8,9},{9,8},{10,11... | collective-permute-start | bytes 196616 | tf_op jit(solution)/shard_map/ppermute | solution.py:283
  15.6 0.3 collective-permute-done.5.rest_2_
  15.9 1.2 %collective-permute-start.7 = (bf16[32,512]{1,0:T(8,128)(2,1)S(1)}, bf16[32,512]{1,0:T(8,128)(2,1)S(1)}, u32[]{:S(2)}, u32[]{:S(2)}) collective-permute-start(bf16[32,512]{1,0:T(8,128)(2,1)S(1)} %get-tuple-element.47.refs_0_), channel_id=1, source_target_pairs={{0,1},{1,0},{2,3},{3,2},{4,5},{5,4},{6,7},{7,6},{8,9},{9,8},{10,11... | collective-permute-start | bytes 98312 | tf_op jit(solution)/shard_map/ppermute | solution.py:283
  17.1 2.5 %collective-permute-start.8 = (bf16[32,512]{1,0:T(8,128)(2,1)S(1)}, bf16[32,512]{1,0:T(8,128)(2,1)S(1)}, u32[]{:S(2)}, u32[]{:S(2)}) collective-permute-start(bf16[32,512]{1,0:T(8,128)(2,1)S(1)} %get-tuple-element.47.refs_0_), channel_id=1, source_target_pairs={{0,3},{1,2},{2,1},{3,0},{4,7},{5,6},{6,5},{7,4},{8,11},{9,10},{10,... | collective-permute-start | bytes 98312 | tf_op jit(solution)/shard_map/ppermute | solution.py:283
  19.5 0.5 %collective-permute-start.9 = (bf16[32,512]{1,0:T(8,128)(2,1)S(1)}, bf16[32,512]{1,0:T(8,128)(2,1)S(1)}, u32[]{:S(2)}, u32[]{:S(2)}) collective-permute-start(bf16[32,512]{1,0:T(8,128)(2,1)S(1)} %get-tuple-element.47.refs_0_), channel_id=1, source_target_pairs={{0,2},{1,3},{2,0},{3,1},{4,6},{5,7},{6,4},{7,5},{8,10},{9,11},{10,... | collective-permute-start | bytes 98312 | tf_op jit(solution)/shard_map/ppermute | solution.py:283
  20.0 1.6 %collective-permute-done.2.rest_2_ = f32[32,512]{1,0:T(8,128)S(1)} collective-permute-done((f32[32,512]{1,0:T(8,128)S(1)}, f32[32,512]{1,0:T(8,128)S(1)}, u32[]{:S(2)}, u32[]{:S(2)}) %collective-permute-start.2) | collective-permute-done | bytes 65568 | tf_op jit(solution)/shard_map/ppermute | solution.py:283
  21.6 1.1 %collective-permute-start.10 = (bf16[32,512]{1,0:T(8,128)(2,1)S(1)}, bf16[32,512]{1,0:T(8,128)(2,1)S(1)}, u32[]{:S(2)}, u32[]{:S(2)}) collective-permute-start(bf16[32,512]{1,0:T(8,128)(2,1)S(1)} %get-tuple-element.51.refs_0_), channel_id=1, source_target_pairs={{0,2},{1,3},{2,0},{3,1},{4,6},{5,7},{6,4},{7,5},{8,10},{9,11},{10,... | collective-permute-start | bytes 98312 | tf_op jit(solution)/shard_map/ppermute | solution.py:283
  22.7 2.3 %collective-permute-start.11 = (bf16[32,512]{1,0:T(8,128)(2,1)S(1)}, bf16[32,512]{1,0:T(8,128)(2,1)S(1)}, u32[]{:S(2)}, u32[]{:S(2)}) collective-permute-start(bf16[32,512]{1,0:T(8,128)(2,1)S(1)} %get-tuple-element.51.refs_0_), channel_id=1, source_target_pairs={{0,3},{1,2},{2,1},{3,0},{4,7},{5,6},{6,5},{7,4},{8,11},{9,10},{10,... | collective-permute-start | bytes 98312 | tf_op jit(solution)/shard_map/ppermute | solution.py:283
  25.2 1.9 %shard_map.64 = (f32[864,128]{1,0:T(8,128)S(1)}, bf16[128,512]{1,0:T(8,128)(2,1)S(1)}, bf16[32,1,4,32]{3,2,1,0:T(4,128)(2,1)}, bf16[32,4,16,128]{3,2,1,0:T(8,128)(2,1)}) custom-call(bf16[864,128]{1,0:T(8,128)(2,1)S(1)} %bitcast.13, f32[32,512]{1,0:T(8,128)S(1)} %get-tuple-element.40.act_one_ref, f32[32,512]{1,0:T(8,128)S(1)} %get-tuple-element.45.act_two_ref, ...), custom_call_target="tpu_custom_call" | custom-call | tf_op jit(solution)/shard_map/pallas_call | solution.py:348
  27.1 0.5 %collective-permute-done.10.refs_1_ = bf16[32,512]{1,0:T(8,128)(2,1)S(1)} collective-permute-done((bf16[32,512]{1,0:T(8,128)(2,1)S(1)}, bf16[32,512]{1,0:T(8,128)(2,1)S(1)}, u32[]{:S(2)}, u32[]{:S(2)}) %collective-permute-start.10) | collective-permute-done | bytes 32800 | tf_op jit(solution)/shard_map/ppermute | solution.py:283
  27.6 0.9 %collective-permute-done.11.refs_2_ = bf16[32,512]{1,0:T(8,128)(2,1)S(1)} collective-permute-done((bf16[32,512]{1,0:T(8,128)(2,1)S(1)}, bf16[32,512]{1,0:T(8,128)(2,1)S(1)}, u32[]{:S(2)}, u32[]{:S(2)}) %collective-permute-start.11) | collective-permute-done | bytes 32800 | tf_op jit(solution)/shard_map/ppermute | solution.py:283
  28.5 0.5 %collective-permute-done.12.refs_3_ = bf16[32,512]{1,0:T(8,128)(2,1)S(1)} collective-permute-done((bf16[32,512]{1,0:T(8,128)(2,1)S(1)}, bf16[32,512]{1,0:T(8,128)(2,1)S(1)}, u32[]{:S(2)}, u32[]{:S(2)}) %collective-permute-start.12) | collective-permute-done | bytes 32800 | tf_op jit(solution)/shard_map/ppermute | solution.py:283
  29.0 0.3 shard_map.65
  29.4 0.3 shard_map.66
  29.6 1.2 %collective-permute-done.13 = f32[432,128]{1,0:T(8,128)S(1)} collective-permute-done((f32[432,128]{1,0:T(8,128)S(1)}, f32[432,128]{1,0:T(8,128)S(1)}, u32[]{:S(2)}, u32[]{:S(2)}) %collective-permute-start.13) | collective-permute-done | bytes 221216 | tf_op jit(solution)/shard_map/ppermute | solution.py:371
  30.9 1.7 %collective-permute-start.14 = (bf16[432,128]{1,0:T(8,128)(2,1)S(1)}, bf16[432,128]{1,0:T(8,128)(2,1)S(1)}, u32[]{:S(2)}, u32[]{:S(2)}) collective-permute-start(bf16[432,128]{1,0:T(8,128)(2,1)S(1)} %add_convert_fusion), channel_id=1, source_target_pairs={{0,8},{4,12},{8,0},{12,4},{16,24},{20,28},{24,16},{28,20},{1,9},{5... | collective-permute-start | bytes 331784 | tf_op jit(solution)/shard_map/ppermute | solution.py:383
  32.6 1.3 %collective-permute-start.15 = (bf16[432,128]{1,0:T(8,128)(2,1)S(1)}, bf16[432,128]{1,0:T(8,128)(2,1)S(1)}, u32[]{:S(2)}, u32[]{:S(2)}) collective-permute-start(bf16[432,128]{1,0:T(8,128)(2,1)S(1)} %add_convert_fusion), channel_id=1, source_target_pairs={{0,16},{4,20},{8,24},{12,28},{16,0},{20,4},{24,8},{28,12},{1,17},{... | collective-permute-start | bytes 331784 | tf_op jit(solution)/shard_map/ppermute | solution.py:383
  33.9 0.6 %collective-permute-start.16 = (bf16[432,128]{1,0:T(8,128)(2,1)S(1)}, bf16[432,128]{1,0:T(8,128)(2,1)S(1)}, u32[]{:S(2)}, u32[]{:S(2)}) collective-permute-start(bf16[432,128]{1,0:T(8,128)(2,1)S(1)} %add_convert_fusion), channel_id=1, source_target_pairs={{0,24},{4,28},{8,16},{12,20},{16,8},{20,12},{24,0},{28,4},{1,25},{... | collective-permute-start | bytes 331784 | tf_op jit(solution)/shard_map/ppermute | solution.py:383
  34.4 1.3 %collective-permute-start.17 = (bf16[128,512]{1,0:T(8,128)(2,1)S(1)}, bf16[128,512]{1,0:T(8,128)(2,1)S(1)}, u32[]{:S(2)}, u32[]{:S(2)}) collective-permute-start(bf16[128,512]{1,0:T(8,128)(2,1)S(1)} %get-tuple-element.57.grad_ref.one_ref), channel_id=1, source_target_pairs={{4,0},{8,4},{12,8},{16,12},{20,16},{24,20},{28,24},{5,1},{9,5},{13... | collective-permute-start | bytes 393224 | tf_op jit(solution)/shard_map/ppermute | solution.py:387
  35.7 1.7 %shard_map.67._ = bf16[32,4,16,128]{3,2,1,0:T(8,128)(2,1)} custom-call(bf16[864,128]{1,0:T(8,128)(2,1)S(1)} %bitcast.14, bf16[128,512]{1,0:T(8,128)(2,1)S(1)} %get-tuple-element.57.grad_ref.one_ref, bf16[128,512]{1,0:T(8,128)(2,1)S(1)} %get-tuple-element.58.two_ref.one_ref, bf16[32,4,16,128]{3,2,1,0:T(8,128)(2,1)} %get-tuple-element.59._), custom_call_target="tpu_custom_call", output_to_operand_aliasing={{}: (3, {})} | custom-call | tf_op jit(solution)/shard_map/pallas_call | solution.py:388
  37.4 2.4 %collective-permute-done.15 = bf16[432,128]{1,0:T(8,128)(2,1)S(1)} collective-permute-done((bf16[432,128]{1,0:T(8,128)(2,1)S(1)}, bf16[432,128]{1,0:T(8,128)(2,1)S(1)}, u32[]{:S(2)}, u32[]{:S(2)}) %collective-permute-start.15) | collective-permute-done | bytes 110624 | tf_op jit(solution)/shard_map/ppermute | solution.py:383
  39.9 0.9 %collective-permute-start.18 = (f32[432,128]{1,0:T(8,128)S(1)}, f32[432,128]{1,0:T(8,128)S(1)}, u32[]{:S(2)}, u32[]{:S(2)}) collective-permute-start(f32[432,128]{1,0:T(8,128)S(1)} %add_add_fusion.own_ref), channel_id=1, source_target_pairs={{0,4},{4,0},{8,12},{12,8},{16,20},{20,16},{24,28},{28,24},{1,5},{5... | collective-permute-start | bytes 663560 | tf_op jit(solution)/shard_map/ppermute | solution.py:408
  40.7 0.6 %shard_map.68.plane_ref = bf16[1,32,16,128]{3,2,1,0:T(8,128)(2,1)S(1)} custom-call(bf16[864,128]{1,0:T(8,128)(2,1)S(1)} %bitcast.15, bf16[128,512]{1,0:T(8,128)(2,1)S(1)} %get-tuple-element.58.two_ref.one_ref, bf16[128,512]{1,0:T(8,128)(2,1)S(1)} %collective-permute-done.17.two_ref), custom_call_target="tpu_custom_call" | custom-call | tf_op jit(solution)/shard_map/pallas_call | solution.py:402
  41.3 0.5 %collective-permute-done.18.other_ref = f32[432,128]{1,0:T(8,128)S(1)} collective-permute-done((f32[432,128]{1,0:T(8,128)S(1)}, f32[432,128]{1,0:T(8,128)S(1)}, u32[]{:S(2)}, u32[]{:S(2)}) %collective-permute-start.18) | collective-permute-done | bytes 221216 | tf_op jit(solution)/shard_map/ppermute | solution.py:408
  41.8 0.8 %shard_map.69 = (f32[864,128]{1,0:T(8,128)}, bf16[32,4,16,128]{3,2,1,0:T(8,128)(2,1)}) custom-call(f32[432,128]{1,0:T(8,128)S(1)} %add_add_fusion.own_ref, f32[432,128]{1,0:T(8,128)S(1)} %collective-permute-done.18.other_ref, bf16[1,32,16,128]{3,2,1,0:T(8,128)(2,1)S(1)} %shard_map.68.plane_ref, ...), custom_call_target="tpu_custom_call", output_to_operand_aliasing={{1}: (3, {})} | custom-call | tf_op jit(solution)/shard_map/pallas_call | solution.py:409
  (25 shorter events, 0.5 us)
Async XLA Ops:
  0.6 3.6 %copy-start = (bf16[32,3,3,3,128]{4,0,3,2,1:T(8,128)(2,1)S(1)}, bf16[32,3,3,3,128]{4,0,3,2,1:T(8,128)(2,1)}, u32[]{:S(2)}) copy-start(bf16[32,3,3,3,128]{4,0,3,2,1:T(8,128)(2,1)} %param.4) | copy-start | bytes 663556
  1.8 8.3 %collective-permute-start = (bf16[32,1,16,128]{3,2,1,0:T(8,128)(2,1)S(1)}, bf16[32,1,16,128]{3,2,1,0:T(8,128)(2,1)S(1)}, u32[]{:S(2)}, u32[]{:S(2)}) collective-permute-start(bf16[32,1,16,128]{3,2,1,0:T(8,128)(2,1)S(1)} %get-tuple-element.34), channel_id=1, source_target_pairs={{0,4},{4,8},{8,12},{12,16},{16,20},{20,24},{24,28},{1,5},{5,9},{9,... | collective-permute-start | bytes 393224 | tf_op jit(solution)/shard_map/ppermute | solution.py:324
  5.0 9.8 %collective-permute-start.4 = (f32[32,512]{1,0:T(8,128)S(1)}, f32[32,512]{1,0:T(8,128)S(1)}, u32[]{:S(2)}, u32[]{:S(2)}) collective-permute-start(f32[32,512]{1,0:T(8,128)S(1)} %get-tuple-element.42), channel_id=1, source_target_pairs={{0,3},{1,2},{2,1},{3,0},{4,7},{5,6},{6,5},{7,4},{8,11},{9,10},{10,... | collective-permute-start | bytes 196616 | tf_op jit(solution)/shard_map/ppermute | solution.py:283
  9.5 6.4 %collective-permute-start.5 = (f32[32,512]{1,0:T(8,128)S(1)}, f32[32,512]{1,0:T(8,128)S(1)}, u32[]{:S(2)}, u32[]{:S(2)}) collective-permute-start(f32[32,512]{1,0:T(8,128)S(1)} %get-tuple-element.43), channel_id=1, source_target_pairs={{0,2},{1,3},{2,0},{3,1},{4,6},{5,7},{6,4},{7,5},{8,10},{9,11},{10,... | collective-permute-start | bytes 196616 | tf_op jit(solution)/shard_map/ppermute | solution.py:283
  9.5 5.9 %copy-start.1 = (bf16[32,1,4,32]{3,2,1,0:T(4,128)(2,1)S(1)}, bf16[32,1,4,32]{3,2,1,0:T(4,128)(2,1)}, u32[]{:S(2)}) copy-start(bf16[32,1,4,32]{3,2,1,0:T(4,128)(2,1)} %param.5) | copy-start | bytes 24580
  9.5 6.4 %collective-permute-start.6 = (f32[32,512]{1,0:T(8,128)S(1)}, f32[32,512]{1,0:T(8,128)S(1)}, u32[]{:S(2)}, u32[]{:S(2)}) collective-permute-start(f32[32,512]{1,0:T(8,128)S(1)} %get-tuple-element.44), channel_id=1, source_target_pairs={{0,1},{1,0},{2,3},{3,2},{4,5},{5,4},{6,7},{7,6},{8,9},{9,8},{10,11... | collective-permute-start | bytes 196616 | tf_op jit(solution)/shard_map/ppermute | solution.py:283
  11.0 8.6 %collective-permute-start.1 = (f32[32,512]{1,0:T(8,128)S(1)}, f32[32,512]{1,0:T(8,128)S(1)}, u32[]{:S(2)}, u32[]{:S(2)}) collective-permute-start(f32[32,512]{1,0:T(8,128)S(1)} %get-tuple-element.37), channel_id=1, source_target_pairs={{0,3},{1,2},{2,1},{3,0},{4,7},{5,6},{6,5},{7,4},{8,11},{9,10},{10,... | collective-permute-start | bytes 196616 | tf_op jit(solution)/shard_map/ppermute | solution.py:283
  14.8 6.8 %collective-permute-start.2 = (f32[32,512]{1,0:T(8,128)S(1)}, f32[32,512]{1,0:T(8,128)S(1)}, u32[]{:S(2)}, u32[]{:S(2)}) collective-permute-start(f32[32,512]{1,0:T(8,128)S(1)} %get-tuple-element.38), channel_id=1, source_target_pairs={{0,2},{1,3},{2,0},{3,1},{4,6},{5,7},{6,4},{7,5},{8,10},{9,11},{10,... | collective-permute-start | bytes 196616 | tf_op jit(solution)/shard_map/ppermute | solution.py:283
  14.8 6.8 %collective-permute-start.3 = (f32[32,512]{1,0:T(8,128)S(1)}, f32[32,512]{1,0:T(8,128)S(1)}, u32[]{:S(2)}, u32[]{:S(2)}) collective-permute-start(f32[32,512]{1,0:T(8,128)S(1)} %get-tuple-element.39), channel_id=1, source_target_pairs={{0,1},{1,0},{2,3},{3,2},{4,5},{5,4},{6,7},{7,6},{8,9},{9,8},{10,11... | collective-permute-start | bytes 196616 | tf_op jit(solution)/shard_map/ppermute | solution.py:283
  15.9 9.2 %collective-permute-start.7 = (bf16[32,512]{1,0:T(8,128)(2,1)S(1)}, bf16[32,512]{1,0:T(8,128)(2,1)S(1)}, u32[]{:S(2)}, u32[]{:S(2)}) collective-permute-start(bf16[32,512]{1,0:T(8,128)(2,1)S(1)} %get-tuple-element.47.refs_0_), channel_id=1, source_target_pairs={{0,1},{1,0},{2,3},{3,2},{4,5},{5,4},{6,7},{7,6},{8,9},{9,8},{10,11... | collective-permute-start | bytes 98312 | tf_op jit(solution)/shard_map/ppermute | solution.py:283
  17.1 8.1 %collective-permute-start.8 = (bf16[32,512]{1,0:T(8,128)(2,1)S(1)}, bf16[32,512]{1,0:T(8,128)(2,1)S(1)}, u32[]{:S(2)}, u32[]{:S(2)}) collective-permute-start(bf16[32,512]{1,0:T(8,128)(2,1)S(1)} %get-tuple-element.47.refs_0_), channel_id=1, source_target_pairs={{0,3},{1,2},{2,1},{3,0},{4,7},{5,6},{6,5},{7,4},{8,11},{9,10},{10,... | collective-permute-start | bytes 98312 | tf_op jit(solution)/shard_map/ppermute | solution.py:283
  19.5 5.6 %collective-permute-start.9 = (bf16[32,512]{1,0:T(8,128)(2,1)S(1)}, bf16[32,512]{1,0:T(8,128)(2,1)S(1)}, u32[]{:S(2)}, u32[]{:S(2)}) collective-permute-start(bf16[32,512]{1,0:T(8,128)(2,1)S(1)} %get-tuple-element.47.refs_0_), channel_id=1, source_target_pairs={{0,2},{1,3},{2,0},{3,1},{4,6},{5,7},{6,4},{7,5},{8,10},{9,11},{10,... | collective-permute-start | bytes 98312 | tf_op jit(solution)/shard_map/ppermute | solution.py:283
  21.6 6.0 %collective-permute-start.10 = (bf16[32,512]{1,0:T(8,128)(2,1)S(1)}, bf16[32,512]{1,0:T(8,128)(2,1)S(1)}, u32[]{:S(2)}, u32[]{:S(2)}) collective-permute-start(bf16[32,512]{1,0:T(8,128)(2,1)S(1)} %get-tuple-element.51.refs_0_), channel_id=1, source_target_pairs={{0,2},{1,3},{2,0},{3,1},{4,6},{5,7},{6,4},{7,5},{8,10},{9,11},{10,... | collective-permute-start | bytes 98312 | tf_op jit(solution)/shard_map/ppermute | solution.py:283
  22.7 5.8 %collective-permute-start.11 = (bf16[32,512]{1,0:T(8,128)(2,1)S(1)}, bf16[32,512]{1,0:T(8,128)(2,1)S(1)}, u32[]{:S(2)}, u32[]{:S(2)}) collective-permute-start(bf16[32,512]{1,0:T(8,128)(2,1)S(1)} %get-tuple-element.51.refs_0_), channel_id=1, source_target_pairs={{0,3},{1,2},{2,1},{3,0},{4,7},{5,6},{6,5},{7,4},{8,11},{9,10},{10,... | collective-permute-start | bytes 98312 | tf_op jit(solution)/shard_map/ppermute | solution.py:283
  25.1 3.9 %collective-permute-start.12 = (bf16[32,512]{1,0:T(8,128)(2,1)S(1)}, bf16[32,512]{1,0:T(8,128)(2,1)S(1)}, u32[]{:S(2)}, u32[]{:S(2)}) collective-permute-start(bf16[32,512]{1,0:T(8,128)(2,1)S(1)} %get-tuple-element.51.refs_0_), channel_id=1, source_target_pairs={{0,1},{1,0},{2,3},{3,2},{4,5},{5,4},{6,7},{7,6},{8,9},{9,8},{10,11... | collective-permute-start | bytes 98312 | tf_op jit(solution)/shard_map/ppermute | solution.py:283
  29.3 1.5 %collective-permute-start.13 = (f32[432,128]{1,0:T(8,128)S(1)}, f32[432,128]{1,0:T(8,128)S(1)}, u32[]{:S(2)}, u32[]{:S(2)}) collective-permute-start(f32[432,128]{1,0:T(8,128)S(1)} %get-tuple-element.53), channel_id=1, source_target_pairs={{0,4},{4,0},{8,12},{12,8},{16,20},{20,16},{24,28},{28,24},{1,5},{5... | collective-permute-start | bytes 663560 | tf_op jit(solution)/shard_map/ppermute | solution.py:371
  30.9 6.5 %collective-permute-start.14 = (bf16[432,128]{1,0:T(8,128)(2,1)S(1)}, bf16[432,128]{1,0:T(8,128)(2,1)S(1)}, u32[]{:S(2)}, u32[]{:S(2)}) collective-permute-start(bf16[432,128]{1,0:T(8,128)(2,1)S(1)} %add_convert_fusion), channel_id=1, source_target_pairs={{0,8},{4,12},{8,0},{12,4},{16,24},{20,28},{24,16},{28,20},{1,9},{5... | collective-permute-start | bytes 331784 | tf_op jit(solution)/shard_map/ppermute | solution.py:383
  32.6 7.2 %collective-permute-start.15 = (bf16[432,128]{1,0:T(8,128)(2,1)S(1)}, bf16[432,128]{1,0:T(8,128)(2,1)S(1)}, u32[]{:S(2)}, u32[]{:S(2)}) collective-permute-start(bf16[432,128]{1,0:T(8,128)(2,1)S(1)} %add_convert_fusion), channel_id=1, source_target_pairs={{0,16},{4,20},{8,24},{12,28},{16,0},{20,4},{24,8},{28,12},{1,17},{... | collective-permute-start | bytes 331784 | tf_op jit(solution)/shard_map/ppermute | solution.py:383
  33.9 5.9 %collective-permute-start.16 = (bf16[432,128]{1,0:T(8,128)(2,1)S(1)}, bf16[432,128]{1,0:T(8,128)(2,1)S(1)}, u32[]{:S(2)}, u32[]{:S(2)}) collective-permute-start(bf16[432,128]{1,0:T(8,128)(2,1)S(1)} %add_convert_fusion), channel_id=1, source_target_pairs={{0,24},{4,28},{8,16},{12,20},{16,8},{20,12},{24,0},{28,4},{1,25},{... | collective-permute-start | bytes 331784 | tf_op jit(solution)/shard_map/ppermute | solution.py:383
  34.4 5.4 %collective-permute-start.17 = (bf16[128,512]{1,0:T(8,128)(2,1)S(1)}, bf16[128,512]{1,0:T(8,128)(2,1)S(1)}, u32[]{:S(2)}, u32[]{:S(2)}) collective-permute-start(bf16[128,512]{1,0:T(8,128)(2,1)S(1)} %get-tuple-element.57.grad_ref.one_ref), channel_id=1, source_target_pairs={{4,0},{8,4},{12,8},{16,12},{20,16},{24,20},{28,24},{5,1},{9,5},{13... | collective-permute-start | bytes 393224 | tf_op jit(solution)/shard_map/ppermute | solution.py:387
  39.9 2.0 %collective-permute-start.18 = (f32[432,128]{1,0:T(8,128)S(1)}, f32[432,128]{1,0:T(8,128)S(1)}, u32[]{:S(2)}, u32[]{:S(2)}) collective-permute-start(f32[432,128]{1,0:T(8,128)S(1)} %add_add_fusion.own_ref), channel_id=1, source_target_pairs={{0,4},{4,0},{8,12},{12,8},{16,20},{20,16},{24,28},{28,24},{1,5},{5... | collective-permute-start | bytes 663560 | tf_op jit(solution)/shard_map/ppermute | solution.py:408

commit v8 on v7

--- a/solution.py
+++ b/solution.py
@@ -60,7 +60,10 @@
     zero = jnp.zeros((cb, wid), jnp.float32)
     for a in range(3):
         plane = vol_ref[:, 2 * z + a - 1] if z or a else rim_ref[:, 0]
-        wide_ref[...] = plane.astype(jnp.float32).reshape(cb * hgt, wid)
+        plane = plane.astype(jnp.float32).reshape(cb * hgt, wid)
+        if not (z or a):
+            plane = jnp.where(lax.axis_index("space") == 0, 0.0, plane)
+        wide_ref[...] = plane
         row = [wide_ref[pl.ds(y, cb, stride=hgt), :] for y in range(hgt)]
         cls = [[row[4 * j + r] for j in range(groups)] for r in range(4)]
 
@@ -275,7 +278,10 @@
 
 
 def edge_kernel(w_ref, one_ref, two_ref, done_ref, wide_ref):
-    input_planes([(one_ref[...], two_ref[...])], w_ref, wide_ref, done_ref)
+    two = two_ref[...]
+    inside = lax.axis_index("space") < lax.axis_size("space") - 1
+    two = jnp.where(inside, two.astype(jnp.float32), 0.0).astype(jnp.bfloat16)
+    input_planes([(one_ref[...], two)], w_ref, wide_ref, done_ref)
 
 
 def moved(block, axis, k):
@@ -321,7 +327,7 @@
         scratch_shapes=[pltpu.SemaphoreType.DMA((planes,))],
         compiler_params=params(),
     )(from_hbm(volume))
-    rim = lax.ppermute(edge, "space", [(i, i + 1) for i in range(n_space - 1)])
+    rim = lax.ppermute(edge, "space", [(i, (i + 1) % n_space) for i in range(n_space)])
     for z in reversed(out_planes):
         cols[z], *parts = pl.pallas_call(
             functools.partial(fwd_kernel, n, ob, z),
@@ -384,7 +390,7 @@
                     sent, "space", [(i, i ^ partners[k]) for i in range(n_space)]
                 )
         if r == len(groups) - 1:
-            after = lax.ppermute(grads[0], "space", [(i + 1, i) for i in range(n_space - 1)])
+            after = lax.ppermute(grads[0], "space", [((i + 1) % n_space, i) for i in range(n_space)])
             input_grad = pl.pallas_call(
                 input_kernel,
                 in_specs=[vmem] * 3 + [hbm],

time: 42.8 us -> 40.5 us (0.946)
  starting transfers between devices: 25.4 us -> 22.8 us
    ppermute x2, starting transfers between devices: 3.64 us -> 1.5 us  [the longest x1 1 us: on_device(): lax.ppermute(grads[0], 'space', [((i + 1) % n_space, i) for i in range(n_...]
    ppermute x1, starting transfers between devices: 0.88 us -> 0.17 us  [on_device(): other = lax.ppermute(rows, 'space', [(i, i ^ 1) for i in range(n_space)])]
  transfers between devices with their start and end apart: 19 -> 19, of which waited for: 8 -> 7; matrix products, arithmetic and copies ran while one was open for 0% -> 0% of each run, Pallas kernels for 15% -> 15%
where the time goes in v8:
time: 40.5 us; the launch traced here: 40.4 us
  starting transfers between devices  22.8 us (56%)
  Pallas kernels  8.49 us (21%)
  waiting for transfers between devices  8.23 us (20%)
  between operations  0.77 us (2%)
    ppermute x12, starting transfers between devices, moved(): lax.ppermute(block, axis, [(i, i ^ k if XOR else (i + k) % n) for i in ra...  17.5 us
    ppermute x12, waiting for transfers between devices, moved(): lax.ppermute(block, axis, [(i, i ^ k if XOR else (i + k) % n) for i in ra...  3.76 us
    ppermute x3, starting transfers between devices, on_device(): lax.ppermute(sent, 'space', [(i, i ^ partners[k]) for i in range(n_space)])  3.55 us
    ppermute x3, waiting for transfers between devices, on_device(): lax.ppermute(sent, 'space', [(i, i ^ partners[k]) for i in range(n_space)])  2.51 us
    pallas_call x1, Pallas kernels, on_device(): pl.pallas_call(functools.partial(middle_kernel, n), out_specs=[vmem, vmem...  1.89 us
    pallas_call x1, Pallas kernels, on_device(): pl.pallas_call(input_kernel, in_specs=[vmem] * 3 + [hbm], out_specs=hbm,...  1.69 us
    pallas_call x2, Pallas kernels, on_device(): pl.pallas_call(functools.partial(fwd_kernel, n, ob, z), out_shape=[cols_s...  1.6 us
    ppermute x1, waiting for transfers between devices, on_device(): lax.ppermute(send, 'space', [(i, i ^ 1) for i in range(n_space)])  1.19 us
  transfers between devices with their start and end apart: 19, of which 7 were waited for; matrix products, arithmetic and copies ran while one was open for 0% of the time, Pallas kernels for 15%

profile of v8, /device:TPU:0, one launch (start us, length us, event | category | flops | bytes accessed | tf_op | source)
XLA Modules:
  0.0 40.4 jit_solution(6156784542584084720)
XLA Ops:
  0.6 1.2 %shard_map.59 = (bf16[32,4,16,128]{3,2,1,0:T(8,128)(2,1)S(1)}, bf16[32,1,16,128]{3,2,1,0:T(8,128)(2,1)S(1)}) custom-call(bf16[32,4,16,128]{3,2,1,0:T(8,128)(2,1)} %vol_hbm.1), custom_call_target="tpu_custom_call" | custom-call | tf_op jit(solution)/shard_map/pallas_call | solution.py:323
  1.8 0.5 %collective-permute-start = (bf16[32,1,16,128]{3,2,1,0:T(8,128)(2,1)S(1)}, bf16[32,1,16,128]{3,2,1,0:T(8,128)(2,1)S(1)}, u32[]{:S(2)}, u32[]{:S(2)}) collective-permute-start(bf16[32,1,16,128]{3,2,1,0:T(8,128)(2,1)S(1)} %get-tuple-element.34), channel_id=1, source_target_pairs={{0,4},{4,8},{8,12},{12,16},{16,20},{20,24},{24,28},{28,0},{1,5},{5... | collective-permute-start | bytes 393224 | tf_op jit(solution)/shard_map/ppermute | solution.py:330
  2.3 0.8 %shard_map.62 = (bf16[864,512]{1,0:T(8,128)(2,1)S(1)}, f32[32,512]{1,0:T(8,128)S(1)}, f32[32,512]{1,0:T(8,128)S(1)}, f32[32,512]{1,0:T(8,128)S(1)}, f32[32,512]{1,0:T(8,128)S(1)}) custom-call(bf16[32,4,16,128]{3,2,1,0:T(8,128)(2,1)S(1)} %get-tuple-element.35.refs_1_.refs_0_, bf16[864,128]{1,0:T(8,128)(2,1)S(1)} %bitcast.11), custom_call_target="tpu_custom_call" | custom-call | tf_op jit(solution)/shard_map/pallas_call | solution.py:332
  3.1 4.7 %collective-permute-start.4 = (f32[32,512]{1,0:T(8,128)S(1)}, f32[32,512]{1,0:T(8,128)S(1)}, u32[]{:S(2)}, u32[]{:S(2)}) collective-permute-start(f32[32,512]{1,0:T(8,128)S(1)} %get-tuple-element.42), channel_id=1, source_target_pairs={{0,3},{1,2},{2,1},{3,0},{4,7},{5,6},{6,5},{7,4},{8,11},{9,10},{10,... | collective-permute-start | bytes 196616 | tf_op jit(solution)/shard_map/ppermute | solution.py:289
  7.8 0.6 %collective-permute-start.6 = (f32[32,512]{1,0:T(8,128)S(1)}, f32[32,512]{1,0:T(8,128)S(1)}, u32[]{:S(2)}, u32[]{:S(2)}) collective-permute-start(f32[32,512]{1,0:T(8,128)S(1)} %get-tuple-element.44), channel_id=1, source_target_pairs={{0,1},{1,0},{2,3},{3,2},{4,5},{5,4},{6,7},{7,6},{8,9},{9,8},{10,11... | collective-permute-start | bytes 196616 | tf_op jit(solution)/shard_map/ppermute | solution.py:289
  8.5 0.8 %shard_map.60 = (bf16[864,512]{1,0:T(8,128)(2,1)S(1)}, f32[32,512]{1,0:T(8,128)S(1)}, f32[32,512]{1,0:T(8,128)S(1)}, f32[32,512]{1,0:T(8,128)S(1)}, f32[32,512]{1,0:T(8,128)S(1)}) custom-call(bf16[32,1,16,128]{3,2,1,0:T(8,128)(2,1)S(1)} %collective-permute-done.refs_0_, bf16[32,4,16,128]{3,2,1,0:T(8,128)(2,1)S(1)} %get-tuple-element.35.refs_1_.refs_0_, ...), custom_call_target="tpu_custom_call" | custom-call | tf_op jit(solution)/shard_map/pallas_call | solution.py:332
  9.3 3.8 %collective-permute-start.1 = (f32[32,512]{1,0:T(8,128)S(1)}, f32[32,512]{1,0:T(8,128)S(1)}, u32[]{:S(2)}, u32[]{:S(2)}) collective-permute-start(f32[32,512]{1,0:T(8,128)S(1)} %get-tuple-element.37), channel_id=1, source_target_pairs={{0,3},{1,2},{2,1},{3,0},{4,7},{5,6},{6,5},{7,4},{8,11},{9,10},{10,... | collective-permute-start | bytes 196616 | tf_op jit(solution)/shard_map/ppermute | solution.py:289
  13.1 0.6 %collective-permute-start.3 = (f32[32,512]{1,0:T(8,128)S(1)}, f32[32,512]{1,0:T(8,128)S(1)}, u32[]{:S(2)}, u32[]{:S(2)}) collective-permute-start(f32[32,512]{1,0:T(8,128)S(1)} %get-tuple-element.39), channel_id=1, source_target_pairs={{0,1},{1,0},{2,3},{3,2},{4,5},{5,4},{6,7},{7,6},{8,9},{9,8},{10,11... | collective-permute-start | bytes 196616 | tf_op jit(solution)/shard_map/ppermute | solution.py:289
  13.9 0.3 collective-permute-done.5.rest_2_
  14.2 1.2 %collective-permute-start.7 = (bf16[32,512]{1,0:T(8,128)(2,1)S(1)}, bf16[32,512]{1,0:T(8,128)(2,1)S(1)}, u32[]{:S(2)}, u32[]{:S(2)}) collective-permute-start(bf16[32,512]{1,0:T(8,128)(2,1)S(1)} %get-tuple-element.47.refs_0_), channel_id=1, source_target_pairs={{0,1},{1,0},{2,3},{3,2},{4,5},{5,4},{6,7},{7,6},{8,9},{9,8},{10,11... | collective-permute-start | bytes 98312 | tf_op jit(solution)/shard_map/ppermute | solution.py:289
  15.4 2.4 %collective-permute-start.8 = (bf16[32,512]{1,0:T(8,128)(2,1)S(1)}, bf16[32,512]{1,0:T(8,128)(2,1)S(1)}, u32[]{:S(2)}, u32[]{:S(2)}) collective-permute-start(bf16[32,512]{1,0:T(8,128)(2,1)S(1)} %get-tuple-element.47.refs_0_), channel_id=1, source_target_pairs={{0,3},{1,2},{2,1},{3,0},{4,7},{5,6},{6,5},{7,4},{8,11},{9,10},{10,... | collective-permute-start | bytes 98312 | tf_op jit(solution)/shard_map/ppermute | solution.py:289
  17.8 0.5 %collective-permute-start.9 = (bf16[32,512]{1,0:T(8,128)(2,1)S(1)}, bf16[32,512]{1,0:T(8,128)(2,1)S(1)}, u32[]{:S(2)}, u32[]{:S(2)}) collective-permute-start(bf16[32,512]{1,0:T(8,128)(2,1)S(1)} %get-tuple-element.47.refs_0_), channel_id=1, source_target_pairs={{0,2},{1,3},{2,0},{3,1},{4,6},{5,7},{6,4},{7,5},{8,10},{9,11},{10,... | collective-permute-start | bytes 98312 | tf_op jit(solution)/shard_map/ppermute | solution.py:289
  18.3 1.6 %collective-permute-done.2.rest_2_ = f32[32,512]{1,0:T(8,128)S(1)} collective-permute-done((f32[32,512]{1,0:T(8,128)S(1)}, f32[32,512]{1,0:T(8,128)S(1)}, u32[]{:S(2)}, u32[]{:S(2)}) %collective-permute-start.2) | collective-permute-done | bytes 65568 | tf_op jit(solution)/shard_map/ppermute | solution.py:289
  19.9 0.9 %collective-permute-start.10 = (bf16[32,512]{1,0:T(8,128)(2,1)S(1)}, bf16[32,512]{1,0:T(8,128)(2,1)S(1)}, u32[]{:S(2)}, u32[]{:S(2)}) collective-permute-start(bf16[32,512]{1,0:T(8,128)(2,1)S(1)} %get-tuple-element.51.refs_0_), channel_id=1, source_target_pairs={{0,2},{1,3},{2,0},{3,1},{4,6},{5,7},{6,4},{7,5},{8,10},{9,11},{10,... | collective-permute-start | bytes 98312 | tf_op jit(solution)/shard_map/ppermute | solution.py:289
  20.9 2.5 %collective-permute-start.11 = (bf16[32,512]{1,0:T(8,128)(2,1)S(1)}, bf16[32,512]{1,0:T(8,128)(2,1)S(1)}, u32[]{:S(2)}, u32[]{:S(2)}) collective-permute-start(bf16[32,512]{1,0:T(8,128)(2,1)S(1)} %get-tuple-element.51.refs_0_), channel_id=1, source_target_pairs={{0,3},{1,2},{2,1},{3,0},{4,7},{5,6},{6,5},{7,4},{8,11},{9,10},{10,... | collective-permute-start | bytes 98312 | tf_op jit(solution)/shard_map/ppermute | solution.py:289
  23.4 0.1 collective-permute-start.12
  23.5 1.9 %shard_map.64 = (f32[864,128]{1,0:T(8,128)S(1)}, bf16[128,512]{1,0:T(8,128)(2,1)S(1)}, bf16[32,1,4,32]{3,2,1,0:T(4,128)(2,1)}, bf16[32,4,16,128]{3,2,1,0:T(8,128)(2,1)}) custom-call(bf16[864,128]{1,0:T(8,128)(2,1)S(1)} %bitcast.13, f32[32,512]{1,0:T(8,128)S(1)} %get-tuple-element.40.act_one_ref, f32[32,512]{1,0:T(8,128)S(1)} %get-tuple-element.45.act_two_ref, ...), custom_call_target="tpu_custom_call" | custom-call | tf_op jit(solution)/shard_map/pallas_call | solution.py:354
  25.4 1.3 %collective-permute-done.11.refs_2_ = bf16[32,512]{1,0:T(8,128)(2,1)S(1)} collective-permute-done((bf16[32,512]{1,0:T(8,128)(2,1)S(1)}, bf16[32,512]{1,0:T(8,128)(2,1)S(1)}, u32[]{:S(2)}, u32[]{:S(2)}) %collective-permute-start.11) | collective-permute-done | bytes 32800 | tf_op jit(solution)/shard_map/ppermute | solution.py:289
  26.7 0.6 %collective-permute-done.12.refs_3_ = bf16[32,512]{1,0:T(8,128)(2,1)S(1)} collective-permute-done((bf16[32,512]{1,0:T(8,128)(2,1)S(1)}, bf16[32,512]{1,0:T(8,128)(2,1)S(1)}, u32[]{:S(2)}, u32[]{:S(2)}) %collective-permute-start.12) | collective-permute-done | bytes 32800 | tf_op jit(solution)/shard_map/ppermute | solution.py:289
  27.3 0.3 shard_map.65
  27.7 0.3 shard_map.66
  27.9 1.2 %collective-permute-done.13 = f32[432,128]{1,0:T(8,128)S(1)} collective-permute-done((f32[432,128]{1,0:T(8,128)S(1)}, f32[432,128]{1,0:T(8,128)S(1)}, u32[]{:S(2)}, u32[]{:S(2)}) %collective-permute-start.13) | collective-permute-done | bytes 221216 | tf_op jit(solution)/shard_map/ppermute | solution.py:377
  29.2 1.6 %collective-permute-start.14 = (bf16[432,128]{1,0:T(8,128)(2,1)S(1)}, bf16[432,128]{1,0:T(8,128)(2,1)S(1)}, u32[]{:S(2)}, u32[]{:S(2)}) collective-permute-start(bf16[432,128]{1,0:T(8,128)(2,1)S(1)} %add_convert_fusion), channel_id=1, source_target_pairs={{0,8},{4,12},{8,0},{12,4},{16,24},{20,28},{24,16},{28,20},{1,9},{5... | collective-permute-start | bytes 331784 | tf_op jit(solution)/shard_map/ppermute | solution.py:389
  30.7 1.2 %collective-permute-start.15 = (bf16[432,128]{1,0:T(8,128)(2,1)S(1)}, bf16[432,128]{1,0:T(8,128)(2,1)S(1)}, u32[]{:S(2)}, u32[]{:S(2)}) collective-permute-start(bf16[432,128]{1,0:T(8,128)(2,1)S(1)} %add_convert_fusion), channel_id=1, source_target_pairs={{0,16},{4,20},{8,24},{12,28},{16,0},{20,4},{24,8},{28,12},{1,17},{... | collective-permute-start | bytes 331784 | tf_op jit(solution)/shard_map/ppermute | solution.py:389
  31.9 0.8 %collective-permute-start.16 = (bf16[432,128]{1,0:T(8,128)(2,1)S(1)}, bf16[432,128]{1,0:T(8,128)(2,1)S(1)}, u32[]{:S(2)}, u32[]{:S(2)}) collective-permute-start(bf16[432,128]{1,0:T(8,128)(2,1)S(1)} %add_convert_fusion), channel_id=1, source_target_pairs={{0,24},{4,28},{8,16},{12,20},{16,8},{20,12},{24,0},{28,4},{1,25},{... | collective-permute-start | bytes 331784 | tf_op jit(solution)/shard_map/ppermute | solution.py:389
  32.7 1.0 %collective-permute-start.17 = (bf16[128,512]{1,0:T(8,128)(2,1)S(1)}, bf16[128,512]{1,0:T(8,128)(2,1)S(1)}, u32[]{:S(2)}, u32[]{:S(2)}) collective-permute-start(bf16[128,512]{1,0:T(8,128)(2,1)S(1)} %get-tuple-element.57.grad_ref.one_ref), channel_id=1, source_target_pairs={{4,0},{8,4},{12,8},{16,12},{20,16},{24,20},{28,24},{0,28},{5,1},{9... | collective-permute-start | bytes 393224 | tf_op jit(solution)/shard_map/ppermute | solution.py:393
  33.7 1.7 %shard_map.67._ = bf16[32,4,16,128]{3,2,1,0:T(8,128)(2,1)} custom-call(bf16[864,128]{1,0:T(8,128)(2,1)S(1)} %bitcast.14, bf16[128,512]{1,0:T(8,128)(2,1)S(1)} %get-tuple-element.57.grad_ref.one_ref, bf16[128,512]{1,0:T(8,128)(2,1)S(1)} %get-tuple-element.58.two_ref.one_ref, bf16[32,4,16,128]{3,2,1,0:T(8,128)(2,1)} %get-tuple-element.59._), custom_call_target="tpu_custom_call", output_to_operand_aliasing={{}: (3, {})} | custom-call | tf_op jit(solution)/shard_map/pallas_call | solution.py:394
  35.4 2.5 %collective-permute-done.15 = bf16[432,128]{1,0:T(8,128)(2,1)S(1)} collective-permute-done((bf16[432,128]{1,0:T(8,128)(2,1)S(1)}, bf16[432,128]{1,0:T(8,128)(2,1)S(1)}, u32[]{:S(2)}, u32[]{:S(2)}) %collective-permute-start.15) | collective-permute-done | bytes 110624 | tf_op jit(solution)/shard_map/ppermute | solution.py:389
  38.0 0.2 collective-permute-start.18
  38.2 0.6 %shard_map.68.plane_ref = bf16[1,32,16,128]{3,2,1,0:T(8,128)(2,1)S(1)} custom-call(bf16[864,128]{1,0:T(8,128)(2,1)S(1)} %bitcast.15, bf16[128,512]{1,0:T(8,128)(2,1)S(1)} %get-tuple-element.58.two_ref.one_ref, bf16[128,512]{1,0:T(8,128)(2,1)S(1)} %collective-permute-done.17.two_ref), custom_call_target="tpu_custom_call" | custom-call | tf_op jit(solution)/shard_map/pallas_call | solution.py:408
  38.8 0.8 %collective-permute-done.18.other_ref = f32[432,128]{1,0:T(8,128)S(1)} collective-permute-done((f32[432,128]{1,0:T(8,128)S(1)}, f32[432,128]{1,0:T(8,128)S(1)}, u32[]{:S(2)}, u32[]{:S(2)}) %collective-permute-start.18) | collective-permute-done | bytes 221216 | tf_op jit(solution)/shard_map/ppermute | solution.py:414
  39.5 0.8 %shard_map.69 = (f32[864,128]{1,0:T(8,128)}, bf16[32,4,16,128]{3,2,1,0:T(8,128)(2,1)}) custom-call(f32[432,128]{1,0:T(8,128)S(1)} %add_add_fusion.own_ref, f32[432,128]{1,0:T(8,128)S(1)} %collective-permute-done.18.other_ref, bf16[1,32,16,128]{3,2,1,0:T(8,128)(2,1)S(1)} %shard_map.68.plane_ref, ...), custom_call_target="tpu_custom_call", output_to_operand_aliasing={{1}: (3, {})} | custom-call | tf_op jit(solution)/shard_map/pallas_call | solution.py:415
  (25 shorter events, 0.4 us)
Async XLA Ops:
  0.6 1.7 %copy-start = (bf16[32,3,3,3,128]{4,0,3,2,1:T(8,128)(2,1)S(1)}, bf16[32,3,3,3,128]{4,0,3,2,1:T(8,128)(2,1)}, u32[]{:S(2)}) copy-start(bf16[32,3,3,3,128]{4,0,3,2,1:T(8,128)(2,1)} %param.4) | copy-start | bytes 663556
  1.8 6.6 %collective-permute-start = (bf16[32,1,16,128]{3,2,1,0:T(8,128)(2,1)S(1)}, bf16[32,1,16,128]{3,2,1,0:T(8,128)(2,1)S(1)}, u32[]{:S(2)}, u32[]{:S(2)}) collective-permute-start(bf16[32,1,16,128]{3,2,1,0:T(8,128)(2,1)S(1)} %get-tuple-element.34), channel_id=1, source_target_pairs={{0,4},{4,8},{8,12},{12,16},{16,20},{20,24},{24,28},{28,0},{1,5},{5... | collective-permute-start | bytes 393224 | tf_op jit(solution)/shard_map/ppermute | solution.py:330
  3.1 10.0 %collective-permute-start.4 = (f32[32,512]{1,0:T(8,128)S(1)}, f32[32,512]{1,0:T(8,128)S(1)}, u32[]{:S(2)}, u32[]{:S(2)}) collective-permute-start(f32[32,512]{1,0:T(8,128)S(1)} %get-tuple-element.42), channel_id=1, source_target_pairs={{0,3},{1,2},{2,1},{3,0},{4,7},{5,6},{6,5},{7,4},{8,11},{9,10},{10,... | collective-permute-start | bytes 196616 | tf_op jit(solution)/shard_map/ppermute | solution.py:289
  7.8 6.4 %collective-permute-start.5 = (f32[32,512]{1,0:T(8,128)S(1)}, f32[32,512]{1,0:T(8,128)S(1)}, u32[]{:S(2)}, u32[]{:S(2)}) collective-permute-start(f32[32,512]{1,0:T(8,128)S(1)} %get-tuple-element.43), channel_id=1, source_target_pairs={{0,2},{1,3},{2,0},{3,1},{4,6},{5,7},{6,4},{7,5},{8,10},{9,11},{10,... | collective-permute-start | bytes 196616 | tf_op jit(solution)/shard_map/ppermute | solution.py:289
  7.8 5.9 %copy-start.1 = (bf16[32,1,4,32]{3,2,1,0:T(4,128)(2,1)S(1)}, bf16[32,1,4,32]{3,2,1,0:T(4,128)(2,1)}, u32[]{:S(2)}) copy-start(bf16[32,1,4,32]{3,2,1,0:T(4,128)(2,1)} %param.5) | copy-start | bytes 24580
  7.8 6.4 %collective-permute-start.6 = (f32[32,512]{1,0:T(8,128)S(1)}, f32[32,512]{1,0:T(8,128)S(1)}, u32[]{:S(2)}, u32[]{:S(2)}) collective-permute-start(f32[32,512]{1,0:T(8,128)S(1)} %get-tuple-element.44), channel_id=1, source_target_pairs={{0,1},{1,0},{2,3},{3,2},{4,5},{5,4},{6,7},{7,6},{8,9},{9,8},{10,11... | collective-permute-start | bytes 196616 | tf_op jit(solution)/shard_map/ppermute | solution.py:289
  9.3 8.6 %collective-permute-start.1 = (f32[32,512]{1,0:T(8,128)S(1)}, f32[32,512]{1,0:T(8,128)S(1)}, u32[]{:S(2)}, u32[]{:S(2)}) collective-permute-start(f32[32,512]{1,0:T(8,128)S(1)} %get-tuple-element.37), channel_id=1, source_target_pairs={{0,3},{1,2},{2,1},{3,0},{4,7},{5,6},{6,5},{7,4},{8,11},{9,10},{10,... | collective-permute-start | bytes 196616 | tf_op jit(solution)/shard_map/ppermute | solution.py:289
  13.1 6.8 %collective-permute-start.2 = (f32[32,512]{1,0:T(8,128)S(1)}, f32[32,512]{1,0:T(8,128)S(1)}, u32[]{:S(2)}, u32[]{:S(2)}) collective-permute-start(f32[32,512]{1,0:T(8,128)S(1)} %get-tuple-element.38), channel_id=1, source_target_pairs={{0,2},{1,3},{2,0},{3,1},{4,6},{5,7},{6,4},{7,5},{8,10},{9,11},{10,... | collective-permute-start | bytes 196616 | tf_op jit(solution)/shard_map/ppermute | solution.py:289
  13.1 6.8 %collective-permute-start.3 = (f32[32,512]{1,0:T(8,128)S(1)}, f32[32,512]{1,0:T(8,128)S(1)}, u32[]{:S(2)}, u32[]{:S(2)}) collective-permute-start(f32[32,512]{1,0:T(8,128)S(1)} %get-tuple-element.39), channel_id=1, source_target_pairs={{0,1},{1,0},{2,3},{3,2},{4,5},{5,4},{6,7},{7,6},{8,9},{9,8},{10,11... | collective-permute-start | bytes 196616 | tf_op jit(solution)/shard_map/ppermute | solution.py:289
  14.2 9.2 %collective-permute-start.7 = (bf16[32,512]{1,0:T(8,128)(2,1)S(1)}, bf16[32,512]{1,0:T(8,128)(2,1)S(1)}, u32[]{:S(2)}, u32[]{:S(2)}) collective-permute-start(bf16[32,512]{1,0:T(8,128)(2,1)S(1)} %get-tuple-element.47.refs_0_), channel_id=1, source_target_pairs={{0,1},{1,0},{2,3},{3,2},{4,5},{5,4},{6,7},{7,6},{8,9},{9,8},{10,11... | collective-permute-start | bytes 98312 | tf_op jit(solution)/shard_map/ppermute | solution.py:289
  15.4 8.1 %collective-permute-start.8 = (bf16[32,512]{1,0:T(8,128)(2,1)S(1)}, bf16[32,512]{1,0:T(8,128)(2,1)S(1)}, u32[]{:S(2)}, u32[]{:S(2)}) collective-permute-start(bf16[32,512]{1,0:T(8,128)(2,1)S(1)} %get-tuple-element.47.refs_0_), channel_id=1, source_target_pairs={{0,3},{1,2},{2,1},{3,0},{4,7},{5,6},{6,5},{7,4},{8,11},{9,10},{10,... | collective-permute-start | bytes 98312 | tf_op jit(solution)/shard_map/ppermute | solution.py:289
  17.8 5.7 %collective-permute-start.9 = (bf16[32,512]{1,0:T(8,128)(2,1)S(1)}, bf16[32,512]{1,0:T(8,128)(2,1)S(1)}, u32[]{:S(2)}, u32[]{:S(2)}) collective-permute-start(bf16[32,512]{1,0:T(8,128)(2,1)S(1)} %get-tuple-element.47.refs_0_), channel_id=1, source_target_pairs={{0,2},{1,3},{2,0},{3,1},{4,6},{5,7},{6,4},{7,5},{8,10},{9,11},{10,... | collective-permute-start | bytes 98312 | tf_op jit(solution)/shard_map/ppermute | solution.py:289
  19.9 5.5 %collective-permute-start.10 = (bf16[32,512]{1,0:T(8,128)(2,1)S(1)}, bf16[32,512]{1,0:T(8,128)(2,1)S(1)}, u32[]{:S(2)}, u32[]{:S(2)}) collective-permute-start(bf16[32,512]{1,0:T(8,128)(2,1)S(1)} %get-tuple-element.51.refs_0_), channel_id=1, source_target_pairs={{0,2},{1,3},{2,0},{3,1},{4,6},{5,7},{6,4},{7,5},{8,10},{9,11},{10,... | collective-permute-start | bytes 98312 | tf_op jit(solution)/shard_map/ppermute | solution.py:289
  20.9 5.9 %collective-permute-start.11 = (bf16[32,512]{1,0:T(8,128)(2,1)S(1)}, bf16[32,512]{1,0:T(8,128)(2,1)S(1)}, u32[]{:S(2)}, u32[]{:S(2)}) collective-permute-start(bf16[32,512]{1,0:T(8,128)(2,1)S(1)} %get-tuple-element.51.refs_0_), channel_id=1, source_target_pairs={{0,3},{1,2},{2,1},{3,0},{4,7},{5,6},{6,5},{7,4},{8,11},{9,10},{10,... | collective-permute-start | bytes 98312 | tf_op jit(solution)/shard_map/ppermute | solution.py:289
  23.4 3.9 %collective-permute-start.12 = (bf16[32,512]{1,0:T(8,128)(2,1)S(1)}, bf16[32,512]{1,0:T(8,128)(2,1)S(1)}, u32[]{:S(2)}, u32[]{:S(2)}) collective-permute-start(bf16[32,512]{1,0:T(8,128)(2,1)S(1)} %get-tuple-element.51.refs_0_), channel_id=1, source_target_pairs={{0,1},{1,0},{2,3},{3,2},{4,5},{5,4},{6,7},{7,6},{8,9},{9,8},{10,11... | collective-permute-start | bytes 98312 | tf_op jit(solution)/shard_map/ppermute | solution.py:289
  27.6 1.5 %collective-permute-start.13 = (f32[432,128]{1,0:T(8,128)S(1)}, f32[432,128]{1,0:T(8,128)S(1)}, u32[]{:S(2)}, u32[]{:S(2)}) collective-permute-start(f32[432,128]{1,0:T(8,128)S(1)} %get-tuple-element.53), channel_id=1, source_target_pairs={{0,4},{4,0},{8,12},{12,8},{16,20},{20,16},{24,28},{28,24},{1,5},{5... | collective-permute-start | bytes 663560 | tf_op jit(solution)/shard_map/ppermute | solution.py:377
  29.2 6.2 %collective-permute-start.14 = (bf16[432,128]{1,0:T(8,128)(2,1)S(1)}, bf16[432,128]{1,0:T(8,128)(2,1)S(1)}, u32[]{:S(2)}, u32[]{:S(2)}) collective-permute-start(bf16[432,128]{1,0:T(8,128)(2,1)S(1)} %add_convert_fusion), channel_id=1, source_target_pairs={{0,8},{4,12},{8,0},{12,4},{16,24},{20,28},{24,16},{28,20},{1,9},{5... | collective-permute-start | bytes 331784 | tf_op jit(solution)/shard_map/ppermute | solution.py:389
  30.7 7.2 %collective-permute-start.15 = (bf16[432,128]{1,0:T(8,128)(2,1)S(1)}, bf16[432,128]{1,0:T(8,128)(2,1)S(1)}, u32[]{:S(2)}, u32[]{:S(2)}) collective-permute-start(bf16[432,128]{1,0:T(8,128)(2,1)S(1)} %add_convert_fusion), channel_id=1, source_target_pairs={{0,16},{4,20},{8,24},{12,28},{16,0},{20,4},{24,8},{28,12},{1,17},{... | collective-permute-start | bytes 331784 | tf_op jit(solution)/shard_map/ppermute | solution.py:389
  31.9 6.0 %collective-permute-start.16 = (bf16[432,128]{1,0:T(8,128)(2,1)S(1)}, bf16[432,128]{1,0:T(8,128)(2,1)S(1)}, u32[]{:S(2)}, u32[]{:S(2)}) collective-permute-start(bf16[432,128]{1,0:T(8,128)(2,1)S(1)} %add_convert_fusion), channel_id=1, source_target_pairs={{0,24},{4,28},{8,16},{12,20},{16,8},{20,12},{24,0},{28,4},{1,25},{... | collective-permute-start | bytes 331784 | tf_op jit(solution)/shard_map/ppermute | solution.py:389
  32.7 5.3 %collective-permute-start.17 = (bf16[128,512]{1,0:T(8,128)(2,1)S(1)}, bf16[128,512]{1,0:T(8,128)(2,1)S(1)}, u32[]{:S(2)}, u32[]{:S(2)}) collective-permute-start(bf16[128,512]{1,0:T(8,128)(2,1)S(1)} %get-tuple-element.57.grad_ref.one_ref), channel_id=1, source_target_pairs={{4,0},{8,4},{12,8},{16,12},{20,16},{24,20},{28,24},{0,28},{5,1},{9... | collective-permute-start | bytes 393224 | tf_op jit(solution)/shard_map/ppermute | solution.py:393
  38.0 1.5 %collective-permute-start.18 = (f32[432,128]{1,0:T(8,128)S(1)}, f32[432,128]{1,0:T(8,128)S(1)}, u32[]{:S(2)}, u32[]{:S(2)}) collective-permute-start(f32[432,128]{1,0:T(8,128)S(1)} %add_add_fusion.own_ref), channel_id=1, source_target_pairs={{0,4},{4,0},{8,12},{12,8},{16,20},{20,16},{24,28},{28,24},{1,5},{5... | collective-permute-start | bytes 663560 | tf_op jit(solution)/shard_map/ppermute | solution.py:414

commit v9 on v8

--- a/solution.py
+++ b/solution.py
@@ -34,17 +34,20 @@
 
 
 def load_kernel(vol_hbm, vol_ref, edge_ref, sems):
-    planes = vol_ref.shape[1]
+    cb, planes = vol_ref.shape[:2]
+    pieces = sems.shape[0]
+    size = cb // pieces
     copies = [
-        pltpu.make_async_copy(vol_hbm.at[:, p], vol_ref.at[:, p], sems.at[p])
-        for p in reversed(range(planes))
+        pltpu.make_async_copy(
+            vol_hbm.at[pl.ds(i * size, size)], vol_ref.at[pl.ds(i * size, size)], sems.at[i]
+        )
+        for i in range(pieces)
     ]
     for copy in copies:
         copy.start()
-    copies[0].wait()
+    for copy in copies:
+        copy.wait()
     edge_ref[...] = vol_ref[:, planes - 1 :]
-    for copy in copies[1:]:
-        copy.wait()
 
 
 def fwd_kernel(n, ob, z, *refs):
@@ -58,13 +61,14 @@
     groups = hgt // 4
     sel = pair_matrix(False, wid, wid // 2)
     zero = jnp.zeros((cb, wid), jnp.float32)
+    left, right = [], []
     for a in range(3):
         plane = vol_ref[:, 2 * z + a - 1] if z or a else rim_ref[:, 0]
         plane = plane.astype(jnp.float32).reshape(cb * hgt, wid)
         if not (z or a):
             plane = jnp.where(lax.axis_index("space") == 0, 0.0, plane)
-        wide_ref[...] = plane
-        row = [wide_ref[pl.ds(y, cb, stride=hgt), :] for y in range(hgt)]
+        wide_ref[a * cb * hgt : (a + 1) * cb * hgt, :] = plane
+        row = [wide_ref[pl.ds(a * cb * hgt + y, cb, stride=hgt), :] for y in range(hgt)]
         cls = [[row[4 * j + r] for j in range(groups)] for r in range(4)]
 
         def stack(blocks):
@@ -72,16 +76,23 @@
 
         back = stack([zero] + cls[3][:-1])
         cls = [stack(c) for c in cls]
-        for b, (left, right) in enumerate(((back, cls[1]), (cls[0], cls[2]), (cls[1], cls[3]))):
-            taps = jnp.dot(
-                jnp.concatenate([left, right], axis=1), sel, preferred_element_type=jnp.float32
+        left += [back, cls[0], cls[1]]
+        right += [cls[1], cls[2], cls[3]]
+    taps = jnp.dot(
+        jnp.concatenate([jnp.concatenate(left, axis=0), jnp.concatenate(right, axis=0)], axis=1),
+        sel,
+        preferred_element_type=jnp.float32,
+    ).astype(jnp.bfloat16)
+    for ab in range(9):
+        for e in range(3):
+            tap = ab * 3 + e
+            cols_ref[tap * cb : (tap + 1) * cb, :] = jnp.concatenate(
+                [
+                    taps[(ab * groups + j) * cb : (ab * groups + j + 1) * cb, e * wid : (e + 1) * wid]
+                    for j in range(groups)
+                ],
+                axis=1,
             )
-            for e in range(3):
-                block = taps[:, e * wid : (e + 1) * wid].astype(jnp.bfloat16)
-                tap = (a * 3 + b) * 3 + e
-                cols_ref[tap * cb : (tap + 1) * cb, :] = jnp.concatenate(
-                    [block[j * cb : (j + 1) * cb] for j in range(groups)], axis=1
-                )
     if cols_ref.shape[0] > 27 * cb:
         pad = (cols_ref.shape[0] - 27 * cb, cols_ref.shape[1])
         cols_ref[27 * cb :, :] = jnp.zeros(pad, jnp.bfloat16)
@@ -306,7 +317,7 @@
         spread_kernel, out_shape=shape((ob, cells), f32), compiler_params=params()
     )(up)
 
-    scratch = [pltpu.VMEM((cb * hgt, wid), f32)]
+    scratch = [pltpu.VMEM((3 * cb * hgt, wid), f32)]
     if n > 1:
         scratch.append(pltpu.VMEM((out_ch, cells), f32))
     part_shapes = [shape((ob if direct else out_ch, cells), f32)] * n
@@ -324,7 +335,7 @@
         load_kernel,
         in_specs=[hbm],
         out_shape=[shape(volume.shape, bf16), shape((cb, 1, hgt, wid), bf16)],
-        scratch_shapes=[pltpu.SemaphoreType.DMA((planes,))],
+        scratch_shapes=[pltpu.SemaphoreType.DMA((1,))],
         compiler_params=params(),
     )(from_hbm(volume))
     rim = lax.ppermute(edge, "space", [(i, (i + 1) % n_space) for i in range(n_space)])

time: 40.5 us -> 40.3 us (level)
  no operation moved by 1% of the time
where the time goes in v9:
time: 40.3 us; the launch traced here: 40.1 us
  starting transfers between devices  22.8 us (57%)
  Pallas kernels  8.21 us (20%)
  waiting for transfers between devices  8.19 us (20%)
  between operations  0.77 us (2%)
    ppermute x12, starting transfers between devices, moved(): lax.ppermute(block, axis, [(i, i ^ k if XOR else (i + k) % n) for i in ra...  17.5 us
    ppermute x12, waiting for transfers between devices, moved(): lax.ppermute(block, axis, [(i, i ^ k if XOR else (i + k) % n) for i in ra...  3.77 us
    ppermute x3, starting transfers between devices, on_device(): lax.ppermute(sent, 'space', [(i, i ^ partners[k]) for i in range(n_space)])  3.55 us
    ppermute x3, waiting for transfers between devices, on_device(): lax.ppermute(sent, 'space', [(i, i ^ partners[k]) for i in range(n_space)])  2.45 us
    pallas_call x1, Pallas kernels, on_device(): pl.pallas_call(functools.partial(middle_kernel, n), out_specs=[vmem, vmem...  1.89 us
    pallas_call x1, Pallas kernels, on_device(): pl.pallas_call(input_kernel, in_specs=[vmem] * 3 + [hbm], out_specs=hbm,...  1.68 us
    pallas_call x2, Pallas kernels, on_device(): pl.pallas_call(functools.partial(fwd_kernel, n, ob, z), out_shape=[cols_s...  1.4 us
    ppermute x1, waiting for transfers between devices, on_device(): lax.ppermute(send, 'space', [(i, i ^ 1) for i in range(n_space)])  1.19 us
  transfers between devices with their start and end apart: 19, of which 7 were waited for; matrix products, arithmetic and copies ran while one was open for 0% of the time, Pallas kernels for 15%

profile of v9, /device:TPU:0, one launch (start us, length us, event | category | flops | bytes accessed | tf_op | source)
XLA Modules:
  0.0 40.1 jit_solution(920051496806097310)
XLA Ops:
  0.6 1.1 %shard_map.59 = (bf16[32,4,16,128]{3,2,1,0:T(8,128)(2,1)S(1)}, bf16[32,1,16,128]{3,2,1,0:T(8,128)(2,1)S(1)}) custom-call(bf16[32,4,16,128]{3,2,1,0:T(8,128)(2,1)} %vol_hbm.1), custom_call_target="tpu_custom_call" | custom-call | tf_op jit(solution)/shard_map/pallas_call | solution.py:334
  1.8 0.5 %collective-permute-start = (bf16[32,1,16,128]{3,2,1,0:T(8,128)(2,1)S(1)}, bf16[32,1,16,128]{3,2,1,0:T(8,128)(2,1)S(1)}, u32[]{:S(2)}, u32[]{:S(2)}) collective-permute-start(bf16[32,1,16,128]{3,2,1,0:T(8,128)(2,1)S(1)} %get-tuple-element.34), channel_id=1, source_target_pairs={{0,4},{4,8},{8,12},{12,16},{16,20},{20,24},{24,28},{28,0},{1,5},{5... | collective-permute-start | bytes 393224 | tf_op jit(solution)/shard_map/ppermute | solution.py:341
  2.3 0.7 %shard_map.62 = (bf16[864,512]{1,0:T(8,128)(2,1)S(1)}, f32[32,512]{1,0:T(8,128)S(1)}, f32[32,512]{1,0:T(8,128)S(1)}, f32[32,512]{1,0:T(8,128)S(1)}, f32[32,512]{1,0:T(8,128)S(1)}) custom-call(bf16[32,4,16,128]{3,2,1,0:T(8,128)(2,1)S(1)} %get-tuple-element.35.refs_1_.refs_0_, bf16[864,128]{1,0:T(8,128)(2,1)S(1)} %bitcast.11), custom_call_target="tpu_custom_call" | custom-call | tf_op jit(solution)/shard_map/pallas_call | solution.py:343
  3.0 4.7 %collective-permute-start.4 = (f32[32,512]{1,0:T(8,128)S(1)}, f32[32,512]{1,0:T(8,128)S(1)}, u32[]{:S(2)}, u32[]{:S(2)}) collective-permute-start(f32[32,512]{1,0:T(8,128)S(1)} %get-tuple-element.42), channel_id=1, source_target_pairs={{0,3},{1,2},{2,1},{3,0},{4,7},{5,6},{6,5},{7,4},{8,11},{9,10},{10,... | collective-permute-start | bytes 196616 | tf_op jit(solution)/shard_map/ppermute | solution.py:300
  7.7 0.6 %collective-permute-start.6 = (f32[32,512]{1,0:T(8,128)S(1)}, f32[32,512]{1,0:T(8,128)S(1)}, u32[]{:S(2)}, u32[]{:S(2)}) collective-permute-start(f32[32,512]{1,0:T(8,128)S(1)} %get-tuple-element.44), channel_id=1, source_target_pairs={{0,1},{1,0},{2,3},{3,2},{4,5},{5,4},{6,7},{7,6},{8,9},{9,8},{10,11... | collective-permute-start | bytes 196616 | tf_op jit(solution)/shard_map/ppermute | solution.py:300
  8.3 0.7 %shard_map.60 = (bf16[864,512]{1,0:T(8,128)(2,1)S(1)}, f32[32,512]{1,0:T(8,128)S(1)}, f32[32,512]{1,0:T(8,128)S(1)}, f32[32,512]{1,0:T(8,128)S(1)}, f32[32,512]{1,0:T(8,128)S(1)}) custom-call(bf16[32,1,16,128]{3,2,1,0:T(8,128)(2,1)S(1)} %collective-permute-done.refs_0_, bf16[32,4,16,128]{3,2,1,0:T(8,128)(2,1)S(1)} %get-tuple-element.35.refs_1_.refs_0_, ...), custom_call_target="tpu_custom_call" | custom-call | tf_op jit(solution)/shard_map/pallas_call | solution.py:343
  9.0 3.9 %collective-permute-start.1 = (f32[32,512]{1,0:T(8,128)S(1)}, f32[32,512]{1,0:T(8,128)S(1)}, u32[]{:S(2)}, u32[]{:S(2)}) collective-permute-start(f32[32,512]{1,0:T(8,128)S(1)} %get-tuple-element.37), channel_id=1, source_target_pairs={{0,3},{1,2},{2,1},{3,0},{4,7},{5,6},{6,5},{7,4},{8,11},{9,10},{10,... | collective-permute-start | bytes 196616 | tf_op jit(solution)/shard_map/ppermute | solution.py:300
  12.9 0.7 %collective-permute-start.3 = (f32[32,512]{1,0:T(8,128)S(1)}, f32[32,512]{1,0:T(8,128)S(1)}, u32[]{:S(2)}, u32[]{:S(2)}) collective-permute-start(f32[32,512]{1,0:T(8,128)S(1)} %get-tuple-element.39), channel_id=1, source_target_pairs={{0,1},{1,0},{2,3},{3,2},{4,5},{5,4},{6,7},{7,6},{8,9},{9,8},{10,11... | collective-permute-start | bytes 196616 | tf_op jit(solution)/shard_map/ppermute | solution.py:300
  13.7 0.3 collective-permute-done.5.rest_2_
  14.1 1.2 %collective-permute-start.7 = (bf16[32,512]{1,0:T(8,128)(2,1)S(1)}, bf16[32,512]{1,0:T(8,128)(2,1)S(1)}, u32[]{:S(2)}, u32[]{:S(2)}) collective-permute-start(bf16[32,512]{1,0:T(8,128)(2,1)S(1)} %get-tuple-element.47.refs_0_), channel_id=1, source_target_pairs={{0,1},{1,0},{2,3},{3,2},{4,5},{5,4},{6,7},{7,6},{8,9},{9,8},{10,11... | collective-permute-start | bytes 98312 | tf_op jit(solution)/shard_map/ppermute | solution.py:300
  15.2 2.4 %collective-permute-start.8 = (bf16[32,512]{1,0:T(8,128)(2,1)S(1)}, bf16[32,512]{1,0:T(8,128)(2,1)S(1)}, u32[]{:S(2)}, u32[]{:S(2)}) collective-permute-start(bf16[32,512]{1,0:T(8,128)(2,1)S(1)} %get-tuple-element.47.refs_0_), channel_id=1, source_target_pairs={{0,3},{1,2},{2,1},{3,0},{4,7},{5,6},{6,5},{7,4},{8,11},{9,10},{10,... | collective-permute-start | bytes 98312 | tf_op jit(solution)/shard_map/ppermute | solution.py:300
  17.7 0.5 %collective-permute-start.9 = (bf16[32,512]{1,0:T(8,128)(2,1)S(1)}, bf16[32,512]{1,0:T(8,128)(2,1)S(1)}, u32[]{:S(2)}, u32[]{:S(2)}) collective-permute-start(bf16[32,512]{1,0:T(8,128)(2,1)S(1)} %get-tuple-element.47.refs_0_), channel_id=1, source_target_pairs={{0,2},{1,3},{2,0},{3,1},{4,6},{5,7},{6,4},{7,5},{8,10},{9,11},{10,... | collective-permute-start | bytes 98312 | tf_op jit(solution)/shard_map/ppermute | solution.py:300
  18.2 1.6 %collective-permute-done.2.rest_2_ = f32[32,512]{1,0:T(8,128)S(1)} collective-permute-done((f32[32,512]{1,0:T(8,128)S(1)}, f32[32,512]{1,0:T(8,128)S(1)}, u32[]{:S(2)}, u32[]{:S(2)}) %collective-permute-start.2) | collective-permute-done | bytes 65568 | tf_op jit(solution)/shard_map/ppermute | solution.py:300
  19.8 0.9 %collective-permute-start.10 = (bf16[32,512]{1,0:T(8,128)(2,1)S(1)}, bf16[32,512]{1,0:T(8,128)(2,1)S(1)}, u32[]{:S(2)}, u32[]{:S(2)}) collective-permute-start(bf16[32,512]{1,0:T(8,128)(2,1)S(1)} %get-tuple-element.51.refs_0_), channel_id=1, source_target_pairs={{0,2},{1,3},{2,0},{3,1},{4,6},{5,7},{6,4},{7,5},{8,10},{9,11},{10,... | collective-permute-start | bytes 98312 | tf_op jit(solution)/shard_map/ppermute | solution.py:300
  20.7 2.5 %collective-permute-start.11 = (bf16[32,512]{1,0:T(8,128)(2,1)S(1)}, bf16[32,512]{1,0:T(8,128)(2,1)S(1)}, u32[]{:S(2)}, u32[]{:S(2)}) collective-permute-start(bf16[32,512]{1,0:T(8,128)(2,1)S(1)} %get-tuple-element.51.refs_0_), channel_id=1, source_target_pairs={{0,3},{1,2},{2,1},{3,0},{4,7},{5,6},{6,5},{7,4},{8,11},{9,10},{10,... | collective-permute-start | bytes 98312 | tf_op jit(solution)/shard_map/ppermute | solution.py:300
  23.2 0.1 collective-permute-start.12
  23.4 1.9 %shard_map.64 = (f32[864,128]{1,0:T(8,128)S(1)}, bf16[128,512]{1,0:T(8,128)(2,1)S(1)}, bf16[32,1,4,32]{3,2,1,0:T(4,128)(2,1)}, bf16[32,4,16,128]{3,2,1,0:T(8,128)(2,1)}) custom-call(bf16[864,128]{1,0:T(8,128)(2,1)S(1)} %bitcast.13, f32[32,512]{1,0:T(8,128)S(1)} %get-tuple-element.40.act_one_ref, f32[32,512]{1,0:T(8,128)S(1)} %get-tuple-element.45.act_two_ref, ...), custom_call_target="tpu_custom_call" | custom-call | tf_op jit(solution)/shard_map/pallas_call | solution.py:365
  25.3 1.3 %collective-permute-done.11.refs_2_ = bf16[32,512]{1,0:T(8,128)(2,1)S(1)} collective-permute-done((bf16[32,512]{1,0:T(8,128)(2,1)S(1)}, bf16[32,512]{1,0:T(8,128)(2,1)S(1)}, u32[]{:S(2)}, u32[]{:S(2)}) %collective-permute-start.11) | collective-permute-done | bytes 32800 | tf_op jit(solution)/shard_map/ppermute | solution.py:300
  26.6 0.5 %collective-permute-done.12.refs_3_ = bf16[32,512]{1,0:T(8,128)(2,1)S(1)} collective-permute-done((bf16[32,512]{1,0:T(8,128)(2,1)S(1)}, bf16[32,512]{1,0:T(8,128)(2,1)S(1)}, u32[]{:S(2)}, u32[]{:S(2)}) %collective-permute-start.12) | collective-permute-done | bytes 32800 | tf_op jit(solution)/shard_map/ppermute | solution.py:300
  27.1 0.3 shard_map.65
  27.5 0.3 shard_map.66
  27.8 1.2 %collective-permute-done.13 = f32[432,128]{1,0:T(8,128)S(1)} collective-permute-done((f32[432,128]{1,0:T(8,128)S(1)}, f32[432,128]{1,0:T(8,128)S(1)}, u32[]{:S(2)}, u32[]{:S(2)}) %collective-permute-start.13) | collective-permute-done | bytes 221216 | tf_op jit(solution)/shard_map/ppermute | solution.py:388
  29.0 1.5 %collective-permute-start.14 = (bf16[432,128]{1,0:T(8,128)(2,1)S(1)}, bf16[432,128]{1,0:T(8,128)(2,1)S(1)}, u32[]{:S(2)}, u32[]{:S(2)}) collective-permute-start(bf16[432,128]{1,0:T(8,128)(2,1)S(1)} %add_convert_fusion), channel_id=1, source_target_pairs={{0,8},{4,12},{8,0},{12,4},{16,24},{20,28},{24,16},{28,20},{1,9},{5... | collective-permute-start | bytes 331784 | tf_op jit(solution)/shard_map/ppermute | solution.py:400
  30.5 1.2 %collective-permute-start.15 = (bf16[432,128]{1,0:T(8,128)(2,1)S(1)}, bf16[432,128]{1,0:T(8,128)(2,1)S(1)}, u32[]{:S(2)}, u32[]{:S(2)}) collective-permute-start(bf16[432,128]{1,0:T(8,128)(2,1)S(1)} %add_convert_fusion), channel_id=1, source_target_pairs={{0,16},{4,20},{8,24},{12,28},{16,0},{20,4},{24,8},{28,12},{1,17},{... | collective-permute-start | bytes 331784 | tf_op jit(solution)/shard_map/ppermute | solution.py:400
  31.7 0.8 %collective-permute-start.16 = (bf16[432,128]{1,0:T(8,128)(2,1)S(1)}, bf16[432,128]{1,0:T(8,128)(2,1)S(1)}, u32[]{:S(2)}, u32[]{:S(2)}) collective-permute-start(bf16[432,128]{1,0:T(8,128)(2,1)S(1)} %add_convert_fusion), channel_id=1, source_target_pairs={{0,24},{4,28},{8,16},{12,20},{16,8},{20,12},{24,0},{28,4},{1,25},{... | collective-permute-start | bytes 331784 | tf_op jit(solution)/shard_map/ppermute | solution.py:400
  32.5 1.0 %collective-permute-start.17 = (bf16[128,512]{1,0:T(8,128)(2,1)S(1)}, bf16[128,512]{1,0:T(8,128)(2,1)S(1)}, u32[]{:S(2)}, u32[]{:S(2)}) collective-permute-start(bf16[128,512]{1,0:T(8,128)(2,1)S(1)} %get-tuple-element.57.grad_ref.one_ref), channel_id=1, source_target_pairs={{4,0},{8,4},{12,8},{16,12},{20,16},{24,20},{28,24},{0,28},{5,1},{9... | collective-permute-start | bytes 393224 | tf_op jit(solution)/shard_map/ppermute | solution.py:404
  33.5 1.7 %shard_map.67._ = bf16[32,4,16,128]{3,2,1,0:T(8,128)(2,1)} custom-call(bf16[864,128]{1,0:T(8,128)(2,1)S(1)} %bitcast.14, bf16[128,512]{1,0:T(8,128)(2,1)S(1)} %get-tuple-element.57.grad_ref.one_ref, bf16[128,512]{1,0:T(8,128)(2,1)S(1)} %get-tuple-element.58.two_ref.one_ref, bf16[32,4,16,128]{3,2,1,0:T(8,128)(2,1)} %get-tuple-element.59._), custom_call_target="tpu_custom_call", output_to_operand_aliasing={{}: (3, {})} | custom-call | tf_op jit(solution)/shard_map/pallas_call | solution.py:405
  35.2 2.4 %collective-permute-done.15 = bf16[432,128]{1,0:T(8,128)(2,1)S(1)} collective-permute-done((bf16[432,128]{1,0:T(8,128)(2,1)S(1)}, bf16[432,128]{1,0:T(8,128)(2,1)S(1)}, u32[]{:S(2)}, u32[]{:S(2)}) %collective-permute-start.15) | collective-permute-done | bytes 110624 | tf_op jit(solution)/shard_map/ppermute | solution.py:400
  37.7 0.2 collective-permute-start.18
  37.9 0.6 %shard_map.68.plane_ref = bf16[1,32,16,128]{3,2,1,0:T(8,128)(2,1)S(1)} custom-call(bf16[864,128]{1,0:T(8,128)(2,1)S(1)} %bitcast.15, bf16[128,512]{1,0:T(8,128)(2,1)S(1)} %get-tuple-element.58.two_ref.one_ref, bf16[128,512]{1,0:T(8,128)(2,1)S(1)} %collective-permute-done.17.two_ref), custom_call_target="tpu_custom_call" | custom-call | tf_op jit(solution)/shard_map/pallas_call | solution.py:419
  38.5 0.8 %collective-permute-done.18.other_ref = f32[432,128]{1,0:T(8,128)S(1)} collective-permute-done((f32[432,128]{1,0:T(8,128)S(1)}, f32[432,128]{1,0:T(8,128)S(1)}, u32[]{:S(2)}, u32[]{:S(2)}) %collective-permute-start.18) | collective-permute-done | bytes 221216 | tf_op jit(solution)/shard_map/ppermute | solution.py:425
  39.3 0.8 %shard_map.69 = (f32[864,128]{1,0:T(8,128)}, bf16[32,4,16,128]{3,2,1,0:T(8,128)(2,1)}) custom-call(f32[432,128]{1,0:T(8,128)S(1)} %add_add_fusion.own_ref, f32[432,128]{1,0:T(8,128)S(1)} %collective-permute-done.18.other_ref, bf16[1,32,16,128]{3,2,1,0:T(8,128)(2,1)S(1)} %shard_map.68.plane_ref, ...), custom_call_target="tpu_custom_call", output_to_operand_aliasing={{1}: (3, {})} | custom-call | tf_op jit(solution)/shard_map/pallas_call | solution.py:426
  (25 shorter events, 0.4 us)
Async XLA Ops:
  0.6 1.6 %copy-start = (bf16[32,3,3,3,128]{4,0,3,2,1:T(8,128)(2,1)S(1)}, bf16[32,3,3,3,128]{4,0,3,2,1:T(8,128)(2,1)}, u32[]{:S(2)}) copy-start(bf16[32,3,3,3,128]{4,0,3,2,1:T(8,128)(2,1)} %param.4) | copy-start | bytes 663556
  1.8 6.6 %collective-permute-start = (bf16[32,1,16,128]{3,2,1,0:T(8,128)(2,1)S(1)}, bf16[32,1,16,128]{3,2,1,0:T(8,128)(2,1)S(1)}, u32[]{:S(2)}, u32[]{:S(2)}) collective-permute-start(bf16[32,1,16,128]{3,2,1,0:T(8,128)(2,1)S(1)} %get-tuple-element.34), channel_id=1, source_target_pairs={{0,4},{4,8},{8,12},{12,16},{16,20},{20,24},{24,28},{28,0},{1,5},{5... | collective-permute-start | bytes 393224 | tf_op jit(solution)/shard_map/ppermute | solution.py:341
  3.0 10.0 %collective-permute-start.4 = (f32[32,512]{1,0:T(8,128)S(1)}, f32[32,512]{1,0:T(8,128)S(1)}, u32[]{:S(2)}, u32[]{:S(2)}) collective-permute-start(f32[32,512]{1,0:T(8,128)S(1)} %get-tuple-element.42), channel_id=1, source_target_pairs={{0,3},{1,2},{2,1},{3,0},{4,7},{5,6},{6,5},{7,4},{8,11},{9,10},{10,... | collective-permute-start | bytes 196616 | tf_op jit(solution)/shard_map/ppermute | solution.py:300
  7.7 6.4 %collective-permute-start.5 = (f32[32,512]{1,0:T(8,128)S(1)}, f32[32,512]{1,0:T(8,128)S(1)}, u32[]{:S(2)}, u32[]{:S(2)}) collective-permute-start(f32[32,512]{1,0:T(8,128)S(1)} %get-tuple-element.43), channel_id=1, source_target_pairs={{0,2},{1,3},{2,0},{3,1},{4,6},{5,7},{6,4},{7,5},{8,10},{9,11},{10,... | collective-permute-start | bytes 196616 | tf_op jit(solution)/shard_map/ppermute | solution.py:300
  7.7 5.9 %copy-start.1 = (bf16[32,1,4,32]{3,2,1,0:T(4,128)(2,1)S(1)}, bf16[32,1,4,32]{3,2,1,0:T(4,128)(2,1)}, u32[]{:S(2)}) copy-start(bf16[32,1,4,32]{3,2,1,0:T(4,128)(2,1)} %param.5) | copy-start | bytes 24580
  7.7 6.4 %collective-permute-start.6 = (f32[32,512]{1,0:T(8,128)S(1)}, f32[32,512]{1,0:T(8,128)S(1)}, u32[]{:S(2)}, u32[]{:S(2)}) collective-permute-start(f32[32,512]{1,0:T(8,128)S(1)} %get-tuple-element.44), channel_id=1, source_target_pairs={{0,1},{1,0},{2,3},{3,2},{4,5},{5,4},{6,7},{7,6},{8,9},{9,8},{10,11... | collective-permute-start | bytes 196616 | tf_op jit(solution)/shard_map/ppermute | solution.py:300
  9.0 8.7 %collective-permute-start.1 = (f32[32,512]{1,0:T(8,128)S(1)}, f32[32,512]{1,0:T(8,128)S(1)}, u32[]{:S(2)}, u32[]{:S(2)}) collective-permute-start(f32[32,512]{1,0:T(8,128)S(1)} %get-tuple-element.37), channel_id=1, source_target_pairs={{0,3},{1,2},{2,1},{3,0},{4,7},{5,6},{6,5},{7,4},{8,11},{9,10},{10,... | collective-permute-start | bytes 196616 | tf_op jit(solution)/shard_map/ppermute | solution.py:300
  12.9 6.8 %collective-permute-start.2 = (f32[32,512]{1,0:T(8,128)S(1)}, f32[32,512]{1,0:T(8,128)S(1)}, u32[]{:S(2)}, u32[]{:S(2)}) collective-permute-start(f32[32,512]{1,0:T(8,128)S(1)} %get-tuple-element.38), channel_id=1, source_target_pairs={{0,2},{1,3},{2,0},{3,1},{4,6},{5,7},{6,4},{7,5},{8,10},{9,11},{10,... | collective-permute-start | bytes 196616 | tf_op jit(solution)/shard_map/ppermute | solution.py:300
  12.9 6.8 %collective-permute-start.3 = (f32[32,512]{1,0:T(8,128)S(1)}, f32[32,512]{1,0:T(8,128)S(1)}, u32[]{:S(2)}, u32[]{:S(2)}) collective-permute-start(f32[32,512]{1,0:T(8,128)S(1)} %get-tuple-element.39), channel_id=1, source_target_pairs={{0,1},{1,0},{2,3},{3,2},{4,5},{5,4},{6,7},{7,6},{8,9},{9,8},{10,11... | collective-permute-start | bytes 196616 | tf_op jit(solution)/shard_map/ppermute | solution.py:300
  14.1 9.1 %collective-permute-start.7 = (bf16[32,512]{1,0:T(8,128)(2,1)S(1)}, bf16[32,512]{1,0:T(8,128)(2,1)S(1)}, u32[]{:S(2)}, u32[]{:S(2)}) collective-permute-start(bf16[32,512]{1,0:T(8,128)(2,1)S(1)} %get-tuple-element.47.refs_0_), channel_id=1, source_target_pairs={{0,1},{1,0},{2,3},{3,2},{4,5},{5,4},{6,7},{7,6},{8,9},{9,8},{10,11... | collective-permute-start | bytes 98312 | tf_op jit(solution)/shard_map/ppermute | solution.py:300
  15.2 8.1 %collective-permute-start.8 = (bf16[32,512]{1,0:T(8,128)(2,1)S(1)}, bf16[32,512]{1,0:T(8,128)(2,1)S(1)}, u32[]{:S(2)}, u32[]{:S(2)}) collective-permute-start(bf16[32,512]{1,0:T(8,128)(2,1)S(1)} %get-tuple-element.47.refs_0_), channel_id=1, source_target_pairs={{0,3},{1,2},{2,1},{3,0},{4,7},{5,6},{6,5},{7,4},{8,11},{9,10},{10,... | collective-permute-start | bytes 98312 | tf_op jit(solution)/shard_map/ppermute | solution.py:300
  17.7 5.7 %collective-permute-start.9 = (bf16[32,512]{1,0:T(8,128)(2,1)S(1)}, bf16[32,512]{1,0:T(8,128)(2,1)S(1)}, u32[]{:S(2)}, u32[]{:S(2)}) collective-permute-start(bf16[32,512]{1,0:T(8,128)(2,1)S(1)} %get-tuple-element.47.refs_0_), channel_id=1, source_target_pairs={{0,2},{1,3},{2,0},{3,1},{4,6},{5,7},{6,4},{7,5},{8,10},{9,11},{10,... | collective-permute-start | bytes 98312 | tf_op jit(solution)/shard_map/ppermute | solution.py:300
  19.8 5.5 %collective-permute-start.10 = (bf16[32,512]{1,0:T(8,128)(2,1)S(1)}, bf16[32,512]{1,0:T(8,128)(2,1)S(1)}, u32[]{:S(2)}, u32[]{:S(2)}) collective-permute-start(bf16[32,512]{1,0:T(8,128)(2,1)S(1)} %get-tuple-element.51.refs_0_), channel_id=1, source_target_pairs={{0,2},{1,3},{2,0},{3,1},{4,6},{5,7},{6,4},{7,5},{8,10},{9,11},{10,... | collective-permute-start | bytes 98312 | tf_op jit(solution)/shard_map/ppermute | solution.py:300
  20.7 5.9 %collective-permute-start.11 = (bf16[32,512]{1,0:T(8,128)(2,1)S(1)}, bf16[32,512]{1,0:T(8,128)(2,1)S(1)}, u32[]{:S(2)}, u32[]{:S(2)}) collective-permute-start(bf16[32,512]{1,0:T(8,128)(2,1)S(1)} %get-tuple-element.51.refs_0_), channel_id=1, source_target_pairs={{0,3},{1,2},{2,1},{3,0},{4,7},{5,6},{6,5},{7,4},{8,11},{9,10},{10,... | collective-permute-start | bytes 98312 | tf_op jit(solution)/shard_map/ppermute | solution.py:300
  23.2 3.9 %collective-permute-start.12 = (bf16[32,512]{1,0:T(8,128)(2,1)S(1)}, bf16[32,512]{1,0:T(8,128)(2,1)S(1)}, u32[]{:S(2)}, u32[]{:S(2)}) collective-permute-start(bf16[32,512]{1,0:T(8,128)(2,1)S(1)} %get-tuple-element.51.refs_0_), channel_id=1, source_target_pairs={{0,1},{1,0},{2,3},{3,2},{4,5},{5,4},{6,7},{7,6},{8,9},{9,8},{10,11... | collective-permute-start | bytes 98312 | tf_op jit(solution)/shard_map/ppermute | solution.py:300
  27.4 1.5 %collective-permute-start.13 = (f32[432,128]{1,0:T(8,128)S(1)}, f32[432,128]{1,0:T(8,128)S(1)}, u32[]{:S(2)}, u32[]{:S(2)}) collective-permute-start(f32[432,128]{1,0:T(8,128)S(1)} %get-tuple-element.53), channel_id=1, source_target_pairs={{0,4},{4,0},{8,12},{12,8},{16,20},{20,16},{24,28},{28,24},{1,5},{5... | collective-permute-start | bytes 663560 | tf_op jit(solution)/shard_map/ppermute | solution.py:388
  29.0 6.2 %collective-permute-start.14 = (bf16[432,128]{1,0:T(8,128)(2,1)S(1)}, bf16[432,128]{1,0:T(8,128)(2,1)S(1)}, u32[]{:S(2)}, u32[]{:S(2)}) collective-permute-start(bf16[432,128]{1,0:T(8,128)(2,1)S(1)} %add_convert_fusion), channel_id=1, source_target_pairs={{0,8},{4,12},{8,0},{12,4},{16,24},{20,28},{24,16},{28,20},{1,9},{5... | collective-permute-start | bytes 331784 | tf_op jit(solution)/shard_map/ppermute | solution.py:400
  30.5 7.2 %collective-permute-start.15 = (bf16[432,128]{1,0:T(8,128)(2,1)S(1)}, bf16[432,128]{1,0:T(8,128)(2,1)S(1)}, u32[]{:S(2)}, u32[]{:S(2)}) collective-permute-start(bf16[432,128]{1,0:T(8,128)(2,1)S(1)} %add_convert_fusion), channel_id=1, source_target_pairs={{0,16},{4,20},{8,24},{12,28},{16,0},{20,4},{24,8},{28,12},{1,17},{... | collective-permute-start | bytes 331784 | tf_op jit(solution)/shard_map/ppermute | solution.py:400
  31.7 6.0 %collective-permute-start.16 = (bf16[432,128]{1,0:T(8,128)(2,1)S(1)}, bf16[432,128]{1,0:T(8,128)(2,1)S(1)}, u32[]{:S(2)}, u32[]{:S(2)}) collective-permute-start(bf16[432,128]{1,0:T(8,128)(2,1)S(1)} %add_convert_fusion), channel_id=1, source_target_pairs={{0,24},{4,28},{8,16},{12,20},{16,8},{20,12},{24,0},{28,4},{1,25},{... | collective-permute-start | bytes 331784 | tf_op jit(solution)/shard_map/ppermute | solution.py:400
  32.5 5.2 %collective-permute-start.17 = (bf16[128,512]{1,0:T(8,128)(2,1)S(1)}, bf16[128,512]{1,0:T(8,128)(2,1)S(1)}, u32[]{:S(2)}, u32[]{:S(2)}) collective-permute-start(bf16[128,512]{1,0:T(8,128)(2,1)S(1)} %get-tuple-element.57.grad_ref.one_ref), channel_id=1, source_target_pairs={{4,0},{8,4},{12,8},{16,12},{20,16},{24,20},{28,24},{0,28},{5,1},{9... | collective-permute-start | bytes 393224 | tf_op jit(solution)/shard_map/ppermute | solution.py:404
  37.7 1.5 %collective-permute-start.18 = (f32[432,128]{1,0:T(8,128)S(1)}, f32[432,128]{1,0:T(8,128)S(1)}, u32[]{:S(2)}, u32[]{:S(2)}) collective-permute-start(f32[432,128]{1,0:T(8,128)S(1)} %add_add_fusion.own_ref), channel_id=1, source_target_pairs={{0,4},{4,0},{8,12},{12,8},{16,20},{20,16},{24,28},{28,24},{1,5},{5... | collective-permute-start | bytes 663560 | tf_op jit(solution)/shard_map/ppermute | solution.py:425

commit v10 on v9

--- a/solution.py
+++ b/solution.py
@@ -9,9 +9,8 @@
 
 SLOPE = 0.3
 VMEM = 24 * 1024 * 1024
-XOR = True
-RS = {1: (3, 2, 1), 0: (3, 2, 1)}
-AG = {1: (1, 3, 2), 0: (2, 3, 1)}
+RS = {1: ((3, 2, 1, 0), (2, 3, 0, 1), (1, 0, 3, 2)), 0: ((3, 2, 1, 0), (2, 0, 3, 1), (1, 3, 0, 2))}
+AG = {1: ((1, 0, 3, 2), (3, 2, 1, 0), (2, 3, 0, 1)), 0: ((1, 3, 0, 2), (3, 2, 1, 0), (2, 0, 3, 1))}
 CHIPS = (0, 1, 2)
 FEW = 4
 
@@ -48,6 +47,13 @@
     for copy in copies:
         copy.wait()
     edge_ref[...] = vol_ref[:, planes - 1 :]
+
+
+def pick(table, i):
+    value = jnp.int32(table[0])
+    for k, entry in enumerate(table[1:], 1):
+        value = jnp.where(i == k, entry, value)
+    return value
 
 
 def fwd_kernel(n, ob, z, *refs):
@@ -108,8 +114,8 @@
     all_ref = rest[-1]
     all_ref[...] = part
     me = lax.axis_index("chan")
-    for k, ref in zip((0,) + RS[z], part_refs):
-        start = pl.multiple_of((me ^ k if XOR else lax.rem(me + k, n)) * ob, ob)
+    for to, ref in zip((tuple(range(n)),) + RS[z], part_refs):
+        start = pl.multiple_of(pick(to, me) * ob, ob)
         ref[...] = all_ref[pl.ds(start, ob), :]
 
 
@@ -161,8 +167,8 @@
         return
     me = lax.axis_index("chan")
     ob = block_refs[0].shape[0]
-    for k, ref in zip((0,) + AG[z], block_refs):
-        start = pl.multiple_of((me ^ k if XOR else lax.rem(me + n - k, n)) * ob, ob)
+    for to, ref in zip((tuple(range(n)),) + AG[z], block_refs):
+        start = pl.multiple_of(pick([to.index(i) for i in range(n)], me) * ob, ob)
         grad_ref[pl.ds(start, ob), :] = ref[...]
 
 
@@ -205,26 +211,27 @@
     )
 
 
-def join_kernel(own_ref, other_ref, plane_ref, _, out_ref, input_ref, sems):
-    half = own_ref.shape[0]
+def half_copy(ref, out_ref, of, sem):
+    half = ref.shape[0]
+    size = min(half, out_ref.shape[0] - of * half)
+    return pltpu.make_async_copy(ref.at[pl.ds(0, size)], out_ref.at[pl.ds(of * half, size)], sem)
+
+
+def on_core(act):
     for core in range(2):
 
         @pl.when(lax.rem(lax.axis_index("space"), 2) == core)
         def _():
-            copies = plane_copies(plane_ref, input_ref, input_ref.shape[1] - 1, sems)
-            for ref, start in ((own_ref, core * half), (other_ref, (1 - core) * half)):
-                size = min(half, out_ref.shape[0] - start)
-                copies.append(
-                    pltpu.make_async_copy(
-                        ref.at[pl.ds(0, size)],
-                        out_ref.at[pl.ds(start, size)],
-                        sems.at[1 + start // half],
-                    )
-                )
-            for copy in copies:
-                copy.start()
-            for copy in copies:
-                copy.wait()
+            act(core)
+
+
+def join_kernel(other_ref, _, out_ref, sem):
+    def place(core):
+        copy = half_copy(other_ref, out_ref, 1 - core, sem)
+        copy.start()
+        copy.wait()
+
+    on_core(place)
 
 
 def input_planes(todo, w_ref, wide_ref, done_ref):
@@ -288,16 +295,22 @@
         copy.wait()
 
 
-def edge_kernel(w_ref, one_ref, two_ref, done_ref, wide_ref):
+def edge_kernel(w_ref, one_ref, two_ref, own_ref, _, out_ref, wgrad_ref, wide_ref, done_ref, sems):
+    on_core(lambda core: half_copy(own_ref, wgrad_ref, core, sems.at[1]).start())
     two = two_ref[...]
     inside = lax.axis_index("space") < lax.axis_size("space") - 1
     two = jnp.where(inside, two.astype(jnp.float32), 0.0).astype(jnp.bfloat16)
     input_planes([(one_ref[...], two)], w_ref, wide_ref, done_ref)
-
-
-def moved(block, axis, k):
-    n = lax.axis_size(axis)
-    return lax.ppermute(block, axis, [(i, i ^ k if XOR else (i + k) % n) for i in range(n)])
+    copies = plane_copies(done_ref, out_ref, out_ref.shape[1] - 1, sems)
+    for copy in copies:
+        copy.start()
+    on_core(lambda core: half_copy(own_ref, wgrad_ref, core, sems.at[1]).wait())
+    for copy in copies:
+        copy.wait()
+
+
+def moved(block, axis, to):
+    return lax.ppermute(block, axis, list(enumerate(to)))
 
 
 def on_device(volume, kernel, upstream):
@@ -305,7 +318,7 @@
     ob = upstream.shape[0]
     out_ch = kernel.shape[4]
     n_chan, n_space = lax.axis_size("chan"), lax.axis_size("space")
-    direct = n_chan <= FEW and n_chan & (n_chan - 1) == 0
+    direct = n_chan == FEW
     n = n_chan if direct else 1
     taps = 27 * cb
     cells = hgt // 4 * wid
@@ -347,7 +360,7 @@
             compiler_params=params(),
         )(*(() if z else (rim,)), vol, weights)
         if direct:
-            parts = parts[:1] + [moved(p, "chan", k) for k, p in zip(RS[z], parts[1:])]
+            parts = parts[:1] + [moved(p, "chan", to) for to, p in zip(RS[z], parts[1:])]
         else:
             parts = [lax.psum_scatter(parts[0], "chan", scatter_dimension=0, tiled=True)]
         own, acts[z] = pl.pallas_call(
@@ -356,7 +369,7 @@
             compiler_params=params(),
         )(spread, *parts)
         if direct:
-            grads[z] = [own] + [moved(own, "chan", k) for k in AG[z]]
+            grads[z] = [own] + [moved(own, "chan", to) for to in AG[z]]
         else:
             grads[z] = [lax.all_gather(own, "chan", axis=0, tiled=True)]
 
@@ -416,22 +429,25 @@
             terms = [a + b for a, b in zip(terms[::2], terms[1::2])]
         rows = terms[0]
     rows, input_grad, after = lax.optimization_barrier((rows, input_grad, after))
-    edge = pl.pallas_call(
+    input_grad, weight_grad = pl.pallas_call(
         edge_kernel,
-        out_shape=shape((1,) + plane, bf16),
-        scratch_shapes=[wide],
-        compiler_params=params(),
-    )(weights, grads[1], after)
+        in_specs=[vmem] * 4 + [hbm],
+        out_specs=[hbm] * 2,
+        out_shape=[shape(volume.shape, bf16), shape((taps, out_ch), f32)],
+        scratch_shapes=[wide, pltpu.VMEM((1,) + plane, bf16), pltpu.SemaphoreType.DMA((2,))],
+        input_output_aliases={4: 0},
+        compiler_params=params(),
+    )(weights, grads[1], after, rows, input_grad)
     other = lax.ppermute(rows, "space", [(i, i ^ 1) for i in range(n_space)])
-    weight_grad, input_grad = pl.pallas_call(
+    weight_grad = pl.pallas_call(
         join_kernel,
-        in_specs=[vmem] * 3 + [hbm],
-        out_specs=[hbm] * 2,
-        out_shape=[shape((taps, out_ch), f32), shape(volume.shape, bf16)],
-        scratch_shapes=[pltpu.SemaphoreType.DMA((3,))],
-        input_output_aliases={3: 1},
-        compiler_params=params(),
-    )(rows, other, edge, input_grad)
+        in_specs=[vmem, hbm],
+        out_specs=hbm,
+        out_shape=shape((taps, out_ch), f32),
+        scratch_shapes=[pltpu.SemaphoreType.DMA],
+        input_output_aliases={1: 0},
+        compiler_params=params(),
+    )(other, weight_grad)
     weight_grad = weight_grad.reshape(3, 3, 3, cb, out_ch).transpose(3, 0, 1, 2, 4)
     return pooled, input_grad, weight_grad
 

time: 40.3 us -> 39.8 us (0.988)
  waiting for transfers between devices: 8.19 us -> 4.94 us
  starting transfers between devices: 22.8 us -> 25.1 us
  Pallas kernels: 8.21 us -> 8.78 us
    ppermute x12, waiting for transfers between devices: 3.77 us -> 1.45 us  [moved(): return lax.ppermute(block, axis, list(enumerate(to)))]
    ppermute x12, starting transfers between devices: 17.5 us -> 19.5 us  [moved(): return lax.ppermute(block, axis, list(enumerate(to)))]
    ppermute x1, waiting for transfers between devices: 0.78 us -> 0.1 us  [on_device(): other = lax.ppermute(rows, 'space', [(i, i ^ 1) for i in range(n_space)])]
    pallas_call x2, Pallas kernels: 1.41 us -> 1.95 us  [the longest x1 1.26 us: on_device(): pl.pallas_call(edge_kernel, in_specs=[vmem] * 4 + [hbm], out_specs=[hbm]...]
  transfers between devices with their start and end apart: 19 -> 19, of which waited for: 7 -> 6; matrix products, arithmetic and copies ran while one was open for 0% -> 0% of each run, Pallas kernels for 15% -> 17%
where the time goes in v10:
time: 39.8 us; the launch traced here: 39.7 us
  starting transfers between devices  25.1 us (63%)
  Pallas kernels  8.78 us (22%)
  waiting for transfers between devices  4.94 us (12%)
  between operations  0.78 us (2%)
    ppermute x12, starting transfers between devices, moved(): return lax.ppermute(block, axis, list(enumerate(to)))  19.5 us
    ppermute x3, starting transfers between devices, on_device(): lax.ppermute(sent, 'space', [(i, i ^ partners[k]) for i in range(n_space)])  3.55 us
    ppermute x3, waiting for transfers between devices, on_device(): lax.ppermute(sent, 'space', [(i, i ^ partners[k]) for i in range(n_space)])  2.2 us
    pallas_call x1, Pallas kernels, on_device(): pl.pallas_call(functools.partial(middle_kernel, n), out_specs=[vmem, vmem...  1.89 us
    pallas_call x1, Pallas kernels, on_device(): pl.pallas_call(input_kernel, in_specs=[vmem] * 3 + [hbm], out_specs=hbm,...  1.69 us
    ppermute x12, waiting for transfers between devices, moved(): return lax.ppermute(block, axis, list(enumerate(to)))  1.45 us
    pallas_call x2, Pallas kernels, on_device(): pl.pallas_call(functools.partial(fwd_kernel, n, ob, z), out_shape=[cols_s...  1.41 us
    ppermute x1, starting transfers between devices, on_device(): lax.ppermute(grads[0], 'space', [((i + 1) % n_space, i) for i in range(n_...  1.29 us
  transfers between devices with their start and end apart: 19, of which 6 were waited for; matrix products, arithmetic and copies ran while one was open for 0% of the time, Pallas kernels for 17%

profile of v10, /device:TPU:0, one launch (start us, length us, event | category | flops | bytes accessed | tf_op | source)
XLA Modules:
  0.0 39.7 jit_solution(7268928349756577625)
XLA Ops:
  0.6 1.1 %shard_map.59 = (bf16[32,4,16,128]{3,2,1,0:T(8,128)(2,1)S(1)}, bf16[32,1,16,128]{3,2,1,0:T(8,128)(2,1)S(1)}) custom-call(bf16[32,4,16,128]{3,2,1,0:T(8,128)(2,1)} %vol_hbm.1), custom_call_target="tpu_custom_call" | custom-call | tf_op jit(solution)/shard_map/pallas_call | solution.py:347
  1.8 0.5 %collective-permute-start = (bf16[32,1,16,128]{3,2,1,0:T(8,128)(2,1)S(1)}, bf16[32,1,16,128]{3,2,1,0:T(8,128)(2,1)S(1)}, u32[]{:S(2)}, u32[]{:S(2)}) collective-permute-start(bf16[32,1,16,128]{3,2,1,0:T(8,128)(2,1)S(1)} %get-tuple-element.34), channel_id=1, source_target_pairs={{0,4},{4,8},{8,12},{12,16},{16,20},{20,24},{24,28},{28,0},{1,5},{5... | collective-permute-start | bytes 393224 | tf_op jit(solution)/shard_map/ppermute | solution.py:354
  2.3 0.7 %shard_map.62 = (bf16[864,512]{1,0:T(8,128)(2,1)S(1)}, f32[32,512]{1,0:T(8,128)S(1)}, f32[32,512]{1,0:T(8,128)S(1)}, f32[32,512]{1,0:T(8,128)S(1)}, f32[32,512]{1,0:T(8,128)S(1)}) custom-call(bf16[32,4,16,128]{3,2,1,0:T(8,128)(2,1)S(1)} %get-tuple-element.35.refs_1_.refs_0_, bf16[864,128]{1,0:T(8,128)(2,1)S(1)} %bitcast.11), custom_call_target="tpu_custom_call" | custom-call | tf_op jit(solution)/shard_map/pallas_call | solution.py:356
  3.0 4.7 %collective-permute-start.4 = (f32[32,512]{1,0:T(8,128)S(1)}, f32[32,512]{1,0:T(8,128)S(1)}, u32[]{:S(2)}, u32[]{:S(2)}) collective-permute-start(f32[32,512]{1,0:T(8,128)S(1)} %get-tuple-element.42), channel_id=1, source_target_pairs={{0,3},{1,2},{2,1},{3,0},{4,7},{5,6},{6,5},{7,4},{8,11},{9,10},{10,... | collective-permute-start | bytes 196616 | tf_op jit(solution)/shard_map/ppermute | solution.py:313
  7.7 0.6 %collective-permute-start.6 = (f32[32,512]{1,0:T(8,128)S(1)}, f32[32,512]{1,0:T(8,128)S(1)}, u32[]{:S(2)}, u32[]{:S(2)}) collective-permute-start(f32[32,512]{1,0:T(8,128)S(1)} %get-tuple-element.44), channel_id=1, source_target_pairs={{0,1},{1,0},{2,3},{3,2},{4,5},{5,4},{6,7},{7,6},{8,9},{9,8},{10,11... | collective-permute-start | bytes 196616 | tf_op jit(solution)/shard_map/ppermute | solution.py:313
  8.3 0.7 %shard_map.60 = (bf16[864,512]{1,0:T(8,128)(2,1)S(1)}, f32[32,512]{1,0:T(8,128)S(1)}, f32[32,512]{1,0:T(8,128)S(1)}, f32[32,512]{1,0:T(8,128)S(1)}, f32[32,512]{1,0:T(8,128)S(1)}) custom-call(bf16[32,1,16,128]{3,2,1,0:T(8,128)(2,1)S(1)} %collective-permute-done.refs_0_, bf16[32,4,16,128]{3,2,1,0:T(8,128)(2,1)S(1)} %get-tuple-element.35.refs_1_.refs_0_, ...), custom_call_target="tpu_custom_call" | custom-call | tf_op jit(solution)/shard_map/pallas_call | solution.py:356
  9.0 3.9 %collective-permute-start.1 = (f32[32,512]{1,0:T(8,128)S(1)}, f32[32,512]{1,0:T(8,128)S(1)}, u32[]{:S(2)}, u32[]{:S(2)}) collective-permute-start(f32[32,512]{1,0:T(8,128)S(1)} %get-tuple-element.37), channel_id=1, source_target_pairs={{0,3},{1,2},{2,1},{3,0},{4,7},{5,6},{6,5},{7,4},{8,11},{9,10},{10,... | collective-permute-start | bytes 196616 | tf_op jit(solution)/shard_map/ppermute | solution.py:313
  12.9 2.0 %collective-permute-start.3 = (f32[32,512]{1,0:T(8,128)S(1)}, f32[32,512]{1,0:T(8,128)S(1)}, u32[]{:S(2)}, u32[]{:S(2)}) collective-permute-start(f32[32,512]{1,0:T(8,128)S(1)} %get-tuple-element.39), channel_id=1, source_target_pairs={{0,1},{1,3},{2,0},{3,2},{4,5},{5,7},{6,4},{7,6},{8,9},{9,11},{10,8... | collective-permute-start | bytes 196616 | tf_op jit(solution)/shard_map/ppermute | solution.py:313
  15.0 0.1 shard_map.58.spread_ref
  15.2 0.5 %collective-permute-start.7 = (bf16[32,512]{1,0:T(8,128)(2,1)S(1)}, bf16[32,512]{1,0:T(8,128)(2,1)S(1)}, u32[]{:S(2)}, u32[]{:S(2)}) collective-permute-start(bf16[32,512]{1,0:T(8,128)(2,1)S(1)} %get-tuple-element.47.refs_0_), channel_id=1, source_target_pairs={{0,1},{1,0},{2,3},{3,2},{4,5},{5,4},{6,7},{7,6},{8,9},{9,8},{10,11... | collective-permute-start | bytes 98312 | tf_op jit(solution)/shard_map/ppermute | solution.py:313
  15.7 1.9 %collective-permute-start.8 = (bf16[32,512]{1,0:T(8,128)(2,1)S(1)}, bf16[32,512]{1,0:T(8,128)(2,1)S(1)}, u32[]{:S(2)}, u32[]{:S(2)}) collective-permute-start(bf16[32,512]{1,0:T(8,128)(2,1)S(1)} %get-tuple-element.47.refs_0_), channel_id=1, source_target_pairs={{0,3},{1,2},{2,1},{3,0},{4,7},{5,6},{6,5},{7,4},{8,11},{9,10},{10,... | collective-permute-start | bytes 98312 | tf_op jit(solution)/shard_map/ppermute | solution.py:313
  17.6 1.1 %collective-permute-start.9 = (bf16[32,512]{1,0:T(8,128)(2,1)S(1)}, bf16[32,512]{1,0:T(8,128)(2,1)S(1)}, u32[]{:S(2)}, u32[]{:S(2)}) collective-permute-start(bf16[32,512]{1,0:T(8,128)(2,1)S(1)} %get-tuple-element.47.refs_0_), channel_id=1, source_target_pairs={{0,2},{1,3},{2,0},{3,1},{4,6},{5,7},{6,4},{7,5},{8,10},{9,11},{10,... | collective-permute-start | bytes 98312 | tf_op jit(solution)/shard_map/ppermute | solution.py:313
  18.7 1.0 %collective-permute-done.3.rest_3_ = f32[32,512]{1,0:T(8,128)S(1)} collective-permute-done((f32[32,512]{1,0:T(8,128)S(1)}, f32[32,512]{1,0:T(8,128)S(1)}, u32[]{:S(2)}, u32[]{:S(2)}) %collective-permute-start.3) | collective-permute-done | bytes 65568 | tf_op jit(solution)/shard_map/ppermute | solution.py:313
  19.8 1.0 %collective-permute-start.10 = (bf16[32,512]{1,0:T(8,128)(2,1)S(1)}, bf16[32,512]{1,0:T(8,128)(2,1)S(1)}, u32[]{:S(2)}, u32[]{:S(2)}) collective-permute-start(bf16[32,512]{1,0:T(8,128)(2,1)S(1)} %get-tuple-element.51.refs_0_), channel_id=1, source_target_pairs={{0,1},{1,3},{2,0},{3,2},{4,5},{5,7},{6,4},{7,6},{8,9},{9,11},{10,8... | collective-permute-start | bytes 98312 | tf_op jit(solution)/shard_map/ppermute | solution.py:313
  20.8 1.7 %collective-permute-start.11 = (bf16[32,512]{1,0:T(8,128)(2,1)S(1)}, bf16[32,512]{1,0:T(8,128)(2,1)S(1)}, u32[]{:S(2)}, u32[]{:S(2)}) collective-permute-start(bf16[32,512]{1,0:T(8,128)(2,1)S(1)} %get-tuple-element.51.refs_0_), channel_id=1, source_target_pairs={{0,3},{1,2},{2,1},{3,0},{4,7},{5,6},{6,5},{7,4},{8,11},{9,10},{10,... | collective-permute-start | bytes 98312 | tf_op jit(solution)/shard_map/ppermute | solution.py:313
  22.5 1.9 %collective-permute-start.12 = (bf16[32,512]{1,0:T(8,128)(2,1)S(1)}, bf16[32,512]{1,0:T(8,128)(2,1)S(1)}, u32[]{:S(2)}, u32[]{:S(2)}) collective-permute-start(bf16[32,512]{1,0:T(8,128)(2,1)S(1)} %get-tuple-element.51.refs_0_), channel_id=1, source_target_pairs={{0,2},{1,0},{2,3},{3,1},{4,6},{5,4},{6,7},{7,5},{8,10},{9,8},{10,1... | collective-permute-start | bytes 98312 | tf_op jit(solution)/shard_map/ppermute | solution.py:313
  24.5 1.9 %shard_map.64 = (f32[864,128]{1,0:T(8,128)S(1)}, bf16[128,512]{1,0:T(8,128)(2,1)S(1)}, bf16[32,1,4,32]{3,2,1,0:T(4,128)(2,1)}, bf16[32,4,16,128]{3,2,1,0:T(8,128)(2,1)}) custom-call(bf16[864,128]{1,0:T(8,128)(2,1)S(1)} %bitcast.13, f32[32,512]{1,0:T(8,128)S(1)} %get-tuple-element.40.act_one_ref, f32[32,512]{1,0:T(8,128)S(1)} %get-tuple-element.45.act_two_ref, ...), custom_call_target="tpu_custom_call" | custom-call | tf_op jit(solution)/shard_map/pallas_call | solution.py:378
  26.4 0.3 collective-permute-done.11.refs_2_
  26.6 0.1 collective-permute-done.12.refs_3_
  26.8 0.3 shard_map.65
  27.1 0.3 shard_map.66
  27.4 1.2 %collective-permute-done.13 = f32[432,128]{1,0:T(8,128)S(1)} collective-permute-done((f32[432,128]{1,0:T(8,128)S(1)}, f32[432,128]{1,0:T(8,128)S(1)}, u32[]{:S(2)}, u32[]{:S(2)}) %collective-permute-start.13) | collective-permute-done | bytes 221216 | tf_op jit(solution)/shard_map/ppermute | solution.py:401
  28.6 1.6 %collective-permute-start.14 = (bf16[432,128]{1,0:T(8,128)(2,1)S(1)}, bf16[432,128]{1,0:T(8,128)(2,1)S(1)}, u32[]{:S(2)}, u32[]{:S(2)}) collective-permute-start(bf16[432,128]{1,0:T(8,128)(2,1)S(1)} %add_convert_fusion), channel_id=1, source_target_pairs={{0,8},{4,12},{8,0},{12,4},{16,24},{20,28},{24,16},{28,20},{1,9},{5... | collective-permute-start | bytes 331784 | tf_op jit(solution)/shard_map/ppermute | solution.py:413
  30.2 1.5 %collective-permute-start.15 = (bf16[432,128]{1,0:T(8,128)(2,1)S(1)}, bf16[432,128]{1,0:T(8,128)(2,1)S(1)}, u32[]{:S(2)}, u32[]{:S(2)}) collective-permute-start(bf16[432,128]{1,0:T(8,128)(2,1)S(1)} %add_convert_fusion), channel_id=1, source_target_pairs={{0,16},{4,20},{8,24},{12,28},{16,0},{20,4},{24,8},{28,12},{1,17},{... | collective-permute-start | bytes 331784 | tf_op jit(solution)/shard_map/ppermute | solution.py:413
  31.7 0.5 %collective-permute-start.16 = (bf16[432,128]{1,0:T(8,128)(2,1)S(1)}, bf16[432,128]{1,0:T(8,128)(2,1)S(1)}, u32[]{:S(2)}, u32[]{:S(2)}) collective-permute-start(bf16[432,128]{1,0:T(8,128)(2,1)S(1)} %add_convert_fusion), channel_id=1, source_target_pairs={{0,24},{4,28},{8,16},{12,20},{16,8},{20,12},{24,0},{28,4},{1,25},{... | collective-permute-start | bytes 331784 | tf_op jit(solution)/shard_map/ppermute | solution.py:413
  32.2 1.3 %collective-permute-start.17 = (bf16[128,512]{1,0:T(8,128)(2,1)S(1)}, bf16[128,512]{1,0:T(8,128)(2,1)S(1)}, u32[]{:S(2)}, u32[]{:S(2)}) collective-permute-start(bf16[128,512]{1,0:T(8,128)(2,1)S(1)} %get-tuple-element.58.grad_ref.one_ref), channel_id=1, source_target_pairs={{4,0},{8,4},{12,8},{16,12},{20,16},{24,20},{28,24},{0,28},{5,1},{9... | collective-permute-start | bytes 393224 | tf_op jit(solution)/shard_map/ppermute | solution.py:417
  33.5 1.7 %shard_map.67._ = bf16[32,4,16,128]{3,2,1,0:T(8,128)(2,1)} custom-call(bf16[864,128]{1,0:T(8,128)(2,1)S(1)} %bitcast.14, bf16[128,512]{1,0:T(8,128)(2,1)S(1)} %get-tuple-element.58.grad_ref.one_ref, bf16[128,512]{1,0:T(8,128)(2,1)S(1)} %get-tuple-element.56.two_ref.one_ref, bf16[32,4,16,128]{3,2,1,0:T(8,128)(2,1)} %get-tuple-element.59._), custom_call_target="tpu_custom_call", output_to_operand_aliasing={{}: (3, {})} | custom-call | tf_op jit(solution)/shard_map/pallas_call | solution.py:418
  35.2 2.2 %collective-permute-done.15 = bf16[432,128]{1,0:T(8,128)(2,1)S(1)} collective-permute-done((bf16[432,128]{1,0:T(8,128)(2,1)S(1)}, bf16[432,128]{1,0:T(8,128)(2,1)S(1)}, u32[]{:S(2)}, u32[]{:S(2)}) %collective-permute-start.15) | collective-permute-done | bytes 110624 | tf_op jit(solution)/shard_map/ppermute | solution.py:413
  37.5 0.2 collective-permute-start.18
  37.6 1.3 %shard_map.68 = (bf16[32,4,16,128]{3,2,1,0:T(8,128)(2,1)}, f32[864,128]{1,0:T(8,128)}) custom-call(bf16[864,128]{1,0:T(8,128)(2,1)S(1)} %bitcast.15, bf16[128,512]{1,0:T(8,128)(2,1)S(1)} %get-tuple-element.56.two_ref.one_ref, bf16[128,512]{1,0:T(8,128)(2,1)S(1)} %collective-permute-done.17.two_ref, ...), custom_call_target="tpu_custom_call", output_to_operand_aliasing={{0}: (4, {})} | custom-call | tf_op jit(solution)/shard_map/pallas_call | solution.py:432
  38.9 0.1 collective-permute-done.18.other_ref
  39.0 0.7 %shard_map.69 = f32[864,128]{1,0:T(8,128)} custom-call(f32[432,128]{1,0:T(8,128)S(1)} %collective-permute-done.18.other_ref, f32[864,128]{1,0:T(8,128)} %get-tuple-element.64._), custom_call_target="tpu_custom_call", output_to_operand_aliasing={{}: (1, {})} | custom-call | tf_op jit(solution)/shard_map/pallas_call | solution.py:442
  (25 shorter events, 0.3 us)
Async XLA Ops:
  0.6 1.6 %copy-start = (bf16[32,3,3,3,128]{4,0,3,2,1:T(8,128)(2,1)S(1)}, bf16[32,3,3,3,128]{4,0,3,2,1:T(8,128)(2,1)}, u32[]{:S(2)}) copy-start(bf16[32,3,3,3,128]{4,0,3,2,1:T(8,128)(2,1)} %param.4) | copy-start | bytes 663556
  1.8 6.6 %collective-permute-start = (bf16[32,1,16,128]{3,2,1,0:T(8,128)(2,1)S(1)}, bf16[32,1,16,128]{3,2,1,0:T(8,128)(2,1)S(1)}, u32[]{:S(2)}, u32[]{:S(2)}) collective-permute-start(bf16[32,1,16,128]{3,2,1,0:T(8,128)(2,1)S(1)} %get-tuple-element.34), channel_id=1, source_target_pairs={{0,4},{4,8},{8,12},{12,16},{16,20},{20,24},{24,28},{28,0},{1,5},{5... | collective-permute-start | bytes 393224 | tf_op jit(solution)/shard_map/ppermute | solution.py:354
  3.0 9.9 %collective-permute-start.4 = (f32[32,512]{1,0:T(8,128)S(1)}, f32[32,512]{1,0:T(8,128)S(1)}, u32[]{:S(2)}, u32[]{:S(2)}) collective-permute-start(f32[32,512]{1,0:T(8,128)S(1)} %get-tuple-element.42), channel_id=1, source_target_pairs={{0,3},{1,2},{2,1},{3,0},{4,7},{5,6},{6,5},{7,4},{8,11},{9,10},{10,... | collective-permute-start | bytes 196616 | tf_op jit(solution)/shard_map/ppermute | solution.py:313
  7.7 7.4 %collective-permute-start.5 = (f32[32,512]{1,0:T(8,128)S(1)}, f32[32,512]{1,0:T(8,128)S(1)}, u32[]{:S(2)}, u32[]{:S(2)}) collective-permute-start(f32[32,512]{1,0:T(8,128)S(1)} %get-tuple-element.43), channel_id=1, source_target_pairs={{0,2},{1,3},{2,0},{3,1},{4,6},{5,7},{6,4},{7,5},{8,10},{9,11},{10,... | collective-permute-start | bytes 196616 | tf_op jit(solution)/shard_map/ppermute | solution.py:313
  7.7 7.3 %copy-start.1 = (bf16[32,1,4,32]{3,2,1,0:T(4,128)(2,1)S(1)}, bf16[32,1,4,32]{3,2,1,0:T(4,128)(2,1)}, u32[]{:S(2)}) copy-start(bf16[32,1,4,32]{3,2,1,0:T(4,128)(2,1)} %param.5) | copy-start | bytes 24580
  7.7 7.4 %collective-permute-start.6 = (f32[32,512]{1,0:T(8,128)S(1)}, f32[32,512]{1,0:T(8,128)S(1)}, u32[]{:S(2)}, u32[]{:S(2)}) collective-permute-start(f32[32,512]{1,0:T(8,128)S(1)} %get-tuple-element.44), channel_id=1, source_target_pairs={{0,1},{1,0},{2,3},{3,2},{4,5},{5,4},{6,7},{7,6},{8,9},{9,8},{10,11... | collective-permute-start | bytes 196616 | tf_op jit(solution)/shard_map/ppermute | solution.py:313
  9.0 8.6 %collective-permute-start.1 = (f32[32,512]{1,0:T(8,128)S(1)}, f32[32,512]{1,0:T(8,128)S(1)}, u32[]{:S(2)}, u32[]{:S(2)}) collective-permute-start(f32[32,512]{1,0:T(8,128)S(1)} %get-tuple-element.37), channel_id=1, source_target_pairs={{0,3},{1,2},{2,1},{3,0},{4,7},{5,6},{6,5},{7,4},{8,11},{9,10},{10,... | collective-permute-start | bytes 196616 | tf_op jit(solution)/shard_map/ppermute | solution.py:313
  12.9 5.8 %collective-permute-start.2 = (f32[32,512]{1,0:T(8,128)S(1)}, f32[32,512]{1,0:T(8,128)S(1)}, u32[]{:S(2)}, u32[]{:S(2)}) collective-permute-start(f32[32,512]{1,0:T(8,128)S(1)} %get-tuple-element.38), channel_id=1, source_target_pairs={{0,2},{1,0},{2,3},{3,1},{4,6},{5,4},{6,7},{7,5},{8,10},{9,8},{10,1... | collective-permute-start | bytes 196616 | tf_op jit(solution)/shard_map/ppermute | solution.py:313
  12.9 6.8 %collective-permute-start.3 = (f32[32,512]{1,0:T(8,128)S(1)}, f32[32,512]{1,0:T(8,128)S(1)}, u32[]{:S(2)}, u32[]{:S(2)}) collective-permute-start(f32[32,512]{1,0:T(8,128)S(1)} %get-tuple-element.39), channel_id=1, source_target_pairs={{0,1},{1,3},{2,0},{3,2},{4,5},{5,7},{6,4},{7,6},{8,9},{9,11},{10,8... | collective-permute-start | bytes 196616 | tf_op jit(solution)/shard_map/ppermute | solution.py:313
  15.2 7.3 %collective-permute-start.7 = (bf16[32,512]{1,0:T(8,128)(2,1)S(1)}, bf16[32,512]{1,0:T(8,128)(2,1)S(1)}, u32[]{:S(2)}, u32[]{:S(2)}) collective-permute-start(bf16[32,512]{1,0:T(8,128)(2,1)S(1)} %get-tuple-element.47.refs_0_), channel_id=1, source_target_pairs={{0,1},{1,0},{2,3},{3,2},{4,5},{5,4},{6,7},{7,6},{8,9},{9,8},{10,11... | collective-permute-start | bytes 98312 | tf_op jit(solution)/shard_map/ppermute | solution.py:313
  15.7 8.8 %collective-permute-start.8 = (bf16[32,512]{1,0:T(8,128)(2,1)S(1)}, bf16[32,512]{1,0:T(8,128)(2,1)S(1)}, u32[]{:S(2)}, u32[]{:S(2)}) collective-permute-start(bf16[32,512]{1,0:T(8,128)(2,1)S(1)} %get-tuple-element.47.refs_0_), channel_id=1, source_target_pairs={{0,3},{1,2},{2,1},{3,0},{4,7},{5,6},{6,5},{7,4},{8,11},{9,10},{10,... | collective-permute-start | bytes 98312 | tf_op jit(solution)/shard_map/ppermute | solution.py:313
  17.6 6.9 %collective-permute-start.9 = (bf16[32,512]{1,0:T(8,128)(2,1)S(1)}, bf16[32,512]{1,0:T(8,128)(2,1)S(1)}, u32[]{:S(2)}, u32[]{:S(2)}) collective-permute-start(bf16[32,512]{1,0:T(8,128)(2,1)S(1)} %get-tuple-element.47.refs_0_), channel_id=1, source_target_pairs={{0,2},{1,3},{2,0},{3,1},{4,6},{5,7},{6,4},{7,5},{8,10},{9,11},{10,... | collective-permute-start | bytes 98312 | tf_op jit(solution)/shard_map/ppermute | solution.py:313
  19.8 6.6 %collective-permute-start.10 = (bf16[32,512]{1,0:T(8,128)(2,1)S(1)}, bf16[32,512]{1,0:T(8,128)(2,1)S(1)}, u32[]{:S(2)}, u32[]{:S(2)}) collective-permute-start(bf16[32,512]{1,0:T(8,128)(2,1)S(1)} %get-tuple-element.51.refs_0_), channel_id=1, source_target_pairs={{0,1},{1,3},{2,0},{3,2},{4,5},{5,7},{6,4},{7,6},{8,9},{9,11},{10,8... | collective-permute-start | bytes 98312 | tf_op jit(solution)/shard_map/ppermute | solution.py:313
  20.8 5.8 %collective-permute-start.11 = (bf16[32,512]{1,0:T(8,128)(2,1)S(1)}, bf16[32,512]{1,0:T(8,128)(2,1)S(1)}, u32[]{:S(2)}, u32[]{:S(2)}) collective-permute-start(bf16[32,512]{1,0:T(8,128)(2,1)S(1)} %get-tuple-element.51.refs_0_), channel_id=1, source_target_pairs={{0,3},{1,2},{2,1},{3,0},{4,7},{5,6},{6,5},{7,4},{8,11},{9,10},{10,... | collective-permute-start | bytes 98312 | tf_op jit(solution)/shard_map/ppermute | solution.py:313
  22.5 4.3 %collective-permute-start.12 = (bf16[32,512]{1,0:T(8,128)(2,1)S(1)}, bf16[32,512]{1,0:T(8,128)(2,1)S(1)}, u32[]{:S(2)}, u32[]{:S(2)}) collective-permute-start(bf16[32,512]{1,0:T(8,128)(2,1)S(1)} %get-tuple-element.51.refs_0_), channel_id=1, source_target_pairs={{0,2},{1,0},{2,3},{3,1},{4,6},{5,4},{6,7},{7,5},{8,10},{9,8},{10,1... | collective-permute-start | bytes 98312 | tf_op jit(solution)/shard_map/ppermute | solution.py:313
  27.1 1.5 %collective-permute-start.13 = (f32[432,128]{1,0:T(8,128)S(1)}, f32[432,128]{1,0:T(8,128)S(1)}, u32[]{:S(2)}, u32[]{:S(2)}) collective-permute-start(f32[432,128]{1,0:T(8,128)S(1)} %get-tuple-element.53), channel_id=1, source_target_pairs={{0,4},{4,0},{8,12},{12,8},{16,20},{20,16},{24,28},{28,24},{1,5},{5... | collective-permute-start | bytes 663560 | tf_op jit(solution)/shard_map/ppermute | solution.py:401
  28.6 6.5 %collective-permute-start.14 = (bf16[432,128]{1,0:T(8,128)(2,1)S(1)}, bf16[432,128]{1,0:T(8,128)(2,1)S(1)}, u32[]{:S(2)}, u32[]{:S(2)}) collective-permute-start(bf16[432,128]{1,0:T(8,128)(2,1)S(1)} %add_convert_fusion), channel_id=1, source_target_pairs={{0,8},{4,12},{8,0},{12,4},{16,24},{20,28},{24,16},{28,20},{1,9},{5... | collective-permute-start | bytes 331784 | tf_op jit(solution)/shard_map/ppermute | solution.py:413
  30.2 7.2 %collective-permute-start.15 = (bf16[432,128]{1,0:T(8,128)(2,1)S(1)}, bf16[432,128]{1,0:T(8,128)(2,1)S(1)}, u32[]{:S(2)}, u32[]{:S(2)}) collective-permute-start(bf16[432,128]{1,0:T(8,128)(2,1)S(1)} %add_convert_fusion), channel_id=1, source_target_pairs={{0,16},{4,20},{8,24},{12,28},{16,0},{20,4},{24,8},{28,12},{1,17},{... | collective-permute-start | bytes 331784 | tf_op jit(solution)/shard_map/ppermute | solution.py:413
  31.7 5.7 %collective-permute-start.16 = (bf16[432,128]{1,0:T(8,128)(2,1)S(1)}, bf16[432,128]{1,0:T(8,128)(2,1)S(1)}, u32[]{:S(2)}, u32[]{:S(2)}) collective-permute-start(bf16[432,128]{1,0:T(8,128)(2,1)S(1)} %add_convert_fusion), channel_id=1, source_target_pairs={{0,24},{4,28},{8,16},{12,20},{16,8},{20,12},{24,0},{28,4},{1,25},{... | collective-permute-start | bytes 331784 | tf_op jit(solution)/shard_map/ppermute | solution.py:413
  32.2 5.3 %collective-permute-start.17 = (bf16[128,512]{1,0:T(8,128)(2,1)S(1)}, bf16[128,512]{1,0:T(8,128)(2,1)S(1)}, u32[]{:S(2)}, u32[]{:S(2)}) collective-permute-start(bf16[128,512]{1,0:T(8,128)(2,1)S(1)} %get-tuple-element.58.grad_ref.one_ref), channel_id=1, source_target_pairs={{4,0},{8,4},{12,8},{16,12},{20,16},{24,20},{28,24},{0,28},{5,1},{9... | collective-permute-start | bytes 393224 | tf_op jit(solution)/shard_map/ppermute | solution.py:417
  37.5 1.5 %collective-permute-start.18 = (f32[432,128]{1,0:T(8,128)S(1)}, f32[432,128]{1,0:T(8,128)S(1)}, u32[]{:S(2)}, u32[]{:S(2)}) collective-permute-start(f32[432,128]{1,0:T(8,128)S(1)} %add_add_fusion.own_ref), channel_id=1, source_target_pairs={{0,4},{4,0},{8,12},{12,8},{16,20},{20,16},{24,28},{28,24},{1,5},{5... | collective-permute-start | bytes 663560 | tf_op jit(solution)/shard_map/ppermute | solution.py:441

commit v11 on v10

--- a/solution.py
+++ b/solution.py
@@ -198,9 +198,8 @@
     in_order(n, 0, block_refs, grad_ref)
     half = send_ref.shape[0]
     start = pl.multiple_of((1 - lax.rem(lax.axis_index("space"), 2)) * half, 16)
-    send_ref[...] = sum_ref[pl.ds(start, half), :] + weight_term(
-        cols_ref[pl.ds(start, half), :], grad_ref
-    )
+    send = sum_ref[pl.ds(start, half), :] + weight_term(cols_ref[pl.ds(start, half), :], grad_ref)
+    send_ref[...] = send.astype(send_ref.dtype)
 
 
 def keep_kernel(sum_ref, cols_ref, grad_ref, keep_ref):
@@ -389,7 +388,7 @@
     )(weights, acts[0], acts[1], cols[1], *grads[1])
     send, grads[0] = pl.pallas_call(
         functools.partial(send_kernel, n),
-        out_shape=[shape((half, out_ch), f32), grad_shape],
+        out_shape=[shape((half, out_ch), bf16), grad_shape],
         compiler_params=params(),
     )(term, cols[0], *grads[0])
     keep = pl.pallas_call(
@@ -398,7 +397,7 @@
         compiler_params=params(),
     )(term, cols[0], grads[0])
 
-    rows = keep + lax.ppermute(send, "space", [(i, i ^ 1) for i in range(n_space)])
+    rows = keep + lax.ppermute(send, "space", [(i, i ^ 1) for i in range(n_space)]).astype(f32)
     bits = [1 << b for b in range(1, n_space.bit_length() - 1)]
     groups = [bits[i : i + 2] for i in range(0, len(bits), 2)]
     after = None

time: 39.8 us -> 39.7 us (level)
  no operation moved by 1% of the time
where the time goes in v11:
time: 39.7 us; the launch traced here: 39.6 us
  starting transfers between devices  25.1 us (63%)
  Pallas kernels  8.77 us (22%)
  waiting for transfers between devices  4.82 us (12%)
  between operations  0.78 us (2%)
    ppermute x12, starting transfers between devices, moved(): return lax.ppermute(block, axis, list(enumerate(to)))  19.5 us
    ppermute x3, starting transfers between devices, on_device(): lax.ppermute(sent, 'space', [(i, i ^ partners[k]) for i in range(n_space)])  3.55 us
    ppermute x3, waiting for transfers between devices, on_device(): lax.ppermute(sent, 'space', [(i, i ^ partners[k]) for i in range(n_space)])  2.21 us
    pallas_call x1, Pallas kernels, on_device(): pl.pallas_call(functools.partial(middle_kernel, n), out_specs=[vmem, vmem...  1.89 us
    pallas_call x1, Pallas kernels, on_device(): pl.pallas_call(input_kernel, in_specs=[vmem] * 3 + [hbm], out_specs=hbm,...  1.68 us
    ppermute x12, waiting for transfers between devices, moved(): return lax.ppermute(block, axis, list(enumerate(to)))  1.45 us
    pallas_call x2, Pallas kernels, on_device(): pl.pallas_call(functools.partial(fwd_kernel, n, ob, z), out_shape=[cols_s...  1.41 us
    ppermute x1, starting transfers between devices, on_device(): lax.ppermute(grads[0], 'space', [((i + 1) % n_space, i) for i in range(n_...  1.3 us
  transfers between devices with their start and end apart: 19, of which 6 were waited for; matrix products, arithmetic and copies ran while one was open for 0% of the time, Pallas kernels for 17%

profile of v11, /device:TPU:0, one launch (start us, length us, event | category | flops | bytes accessed | tf_op | source)
XLA Modules:
  0.0 39.6 jit_solution(8388705479454765627)
XLA Ops:
  0.6 1.1 %shard_map.59 = (bf16[32,4,16,128]{3,2,1,0:T(8,128)(2,1)S(1)}, bf16[32,1,16,128]{3,2,1,0:T(8,128)(2,1)S(1)}) custom-call(bf16[32,4,16,128]{3,2,1,0:T(8,128)(2,1)} %vol_hbm.1), custom_call_target="tpu_custom_call" | custom-call | tf_op jit(solution)/shard_map/pallas_call | solution.py:346
  1.8 0.5 %collective-permute-start = (bf16[32,1,16,128]{3,2,1,0:T(8,128)(2,1)S(1)}, bf16[32,1,16,128]{3,2,1,0:T(8,128)(2,1)S(1)}, u32[]{:S(2)}, u32[]{:S(2)}) collective-permute-start(bf16[32,1,16,128]{3,2,1,0:T(8,128)(2,1)S(1)} %get-tuple-element.34), channel_id=1, source_target_pairs={{0,4},{4,8},{8,12},{12,16},{16,20},{20,24},{24,28},{28,0},{1,5},{5... | collective-permute-start | bytes 393224 | tf_op jit(solution)/shard_map/ppermute | solution.py:353
  2.3 0.7 %shard_map.62 = (bf16[864,512]{1,0:T(8,128)(2,1)S(1)}, f32[32,512]{1,0:T(8,128)S(1)}, f32[32,512]{1,0:T(8,128)S(1)}, f32[32,512]{1,0:T(8,128)S(1)}, f32[32,512]{1,0:T(8,128)S(1)}) custom-call(bf16[32,4,16,128]{3,2,1,0:T(8,128)(2,1)S(1)} %get-tuple-element.35.refs_1_.refs_0_, bf16[864,128]{1,0:T(8,128)(2,1)S(1)} %bitcast.11), custom_call_target="tpu_custom_call" | custom-call | tf_op jit(solution)/shard_map/pallas_call | solution.py:355
  3.0 4.7 %collective-permute-start.4 = (f32[32,512]{1,0:T(8,128)S(1)}, f32[32,512]{1,0:T(8,128)S(1)}, u32[]{:S(2)}, u32[]{:S(2)}) collective-permute-start(f32[32,512]{1,0:T(8,128)S(1)} %get-tuple-element.42), channel_id=1, source_target_pairs={{0,3},{1,2},{2,1},{3,0},{4,7},{5,6},{6,5},{7,4},{8,11},{9,10},{10,... | collective-permute-start | bytes 196616 | tf_op jit(solution)/shard_map/ppermute | solution.py:312
  7.7 0.6 %collective-permute-start.6 = (f32[32,512]{1,0:T(8,128)S(1)}, f32[32,512]{1,0:T(8,128)S(1)}, u32[]{:S(2)}, u32[]{:S(2)}) collective-permute-start(f32[32,512]{1,0:T(8,128)S(1)} %get-tuple-element.44), channel_id=1, source_target_pairs={{0,1},{1,0},{2,3},{3,2},{4,5},{5,4},{6,7},{7,6},{8,9},{9,8},{10,11... | collective-permute-start | bytes 196616 | tf_op jit(solution)/shard_map/ppermute | solution.py:312
  8.3 0.7 %shard_map.60 = (bf16[864,512]{1,0:T(8,128)(2,1)S(1)}, f32[32,512]{1,0:T(8,128)S(1)}, f32[32,512]{1,0:T(8,128)S(1)}, f32[32,512]{1,0:T(8,128)S(1)}, f32[32,512]{1,0:T(8,128)S(1)}) custom-call(bf16[32,1,16,128]{3,2,1,0:T(8,128)(2,1)S(1)} %collective-permute-done.refs_0_, bf16[32,4,16,128]{3,2,1,0:T(8,128)(2,1)S(1)} %get-tuple-element.35.refs_1_.refs_0_, ...), custom_call_target="tpu_custom_call" | custom-call | tf_op jit(solution)/shard_map/pallas_call | solution.py:355
  9.0 3.9 %collective-permute-start.1 = (f32[32,512]{1,0:T(8,128)S(1)}, f32[32,512]{1,0:T(8,128)S(1)}, u32[]{:S(2)}, u32[]{:S(2)}) collective-permute-start(f32[32,512]{1,0:T(8,128)S(1)} %get-tuple-element.37), channel_id=1, source_target_pairs={{0,3},{1,2},{2,1},{3,0},{4,7},{5,6},{6,5},{7,4},{8,11},{9,10},{10,... | collective-permute-start | bytes 196616 | tf_op jit(solution)/shard_map/ppermute | solution.py:312
  12.9 2.0 %collective-permute-start.3 = (f32[32,512]{1,0:T(8,128)S(1)}, f32[32,512]{1,0:T(8,128)S(1)}, u32[]{:S(2)}, u32[]{:S(2)}) collective-permute-start(f32[32,512]{1,0:T(8,128)S(1)} %get-tuple-element.39), channel_id=1, source_target_pairs={{0,1},{1,3},{2,0},{3,2},{4,5},{5,7},{6,4},{7,6},{8,9},{9,11},{10,8... | collective-permute-start | bytes 196616 | tf_op jit(solution)/shard_map/ppermute | solution.py:312
  15.0 0.1 shard_map.58.spread_ref
  15.2 0.5 %collective-permute-start.7 = (bf16[32,512]{1,0:T(8,128)(2,1)S(1)}, bf16[32,512]{1,0:T(8,128)(2,1)S(1)}, u32[]{:S(2)}, u32[]{:S(2)}) collective-permute-start(bf16[32,512]{1,0:T(8,128)(2,1)S(1)} %get-tuple-element.47.refs_0_), channel_id=1, source_target_pairs={{0,1},{1,0},{2,3},{3,2},{4,5},{5,4},{6,7},{7,6},{8,9},{9,8},{10,11... | collective-permute-start | bytes 98312 | tf_op jit(solution)/shard_map/ppermute | solution.py:312
  15.7 1.9 %collective-permute-start.8 = (bf16[32,512]{1,0:T(8,128)(2,1)S(1)}, bf16[32,512]{1,0:T(8,128)(2,1)S(1)}, u32[]{:S(2)}, u32[]{:S(2)}) collective-permute-start(bf16[32,512]{1,0:T(8,128)(2,1)S(1)} %get-tuple-element.47.refs_0_), channel_id=1, source_target_pairs={{0,3},{1,2},{2,1},{3,0},{4,7},{5,6},{6,5},{7,4},{8,11},{9,10},{10,... | collective-permute-start | bytes 98312 | tf_op jit(solution)/shard_map/ppermute | solution.py:312
  17.6 1.1 %collective-permute-start.9 = (bf16[32,512]{1,0:T(8,128)(2,1)S(1)}, bf16[32,512]{1,0:T(8,128)(2,1)S(1)}, u32[]{:S(2)}, u32[]{:S(2)}) collective-permute-start(bf16[32,512]{1,0:T(8,128)(2,1)S(1)} %get-tuple-element.47.refs_0_), channel_id=1, source_target_pairs={{0,2},{1,3},{2,0},{3,1},{4,6},{5,7},{6,4},{7,5},{8,10},{9,11},{10,... | collective-permute-start | bytes 98312 | tf_op jit(solution)/shard_map/ppermute | solution.py:312
  18.7 1.0 %collective-permute-done.3.rest_3_ = f32[32,512]{1,0:T(8,128)S(1)} collective-permute-done((f32[32,512]{1,0:T(8,128)S(1)}, f32[32,512]{1,0:T(8,128)S(1)}, u32[]{:S(2)}, u32[]{:S(2)}) %collective-permute-start.3) | collective-permute-done | bytes 65568 | tf_op jit(solution)/shard_map/ppermute | solution.py:312
  19.8 1.0 %collective-permute-start.10 = (bf16[32,512]{1,0:T(8,128)(2,1)S(1)}, bf16[32,512]{1,0:T(8,128)(2,1)S(1)}, u32[]{:S(2)}, u32[]{:S(2)}) collective-permute-start(bf16[32,512]{1,0:T(8,128)(2,1)S(1)} %get-tuple-element.51.refs_0_), channel_id=1, source_target_pairs={{0,1},{1,3},{2,0},{3,2},{4,5},{5,7},{6,4},{7,6},{8,9},{9,11},{10,8... | collective-permute-start | bytes 98312 | tf_op jit(solution)/shard_map/ppermute | solution.py:312
  20.8 1.7 %collective-permute-start.11 = (bf16[32,512]{1,0:T(8,128)(2,1)S(1)}, bf16[32,512]{1,0:T(8,128)(2,1)S(1)}, u32[]{:S(2)}, u32[]{:S(2)}) collective-permute-start(bf16[32,512]{1,0:T(8,128)(2,1)S(1)} %get-tuple-element.51.refs_0_), channel_id=1, source_target_pairs={{0,3},{1,2},{2,1},{3,0},{4,7},{5,6},{6,5},{7,4},{8,11},{9,10},{10,... | collective-permute-start | bytes 98312 | tf_op jit(solution)/shard_map/ppermute | solution.py:312
  22.5 1.9 %collective-permute-start.12 = (bf16[32,512]{1,0:T(8,128)(2,1)S(1)}, bf16[32,512]{1,0:T(8,128)(2,1)S(1)}, u32[]{:S(2)}, u32[]{:S(2)}) collective-permute-start(bf16[32,512]{1,0:T(8,128)(2,1)S(1)} %get-tuple-element.51.refs_0_), channel_id=1, source_target_pairs={{0,2},{1,0},{2,3},{3,1},{4,6},{5,4},{6,7},{7,5},{8,10},{9,8},{10,1... | collective-permute-start | bytes 98312 | tf_op jit(solution)/shard_map/ppermute | solution.py:312
  24.5 1.9 %shard_map.64 = (f32[864,128]{1,0:T(8,128)S(1)}, bf16[128,512]{1,0:T(8,128)(2,1)S(1)}, bf16[32,1,4,32]{3,2,1,0:T(4,128)(2,1)}, bf16[32,4,16,128]{3,2,1,0:T(8,128)(2,1)}) custom-call(bf16[864,128]{1,0:T(8,128)(2,1)S(1)} %bitcast.13, f32[32,512]{1,0:T(8,128)S(1)} %get-tuple-element.40.act_one_ref, f32[32,512]{1,0:T(8,128)S(1)} %get-tuple-element.45.act_two_ref, ...), custom_call_target="tpu_custom_call" | custom-call | tf_op jit(solution)/shard_map/pallas_call | solution.py:377
  26.4 0.3 collective-permute-done.11.refs_2_
  26.6 0.1 collective-permute-done.12.refs_3_
  26.8 0.3 shard_map.65
  27.1 0.3 shard_map.66
  27.4 1.0 %collective-permute-done.13 = bf16[432,128]{1,0:T(8,128)(2,1)S(1)} collective-permute-done((bf16[432,128]{1,0:T(8,128)(2,1)S(1)}, bf16[432,128]{1,0:T(8,128)(2,1)S(1)}, u32[]{:S(2)}, u32[]{:S(2)}) %collective-permute-start.13) | collective-permute-done | bytes 110624 | tf_op jit(solution)/shard_map/ppermute | solution.py:400
  28.5 1.6 %collective-permute-start.14 = (bf16[432,128]{1,0:T(8,128)(2,1)S(1)}, bf16[432,128]{1,0:T(8,128)(2,1)S(1)}, u32[]{:S(2)}, u32[]{:S(2)}) collective-permute-start(bf16[432,128]{1,0:T(8,128)(2,1)S(1)} %add_convert_fusion), channel_id=1, source_target_pairs={{0,8},{4,12},{8,0},{12,4},{16,24},{20,28},{24,16},{28,20},{1,9},{5... | collective-permute-start | bytes 331784 | tf_op jit(solution)/shard_map/ppermute | solution.py:412
  30.0 1.5 %collective-permute-start.15 = (bf16[432,128]{1,0:T(8,128)(2,1)S(1)}, bf16[432,128]{1,0:T(8,128)(2,1)S(1)}, u32[]{:S(2)}, u32[]{:S(2)}) collective-permute-start(bf16[432,128]{1,0:T(8,128)(2,1)S(1)} %add_convert_fusion), channel_id=1, source_target_pairs={{0,16},{4,20},{8,24},{12,28},{16,0},{20,4},{24,8},{28,12},{1,17},{... | collective-permute-start | bytes 331784 | tf_op jit(solution)/shard_map/ppermute | solution.py:412
  31.5 0.5 %collective-permute-start.16 = (bf16[432,128]{1,0:T(8,128)(2,1)S(1)}, bf16[432,128]{1,0:T(8,128)(2,1)S(1)}, u32[]{:S(2)}, u32[]{:S(2)}) collective-permute-start(bf16[432,128]{1,0:T(8,128)(2,1)S(1)} %add_convert_fusion), channel_id=1, source_target_pairs={{0,24},{4,28},{8,16},{12,20},{16,8},{20,12},{24,0},{28,4},{1,25},{... | collective-permute-start | bytes 331784 | tf_op jit(solution)/shard_map/ppermute | solution.py:412
  32.0 1.3 %collective-permute-start.17 = (bf16[128,512]{1,0:T(8,128)(2,1)S(1)}, bf16[128,512]{1,0:T(8,128)(2,1)S(1)}, u32[]{:S(2)}, u32[]{:S(2)}) collective-permute-start(bf16[128,512]{1,0:T(8,128)(2,1)S(1)} %get-tuple-element.58.grad_ref.one_ref), channel_id=1, source_target_pairs={{4,0},{8,4},{12,8},{16,12},{20,16},{24,20},{28,24},{0,28},{5,1},{9... | collective-permute-start | bytes 393224 | tf_op jit(solution)/shard_map/ppermute | solution.py:416
  33.3 1.7 %shard_map.67._ = bf16[32,4,16,128]{3,2,1,0:T(8,128)(2,1)} custom-call(bf16[864,128]{1,0:T(8,128)(2,1)S(1)} %bitcast.14, bf16[128,512]{1,0:T(8,128)(2,1)S(1)} %get-tuple-element.58.grad_ref.one_ref, bf16[128,512]{1,0:T(8,128)(2,1)S(1)} %get-tuple-element.56.two_ref.one_ref, bf16[32,4,16,128]{3,2,1,0:T(8,128)(2,1)} %get-tuple-element.59._), custom_call_target="tpu_custom_call", output_to_operand_aliasing={{}: (3, {})} | custom-call | tf_op jit(solution)/shard_map/pallas_call | solution.py:417
  35.0 2.2 %collective-permute-done.15 = bf16[432,128]{1,0:T(8,128)(2,1)S(1)} collective-permute-done((bf16[432,128]{1,0:T(8,128)(2,1)S(1)}, bf16[432,128]{1,0:T(8,128)(2,1)S(1)}, u32[]{:S(2)}, u32[]{:S(2)}) %collective-permute-start.15) | collective-permute-done | bytes 110624 | tf_op jit(solution)/shard_map/ppermute | solution.py:412
  37.3 0.2 collective-permute-start.18
  37.5 1.3 %shard_map.68 = (bf16[32,4,16,128]{3,2,1,0:T(8,128)(2,1)}, f32[864,128]{1,0:T(8,128)}) custom-call(bf16[864,128]{1,0:T(8,128)(2,1)S(1)} %bitcast.15, bf16[128,512]{1,0:T(8,128)(2,1)S(1)} %get-tuple-element.56.two_ref.one_ref, bf16[128,512]{1,0:T(8,128)(2,1)S(1)} %collective-permute-done.17.two_ref, ...), custom_call_target="tpu_custom_call", output_to_operand_aliasing={{0}: (4, {})} | custom-call | tf_op jit(solution)/shard_map/pallas_call | solution.py:431
  38.7 0.1 collective-permute-done.18.other_ref
  38.9 0.7 %shard_map.69 = f32[864,128]{1,0:T(8,128)} custom-call(f32[432,128]{1,0:T(8,128)S(1)} %collective-permute-done.18.other_ref, f32[864,128]{1,0:T(8,128)} %get-tuple-element.64._), custom_call_target="tpu_custom_call", output_to_operand_aliasing={{}: (1, {})} | custom-call | tf_op jit(solution)/shard_map/pallas_call | solution.py:441
  (25 shorter events, 0.3 us)
Async XLA Ops:
  0.6 1.6 %copy-start = (bf16[32,3,3,3,128]{4,0,3,2,1:T(8,128)(2,1)S(1)}, bf16[32,3,3,3,128]{4,0,3,2,1:T(8,128)(2,1)}, u32[]{:S(2)}) copy-start(bf16[32,3,3,3,128]{4,0,3,2,1:T(8,128)(2,1)} %param.4) | copy-start | bytes 663556
  1.8 6.6 %collective-permute-start = (bf16[32,1,16,128]{3,2,1,0:T(8,128)(2,1)S(1)}, bf16[32,1,16,128]{3,2,1,0:T(8,128)(2,1)S(1)}, u32[]{:S(2)}, u32[]{:S(2)}) collective-permute-start(bf16[32,1,16,128]{3,2,1,0:T(8,128)(2,1)S(1)} %get-tuple-element.34), channel_id=1, source_target_pairs={{0,4},{4,8},{8,12},{12,16},{16,20},{20,24},{24,28},{28,0},{1,5},{5... | collective-permute-start | bytes 393224 | tf_op jit(solution)/shard_map/ppermute | solution.py:353
  3.0 9.9 %collective-permute-start.4 = (f32[32,512]{1,0:T(8,128)S(1)}, f32[32,512]{1,0:T(8,128)S(1)}, u32[]{:S(2)}, u32[]{:S(2)}) collective-permute-start(f32[32,512]{1,0:T(8,128)S(1)} %get-tuple-element.42), channel_id=1, source_target_pairs={{0,3},{1,2},{2,1},{3,0},{4,7},{5,6},{6,5},{7,4},{8,11},{9,10},{10,... | collective-permute-start | bytes 196616 | tf_op jit(solution)/shard_map/ppermute | solution.py:312
  7.7 7.4 %collective-permute-start.5 = (f32[32,512]{1,0:T(8,128)S(1)}, f32[32,512]{1,0:T(8,128)S(1)}, u32[]{:S(2)}, u32[]{:S(2)}) collective-permute-start(f32[32,512]{1,0:T(8,128)S(1)} %get-tuple-element.43), channel_id=1, source_target_pairs={{0,2},{1,3},{2,0},{3,1},{4,6},{5,7},{6,4},{7,5},{8,10},{9,11},{10,... | collective-permute-start | bytes 196616 | tf_op jit(solution)/shard_map/ppermute | solution.py:312
  7.7 7.3 %copy-start.1 = (bf16[32,1,4,32]{3,2,1,0:T(4,128)(2,1)S(1)}, bf16[32,1,4,32]{3,2,1,0:T(4,128)(2,1)}, u32[]{:S(2)}) copy-start(bf16[32,1,4,32]{3,2,1,0:T(4,128)(2,1)} %param.5) | copy-start | bytes 24580
  7.7 7.4 %collective-permute-start.6 = (f32[32,512]{1,0:T(8,128)S(1)}, f32[32,512]{1,0:T(8,128)S(1)}, u32[]{:S(2)}, u32[]{:S(2)}) collective-permute-start(f32[32,512]{1,0:T(8,128)S(1)} %get-tuple-element.44), channel_id=1, source_target_pairs={{0,1},{1,0},{2,3},{3,2},{4,5},{5,4},{6,7},{7,6},{8,9},{9,8},{10,11... | collective-permute-start | bytes 196616 | tf_op jit(solution)/shard_map/ppermute | solution.py:312
  9.0 8.6 %collective-permute-start.1 = (f32[32,512]{1,0:T(8,128)S(1)}, f32[32,512]{1,0:T(8,128)S(1)}, u32[]{:S(2)}, u32[]{:S(2)}) collective-permute-start(f32[32,512]{1,0:T(8,128)S(1)} %get-tuple-element.37), channel_id=1, source_target_pairs={{0,3},{1,2},{2,1},{3,0},{4,7},{5,6},{6,5},{7,4},{8,11},{9,10},{10,... | collective-permute-start | bytes 196616 | tf_op jit(solution)/shard_map/ppermute | solution.py:312
  12.9 5.8 %collective-permute-start.2 = (f32[32,512]{1,0:T(8,128)S(1)}, f32[32,512]{1,0:T(8,128)S(1)}, u32[]{:S(2)}, u32[]{:S(2)}) collective-permute-start(f32[32,512]{1,0:T(8,128)S(1)} %get-tuple-element.38), channel_id=1, source_target_pairs={{0,2},{1,0},{2,3},{3,1},{4,6},{5,4},{6,7},{7,5},{8,10},{9,8},{10,1... | collective-permute-start | bytes 196616 | tf_op jit(solution)/shard_map/ppermute | solution.py:312
  12.9 6.8 %collective-permute-start.3 = (f32[32,512]{1,0:T(8,128)S(1)}, f32[32,512]{1,0:T(8,128)S(1)}, u32[]{:S(2)}, u32[]{:S(2)}) collective-permute-start(f32[32,512]{1,0:T(8,128)S(1)} %get-tuple-element.39), channel_id=1, source_target_pairs={{0,1},{1,3},{2,0},{3,2},{4,5},{5,7},{6,4},{7,6},{8,9},{9,11},{10,8... | collective-permute-start | bytes 196616 | tf_op jit(solution)/shard_map/ppermute | solution.py:312
  15.2 7.3 %collective-permute-start.7 = (bf16[32,512]{1,0:T(8,128)(2,1)S(1)}, bf16[32,512]{1,0:T(8,128)(2,1)S(1)}, u32[]{:S(2)}, u32[]{:S(2)}) collective-permute-start(bf16[32,512]{1,0:T(8,128)(2,1)S(1)} %get-tuple-element.47.refs_0_), channel_id=1, source_target_pairs={{0,1},{1,0},{2,3},{3,2},{4,5},{5,4},{6,7},{7,6},{8,9},{9,8},{10,11... | collective-permute-start | bytes 98312 | tf_op jit(solution)/shard_map/ppermute | solution.py:312
  15.7 8.8 %collective-permute-start.8 = (bf16[32,512]{1,0:T(8,128)(2,1)S(1)}, bf16[32,512]{1,0:T(8,128)(2,1)S(1)}, u32[]{:S(2)}, u32[]{:S(2)}) collective-permute-start(bf16[32,512]{1,0:T(8,128)(2,1)S(1)} %get-tuple-element.47.refs_0_), channel_id=1, source_target_pairs={{0,3},{1,2},{2,1},{3,0},{4,7},{5,6},{6,5},{7,4},{8,11},{9,10},{10,... | collective-permute-start | bytes 98312 | tf_op jit(solution)/shard_map/ppermute | solution.py:312
  17.6 6.9 %collective-permute-start.9 = (bf16[32,512]{1,0:T(8,128)(2,1)S(1)}, bf16[32,512]{1,0:T(8,128)(2,1)S(1)}, u32[]{:S(2)}, u32[]{:S(2)}) collective-permute-start(bf16[32,512]{1,0:T(8,128)(2,1)S(1)} %get-tuple-element.47.refs_0_), channel_id=1, source_target_pairs={{0,2},{1,3},{2,0},{3,1},{4,6},{5,7},{6,4},{7,5},{8,10},{9,11},{10,... | collective-permute-start | bytes 98312 | tf_op jit(solution)/shard_map/ppermute | solution.py:312
  19.8 6.6 %collective-permute-start.10 = (bf16[32,512]{1,0:T(8,128)(2,1)S(1)}, bf16[32,512]{1,0:T(8,128)(2,1)S(1)}, u32[]{:S(2)}, u32[]{:S(2)}) collective-permute-start(bf16[32,512]{1,0:T(8,128)(2,1)S(1)} %get-tuple-element.51.refs_0_), channel_id=1, source_target_pairs={{0,1},{1,3},{2,0},{3,2},{4,5},{5,7},{6,4},{7,6},{8,9},{9,11},{10,8... | collective-permute-start | bytes 98312 | tf_op jit(solution)/shard_map/ppermute | solution.py:312
  20.8 5.8 %collective-permute-start.11 = (bf16[32,512]{1,0:T(8,128)(2,1)S(1)}, bf16[32,512]{1,0:T(8,128)(2,1)S(1)}, u32[]{:S(2)}, u32[]{:S(2)}) collective-permute-start(bf16[32,512]{1,0:T(8,128)(2,1)S(1)} %get-tuple-element.51.refs_0_), channel_id=1, source_target_pairs={{0,3},{1,2},{2,1},{3,0},{4,7},{5,6},{6,5},{7,4},{8,11},{9,10},{10,... | collective-permute-start | bytes 98312 | tf_op jit(solution)/shard_map/ppermute | solution.py:312
  22.5 4.3 %collective-permute-start.12 = (bf16[32,512]{1,0:T(8,128)(2,1)S(1)}, bf16[32,512]{1,0:T(8,128)(2,1)S(1)}, u32[]{:S(2)}, u32[]{:S(2)}) collective-permute-start(bf16[32,512]{1,0:T(8,128)(2,1)S(1)} %get-tuple-element.51.refs_0_), channel_id=1, source_target_pairs={{0,2},{1,0},{2,3},{3,1},{4,6},{5,4},{6,7},{7,5},{8,10},{9,8},{10,1... | collective-permute-start | bytes 98312 | tf_op jit(solution)/shard_map/ppermute | solution.py:312
  27.1 1.4 %collective-permute-start.13 = (bf16[432,128]{1,0:T(8,128)(2,1)S(1)}, bf16[432,128]{1,0:T(8,128)(2,1)S(1)}, u32[]{:S(2)}, u32[]{:S(2)}) collective-permute-start(bf16[432,128]{1,0:T(8,128)(2,1)S(1)} %get-tuple-element.53), channel_id=1, source_target_pairs={{0,4},{4,0},{8,12},{12,8},{16,20},{20,16},{24,28},{28,24},{1,5},{5... | collective-permute-start | bytes 331784 | tf_op jit(solution)/shard_map/ppermute | solution.py:400
  28.5 6.5 %collective-permute-start.14 = (bf16[432,128]{1,0:T(8,128)(2,1)S(1)}, bf16[432,128]{1,0:T(8,128)(2,1)S(1)}, u32[]{:S(2)}, u32[]{:S(2)}) collective-permute-start(bf16[432,128]{1,0:T(8,128)(2,1)S(1)} %add_convert_fusion), channel_id=1, source_target_pairs={{0,8},{4,12},{8,0},{12,4},{16,24},{20,28},{24,16},{28,20},{1,9},{5... | collective-permute-start | bytes 331784 | tf_op jit(solution)/shard_map/ppermute | solution.py:412
  30.0 7.2 %collective-permute-start.15 = (bf16[432,128]{1,0:T(8,128)(2,1)S(1)}, bf16[432,128]{1,0:T(8,128)(2,1)S(1)}, u32[]{:S(2)}, u32[]{:S(2)}) collective-permute-start(bf16[432,128]{1,0:T(8,128)(2,1)S(1)} %add_convert_fusion), channel_id=1, source_target_pairs={{0,16},{4,20},{8,24},{12,28},{16,0},{20,4},{24,8},{28,12},{1,17},{... | collective-permute-start | bytes 331784 | tf_op jit(solution)/shard_map/ppermute | solution.py:412
  31.5 5.7 %collective-permute-start.16 = (bf16[432,128]{1,0:T(8,128)(2,1)S(1)}, bf16[432,128]{1,0:T(8,128)(2,1)S(1)}, u32[]{:S(2)}, u32[]{:S(2)}) collective-permute-start(bf16[432,128]{1,0:T(8,128)(2,1)S(1)} %add_convert_fusion), channel_id=1, source_target_pairs={{0,24},{4,28},{8,16},{12,20},{16,8},{20,12},{24,0},{28,4},{1,25},{... | collective-permute-start | bytes 331784 | tf_op jit(solution)/shard_map/ppermute | solution.py:412
  32.0 5.3 %collective-permute-start.17 = (bf16[128,512]{1,0:T(8,128)(2,1)S(1)}, bf16[128,512]{1,0:T(8,128)(2,1)S(1)}, u32[]{:S(2)}, u32[]{:S(2)}) collective-permute-start(bf16[128,512]{1,0:T(8,128)(2,1)S(1)} %get-tuple-element.58.grad_ref.one_ref), channel_id=1, source_target_pairs={{4,0},{8,4},{12,8},{16,12},{20,16},{24,20},{28,24},{0,28},{5,1},{9... | collective-permute-start | bytes 393224 | tf_op jit(solution)/shard_map/ppermute | solution.py:416
  37.3 1.5 %collective-permute-start.18 = (f32[432,128]{1,0:T(8,128)S(1)}, f32[432,128]{1,0:T(8,128)S(1)}, u32[]{:S(2)}, u32[]{:S(2)}) collective-permute-start(f32[432,128]{1,0:T(8,128)S(1)} %add_add_fusion.own_ref), channel_id=1, source_target_pairs={{0,4},{4,0},{8,12},{12,8},{16,20},{20,16},{24,28},{28,24},{1,5},{5... | collective-permute-start | bytes 663560 | tf_op jit(solution)/shard_map/ppermute | solution.py:440

commit v12 on v11

--- a/solution.py
+++ b/solution.py
@@ -427,6 +427,7 @@
         while len(terms) > 1:
             terms = [a + b for a, b in zip(terms[::2], terms[1::2])]
         rows = terms[0]
+    rows = rows.astype(bf16)
     rows, input_grad, after = lax.optimization_barrier((rows, input_grad, after))
     input_grad, weight_grad = pl.pallas_call(
         edge_kernel,
@@ -436,7 +437,7 @@
         scratch_shapes=[wide, pltpu.VMEM((1,) + plane, bf16), pltpu.SemaphoreType.DMA((2,))],
         input_output_aliases={4: 0},
         compiler_params=params(),
-    )(weights, grads[1], after, rows, input_grad)
+    )(weights, grads[1], after, rows.astype(f32), input_grad)
     other = lax.ppermute(rows, "space", [(i, i ^ 1) for i in range(n_space)])
     weight_grad = pl.pallas_call(
         join_kernel,
@@ -446,7 +447,7 @@
         scratch_shapes=[pltpu.SemaphoreType.DMA],
         input_output_aliases={1: 0},
         compiler_params=params(),
-    )(other, weight_grad)
+    )(other.astype(f32), weight_grad)
     weight_grad = weight_grad.reshape(3, 3, 3, cb, out_ch).transpose(3, 0, 1, 2, 4)
     return pooled, input_grad, weight_grad
 

time: 39.7 us -> 39.7 us (level)
  transfers between devices with their start and end apart: 19 -> 19, of which waited for: 6 -> 5; matrix products, arithmetic and copies ran while one was open for 0% -> 0% of each run, Pallas kernels for 17% -> 17%
where the time goes in v12:
time: 39.7 us; the launch traced here: 39.5 us
  starting transfers between devices  25.1 us (63%)
  Pallas kernels  8.79 us (22%)
  waiting for transfers between devices  4.7 us (12%)
  between operations  0.8 us (2%)
    ppermute x12, starting transfers between devices, moved(): return lax.ppermute(block, axis, list(enumerate(to)))  19.5 us
    ppermute x3, starting transfers between devices, on_device(): lax.ppermute(sent, 'space', [(i, i ^ partners[k]) for i in range(n_space)])  3.55 us
    ppermute x3, waiting for transfers between devices, on_device(): lax.ppermute(sent, 'space', [(i, i ^ partners[k]) for i in range(n_space)])  2.21 us
    pallas_call x1, Pallas kernels, on_device(): pl.pallas_call(functools.partial(middle_kernel, n), out_specs=[vmem, vmem...  1.89 us
    pallas_call x1, Pallas kernels, on_device(): pl.pallas_call(input_kernel, in_specs=[vmem] * 3 + [hbm], out_specs=hbm,...  1.68 us
    ppermute x12, waiting for transfers between devices, moved(): return lax.ppermute(block, axis, list(enumerate(to)))  1.45 us
    pallas_call x2, Pallas kernels, on_device(): pl.pallas_call(functools.partial(fwd_kernel, n, ob, z), out_shape=[cols_s...  1.41 us
    ppermute x1, starting transfers between devices, on_device(): lax.ppermute(grads[0], 'space', [((i + 1) % n_space, i) for i in range(n_...  1.3 us
  transfers between devices with their start and end apart: 19, of which 5 were waited for; matrix products, arithmetic and copies ran while one was open for 0% of the time, Pallas kernels for 17%

profile of v12, /device:TPU:0, one launch (start us, length us, event | category | flops | bytes accessed | tf_op | source)
XLA Modules:
  0.0 39.5 jit_solution(14373618178675604699)
XLA Ops:
  0.6 1.1 %shard_map.59 = (bf16[32,4,16,128]{3,2,1,0:T(8,128)(2,1)S(1)}, bf16[32,1,16,128]{3,2,1,0:T(8,128)(2,1)S(1)}) custom-call(bf16[32,4,16,128]{3,2,1,0:T(8,128)(2,1)} %vol_hbm.1), custom_call_target="tpu_custom_call" | custom-call | tf_op jit(solution)/shard_map/pallas_call | solution.py:346
  1.8 0.5 %collective-permute-start = (bf16[32,1,16,128]{3,2,1,0:T(8,128)(2,1)S(1)}, bf16[32,1,16,128]{3,2,1,0:T(8,128)(2,1)S(1)}, u32[]{:S(2)}, u32[]{:S(2)}) collective-permute-start(bf16[32,1,16,128]{3,2,1,0:T(8,128)(2,1)S(1)} %get-tuple-element.34), channel_id=1, source_target_pairs={{0,4},{4,8},{8,12},{12,16},{16,20},{20,24},{24,28},{28,0},{1,5},{5... | collective-permute-start | bytes 393224 | tf_op jit(solution)/shard_map/ppermute | solution.py:353
  2.3 0.7 %shard_map.62 = (bf16[864,512]{1,0:T(8,128)(2,1)S(1)}, f32[32,512]{1,0:T(8,128)S(1)}, f32[32,512]{1,0:T(8,128)S(1)}, f32[32,512]{1,0:T(8,128)S(1)}, f32[32,512]{1,0:T(8,128)S(1)}) custom-call(bf16[32,4,16,128]{3,2,1,0:T(8,128)(2,1)S(1)} %get-tuple-element.35.refs_1_.refs_0_, bf16[864,128]{1,0:T(8,128)(2,1)S(1)} %bitcast.11), custom_call_target="tpu_custom_call" | custom-call | tf_op jit(solution)/shard_map/pallas_call | solution.py:355
  3.0 4.7 %collective-permute-start.4 = (f32[32,512]{1,0:T(8,128)S(1)}, f32[32,512]{1,0:T(8,128)S(1)}, u32[]{:S(2)}, u32[]{:S(2)}) collective-permute-start(f32[32,512]{1,0:T(8,128)S(1)} %get-tuple-element.42), channel_id=1, source_target_pairs={{0,3},{1,2},{2,1},{3,0},{4,7},{5,6},{6,5},{7,4},{8,11},{9,10},{10,... | collective-permute-start | bytes 196616 | tf_op jit(solution)/shard_map/ppermute | solution.py:312
  7.7 0.6 %collective-permute-start.6 = (f32[32,512]{1,0:T(8,128)S(1)}, f32[32,512]{1,0:T(8,128)S(1)}, u32[]{:S(2)}, u32[]{:S(2)}) collective-permute-start(f32[32,512]{1,0:T(8,128)S(1)} %get-tuple-element.44), channel_id=1, source_target_pairs={{0,1},{1,0},{2,3},{3,2},{4,5},{5,4},{6,7},{7,6},{8,9},{9,8},{10,11... | collective-permute-start | bytes 196616 | tf_op jit(solution)/shard_map/ppermute | solution.py:312
  8.3 0.7 %shard_map.60 = (bf16[864,512]{1,0:T(8,128)(2,1)S(1)}, f32[32,512]{1,0:T(8,128)S(1)}, f32[32,512]{1,0:T(8,128)S(1)}, f32[32,512]{1,0:T(8,128)S(1)}, f32[32,512]{1,0:T(8,128)S(1)}) custom-call(bf16[32,1,16,128]{3,2,1,0:T(8,128)(2,1)S(1)} %collective-permute-done.refs_0_, bf16[32,4,16,128]{3,2,1,0:T(8,128)(2,1)S(1)} %get-tuple-element.35.refs_1_.refs_0_, ...), custom_call_target="tpu_custom_call" | custom-call | tf_op jit(solution)/shard_map/pallas_call | solution.py:355
  9.0 3.9 %collective-permute-start.1 = (f32[32,512]{1,0:T(8,128)S(1)}, f32[32,512]{1,0:T(8,128)S(1)}, u32[]{:S(2)}, u32[]{:S(2)}) collective-permute-start(f32[32,512]{1,0:T(8,128)S(1)} %get-tuple-element.37), channel_id=1, source_target_pairs={{0,3},{1,2},{2,1},{3,0},{4,7},{5,6},{6,5},{7,4},{8,11},{9,10},{10,... | collective-permute-start | bytes 196616 | tf_op jit(solution)/shard_map/ppermute | solution.py:312
  12.9 2.0 %collective-permute-start.3 = (f32[32,512]{1,0:T(8,128)S(1)}, f32[32,512]{1,0:T(8,128)S(1)}, u32[]{:S(2)}, u32[]{:S(2)}) collective-permute-start(f32[32,512]{1,0:T(8,128)S(1)} %get-tuple-element.39), channel_id=1, source_target_pairs={{0,1},{1,3},{2,0},{3,2},{4,5},{5,7},{6,4},{7,6},{8,9},{9,11},{10,8... | collective-permute-start | bytes 196616 | tf_op jit(solution)/shard_map/ppermute | solution.py:312
  15.0 0.1 shard_map.58.spread_ref
  15.2 0.5 %collective-permute-start.7 = (bf16[32,512]{1,0:T(8,128)(2,1)S(1)}, bf16[32,512]{1,0:T(8,128)(2,1)S(1)}, u32[]{:S(2)}, u32[]{:S(2)}) collective-permute-start(bf16[32,512]{1,0:T(8,128)(2,1)S(1)} %get-tuple-element.47.refs_0_), channel_id=1, source_target_pairs={{0,1},{1,0},{2,3},{3,2},{4,5},{5,4},{6,7},{7,6},{8,9},{9,8},{10,11... | collective-permute-start | bytes 98312 | tf_op jit(solution)/shard_map/ppermute | solution.py:312
  15.7 1.9 %collective-permute-start.8 = (bf16[32,512]{1,0:T(8,128)(2,1)S(1)}, bf16[32,512]{1,0:T(8,128)(2,1)S(1)}, u32[]{:S(2)}, u32[]{:S(2)}) collective-permute-start(bf16[32,512]{1,0:T(8,128)(2,1)S(1)} %get-tuple-element.47.refs_0_), channel_id=1, source_target_pairs={{0,3},{1,2},{2,1},{3,0},{4,7},{5,6},{6,5},{7,4},{8,11},{9,10},{10,... | collective-permute-start | bytes 98312 | tf_op jit(solution)/shard_map/ppermute | solution.py:312
  17.6 1.1 %collective-permute-start.9 = (bf16[32,512]{1,0:T(8,128)(2,1)S(1)}, bf16[32,512]{1,0:T(8,128)(2,1)S(1)}, u32[]{:S(2)}, u32[]{:S(2)}) collective-permute-start(bf16[32,512]{1,0:T(8,128)(2,1)S(1)} %get-tuple-element.47.refs_0_), channel_id=1, source_target_pairs={{0,2},{1,3},{2,0},{3,1},{4,6},{5,7},{6,4},{7,5},{8,10},{9,11},{10,... | collective-permute-start | bytes 98312 | tf_op jit(solution)/shard_map/ppermute | solution.py:312
  18.7 1.0 %collective-permute-done.3.rest_3_ = f32[32,512]{1,0:T(8,128)S(1)} collective-permute-done((f32[32,512]{1,0:T(8,128)S(1)}, f32[32,512]{1,0:T(8,128)S(1)}, u32[]{:S(2)}, u32[]{:S(2)}) %collective-permute-start.3) | collective-permute-done | bytes 65568 | tf_op jit(solution)/shard_map/ppermute | solution.py:312
  19.8 1.0 %collective-permute-start.10 = (bf16[32,512]{1,0:T(8,128)(2,1)S(1)}, bf16[32,512]{1,0:T(8,128)(2,1)S(1)}, u32[]{:S(2)}, u32[]{:S(2)}) collective-permute-start(bf16[32,512]{1,0:T(8,128)(2,1)S(1)} %get-tuple-element.51.refs_0_), channel_id=1, source_target_pairs={{0,1},{1,3},{2,0},{3,2},{4,5},{5,7},{6,4},{7,6},{8,9},{9,11},{10,8... | collective-permute-start | bytes 98312 | tf_op jit(solution)/shard_map/ppermute | solution.py:312
  20.8 1.7 %collective-permute-start.11 = (bf16[32,512]{1,0:T(8,128)(2,1)S(1)}, bf16[32,512]{1,0:T(8,128)(2,1)S(1)}, u32[]{:S(2)}, u32[]{:S(2)}) collective-permute-start(bf16[32,512]{1,0:T(8,128)(2,1)S(1)} %get-tuple-element.51.refs_0_), channel_id=1, source_target_pairs={{0,3},{1,2},{2,1},{3,0},{4,7},{5,6},{6,5},{7,4},{8,11},{9,10},{10,... | collective-permute-start | bytes 98312 | tf_op jit(solution)/shard_map/ppermute | solution.py:312
  22.5 1.9 %collective-permute-start.12 = (bf16[32,512]{1,0:T(8,128)(2,1)S(1)}, bf16[32,512]{1,0:T(8,128)(2,1)S(1)}, u32[]{:S(2)}, u32[]{:S(2)}) collective-permute-start(bf16[32,512]{1,0:T(8,128)(2,1)S(1)} %get-tuple-element.51.refs_0_), channel_id=1, source_target_pairs={{0,2},{1,0},{2,3},{3,1},{4,6},{5,4},{6,7},{7,5},{8,10},{9,8},{10,1... | collective-permute-start | bytes 98312 | tf_op jit(solution)/shard_map/ppermute | solution.py:312
  24.5 1.9 %shard_map.64 = (f32[864,128]{1,0:T(8,128)S(1)}, bf16[128,512]{1,0:T(8,128)(2,1)S(1)}, bf16[32,1,4,32]{3,2,1,0:T(4,128)(2,1)}, bf16[32,4,16,128]{3,2,1,0:T(8,128)(2,1)}) custom-call(bf16[864,128]{1,0:T(8,128)(2,1)S(1)} %bitcast.13, f32[32,512]{1,0:T(8,128)S(1)} %get-tuple-element.40.act_one_ref, f32[32,512]{1,0:T(8,128)S(1)} %get-tuple-element.45.act_two_ref, ...), custom_call_target="tpu_custom_call" | custom-call | tf_op jit(solution)/shard_map/pallas_call | solution.py:377
  26.4 0.3 collective-permute-done.11.refs_2_
  26.6 0.1 collective-permute-done.12.refs_3_
  26.8 0.3 shard_map.65
  27.1 0.1 collective-permute-start.13
  27.1 0.3 shard_map.66
  27.4 1.0 %collective-permute-done.13 = bf16[432,128]{1,0:T(8,128)(2,1)S(1)} collective-permute-done((bf16[432,128]{1,0:T(8,128)(2,1)S(1)}, bf16[432,128]{1,0:T(8,128)(2,1)S(1)}, u32[]{:S(2)}, u32[]{:S(2)}) %collective-permute-start.13) | collective-permute-done | bytes 110624 | tf_op jit(solution)/shard_map/ppermute | solution.py:400
  28.5 1.6 %collective-permute-start.14 = (bf16[432,128]{1,0:T(8,128)(2,1)S(1)}, bf16[432,128]{1,0:T(8,128)(2,1)S(1)}, u32[]{:S(2)}, u32[]{:S(2)}) collective-permute-start(bf16[432,128]{1,0:T(8,128)(2,1)S(1)} %add_convert_fusion.1), channel_id=1, source_target_pairs={{0,8},{4,12},{8,0},{12,4},{16,24},{20,28},{24,16},{28,20},{1,9},{5... | collective-permute-start | bytes 331784 | tf_op jit(solution)/shard_map/ppermute | solution.py:412
  30.0 1.5 %collective-permute-start.15 = (bf16[432,128]{1,0:T(8,128)(2,1)S(1)}, bf16[432,128]{1,0:T(8,128)(2,1)S(1)}, u32[]{:S(2)}, u32[]{:S(2)}) collective-permute-start(bf16[432,128]{1,0:T(8,128)(2,1)S(1)} %add_convert_fusion.1), channel_id=1, source_target_pairs={{0,16},{4,20},{8,24},{12,28},{16,0},{20,4},{24,8},{28,12},{1,17},{... | collective-permute-start | bytes 331784 | tf_op jit(solution)/shard_map/ppermute | solution.py:412
  31.5 0.5 %collective-permute-start.16 = (bf16[432,128]{1,0:T(8,128)(2,1)S(1)}, bf16[432,128]{1,0:T(8,128)(2,1)S(1)}, u32[]{:S(2)}, u32[]{:S(2)}) collective-permute-start(bf16[432,128]{1,0:T(8,128)(2,1)S(1)} %add_convert_fusion.1), channel_id=1, source_target_pairs={{0,24},{4,28},{8,16},{12,20},{16,8},{20,12},{24,0},{28,4},{1,25},{... | collective-permute-start | bytes 331784 | tf_op jit(solution)/shard_map/ppermute | solution.py:412
  32.0 1.3 %collective-permute-start.17 = (bf16[128,512]{1,0:T(8,128)(2,1)S(1)}, bf16[128,512]{1,0:T(8,128)(2,1)S(1)}, u32[]{:S(2)}, u32[]{:S(2)}) collective-permute-start(bf16[128,512]{1,0:T(8,128)(2,1)S(1)} %get-tuple-element.58.grad_ref.one_ref), channel_id=1, source_target_pairs={{4,0},{8,4},{12,8},{16,12},{20,16},{24,20},{28,24},{0,28},{5,1},{9... | collective-permute-start | bytes 393224 | tf_op jit(solution)/shard_map/ppermute | solution.py:416
  33.3 1.7 %shard_map.67._ = bf16[32,4,16,128]{3,2,1,0:T(8,128)(2,1)} custom-call(bf16[864,128]{1,0:T(8,128)(2,1)S(1)} %bitcast.14, bf16[128,512]{1,0:T(8,128)(2,1)S(1)} %get-tuple-element.58.grad_ref.one_ref, bf16[128,512]{1,0:T(8,128)(2,1)S(1)} %get-tuple-element.56.two_ref.one_ref, bf16[32,4,16,128]{3,2,1,0:T(8,128)(2,1)} %get-tuple-element.59._), custom_call_target="tpu_custom_call", output_to_operand_aliasing={{}: (3, {})} | custom-call | tf_op jit(solution)/shard_map/pallas_call | solution.py:417
  35.0 2.2 %collective-permute-done.15 = bf16[432,128]{1,0:T(8,128)(2,1)S(1)} collective-permute-done((bf16[432,128]{1,0:T(8,128)(2,1)S(1)}, bf16[432,128]{1,0:T(8,128)(2,1)S(1)}, u32[]{:S(2)}, u32[]{:S(2)}) %collective-permute-start.15) | collective-permute-done | bytes 110624 | tf_op jit(solution)/shard_map/ppermute | solution.py:412
  37.3 0.2 collective-permute-start.18
  37.5 1.3 %shard_map.68 = (bf16[32,4,16,128]{3,2,1,0:T(8,128)(2,1)}, f32[864,128]{1,0:T(8,128)}) custom-call(bf16[864,128]{1,0:T(8,128)(2,1)S(1)} %bitcast.15, bf16[128,512]{1,0:T(8,128)(2,1)S(1)} %get-tuple-element.56.two_ref.one_ref, bf16[128,512]{1,0:T(8,128)(2,1)S(1)} %collective-permute-done.17.two_ref, ...), custom_call_target="tpu_custom_call", output_to_operand_aliasing={{0}: (4, {})} | custom-call | tf_op jit(solution)/shard_map/pallas_call | solution.py:432
  38.8 0.7 %shard_map.69 = f32[864,128]{1,0:T(8,128)} custom-call(f32[432,128]{1,0:T(8,128)S(1)} %convert_element_type.35.other_ref, f32[864,128]{1,0:T(8,128)} %get-tuple-element.64._), custom_call_target="tpu_custom_call", output_to_operand_aliasing={{}: (1, {})} | custom-call | tf_op jit(solution)/shard_map/pallas_call | solution.py:442
  (27 shorter events, 0.2 us)
Async XLA Ops:
  0.6 1.6 %copy-start = (bf16[32,3,3,3,128]{4,0,3,2,1:T(8,128)(2,1)S(1)}, bf16[32,3,3,3,128]{4,0,3,2,1:T(8,128)(2,1)}, u32[]{:S(2)}) copy-start(bf16[32,3,3,3,128]{4,0,3,2,1:T(8,128)(2,1)} %param.4) | copy-start | bytes 663556
  1.8 6.6 %collective-permute-start = (bf16[32,1,16,128]{3,2,1,0:T(8,128)(2,1)S(1)}, bf16[32,1,16,128]{3,2,1,0:T(8,128)(2,1)S(1)}, u32[]{:S(2)}, u32[]{:S(2)}) collective-permute-start(bf16[32,1,16,128]{3,2,1,0:T(8,128)(2,1)S(1)} %get-tuple-element.34), channel_id=1, source_target_pairs={{0,4},{4,8},{8,12},{12,16},{16,20},{20,24},{24,28},{28,0},{1,5},{5... | collective-permute-start | bytes 393224 | tf_op jit(solution)/shard_map/ppermute | solution.py:353
  3.0 9.9 %collective-permute-start.4 = (f32[32,512]{1,0:T(8,128)S(1)}, f32[32,512]{1,0:T(8,128)S(1)}, u32[]{:S(2)}, u32[]{:S(2)}) collective-permute-start(f32[32,512]{1,0:T(8,128)S(1)} %get-tuple-element.42), channel_id=1, source_target_pairs={{0,3},{1,2},{2,1},{3,0},{4,7},{5,6},{6,5},{7,4},{8,11},{9,10},{10,... | collective-permute-start | bytes 196616 | tf_op jit(solution)/shard_map/ppermute | solution.py:312
  7.7 7.4 %collective-permute-start.5 = (f32[32,512]{1,0:T(8,128)S(1)}, f32[32,512]{1,0:T(8,128)S(1)}, u32[]{:S(2)}, u32[]{:S(2)}) collective-permute-start(f32[32,512]{1,0:T(8,128)S(1)} %get-tuple-element.43), channel_id=1, source_target_pairs={{0,2},{1,3},{2,0},{3,1},{4,6},{5,7},{6,4},{7,5},{8,10},{9,11},{10,... | collective-permute-start | bytes 196616 | tf_op jit(solution)/shard_map/ppermute | solution.py:312
  7.7 7.3 %copy-start.1 = (bf16[32,1,4,32]{3,2,1,0:T(4,128)(2,1)S(1)}, bf16[32,1,4,32]{3,2,1,0:T(4,128)(2,1)}, u32[]{:S(2)}) copy-start(bf16[32,1,4,32]{3,2,1,0:T(4,128)(2,1)} %param.5) | copy-start | bytes 24580
  7.7 7.4 %collective-permute-start.6 = (f32[32,512]{1,0:T(8,128)S(1)}, f32[32,512]{1,0:T(8,128)S(1)}, u32[]{:S(2)}, u32[]{:S(2)}) collective-permute-start(f32[32,512]{1,0:T(8,128)S(1)} %get-tuple-element.44), channel_id=1, source_target_pairs={{0,1},{1,0},{2,3},{3,2},{4,5},{5,4},{6,7},{7,6},{8,9},{9,8},{10,11... | collective-permute-start | bytes 196616 | tf_op jit(solution)/shard_map/ppermute | solution.py:312
  9.0 8.6 %collective-permute-start.1 = (f32[32,512]{1,0:T(8,128)S(1)}, f32[32,512]{1,0:T(8,128)S(1)}, u32[]{:S(2)}, u32[]{:S(2)}) collective-permute-start(f32[32,512]{1,0:T(8,128)S(1)} %get-tuple-element.37), channel_id=1, source_target_pairs={{0,3},{1,2},{2,1},{3,0},{4,7},{5,6},{6,5},{7,4},{8,11},{9,10},{10,... | collective-permute-start | bytes 196616 | tf_op jit(solution)/shard_map/ppermute | solution.py:312
  12.9 5.8 %collective-permute-start.2 = (f32[32,512]{1,0:T(8,128)S(1)}, f32[32,512]{1,0:T(8,128)S(1)}, u32[]{:S(2)}, u32[]{:S(2)}) collective-permute-start(f32[32,512]{1,0:T(8,128)S(1)} %get-tuple-element.38), channel_id=1, source_target_pairs={{0,2},{1,0},{2,3},{3,1},{4,6},{5,4},{6,7},{7,5},{8,10},{9,8},{10,1... | collective-permute-start | bytes 196616 | tf_op jit(solution)/shard_map/ppermute | solution.py:312
  12.9 6.8 %collective-permute-start.3 = (f32[32,512]{1,0:T(8,128)S(1)}, f32[32,512]{1,0:T(8,128)S(1)}, u32[]{:S(2)}, u32[]{:S(2)}) collective-permute-start(f32[32,512]{1,0:T(8,128)S(1)} %get-tuple-element.39), channel_id=1, source_target_pairs={{0,1},{1,3},{2,0},{3,2},{4,5},{5,7},{6,4},{7,6},{8,9},{9,11},{10,8... | collective-permute-start | bytes 196616 | tf_op jit(solution)/shard_map/ppermute | solution.py:312
  15.2 7.3 %collective-permute-start.7 = (bf16[32,512]{1,0:T(8,128)(2,1)S(1)}, bf16[32,512]{1,0:T(8,128)(2,1)S(1)}, u32[]{:S(2)}, u32[]{:S(2)}) collective-permute-start(bf16[32,512]{1,0:T(8,128)(2,1)S(1)} %get-tuple-element.47.refs_0_), channel_id=1, source_target_pairs={{0,1},{1,0},{2,3},{3,2},{4,5},{5,4},{6,7},{7,6},{8,9},{9,8},{10,11... | collective-permute-start | bytes 98312 | tf_op jit(solution)/shard_map/ppermute | solution.py:312
  15.7 8.8 %collective-permute-start.8 = (bf16[32,512]{1,0:T(8,128)(2,1)S(1)}, bf16[32,512]{1,0:T(8,128)(2,1)S(1)}, u32[]{:S(2)}, u32[]{:S(2)}) collective-permute-start(bf16[32,512]{1,0:T(8,128)(2,1)S(1)} %get-tuple-element.47.refs_0_), channel_id=1, source_target_pairs={{0,3},{1,2},{2,1},{3,0},{4,7},{5,6},{6,5},{7,4},{8,11},{9,10},{10,... | collective-permute-start | bytes 98312 | tf_op jit(solution)/shard_map/ppermute | solution.py:312
  17.6 6.9 %collective-permute-start.9 = (bf16[32,512]{1,0:T(8,128)(2,1)S(1)}, bf16[32,512]{1,0:T(8,128)(2,1)S(1)}, u32[]{:S(2)}, u32[]{:S(2)}) collective-permute-start(bf16[32,512]{1,0:T(8,128)(2,1)S(1)} %get-tuple-element.47.refs_0_), channel_id=1, source_target_pairs={{0,2},{1,3},{2,0},{3,1},{4,6},{5,7},{6,4},{7,5},{8,10},{9,11},{10,... | collective-permute-start | bytes 98312 | tf_op jit(solution)/shard_map/ppermute | solution.py:312
  19.8 6.6 %collective-permute-start.10 = (bf16[32,512]{1,0:T(8,128)(2,1)S(1)}, bf16[32,512]{1,0:T(8,128)(2,1)S(1)}, u32[]{:S(2)}, u32[]{:S(2)}) collective-permute-start(bf16[32,512]{1,0:T(8,128)(2,1)S(1)} %get-tuple-element.51.refs_0_), channel_id=1, source_target_pairs={{0,1},{1,3},{2,0},{3,2},{4,5},{5,7},{6,4},{7,6},{8,9},{9,11},{10,8... | collective-permute-start | bytes 98312 | tf_op jit(solution)/shard_map/ppermute | solution.py:312
  20.8 5.8 %collective-permute-start.11 = (bf16[32,512]{1,0:T(8,128)(2,1)S(1)}, bf16[32,512]{1,0:T(8,128)(2,1)S(1)}, u32[]{:S(2)}, u32[]{:S(2)}) collective-permute-start(bf16[32,512]{1,0:T(8,128)(2,1)S(1)} %get-tuple-element.51.refs_0_), channel_id=1, source_target_pairs={{0,3},{1,2},{2,1},{3,0},{4,7},{5,6},{6,5},{7,4},{8,11},{9,10},{10,... | collective-permute-start | bytes 98312 | tf_op jit(solution)/shard_map/ppermute | solution.py:312
  22.5 4.3 %collective-permute-start.12 = (bf16[32,512]{1,0:T(8,128)(2,1)S(1)}, bf16[32,512]{1,0:T(8,128)(2,1)S(1)}, u32[]{:S(2)}, u32[]{:S(2)}) collective-permute-start(bf16[32,512]{1,0:T(8,128)(2,1)S(1)} %get-tuple-element.51.refs_0_), channel_id=1, source_target_pairs={{0,2},{1,0},{2,3},{3,1},{4,6},{5,4},{6,7},{7,5},{8,10},{9,8},{10,1... | collective-permute-start | bytes 98312 | tf_op jit(solution)/shard_map/ppermute | solution.py:312
  27.1 1.4 %collective-permute-start.13 = (bf16[432,128]{1,0:T(8,128)(2,1)S(1)}, bf16[432,128]{1,0:T(8,128)(2,1)S(1)}, u32[]{:S(2)}, u32[]{:S(2)}) collective-permute-start(bf16[432,128]{1,0:T(8,128)(2,1)S(1)} %get-tuple-element.53), channel_id=1, source_target_pairs={{0,4},{4,0},{8,12},{12,8},{16,20},{20,16},{24,28},{28,24},{1,5},{5... | collective-permute-start | bytes 331784 | tf_op jit(solution)/shard_map/ppermute | solution.py:400
  28.5 6.5 %collective-permute-start.14 = (bf16[432,128]{1,0:T(8,128)(2,1)S(1)}, bf16[432,128]{1,0:T(8,128)(2,1)S(1)}, u32[]{:S(2)}, u32[]{:S(2)}) collective-permute-start(bf16[432,128]{1,0:T(8,128)(2,1)S(1)} %add_convert_fusion.1), channel_id=1, source_target_pairs={{0,8},{4,12},{8,0},{12,4},{16,24},{20,28},{24,16},{28,20},{1,9},{5... | collective-permute-start | bytes 331784 | tf_op jit(solution)/shard_map/ppermute | solution.py:412
  30.0 7.2 %collective-permute-start.15 = (bf16[432,128]{1,0:T(8,128)(2,1)S(1)}, bf16[432,128]{1,0:T(8,128)(2,1)S(1)}, u32[]{:S(2)}, u32[]{:S(2)}) collective-permute-start(bf16[432,128]{1,0:T(8,128)(2,1)S(1)} %add_convert_fusion.1), channel_id=1, source_target_pairs={{0,16},{4,20},{8,24},{12,28},{16,0},{20,4},{24,8},{28,12},{1,17},{... | collective-permute-start | bytes 331784 | tf_op jit(solution)/shard_map/ppermute | solution.py:412
  31.5 5.7 %collective-permute-start.16 = (bf16[432,128]{1,0:T(8,128)(2,1)S(1)}, bf16[432,128]{1,0:T(8,128)(2,1)S(1)}, u32[]{:S(2)}, u32[]{:S(2)}) collective-permute-start(bf16[432,128]{1,0:T(8,128)(2,1)S(1)} %add_convert_fusion.1), channel_id=1, source_target_pairs={{0,24},{4,28},{8,16},{12,20},{16,8},{20,12},{24,0},{28,4},{1,25},{... | collective-permute-start | bytes 331784 | tf_op jit(solution)/shard_map/ppermute | solution.py:412
  32.0 5.3 %collective-permute-start.17 = (bf16[128,512]{1,0:T(8,128)(2,1)S(1)}, bf16[128,512]{1,0:T(8,128)(2,1)S(1)}, u32[]{:S(2)}, u32[]{:S(2)}) collective-permute-start(bf16[128,512]{1,0:T(8,128)(2,1)S(1)} %get-tuple-element.58.grad_ref.one_ref), channel_id=1, source_target_pairs={{4,0},{8,4},{12,8},{16,12},{20,16},{24,20},{28,24},{0,28},{5,1},{9... | collective-permute-start | bytes 393224 | tf_op jit(solution)/shard_map/ppermute | solution.py:416
  37.3 1.4 %collective-permute-start.18 = (bf16[432,128]{1,0:T(8,128)(2,1)S(1)}, bf16[432,128]{1,0:T(8,128)(2,1)S(1)}, u32[]{:S(2)}, u32[]{:S(2)}) collective-permute-start(bf16[432,128]{1,0:T(8,128)(2,1)S(1)} %add_convert_fusion), channel_id=1, source_target_pairs={{0,4},{4,0},{8,12},{12,8},{16,20},{20,16},{24,28},{28,24},{1,5},{5... | collective-permute-start | bytes 331784 | tf_op jit(solution)/shard_map/ppermute | solution.py:441
